TPU v7x, 256 devices: a whole 4x4x8 slice. The times are simulated.
256 devices in a mesh: tm: 16 (over x, z_lo, core), space: 16 (over z_hi, y).
Axes of the slice: x: 4, y: 4, z: 8 (z_hi: 4, z_lo: 2; z = z_hi * 2 + z_lo), core: 2. Of those that a mesh axis runs over, the one named last changes fastest.
Arguments:
- activations: bfloat16 [32, 32, 192, 512], P('tm', 'space'), may hold values from -6 to 6
- cotangent: bfloat16 [32, 32, 192, 512], P('tm', 'space'), may hold values from -6 to 6
- spatial_kernel: bfloat16 [512, 9, 512], P('space'), may hold values from -0.09375 to 0.09375
- temporal_kernel: bfloat16 [512, 3, 512], P('space'), may hold values from -0.15625 to 0.15625
Outputs:
- grad_input: float32 [32, 32, 192, 512], P('tm', 'space')
- grad_spatial: float32 [512, 9, 512], P('space')
- grad_temporal: float32 [512, 3, 512], P('space')
All inputs are finite; a program needn't handle non-finite values.
Results may differ from a plain program's by a relative error of at most 0.0029.
Values may be sent and summed in bfloat16 or wider, within the bound.
No kernel may reach another device: no remote copies, remote signals or barrier semaphores. Data moves between devices by JAX's collectives and lax.ppermute only.
A program may use at most 128 MiB of HBM per device.

v0:
```python
import functools
import math

import jax
import jax.numpy as jnp
from jax import lax
from jax.experimental import pallas as pl
from jax.experimental.pallas import tpu as pltpu
from jax.sharding import Mesh, PartitionSpec as P

TM = ("x", "zl", "core")
SPACE = ("zh", "y")
PAIR = [(0, 1), (1, 0)]
ORDER = ((1, 3), (3, 1))
VMEM = pl.BlockSpec(memory_space=pltpu.VMEM)
ANY = pl.BlockSpec(memory_space=pl.ANY)
SMEM = pl.BlockSpec(memory_space=pltpu.SMEM)
PARAMS = pltpu.CompilerParams(vmem_limit_bytes=40 * 1024 * 1024)


def swap(block):
    return lax.ppermute(block, "core", PAIR)


def exchange(block, axis, stage):
    if axis == "x":
        names, number = ("x", "core"), lambda core, p: 2 * p + core
    else:
        names, number = ("core", axis), lambda core, p: 4 * core + p
    pairs = [
        (number(core, p), number(core, p ^ ORDER[core][stage]))
        for core in range(2)
        for p in range(4)
    ]
    return lax.ppermute(block, names, pairs)


def positions(axis):
    p = lax.axis_index(axis)
    core = lax.axis_index("core")
    return p, p ^ (1 + 2 * core), p ^ (3 - 2 * core), p ^ 2


def slots_of(axis):
    own, first, second, far = positions(axis)
    q = jnp.arange(4, dtype=jnp.int32)
    return jnp.where(q == own, 0, jnp.where(q == second, 1, jnp.where(q == first, 2, 3)))


def ring_scatter(terms, sent, axis):
    came = exchange(sent, axis, 0).astype(jnp.float32)
    passed = (terms[1] + came[1]).astype(sent.dtype)
    return terms[0] + came[0] + exchange(passed, axis, 1).astype(jnp.float32)


def ring_first(block, axis):
    return block, exchange(block, axis, 0)


def ring_second(pair, axis):
    rest = exchange(jnp.stack(pair), axis, 1)
    return list(zip(positions(axis), (*pair, rest[0], rest[1])))


def placed(target, slots, dim, *fixed):
    for index, block in slots:
        start = [0] * target.ndim
        for where, value in fixed:
            start[where] = value
        start[dim] = index
        target = lax.dynamic_update_slice(target, jnp.expand_dims(block, dim), start)
    return target


def gathered(block, axis):
    spread = jnp.broadcast_to(block[None], (lax.axis_size(axis),) + block.shape)
    return lax.all_to_all(spread, axis, 0, 0, tiled=True)


def scattered(block, axis):
    return jnp.sum(lax.all_to_all(block, axis, 0, 0, tiled=True).astype(jnp.float32), axis=0)


def halo(block, axis, dim):
    count = lax.axis_size(axis)
    forward = [(i, i + 1) for i in range(count - 1)]
    backward = [(target, source) for source, target in forward]
    size = block.shape[dim]
    low = lax.ppermute(lax.slice_in_dim(block, size - 1, size, axis=dim), axis, forward)
    high = lax.ppermute(lax.slice_in_dim(block, 0, 1, axis=dim), axis, backward)
    return jnp.concatenate([low, block, high], axis=dim)


def column_shifts(maps):
    edge = jnp.zeros_like(maps[:, :, :1])
    return jnp.stack(
        [
            jnp.concatenate([edge, maps[:, :, :-1]], axis=2),
            maps,
            jnp.concatenate([maps[:, :, 1:], edge], axis=2),
        ]
    )


def lanes(index, half):
    return pl.ds(pl.multiple_of(index * half, half), half)


def add_terms(index, x_ref, cot_ref, kernel_hbm, kernel_ref, sems, pre_ref, slope_ref, start_ref):
    frames, block, chans = pre_ref.shape
    half = chans // 2
    copies = []
    for group in range(4):
        taps = pl.ds(3 * group, 3)
        copies.append(
            pltpu.make_async_copy(kernel_hbm.at[taps], kernel_ref.at[taps], sems.at[group])
        )
        copies[group].start()

    def convolve(f, _, a):
        if a > 0:
            total = pre_ref[f]
        elif start_ref is not None:
            total = start_ref[f]
        else:
            total = jnp.zeros((block, chans), jnp.float32)
        for b in range(3):
            piece = x_ref[b, f, a : a + 2, :, lanes(index, half)].reshape(block, half)
            total += lax.dot_general(
                piece,
                kernel_ref[3 * a + b],
                (((1,), (1,)), ((), ())),
                preferred_element_type=jnp.float32,
            )
        pre_ref[f] = total
        return 0

    def blend(f, _):
        total = jnp.zeros((block, half), jnp.float32)
        for k in range(3):
            piece = cot_ref[2 - k + f].reshape(block, chans)
            total += jnp.dot(piece, kernel_ref[9 + k], preferred_element_type=jnp.float32)
        slope_ref[f] = total
        return 0

    for a in range(3):
        copies[a].wait()
        lax.fori_loop(0, frames, functools.partial(convolve, a=a), 0)
    copies[3].wait()
    lax.fori_loop(0, frames, blend, 0)


def first_kernel(core_ref, x_ref, cot_ref, kernel_hbm, pre_ref, slope_ref, kernel_ref, sems):
    add_terms(
        core_ref[0], x_ref, cot_ref, kernel_hbm, kernel_ref, sems, pre_ref, slope_ref, None
    )


def second_kernel(
    core_ref,
    x_ref,
    cot_ref,
    kernel_hbm,
    start_ref,
    mine_ref,
    hid_mine_ref,
    hid_other_ref,
    slope_ref,
    turned_ref,
    pre_ref,
    other_ref,
    work_ref,
    kernel_ref,
    sems,
):
    core = core_ref[0]
    add_terms(
        1 - core, x_ref, cot_ref, kernel_hbm, kernel_ref, sems, pre_ref, other_ref, start_ref
    )
    frames, block, chans = pre_ref.shape
    half = chans // 2
    part = 32
    for hid_ref, source_ref, index in (
        (hid_mine_ref, mine_ref, core),
        (hid_other_ref, other_ref, 1 - core),
    ):

        def finish(step, _, hid_ref=hid_ref, source_ref=source_ref, index=index):
            f, r = step // (block // part), step % (block // part)
            rows = pl.ds(pl.multiple_of(r * part, part), part)
            pre = pre_ref[f, rows, lanes(index, half)]
            sigma = 1.0 / (1.0 + jnp.exp(-pre))
            hid_ref[f, rows] = (pre * sigma).astype(jnp.bfloat16)
            slope = source_ref[f, rows] * sigma * (1.0 + pre * (1.0 - sigma))
            work_ref[f, rows, lanes(index, half)] = slope
            return 0

        lax.fori_loop(0, frames * (block // part), finish, 0)
    for f in range(frames):
        slope = work_ref[f].astype(jnp.bfloat16)
        slope_ref[f] = slope
        turned_ref[:, f * block : (f + 1) * block] = slope.T


def forward(core, shifts, cot_pad, k_mine, k_other):
    frames, _, width, chans = shifts.shape[1:]
    block = 2 * width
    half = chans // 2
    full = jax.ShapeDtypeStruct((frames, block, chans), jnp.float32)
    part = jax.ShapeDtypeStruct((frames, block, half), jnp.float32)
    held = [pltpu.VMEM(k_mine.shape, k_mine.dtype), pltpu.SemaphoreType.DMA((4,))]
    pre, mine = pl.pallas_call(
        first_kernel,
        out_shape=(full, part),
        in_specs=[SMEM, VMEM, VMEM, ANY],
        out_specs=(VMEM, VMEM),
        scratch_shapes=held,
        compiler_params=PARAMS,
        cost_estimate=pl.CostEstimate(flops=3200000000, bytes_accessed=12000000, transcendentals=0),
    )(core, shifts, cot_pad, k_mine)
    hid = jax.ShapeDtypeStruct((frames, block, half), jnp.bfloat16)
    return pl.pallas_call(
        second_kernel,
        out_shape=(
            hid,
            hid,
            jax.ShapeDtypeStruct((frames, block, chans), jnp.bfloat16),
            jax.ShapeDtypeStruct((chans, frames * block), jnp.bfloat16),
        ),
        in_specs=[SMEM, VMEM, VMEM, ANY, VMEM, VMEM],
        out_specs=(VMEM,) * 4,
        scratch_shapes=[
            pltpu.VMEM(full.shape, jnp.float32),
            pltpu.VMEM(part.shape, jnp.float32),
            pltpu.VMEM(full.shape, jnp.float32),
        ]
        + held,
        compiler_params=PARAMS,
        cost_estimate=pl.CostEstimate(flops=3200000000, bytes_accessed=15000000, transcendentals=0),
    )(core, shifts, cot_pad, k_other, pre, mine)


def weight_kernel(
    upper,
    info_ref,
    turned_ref,
    turned_pair_ref,
    x_ref,
    x_pair_ref,
    cot_ref,
    cot_pair_ref,
    hid_ref,
    hid_pair_ref,
    terms_ref,
    sent_ref,
):
    half = x_pair_ref.shape[-1]
    count = turned_ref.shape[1]
    block = count // 2
    own = terms_ref.shape[-2]
    outs = pl.ds(half * upper, half)

    def keep(total, group, b):
        for zh in range(2):
            for y in range(4):
                row = (4 * zh + y) * own
                if upper:
                    terms_ref[info_ref[1 + y], group, b, zh] = total[row : row + own]
                else:
                    terms_ref[info_ref[1 + group], y, b, zh] = total[row : row + own]

    def spatial(a, _):
        for b in range(3):
            piece = x_ref[b, :, pl.ds(a, 2), :, lanes(info_ref[0], half)].reshape(count, half)
            total = jnp.dot(turned_ref[outs], piece, preferred_element_type=jnp.float32)
            piece = x_pair_ref[b, :, pl.ds(a, 2)].reshape(count, half)
            total += jnp.dot(turned_pair_ref[outs], piece, preferred_element_type=jnp.float32)
            keep(total, a, b)
        return 0

    lax.fori_loop(0, 3, spatial, 0)
    for k in range(3):
        piece = cot_ref[outs, (2 - k) * block : (4 - k) * block]
        total = jnp.dot(piece, hid_ref[...], preferred_element_type=jnp.float32)
        piece = cot_pair_ref[outs, (2 - k) * block : (4 - k) * block]
        total += jnp.dot(piece, hid_pair_ref[...], preferred_element_type=jnp.float32)
        keep(total, 3, k)
    for slot in range(2):
        for i in range(4):
            sent_ref[slot, i] = terms_ref[2 + slot, i].astype(jnp.bfloat16)


def weight_terms(upper, own, info, *operands):
    half = operands[-1].shape[-1]
    shape = (4, 4, 3, 2, own, half)
    return pl.pallas_call(
        functools.partial(weight_kernel, upper),
        out_shape=(
            jax.ShapeDtypeStruct(shape, jnp.float32),
            jax.ShapeDtypeStruct((2,) + shape[1:], jnp.bfloat16),
        ),
        in_specs=[SMEM] + [VMEM] * 8,
        out_specs=(VMEM, VMEM),
        compiler_params=PARAMS,
        cost_estimate=pl.CostEstimate(flops=2400000000, bytes_accessed=16000000, transcendentals=0),
    )(info, *operands)


def kernel_unit(spatial_kernel, temporal_kernel, half):
    both = jnp.concatenate(
        [spatial_kernel.transpose(1, 0, 2), temporal_kernel.transpose(1, 0, 2)], axis=0
    )
    start = (3 * lax.axis_index("x"), 0, lax.axis_index("core") * half)
    unit = lax.dynamic_slice(both, start, (3, both.shape[1], half))
    return gathered(unit, "zh").transpose(1, 0, 2, 3)


def kernel_half(unit, waited):
    own, half = unit.shape[-2:]
    lower = gathered(unit[:, :2], "y").transpose(1, 2, 0, 3, 4)
    upper = gathered(unit[:, 2:], "x")
    lower, upper, waited = lax.optimization_barrier(
        (ring_first(lower, "x"), ring_first(upper, "y"), waited)
    )
    whole = jnp.zeros((4, 3, 4, 4, own, half), unit.dtype)
    whole = placed(whole, ring_second(lower, "x"), 0)
    whole = placed(whole, ring_second(upper, "y"), 3, (2, 2))
    return whole.reshape(12, 16 * own, half), waited


def per_device(activations, cotangent, spatial_kernel, temporal_kernel):
    frames, rows, width, chans = activations.shape
    count = frames * rows * width
    half = chans // 2
    core = lax.axis_index("core")
    own = spatial_kernel.shape[0]
    core_info = core.astype(jnp.int32).reshape(1)

    unit = kernel_unit(spatial_kernel, temporal_kernel, half)
    edges = (activations, cotangent)
    edges, unit = lax.optimization_barrier((edges, unit))
    x_wide = halo(edges[0], SPACE, 1)
    cot_pad = halo(edges[1], TM, 0)
    k_mine, (x_wide, cot_pad) = kernel_half(unit, (x_wide, cot_pad))
    x_pair = swap(lax.dynamic_slice_in_dim(x_wide, (1 - core) * half, half, axis=3))
    shifts = column_shifts(x_wide)
    shifts_pair = column_shifts(x_pair)
    cot_turned = cot_pad.reshape((frames + 2) * rows * width, chans).T
    cot_turned_pair = swap(cot_turned)
    k_mine, shifts, cot_turned = lax.optimization_barrier((k_mine, shifts, cot_turned))
    k_other = swap(k_mine)

    hid_mine, hid_other, slope_pre, turned = forward(core_info, shifts, cot_pad, k_mine, k_other)
    turned_pair = swap(turned)
    operands = (
        turned,
        turned_pair,
        shifts,
        shifts_pair,
        cot_turned,
        cot_turned_pair,
        hid_mine.reshape(count, half),
        swap(hid_other).reshape(count, half),
    )
    info = jnp.concatenate([core_info, slots_of("x")])
    lower, sent_lower = weight_terms(0, own, info, *operands)
    info = jnp.concatenate([core_info, slots_of("y")])
    upper, sent_upper = weight_terms(1, own, info, *operands)
    slope_pre, _ = lax.optimization_barrier((slope_pre, sent_upper))

    lower = ring_scatter(lower, sent_lower, "x")
    upper = ring_scatter(upper, sent_upper, "y")
    lower = scattered(lower, "y")
    upper = scattered(upper, "x")
    terms = jnp.concatenate([lower, upper], axis=1)
    terms = terms.reshape(3, 4, 2, own // 2, half).transpose(1, 2, 0, 3, 4)
    terms = scattered(terms.reshape(8, 3, own // 2, half), ("zh", "zl"))
    pixels = count * lax.axis_size(TM) * lax.axis_size(SPACE)
    terms = gathered(terms * (1.0 / math.sqrt(pixels)), TM)
    terms = terms.reshape(4, 2, 2, 3, own // 2, half).transpose(1, 4, 0, 3, 2, 5)
    terms = terms.reshape(own, 12, chans)

    slope_maps = halo(slope_pre.reshape(frames, rows, width, chans), SPACE, 1)
    slope_pad = jnp.pad(slope_maps, ((0, 0), (0, 0), (1, 1), (0, 0)))
    grads = []
    for kernel in (k_mine, k_other):
        total = jnp.zeros((count, half), jnp.float32)
        for tap in range(9):
            a, b = 2 - tap // 3, 2 - tap % 3
            piece = slope_pad[:, a : a + rows, b : b + width].reshape(count, chans)
            total = total + jnp.dot(piece, kernel[tap], preferred_element_type=jnp.float32)
        grads.append(total)
    grad = jnp.where(
        core == 0, jnp.concatenate(grads, axis=1), jnp.concatenate(grads[::-1], axis=1)
    )
    grad = grad + cotangent.reshape(count, chans).astype(jnp.float32)
    return grad.reshape(frames, rows, width, chans), terms[:, :9], terms[:, 9:]


def solution(mesh):
    split = Mesh(mesh.devices.reshape(4, 2, 2, 4, 4), TM + SPACE)
    maps = P(TM, SPACE, None, None)
    kernels = P(SPACE, None, None)
    return jax.shard_map(
        per_device,
        mesh=split,
        in_specs=(maps, maps, kernels, kernels),
        out_specs=(maps, kernels, kernels),
        check_vma=False,
    )
```

profile of v0, /device:TPU:1, one launch (start us, length us, event | category | flops | bytes accessed | tf_op | source)
XLA Modules:
  0.0 240.4 jit_solution(16472193307149289108)
XLA Ops:
  1.6 16.8 %all_to_all.35 = bf16[4,3,32,256]{3,2,1,0:T(8,128)(2,1)S(1)} all-to-all(bf16[4,3,32,256]{3,2,1,0:T(8,128)(2,1)S(1)} %broadcast_in_dim.61), channel_id=1, replica_groups=mesh['x'=4,'zl'=2,'core'=2,'zh'=4,'y'=4] {'zh'}, dimensions={0} | all-to-all | bytes 393216 | tf_op jit(solution)/shard_map/all_to_all | solution.py:77
  19.3 4.2 %all-to-all-start.1 = ((bf16[4,3,2,32,256]{4,3,2,1,0:T(8,128)(2,1)}), bf16[4,3,2,32,256]{4,3,2,1,0:T(8,128)(2,1)S(1)}, u32[]{:S(2)}, u32[]{:S(2)}) async-start(bf16[4,3,2,32,256]{4,3,2,1,0:T(8,128)(2,1)} %broadcast_in_dim.62), calls=%async_computation.1 | async-start | bytes 786432 | tf_op jit(solution)/shard_map/all_to_all | solution.py:77
  24.4 3.4 %collective-permute-start.2 = (bf16[2,1,192,512]{3,2,1,0:T(8,128)(2,1)}, bf16[2,1,192,512]{3,2,1,0:T(8,128)(2,1)S(1)}, u32[]{:S(2)}, u32[]{:S(2)}) collective-permute-start(bf16[2,1,192,512]{3,2,1,0:T(8,128)(2,1)} %get-tuple-element.67), channel_id=1, source_target_pairs={{0,1},{1,2},{2,3},{3,4},{4,5},{5,6},{6,7},{7,8},{8,9},{9,10},{10,1... | collective-permute-start | bytes 1179656 | tf_op jit(solution)/shard_map/ppermute | solution.py:89
  27.8 1.3 collective-permute-start.3
  30.5 4.0 %all-to-all-start.2 = ((bf16[4,3,2,32,256]{4,3,2,1,0:T(8,128)(2,1)}), bf16[4,3,2,32,256]{4,3,2,1,0:T(8,128)(2,1)S(1)}, u32[]{:S(2)}, u32[]{:S(2)}) async-start(bf16[4,3,2,32,256]{4,3,2,1,0:T(8,128)(2,1)} %broadcast_in_dim.63), calls=%async_computation.2 | async-start | bytes 786432 | tf_op jit(solution)/shard_map/all_to_all | solution.py:77
  35.5 8.8 %collective-permute-start.4 = (bf16[1,2,192,512]{3,2,1,0:T(8,128)(2,1)}, bf16[1,2,192,512]{3,2,1,0:T(8,128)(2,1)S(1)}, u32[]{:S(2)}, u32[]{:S(2)}) collective-permute-start(bf16[1,2,192,512]{3,2,1,0:T(8,128)(2,1)} %get-tuple-element.65), channel_id=1, source_target_pairs={{0,16},{16,32},{32,48},{48,64},{64,80},{80,96},{96,112},{112,128},... | collective-permute-start | bytes 1179656 | tf_op jit(solution)/shard_map/ppermute | solution.py:89
  44.4 1.9 collective-permute-start.5
  46.3 3.0 %collective-permute-start = (bf16[3,2,4,32,256]{4,3,1,0,2:T(8,128)(2,1)S(1)}, bf16[3,2,4,32,256]{4,3,1,0,2:T(8,128)(2,1)}, u32[]{:S(2)}, u32[]{:S(2)}) collective-permute-start(bf16[3,2,4,32,256]{4,3,1,0,2:T(8,128)(2,1)S(1)} %bitcast.184), channel_id=1, source_target_pairs={{0,64},{64,0},{128,192},{192,128},{16,208},{80,144},{144,80},{208,... | collective-permute-start | bytes 1179656 | tf_op jit(solution)/shard_map/ppermute | solution.py:35
  50.9 8.2 %collective-permute-done.5 = bf16[1,2,192,512]{3,2,1,0:T(8,128)(2,1)} collective-permute-done((bf16[1,2,192,512]{3,2,1,0:T(8,128)(2,1)}, bf16[1,2,192,512]{3,2,1,0:T(8,128)(2,1)}, u32[]{:S(2)}, u32[]{:S(2)}) %collective-permute-start.5) | collective-permute-done | bytes 393248 | tf_op jit(solution)/shard_map/ppermute | solution.py:90
  59.1 1.3 pad_maximum_fusion.3.cot_ref
  60.4 2.3 fusion.63
  62.7 2.0 pad_maximum_fusion.6
  64.7 1.5 collective-permute-start.6
  66.2 2.0 pad_maximum_fusion.7
  68.9 2.3 pad_bitcast_fusion
  71.3 2.0 broadcast_in_dim.60
  74.1 1.8 copy_dynamic-update-slice_fusion.2
  75.9 2.5 %pad_maximum_fusion.x_ref = bf16[3,2,4,192,512]{4,3,2,1,0:T(8,128)(2,1)} fusion(bf16[1,2,4,192,512]{4,3,2,1,0:T(8,128)(2,1)S(1)} %get-tuple-element.73, bf16[1,2,4,192,512]{4,3,2,1,0:T(8,128)(2,1)S(1)} %bitcast.165, bf16[1,2,4,192,512]{4,3,2,1,0:T(8,128)(2,1)S(1)} %get-tuple-element.74), kind=kLoop, calls=%fused_computation.2 | loop fusion | flops 4718592 | bytes 9437184 | tf_op jit(solution)/shard_map/stack | solution.py:96
  81.9 1.8 bitcast_dynamic-update-slice_fusion
  83.7 1.8 fusion.26
  85.5 1.8 fusion.25
  87.4 2.8 %collective-permute-start.8 = (bf16[12,512,256]{2,1,0:T(8,128)(2,1)}, bf16[12,512,256]{2,1,0:T(8,128)(2,1)}, u32[]{:S(2)}, u32[]{:S(2)}) collective-permute-start(bf16[12,512,256]{2,1,0:T(8,128)(2,1)} %bitcast.16.kernel_hbm), channel_id=1, source_target_pairs={{0,16},{16,0},{1,17},{17,1},{2,18},{18,2},{3,19},{19,3},{4,20},{20... | collective-permute-start | bytes 9437192 | tf_op jit(solution)/shard_map/ppermute | solution.py:22
  91.9 2.3 copy-done
  94.3 1.4 copy-done.2
  95.7 5.1 %shard_map.67 = (f32[2,384,512]{2,1,0:T(8,128)S(1)}, f32[2,384,256]{2,1,0:T(8,128)S(1)}) custom-call(s32[1]{0:T(128)} %bitcast.core_ref, bf16[3,2,4,192,512]{4,3,2,1,0:T(8,128)(2,1)S(1)} %copy-done, bf16[4,2,192,512]{3,2,1,0:T(8,128)(2,1)S(1)} %copy-done.2, bf16[12,512,256]{2,1,0:T(8,128)(2,1)} %bitcast.16.kernel_hbm), custom_call_target="tpu_custom_call" | custom-call | flops 3200000000 | bytes 12000000 | tf_op jit(solution)/shard_map/pallas_call | solution.py:212
  100.8 7.1 %shard_map.68 = (bf16[2,384,256]{2,1,0:T(8,128)(2,1)S(1)}, bf16[2,384,256]{2,1,0:T(8,128)(2,1)S(1)}, bf16[2,384,512]{2,1,0:T(8,128)(2,1)S(1)}, bf16[512,768]{1,0:T(8,128)(2,1)S(1)}) custom-call(s32[1]{0:T(128)} %bitcast.core_ref, bf16[3,2,4,192,512]{4,3,2,1,0:T(8,128)(2,1)S(1)} %copy-done, bf16[4,2,192,512]{3,2,1,0:T(8,128)(2,1)S(1)} %copy-done.2, ...), custom_call_target="tpu_custom_call" | custom-call | flops 3200000000 | bytes 15000000 | tf_op jit(solution)/shard_map/pallas_call | solution.py:222
  109.6 1.3 collective-permute-done.12
  110.9 5.6 %shard_map.70 = (f32[4,4,3,2,32,256]{5,4,3,2,1,0:T(8,128)S(1)}, bf16[2,4,3,2,32,256]{5,4,3,2,1,0:T(8,128)(2,1)S(1)}) custom-call(s32[5]{0:T(128)S(1)} %get-tuple-element.72.info_ref, bf16[512,768]{1,0:T(8,128)(2,1)S(1)} %get-tuple-element.40.turned_ref, bf16[512,768]{1,0:T(8,128)(2,1)S(1)} %collective-permute-done.9.turned_pair_ref, ...), custom_call_target="tpu_custom_call" | custom-call | flops 2400000000 | bytes 16000000 | tf_op jit(solution)/shard_map/pallas_call | solution.py:296
  117.7 5.6 %shard_map.69 = (f32[4,4,3,2,32,256]{5,4,3,2,1,0:T(8,128)S(1)}, bf16[2,4,3,2,32,256]{5,4,3,2,1,0:T(8,128)(2,1)S(1)}) custom-call(s32[5]{0:T(128)S(1)} %get-tuple-element.71.info_ref, bf16[512,768]{1,0:T(8,128)(2,1)S(1)} %get-tuple-element.40.turned_ref, bf16[512,768]{1,0:T(8,128)(2,1)S(1)} %collective-permute-done.9.turned_pair_ref, ...), custom_call_target="tpu_custom_call" | custom-call | flops 2400000000 | bytes 16000000 | tf_op jit(solution)/shard_map/pallas_call | solution.py:296
  123.3 2.0 collective-permute-start.17
  125.3 1.3 collective-permute-start.13
  126.6 1.3 collective-permute-start.14
  127.9 2.2 fusion.42
  130.1 2.2 fusion.31
  132.3 3.2 %collective-permute-done.13 = bf16[2,1,192,512]{3,2,1,0:T(8,128)(2,1)S(1)} collective-permute-done((bf16[2,1,192,512]{3,2,1,0:T(8,128)(2,1)S(1)}, bf16[2,1,192,512]{3,2,1,0:T(8,128)(2,1)S(1)}, u32[]{:S(2)}, u32[]{:S(2)}) %collective-permute-start.13) | collective-permute-done | bytes 393248 | tf_op jit(solution)/shard_map/ppermute | solution.py:89
  135.6 4.1 %collective-permute-done.14 = bf16[2,1,192,512]{3,2,1,0:T(8,128)(2,1)S(1)} collective-permute-done((bf16[2,1,192,512]{3,2,1,0:T(8,128)(2,1)S(1)}, bf16[2,1,192,512]{3,2,1,0:T(8,128)(2,1)S(1)}, u32[]{:S(2)}, u32[]{:S(2)}) %collective-permute-start.14) | collective-permute-done | bytes 393248 | tf_op jit(solution)/shard_map/ppermute | solution.py:90
  140.1 1.6 fusion.62
  142.9 2.4 fusion.48
  145.3 2.2 fusion.50
  147.5 2.2 fusion.46
  150.2 2.2 fusion.44
  153.8 2.5 %collective-permute-start.18 = (bf16[4,3,2,32,256]{4,3,2,1,0:T(8,128)(2,1)}, bf16[4,3,2,32,256]{4,3,2,1,0:T(8,128)(2,1)S(1)}, u32[]{:S(2)}, u32[]{:S(2)}) collective-permute-start(bf16[4,3,2,32,256]{4,3,2,1,0:T(8,128)(2,1)} %fusion.24), channel_id=1, source_target_pairs={{0,3},{1,2},{2,1},{3,0},{16,17},{17,16},{18,19},{19,18},{4,7},{5,6... | collective-permute-start | bytes 1179656 | tf_op jit(solution)/shard_map/ppermute | solution.py:35
  157.9 16.1 %all-to-all-start.3 = ((f32[4,3,2,32,256]{4,3,2,1,0:T(8,128)}), f32[4,3,2,32,256]{4,3,2,1,0:T(8,128)}, u32[]{:S(2)}, u32[]{:S(2)}) async-start(f32[4,3,2,32,256]{4,3,2,1,0:T(8,128)} %fusion.22), calls=%async_computation.3 | async-start | bytes 1572864 | tf_op jit(solution)/shard_map/all_to_all | solution.py:81
  174.0 2.3 fusion.39
  176.3 2.4 %fusion.37 = f32[768,256]{1,0:T(8,128)} fusion(bf16[768,512]{1,0:T(8,128)(2,1)} %bitcast.174, bf16[12,512,256]{2,1,0:T(8,128)(2,1)} %bitcast.16.kernel_hbm), kind=kOutput, calls=%fused_computation.78 | convolution fusion | flops 201326592 | bytes 1835008 | tf_op jit(solution)/shard_map/dot_general | solution.py:391
  178.8 2.2 fusion.19
  181.0 2.4 all-to-all-done.3
  183.4 4.4 %all-to-all-start.4 = ((f32[4,3,2,32,256]{4,3,2,1,0:T(8,128)}), f32[4,3,2,32,256]{4,3,2,1,0:T(8,128)}, u32[]{:S(2)}, u32[]{:S(2)}) async-start(f32[4,3,2,32,256]{4,3,2,1,0:T(8,128)} %fusion.19), calls=%async_computation.4 | async-start | bytes 1572864 | tf_op jit(solution)/shard_map/all_to_all | solution.py:81
  187.8 2.2 fusion.35
  190.0 2.5 %fusion.34 = f32[768,256]{1,0:T(8,128)} fusion(bf16[768,512]{1,0:T(8,128)(2,1)} %bitcast.177, bf16[12,512,256]{2,1,0:T(8,128)(2,1)} %collective-permute-done.8.kernel_hbm), kind=kOutput, calls=%fused_computation.74 | convolution fusion | flops 201326592 | bytes 1835008 | tf_op jit(solution)/shard_map/dot_general | solution.py:391
  192.5 2.2 fusion.33
  196.3 1.2 reduce_sum.28
  198.3 6.1 %all-to-all-start.5 = ((f32[8,3,16,256]{3,2,1,0:T(8,128)}), f32[8,3,16,256]{3,2,1,0:T(8,128)S(1)}, u32[]{:S(2)}, u32[]{:S(2)}) async-start(f32[8,3,16,256]{3,2,1,0:T(8,128)} %copy.41), calls=%async_computation.5 | async-start | bytes 786432 | tf_op jit(solution)/shard_map/all_to_all | solution.py:81
  204.4 2.2 fusion.32
  206.6 2.2 fusion.29
  208.9 2.3 fusion.28
  211.1 3.8 %all-to-all-done.5 = f32[8,3,16,256]{3,2,1,0:T(8,128)S(1)} async-done(((f32[8,3,16,256]{3,2,1,0:T(8,128)}), f32[8,3,16,256]{3,2,1,0:T(8,128)S(1)}, u32[]{:S(2)}, u32[]{:S(2)}) %all-to-all-start.5) | async-done | bytes 393248 | tf_op jit(solution)/shard_map/all_to_all | solution.py:81
  216.0 8.5 %all-to-all-start.6 = ((f32[16,3,16,256]{3,2,1,0:T(8,128)}), f32[16,3,16,256]{3,2,1,0:T(8,128)S(1)}, u32[]{:S(2)}, u32[]{:S(2)}) async-start(f32[16,3,16,256]{3,2,1,0:T(8,128)} %broadcast_in_dim.72), calls=%async_computation.6 | async-start | bytes 1572864 | tf_op jit(solution)/shard_map/all_to_all | solution.py:77
  224.5 1.5 fusion.27
  226.0 1.3 fusion.30
  227.5 2.4 %fusion.16 = f32[768,256]{1,0:T(8,128)S(1)} fusion(f32[768,256]{1,0:T(8,128)} %fusion.35, f32[768,256]{1,0:T(8,128)} %fusion.37, f32[768,256]{1,0:T(8,128)} %fusion.39, bf16[768,512]{1,0:T(8,128)(2,1)S(1)} %bitcast.182, f32[768,256]{1,0:T(8,128)S(1)} %copy-done.19, f32[768,256]{1,0:T(8,128)S(1)} %copy-done.23, f32[768,256]{1,0:T(8,128)S(1)} %copy-done.22, ...), kind=kOutput, calls=%fused_computation.27 | convolution fusion | flops 202899456 | bytes 8126464 | tf_op jit(solution)/shard_map/dot_general | solution.py:391
  230.8 1.5 fusion.13
  232.3 1.4 fusion.6
  233.7 3.9 %all-to-all-done.6 = f32[16,3,16,256]{3,2,1,0:T(8,128)S(1)} async-done(((f32[16,3,16,256]{3,2,1,0:T(8,128)}), f32[16,3,16,256]{3,2,1,0:T(8,128)S(1)}, u32[]{:S(2)}, u32[]{:S(2)}) %all-to-all-start.6) | async-done | bytes 786464 | tf_op jit(solution)/shard_map/all_to_all | solution.py:77
  (125 shorter events, 28.5 us)
Async XLA Ops:
  0.6 22.9 %copy-start.17 = (bf16[2,2,192,512]{3,2,1,0:T(8,128)(2,1)S(1)}, bf16[2,2,192,512]{3,2,1,0:T(8,128)(2,1)}, u32[]{:S(2)}) copy-start(bf16[2,2,192,512]{3,2,1,0:T(8,128)(2,1)} %param.4) | copy-start | bytes 2359300
  0.6 33.9 %copy-start.8 = (bf16[2,2,192,512]{3,2,1,0:T(8,128)(2,1)S(1)}, bf16[2,2,192,512]{3,2,1,0:T(8,128)(2,1)}, u32[]{:S(2)}) copy-start(bf16[2,2,192,512]{3,2,1,0:T(8,128)(2,1)} %param.5) | copy-start | bytes 2359300
  19.3 10.4 %all-to-all-start.1 = ((bf16[4,3,2,32,256]{4,3,2,1,0:T(8,128)(2,1)}), bf16[4,3,2,32,256]{4,3,2,1,0:T(8,128)(2,1)S(1)}, u32[]{:S(2)}, u32[]{:S(2)}) async-start(bf16[4,3,2,32,256]{4,3,2,1,0:T(8,128)(2,1)} %broadcast_in_dim.62), calls=%async_computation.1 | async-start | bytes 786432 | tf_op jit(solution)/shard_map/all_to_all | solution.py:77
  24.4 24.9 %collective-permute-start.2 = (bf16[2,1,192,512]{3,2,1,0:T(8,128)(2,1)}, bf16[2,1,192,512]{3,2,1,0:T(8,128)(2,1)S(1)}, u32[]{:S(2)}, u32[]{:S(2)}) collective-permute-start(bf16[2,1,192,512]{3,2,1,0:T(8,128)(2,1)} %get-tuple-element.67), channel_id=1, source_target_pairs={{0,1},{1,2},{2,3},{3,4},{4,5},{5,6},{6,7},{7,8},{8,9},{9,10},{10,1... | collective-permute-start | bytes 1179656 | tf_op jit(solution)/shard_map/ppermute | solution.py:89
  27.8 22.1 %collective-permute-start.3 = (bf16[2,1,192,512]{3,2,1,0:T(8,128)(2,1)}, bf16[2,1,192,512]{3,2,1,0:T(8,128)(2,1)S(1)}, u32[]{:S(2)}, u32[]{:S(2)}) collective-permute-start(bf16[2,1,192,512]{3,2,1,0:T(8,128)(2,1)} %get-tuple-element.68), channel_id=1, source_target_pairs={{1,0},{2,1},{3,2},{4,3},{5,4},{6,5},{7,6},{8,7},{9,8},{10,9},{11,1... | collective-permute-start | bytes 1179656 | tf_op jit(solution)/shard_map/ppermute | solution.py:90
  29.7 33.0 %copy-start.15 = (bf16[4,3,2,32,256]{4,3,2,1,0:T(8,128)(2,1)}, bf16[4,3,2,32,256]{4,3,2,1,0:T(8,128)(2,1)S(1)}, u32[]{:S(2)}) copy-start(bf16[4,3,2,32,256]{4,3,2,1,0:T(8,128)(2,1)S(1)} %all-to-all-done.1) | copy-start | bytes 1179652
  30.5 18.8 %all-to-all-start.2 = ((bf16[4,3,2,32,256]{4,3,2,1,0:T(8,128)(2,1)}), bf16[4,3,2,32,256]{4,3,2,1,0:T(8,128)(2,1)S(1)}, u32[]{:S(2)}, u32[]{:S(2)}) async-start(bf16[4,3,2,32,256]{4,3,2,1,0:T(8,128)(2,1)} %broadcast_in_dim.63), calls=%async_computation.2 | async-start | bytes 786432 | tf_op jit(solution)/shard_map/all_to_all | solution.py:77
  35.5 14.5 %collective-permute-start.4 = (bf16[1,2,192,512]{3,2,1,0:T(8,128)(2,1)}, bf16[1,2,192,512]{3,2,1,0:T(8,128)(2,1)S(1)}, u32[]{:S(2)}, u32[]{:S(2)}) collective-permute-start(bf16[1,2,192,512]{3,2,1,0:T(8,128)(2,1)} %get-tuple-element.65), channel_id=1, source_target_pairs={{0,16},{16,32},{32,48},{48,64},{64,80},{80,96},{96,112},{112,128},... | collective-permute-start | bytes 1179656 | tf_op jit(solution)/shard_map/ppermute | solution.py:89
  44.4 14.7 %collective-permute-start.5 = (bf16[1,2,192,512]{3,2,1,0:T(8,128)(2,1)}, bf16[1,2,192,512]{3,2,1,0:T(8,128)(2,1)}, u32[]{:S(2)}, u32[]{:S(2)}) collective-permute-start(bf16[1,2,192,512]{3,2,1,0:T(8,128)(2,1)} %get-tuple-element.66), channel_id=1, source_target_pairs={{16,0},{32,16},{48,32},{64,48},{80,64},{96,80},{112,96},{128,112},... | collective-permute-start | bytes 1179656 | tf_op jit(solution)/shard_map/ppermute | solution.py:90
  46.3 14.1 %collective-permute-start = (bf16[3,2,4,32,256]{4,3,1,0,2:T(8,128)(2,1)S(1)}, bf16[3,2,4,32,256]{4,3,1,0,2:T(8,128)(2,1)}, u32[]{:S(2)}, u32[]{:S(2)}) collective-permute-start(bf16[3,2,4,32,256]{4,3,1,0,2:T(8,128)(2,1)S(1)} %bitcast.184), channel_id=1, source_target_pairs={{0,64},{64,0},{128,192},{192,128},{16,208},{80,144},{144,80},{208,... | collective-permute-start | bytes 1179656 | tf_op jit(solution)/shard_map/ppermute | solution.py:35
  49.3 11.1 %collective-permute-start.1 = (bf16[4,3,2,32,256]{4,3,2,1,0:T(8,128)(2,1)S(1)}, bf16[4,3,2,32,256]{4,3,2,1,0:T(8,128)(2,1)}, u32[]{:S(2)}, u32[]{:S(2)}) collective-permute-start(bf16[4,3,2,32,256]{4,3,2,1,0:T(8,128)(2,1)S(1)} %all-to-all-done.2), channel_id=1, source_target_pairs={{0,1},{1,0},{2,3},{3,2},{16,19},{17,18},{18,17},{19,16},{4,5},{5,4... | collective-permute-start | bytes 1179656 | tf_op jit(solution)/shard_map/ppermute | solution.py:35
  50.1 12.6 %copy-start.4 = (bf16[2,4,192,512]{3,2,1,0:T(8,128)(2,1)}, bf16[2,4,192,512]{3,2,1,0:T(8,128)(2,1)S(1)}, u32[]{:S(2)}) copy-start(bf16[2,4,192,512]{3,2,1,0:T(8,128)(2,1)S(1)} %pad_maximum_fusion.2) | copy-start | bytes 4718596
  50.1 0.8 copy-start.29
  60.4 7.8 %copy-start.1 = (bf16[4,2,192,512]{3,2,1,0:T(8,128)(2,1)}, bf16[4,2,192,512]{3,2,1,0:T(8,128)(2,1)S(1)}, u32[]{:S(2)}) copy-start(bf16[4,2,192,512]{3,2,1,0:T(8,128)(2,1)S(1)} %pad_maximum_fusion.3.cot_ref) | copy-start | bytes 4718596
  64.7 13.7 %collective-permute-start.6 = (bf16[2,3,2,4,32,256]{5,4,2,1,3,0:T(8,128)(2,1)}, bf16[2,3,2,4,32,256]{5,4,2,1,3,0:T(8,128)(2,1)}, u32[]{:S(2)}, u32[]{:S(2)}) collective-permute-start(bf16[2,3,2,4,32,256]{5,4,2,1,3,0:T(8,128)(2,1)} %pad_maximum_fusion.6), channel_id=1, source_target_pairs={{0,192},{64,128},{128,64},{192,0},{16,80},{80,16},{144,208},{208,1... | collective-permute-start | bytes 2359304 | tf_op jit(solution)/shard_map/ppermute | solution.py:35
  68.2 15.5 %collective-permute-start.7 = (bf16[2,4,3,2,32,256]{5,4,3,2,1,0:T(8,128)(2,1)}, bf16[2,4,3,2,32,256]{5,4,3,2,1,0:T(8,128)(2,1)}, u32[]{:S(2)}, u32[]{:S(2)}) collective-permute-start(bf16[2,4,3,2,32,256]{5,4,3,2,1,0:T(8,128)(2,1)} %pad_maximum_fusion.7), channel_id=1, source_target_pairs={{0,3},{1,2},{2,1},{3,0},{16,17},{17,16},{18,19},{19,18},{4,7},{5,6... | collective-permute-start | bytes 2359304 | tf_op jit(solution)/shard_map/ppermute | solution.py:35
  71.2 2.1 copy-start.16
  71.2 4.7 %copy-start.5 = (bf16[2,4,192,512]{3,2,1,0:T(8,128)(2,1)S(1)}, bf16[2,4,192,512]{3,2,1,0:T(8,128)(2,1)}, u32[]{:S(2)}) copy-start(bf16[2,4,192,512]{3,2,1,0:T(8,128)(2,1)} %copy-done.4) | copy-start | bytes 4718596
  87.4 13.4 %collective-permute-start.8 = (bf16[12,512,256]{2,1,0:T(8,128)(2,1)}, bf16[12,512,256]{2,1,0:T(8,128)(2,1)}, u32[]{:S(2)}, u32[]{:S(2)}) collective-permute-start(bf16[12,512,256]{2,1,0:T(8,128)(2,1)} %bitcast.16.kernel_hbm), channel_id=1, source_target_pairs={{0,16},{16,0},{1,17},{17,1},{2,18},{18,2},{3,19},{19,3},{4,20},{20... | collective-permute-start | bytes 9437192 | tf_op jit(solution)/shard_map/ppermute | solution.py:22
  90.1 19.5 %collective-permute-start.11 = (bf16[512,1536]{1,0:T(8,128)(2,1)S(1)}, bf16[512,1536]{1,0:T(8,128)(2,1)S(1)}, u32[]{:S(2)}, u32[]{:S(2)}) collective-permute-start(bf16[512,1536]{1,0:T(8,128)(2,1)S(1)} %bitcast.157), channel_id=1, source_target_pairs={{0,16},{16,0},{1,17},{17,1},{2,18},{18,2},{3,19},{19,3},{4,20},{20... | collective-permute-start | bytes 4718600 | tf_op jit(solution)/shard_map/ppermute | solution.py:22
  91.3 17.5 %collective-permute-start.10 = (bf16[2,4,192,256]{3,2,1,0:T(8,128)(2,1)S(1)}, bf16[2,4,192,256]{3,2,1,0:T(8,128)(2,1)S(1)}, u32[]{:S(2)}, u32[]{:S(2)}) collective-permute-start(bf16[2,4,192,256]{3,2,1,0:T(8,128)(2,1)S(1)} %constant_dynamic-slice_fusion), channel_id=1, source_target_pairs={{0,16},{16,0},{1,17},{17,1},{2,18},{18,2},{3,19},{19,3},{4,20},{20... | collective-permute-start | bytes 2359304 | tf_op jit(solution)/shard_map/ppermute | solution.py:22
  91.9 2.3 copy-start
  94.3 1.4 copy-start.2
  108.0 2.9 %collective-permute-start.9 = (bf16[512,768]{1,0:T(8,128)(2,1)S(1)}, bf16[512,768]{1,0:T(8,128)(2,1)S(1)}, u32[]{:S(2)}, u32[]{:S(2)}) collective-permute-start(bf16[512,768]{1,0:T(8,128)(2,1)S(1)} %get-tuple-element.40.turned_ref), channel_id=1, source_target_pairs={{0,16},{16,0},{1,17},{17,1},{2,18},{18,2},{3,19},{19,3},{4,20},{20... | collective-permute-start | bytes 2359304 | tf_op jit(solution)/shard_map/ppermute | solution.py:22
  108.2 2.7 %collective-permute-start.12 = (bf16[2,384,256]{2,1,0:T(8,128)(2,1)S(1)}, bf16[2,384,256]{2,1,0:T(8,128)(2,1)S(1)}, u32[]{:S(2)}, u32[]{:S(2)}) collective-permute-start(bf16[2,384,256]{2,1,0:T(8,128)(2,1)S(1)} %get-tuple-element.43), channel_id=1, source_target_pairs={{0,16},{16,0},{1,17},{17,1},{2,18},{18,2},{3,19},{19,3},{4,20},{20... | collective-permute-start | bytes 1179656 | tf_op jit(solution)/shard_map/ppermute | solution.py:22
  116.5 33.2 %collective-permute-start.15 = (bf16[2,4,3,2,32,256]{5,4,3,2,1,0:T(8,128)(2,1)S(1)}, bf16[2,4,3,2,32,256]{5,4,3,2,1,0:T(8,128)(2,1)S(1)}, u32[]{:S(2)}, u32[]{:S(2)}) collective-permute-start(bf16[2,4,3,2,32,256]{5,4,3,2,1,0:T(8,128)(2,1)S(1)} %get-tuple-element.47), channel_id=1, source_target_pairs={{0,64},{64,0},{128,192},{192,128},{16,208},{80,144},{144,80},{208,... | collective-permute-start | bytes 2359304 | tf_op jit(solution)/shard_map/ppermute | solution.py:35
  123.3 29.3 %copy-start.3 = (f32[4,4,3,2,32,256]{5,4,3,2,1,0:T(8,128)}, f32[4,4,3,2,32,256]{5,4,3,2,1,0:T(8,128)S(1)}, u32[]{:S(2)}) copy-start(f32[4,4,3,2,32,256]{5,4,3,2,1,0:T(8,128)S(1)} %get-tuple-element.48) | copy-start | bytes 9437188
  123.3 29.1 %collective-permute-start.17 = (bf16[2,4,3,2,32,256]{5,4,3,2,1,0:T(8,128)(2,1)S(1)}, bf16[2,4,3,2,32,256]{5,4,3,2,1,0:T(8,128)(2,1)S(1)}, u32[]{:S(2)}, u32[]{:S(2)}) collective-permute-start(bf16[2,4,3,2,32,256]{5,4,3,2,1,0:T(8,128)(2,1)S(1)} %get-tuple-element.44), channel_id=1, source_target_pairs={{0,1},{1,0},{2,3},{3,2},{16,19},{17,18},{18,17},{19,16},{4,5},{5,4... | collective-permute-start | bytes 2359304 | tf_op jit(solution)/shard_map/ppermute | solution.py:35
  125.3 10.3 %collective-permute-start.13 = (bf16[2,1,192,512]{3,2,1,0:T(8,128)(2,1)S(1)}, bf16[2,1,192,512]{3,2,1,0:T(8,128)(2,1)S(1)}, u32[]{:S(2)}, u32[]{:S(2)}) collective-permute-start(bf16[2,1,192,512]{3,2,1,0:T(8,128)(2,1)S(1)} %get-tuple-element.59), channel_id=1, source_target_pairs={{0,1},{1,2},{2,3},{3,4},{4,5},{5,6},{6,7},{7,8},{8,9},{9,10},{10,1... | collective-permute-start | bytes 1179656 | tf_op jit(solution)/shard_map/ppermute | solution.py:89
  126.6 13.1 %collective-permute-start.14 = (bf16[2,1,192,512]{3,2,1,0:T(8,128)(2,1)S(1)}, bf16[2,1,192,512]{3,2,1,0:T(8,128)(2,1)S(1)}, u32[]{:S(2)}, u32[]{:S(2)}) collective-permute-start(bf16[2,1,192,512]{3,2,1,0:T(8,128)(2,1)S(1)} %get-tuple-element.60), channel_id=1, source_target_pairs={{1,0},{2,1},{3,2},{4,3},{5,4},{6,5},{7,6},{8,7},{9,8},{10,9},{11,1... | collective-permute-start | bytes 1179656 | tf_op jit(solution)/shard_map/ppermute | solution.py:90
  141.8 5.8 %copy-start.10 = (bf16[2,2,192,512]{3,2,1,0:T(8,128)(2,1)}, bf16[2,2,192,512]{3,2,1,0:T(8,128)(2,1)S(1)}, u32[]{:S(2)}) copy-start(bf16[2,2,192,512]{3,2,1,0:T(8,128)(2,1)S(1)} %get-tuple-element.49) | copy-start | bytes 2359300
  142.9 7.0 %copy-start.7 = (bf16[2,2,192,512]{3,2,1,0:T(8,128)(2,1)}, bf16[2,2,192,512]{3,2,1,0:T(8,128)(2,1)S(1)}, u32[]{:S(2)}) copy-start(bf16[2,2,192,512]{3,2,1,0:T(8,128)(2,1)S(1)} %get-tuple-element.57) | copy-start | bytes 2359300
  150.1 6.7 %collective-permute-start.16 = (bf16[4,3,2,32,256]{4,3,2,1,0:T(8,128)(2,1)S(1)}, bf16[4,3,2,32,256]{4,3,2,1,0:T(8,128)(2,1)S(1)}, u32[]{:S(2)}, u32[]{:S(2)}) collective-permute-start(bf16[4,3,2,32,256]{4,3,2,1,0:T(8,128)(2,1)S(1)} %fusion.23), channel_id=1, source_target_pairs={{0,192},{64,128},{128,64},{192,0},{16,80},{80,16},{144,208},{208,1... | collective-permute-start | bytes 1179656 | tf_op jit(solution)/shard_map/ppermute | solution.py:35
  152.6 1.3 copy-start.13
  153.8 25.0 %collective-permute-start.18 = (bf16[4,3,2,32,256]{4,3,2,1,0:T(8,128)(2,1)}, bf16[4,3,2,32,256]{4,3,2,1,0:T(8,128)(2,1)S(1)}, u32[]{:S(2)}, u32[]{:S(2)}) collective-permute-start(bf16[4,3,2,32,256]{4,3,2,1,0:T(8,128)(2,1)} %fusion.24), channel_id=1, source_target_pairs={{0,3},{1,2},{2,1},{3,0},{16,17},{17,16},{18,19},{19,18},{4,7},{5,6... | collective-permute-start | bytes 1179656 | tf_op jit(solution)/shard_map/ppermute | solution.py:35
  157.9 25.5 %all-to-all-start.3 = ((f32[4,3,2,32,256]{4,3,2,1,0:T(8,128)}), f32[4,3,2,32,256]{4,3,2,1,0:T(8,128)}, u32[]{:S(2)}, u32[]{:S(2)}) async-start(f32[4,3,2,32,256]{4,3,2,1,0:T(8,128)} %fusion.22), calls=%async_computation.3 | async-start | bytes 1572864 | tf_op jit(solution)/shard_map/all_to_all | solution.py:81
  174.0 4.8 %copy-start.14 = (f32[2,4,3,2,32,256]{5,4,3,2,1,0:T(8,128)S(1)}, f32[2,4,3,2,32,256]{5,4,3,2,1,0:T(8,128)}, u32[]{:S(2)}) copy-start(f32[2,4,3,2,32,256]{5,4,3,2,1,0:T(8,128)} %copy-done.13) | copy-start | bytes 4718596
  183.4 12.9 %all-to-all-start.4 = ((f32[4,3,2,32,256]{4,3,2,1,0:T(8,128)}), f32[4,3,2,32,256]{4,3,2,1,0:T(8,128)}, u32[]{:S(2)}, u32[]{:S(2)}) async-start(f32[4,3,2,32,256]{4,3,2,1,0:T(8,128)} %fusion.19), calls=%async_computation.4 | async-start | bytes 1572864 | tf_op jit(solution)/shard_map/all_to_all | solution.py:81
  197.5 11.4 %copy-start.6 = (bf16[2,2,192,512]{3,2,1,0:T(8,128)(2,1)S(1)}, bf16[2,2,192,512]{3,2,1,0:T(8,128)(2,1)}, u32[]{:S(2)}) copy-start(bf16[2,2,192,512]{3,2,1,0:T(8,128)(2,1)} %get-tuple-element.58) | copy-start | bytes 2359300
  198.3 16.7 %all-to-all-start.5 = ((f32[8,3,16,256]{3,2,1,0:T(8,128)}), f32[8,3,16,256]{3,2,1,0:T(8,128)S(1)}, u32[]{:S(2)}, u32[]{:S(2)}) async-start(f32[8,3,16,256]{3,2,1,0:T(8,128)} %copy.41), calls=%async_computation.5 | async-start | bytes 786432 | tf_op jit(solution)/shard_map/all_to_all | solution.py:81
  208.9 17.2 %copy-start.12 = (bf16[2,2,192,512]{3,2,1,0:T(8,128)(2,1)S(1)}, bf16[2,2,192,512]{3,2,1,0:T(8,128)(2,1)}, u32[]{:S(2)}) copy-start(bf16[2,2,192,512]{3,2,1,0:T(8,128)(2,1)} %get-tuple-element.51) | copy-start | bytes 2359300
  215.0 12.4 %copy-start.19 = (f32[768,256]{1,0:T(8,128)S(1)}, f32[768,256]{1,0:T(8,128)}, u32[]{:S(2)}) copy-start(f32[768,256]{1,0:T(8,128)} %fusion.42) | copy-start | bytes 2359300
  216.0 21.6 %all-to-all-start.6 = ((f32[16,3,16,256]{3,2,1,0:T(8,128)}), f32[16,3,16,256]{3,2,1,0:T(8,128)S(1)}, u32[]{:S(2)}, u32[]{:S(2)}) async-start(f32[16,3,16,256]{3,2,1,0:T(8,128)} %broadcast_in_dim.72), calls=%async_computation.6 | async-start | bytes 1572864 | tf_op jit(solution)/shard_map/all_to_all | solution.py:77
  224.5 2.8 %copy-start.20 = (f32[768,256]{1,0:T(8,128)S(1)}, f32[768,256]{1,0:T(8,128)}, u32[]{:S(2)}) copy-start(f32[768,256]{1,0:T(8,128)} %fusion.48) | copy-start | bytes 2359300
  224.5 2.9 %copy-start.21 = (f32[768,256]{1,0:T(8,128)S(1)}, f32[768,256]{1,0:T(8,128)}, u32[]{:S(2)}) copy-start(f32[768,256]{1,0:T(8,128)} %fusion.50) | copy-start | bytes 2359300
  224.5 2.9 %copy-start.22 = (f32[768,256]{1,0:T(8,128)S(1)}, f32[768,256]{1,0:T(8,128)}, u32[]{:S(2)}) copy-start(f32[768,256]{1,0:T(8,128)} %fusion.46) | copy-start | bytes 2359300
  224.5 2.9 %copy-start.23 = (f32[768,256]{1,0:T(8,128)S(1)}, f32[768,256]{1,0:T(8,128)}, u32[]{:S(2)}) copy-start(f32[768,256]{1,0:T(8,128)} %fusion.44) | copy-start | bytes 2359300
  227.4 2.5 %copy-start.11 = (bf16[2,2,192,512]{3,2,1,0:T(8,128)(2,1)S(1)}, bf16[2,2,192,512]{3,2,1,0:T(8,128)(2,1)}, u32[]{:S(2)}) copy-start(bf16[2,2,192,512]{3,2,1,0:T(8,128)(2,1)} %copy-done.10) | copy-start | bytes 2359300
  227.4 2.5 %copy-start.18 = (f32[768,256]{1,0:T(8,128)S(1)}, f32[768,256]{1,0:T(8,128)}, u32[]{:S(2)}) copy-start(f32[768,256]{1,0:T(8,128)} %fusion.31) | copy-start | bytes 2359300
  227.4 2.5 %copy-start.24 = (f32[768,256]{1,0:T(8,128)S(1)}, f32[768,256]{1,0:T(8,128)}, u32[]{:S(2)}) copy-start(f32[768,256]{1,0:T(8,128)} %fusion.34) | copy-start | bytes 2359300
  227.4 2.6 %copy-start.25 = (f32[768,256]{1,0:T(8,128)S(1)}, f32[768,256]{1,0:T(8,128)}, u32[]{:S(2)}) copy-start(f32[768,256]{1,0:T(8,128)} %fusion.33) | copy-start | bytes 2359300
  227.4 2.8 %copy-start.26 = (f32[768,256]{1,0:T(8,128)S(1)}, f32[768,256]{1,0:T(8,128)}, u32[]{:S(2)}) copy-start(f32[768,256]{1,0:T(8,128)} %fusion.32) | copy-start | bytes 2359300
  227.4 3.1 %copy-start.27 = (f32[768,256]{1,0:T(8,128)S(1)}, f32[768,256]{1,0:T(8,128)}, u32[]{:S(2)}) copy-start(f32[768,256]{1,0:T(8,128)} %fusion.29) | copy-start | bytes 2359300
  227.5 3.3 %copy-start.28 = (f32[768,256]{1,0:T(8,128)S(1)}, f32[768,256]{1,0:T(8,128)}, u32[]{:S(2)}) copy-start(f32[768,256]{1,0:T(8,128)} %fusion.28) | copy-start | bytes 2359300
  230.8 1.5 copy-start.9
where the time goes:
time: 242 us; the launch traced here: 240 us
  starting transfers between devices  76.3 us (32%)
  matrix products  38.5 us (16%)
  local copies, waits for them, and re-layouts  36.2 us (15%)
  waiting for transfers between devices  28.5 us (12%)
  Pallas kernels  23.5 us (10%)
  other arithmetic  19.4 us (8%)
  blocking collectives  16.8 us (7%)
    dot_general x18, matrix products, per_device(): jnp.dot(piece, kernel[tap], preferred_element_type=jnp.float32)  38.5 us
    all_to_all x3, starting transfers between devices, scattered(): lax.all_to_all(block, axis, 0, 0, tiled=True).astype(jnp.float32)  26.7 us
    all_to_all x1, blocking collectives, gathered(): return lax.all_to_all(spread, axis, 0, 0, tiled=True)  16.8 us
    all_to_all x3, starting transfers between devices, gathered(): return lax.all_to_all(spread, axis, 0, 0, tiled=True)  16.7 us
    ppermute x3, starting transfers between devices, halo(): lax.ppermute(lax.slice_in_dim(block, size - 1, size, axis=dim), axis, for...  13.5 us
    ppermute x3, waiting for transfers between devices, halo(): high = lax.ppermute(lax.slice_in_dim(block, 0, 1, axis=dim), axis, backward)  12.4 us
    pallas_call x2, Pallas kernels, weight_terms(): pl.pallas_call(functools.partial(weight_kernel, upper), out_shape=(jax.Sh...  11.2 us
    ppermute x8, starting transfers between devices, exchange(): return lax.ppermute(block, names, pairs)  10.8 us
  transfers between devices with their start and end apart: 25, of which 10 were waited for; matrix products, arithmetic and copies ran while one was open for 30% of the time, Pallas kernels for 7%

commit v1 on v0

v1 whole, which is shorter than its diff:
```python
import functools
import math

import jax
import jax.numpy as jnp
from jax import lax
from jax.experimental import pallas as pl
from jax.experimental.pallas import tpu as pltpu
from jax.sharding import Mesh, PartitionSpec as P

TM = ("x", "zl", "core")
SPACE = ("zh", "y")
PAIR = [(0, 1), (1, 0)]
ORDER = ((1, 3), (3, 1))
VMEM = pl.BlockSpec(memory_space=pltpu.VMEM)
ANY = pl.BlockSpec(memory_space=pl.ANY)
SMEM = pl.BlockSpec(memory_space=pltpu.SMEM)
PARAMS = pltpu.CompilerParams(vmem_limit_bytes=24 * 1024 * 1024)


def swap(block):
    return lax.ppermute(block, "core", PAIR)


def exchange(block, axis, stage):
    if axis == "x":
        names, number = ("x", "core"), lambda core, p: 2 * p + core
    else:
        names, number = ("core", axis), lambda core, p: 4 * core + p
    pairs = [
        (number(core, p), number(core, p ^ ORDER[core][stage]))
        for core in range(2)
        for p in range(4)
    ]
    return lax.ppermute(block, names, pairs)


def positions(axis):
    p = lax.axis_index(axis)
    core = lax.axis_index("core")
    return p, p ^ (1 + 2 * core), p ^ (3 - 2 * core), p ^ 2


def slots_of(axis):
    own, first, second, far = positions(axis)
    q = jnp.arange(4, dtype=jnp.int32)
    return jnp.where(q == own, 0, jnp.where(q == second, 1, jnp.where(q == first, 2, 3)))


def slots_in(axis, turn):
    p = lax.axis_index(axis)
    core = lax.axis_index("core") ^ turn
    return jnp.stack([p, p ^ (1 + 2 * core), p ^ (3 - 2 * core), p ^ 2]).astype(jnp.int32)


def ring_scatter(terms, sent, axis, waited=None):
    came = exchange(sent, axis, 0)
    if waited is not None:
        came, waited = lax.optimization_barrier((came, waited))
    came = came.astype(jnp.float32)
    passed = (terms[1] + came[1]).astype(sent.dtype)
    return terms[0] + came[0] + exchange(passed, axis, 1).astype(jnp.float32)


def ring_gather(block, axis):
    pair = jnp.stack([block, exchange(block, axis, 0)])
    return pair, exchange(pair, axis, 1)


def gathered(block, axis):
    spread = jnp.broadcast_to(block[None], (lax.axis_size(axis),) + block.shape)
    return lax.all_to_all(spread, axis, 0, 0, tiled=True)


def scattered(block, axis):
    return jnp.sum(lax.all_to_all(block, axis, 0, 0, tiled=True).astype(jnp.float32), axis=0)


def edges_of(block, axis, dim):
    count = lax.axis_size(axis)
    forward = [(i, (i + 1) % count) for i in range(count)]
    backward = [(target, source) for source, target in forward]
    size = block.shape[dim]
    low = lax.ppermute(lax.slice_in_dim(block, size - 1, size, axis=dim), axis, forward)
    high = lax.ppermute(lax.slice_in_dim(block, 0, 1, axis=dim), axis, backward)
    return low, high


def widened(block, edges, axis, dim):
    low, high = edges
    index = lax.axis_index(axis)
    low = jnp.where(index == 0, jnp.zeros_like(low), low)
    high = jnp.where(index == lax.axis_size(axis) - 1, jnp.zeros_like(high), high)
    return jnp.concatenate([low, block, high], axis=dim)


def column_shifts(maps):
    edge = jnp.zeros_like(maps[:, :, :1])
    return jnp.stack(
        [
            jnp.concatenate([edge, maps[:, :, :-1]], axis=2),
            maps,
            jnp.concatenate([maps[:, :, 1:], edge], axis=2),
        ]
    )


def lanes(index, half):
    return pl.ds(pl.multiple_of(index * half, half), half)


def assemble(info_ref, parts, kernel_ref, sems):
    copies = []
    for pair in range(2):
        for j in range(2):
            slot = 2 * pair + j
            for t in range(4):
                x, y = info_ref[1 + slot], info_ref[5 + t]
                target = kernel_ref.at[x, :, pl.ds(0, 2), y]
                copies.append((parts[pair].at[j, t], target))
                x, y = info_ref[1 + t], info_ref[5 + slot]
                target = kernel_ref.at[x, :, pl.ds(2, 2), y]
                copies.append((parts[2 + pair].at[j, t], target))
    copies = [
        pltpu.make_async_copy(source, target, sems.at[i])
        for i, (source, target) in enumerate(copies)
    ]
    for copy in copies:
        copy.start()
    for copy in copies:
        copy.wait()


def add_terms(index, x_ref, cot_ref, kernel_ref, pre_ref, slope_ref, start_ref):
    frames, block, chans = pre_ref.shape
    half = chans // 2

    def convolve(f, _, a):
        if a > 0:
            total = pre_ref[f]
        elif start_ref is not None:
            total = start_ref[f]
        else:
            total = jnp.zeros((block, chans), jnp.float32)
        for b in range(3):
            piece = x_ref[b, f, a : a + 2, :, lanes(index, half)].reshape(block, half)
            total += lax.dot_general(
                piece,
                kernel_ref[a, b].reshape(chans, half),
                (((1,), (1,)), ((), ())),
                preferred_element_type=jnp.float32,
            )
        pre_ref[f] = total
        return 0

    def blend(f, _):
        total = jnp.zeros((block, half), jnp.float32)
        for k in range(3):
            piece = cot_ref[2 - k + f].reshape(block, chans)
            kernel = kernel_ref[3, k].reshape(chans, half)
            total += jnp.dot(piece, kernel, preferred_element_type=jnp.float32)
        slope_ref[f] = total
        return 0

    for a in range(3):
        lax.fori_loop(0, frames, functools.partial(convolve, a=a), 0)
    lax.fori_loop(0, frames, blend, 0)


def first_kernel(info_ref, x_ref, cot_ref, *refs):
    parts, (pre_ref, slope_ref, kernel_ref, sems) = refs[:4], refs[4:]
    assemble(info_ref, parts, kernel_ref, sems)
    add_terms(info_ref[0], x_ref, cot_ref, kernel_ref, pre_ref, slope_ref, None)


def second_kernel(info_ref, x_ref, cot_ref, *refs):
    parts, (start_ref, mine_ref), refs = refs[:4], refs[4:6], refs[6:]
    hid_mine_ref, hid_other_ref, slope_ref, turned_ref, kernel_ref = refs[:5]
    pre_ref, other_ref, work_ref, sems = refs[5:]
    assemble(info_ref, parts, kernel_ref, sems)
    other = info_ref[0]
    add_terms(other, x_ref, cot_ref, kernel_ref, pre_ref, other_ref, start_ref)
    frames, block, chans = pre_ref.shape
    half = chans // 2
    part = 32
    for hid_ref, source_ref, index in (
        (hid_mine_ref, mine_ref, 1 - other),
        (hid_other_ref, other_ref, other),
    ):

        def finish(step, _, hid_ref=hid_ref, source_ref=source_ref, index=index):
            f, r = step // (block // part), step % (block // part)
            rows = pl.ds(pl.multiple_of(r * part, part), part)
            pre = pre_ref[f, rows, lanes(index, half)]
            sigma = 1.0 / (1.0 + jnp.exp(-pre))
            hid_ref[f, rows] = (pre * sigma).astype(jnp.bfloat16)
            slope = source_ref[f, rows] * sigma * (1.0 + pre * (1.0 - sigma))
            work_ref[f, rows, lanes(index, half)] = slope
            return 0

        lax.fori_loop(0, frames * (block // part), finish, 0)
    for f in range(frames):
        slope = work_ref[f].astype(jnp.bfloat16)
        slope_ref[f] = slope
        turned_ref[:, f * block : (f + 1) * block] = slope.T


def forward(infos, shifts, cot_pad, parts, parts_other):
    frames, _, width, chans = shifts.shape[1:]
    block = 2 * width
    half = chans // 2
    full = jax.ShapeDtypeStruct((frames, block, chans), jnp.float32)
    part = jax.ShapeDtypeStruct((frames, block, half), jnp.float32)
    hid = jax.ShapeDtypeStruct((frames, block, half), jnp.bfloat16)
    kernel = jax.ShapeDtypeStruct((4, 3, 4, 4) + parts[0].shape[-2:], parts[0].dtype)
    sems = pltpu.SemaphoreType.DMA((32,))
    pre, mine, k_mine = pl.pallas_call(
        first_kernel,
        out_shape=(full, part, kernel),
        in_specs=[SMEM, VMEM, VMEM] + [ANY] * 4,
        out_specs=(VMEM,) * 3,
        scratch_shapes=[sems],
        compiler_params=PARAMS,
        cost_estimate=pl.CostEstimate(flops=3200000000, bytes_accessed=12000000, transcendentals=0),
    )(infos[0], shifts, cot_pad, *parts)
    results = pl.pallas_call(
        second_kernel,
        out_shape=(
            hid,
            hid,
            jax.ShapeDtypeStruct((frames, block, chans), jnp.bfloat16),
            jax.ShapeDtypeStruct((chans, frames * block), jnp.bfloat16),
            kernel,
        ),
        in_specs=[SMEM, VMEM, VMEM] + [ANY] * 4 + [VMEM] * 2,
        out_specs=(VMEM,) * 5,
        scratch_shapes=[
            pltpu.VMEM(full.shape, jnp.float32),
            pltpu.VMEM(part.shape, jnp.float32),
            pltpu.VMEM(full.shape, jnp.float32),
            sems,
        ],
        compiler_params=PARAMS,
        cost_estimate=pl.CostEstimate(flops=3200000000, bytes_accessed=15000000, transcendentals=0),
    )(infos[1], shifts, cot_pad, *parts_other, pre, mine)
    return k_mine, results


def weight_kernel(
    upper,
    info_ref,
    turned_ref,
    turned_pair_ref,
    x_ref,
    x_pair_ref,
    cot_ref,
    cot_pair_ref,
    hid_ref,
    hid_pair_ref,
    terms_ref,
    sent_ref,
):
    half = x_pair_ref.shape[-1]
    count = turned_ref.shape[1]
    block = count // 2
    own = terms_ref.shape[-2]
    outs = pl.ds(half * upper, half)

    def keep(total, group, b):
        for zh in range(2):
            for y in range(4):
                row = (4 * zh + y) * own
                slots = info_ref[1 + group], info_ref[5 + y]
                slots = slots[::-1] if upper else slots
                terms_ref[slots[0], slots[1], b, zh] = total[row : row + own]

    def spatial(a, _):
        for b in range(3):
            piece = x_ref[b, :, pl.ds(a, 2), :, lanes(info_ref[0], half)].reshape(count, half)
            total = jnp.dot(turned_ref[outs], piece, preferred_element_type=jnp.float32)
            piece = x_pair_ref[b, :, pl.ds(a, 2)].reshape(count, half)
            total += jnp.dot(turned_pair_ref[outs], piece, preferred_element_type=jnp.float32)
            keep(total, a, b)
        return 0

    lax.fori_loop(0, 3, spatial, 0)
    for k in range(3):
        piece = cot_ref[outs, (2 - k) * block : (4 - k) * block]
        total = jnp.dot(piece, hid_ref[...], preferred_element_type=jnp.float32)
        piece = cot_pair_ref[outs, (2 - k) * block : (4 - k) * block]
        total += jnp.dot(piece, hid_pair_ref[...], preferred_element_type=jnp.float32)
        keep(total, 3, k)
    for slot in range(2):
        for i in range(4):
            sent_ref[slot, i] = terms_ref[2 + slot, i].astype(jnp.bfloat16)


def weight_terms(upper, own, info, *operands):
    half = operands[-1].shape[-1]
    shape = (4, 4, 3, 2, own, half)
    return pl.pallas_call(
        functools.partial(weight_kernel, upper),
        out_shape=(
            jax.ShapeDtypeStruct(shape, jnp.float32),
            jax.ShapeDtypeStruct((2,) + shape[1:], jnp.bfloat16),
        ),
        in_specs=[SMEM] + [VMEM] * 8,
        out_specs=(VMEM, VMEM),
        compiler_params=PARAMS,
        cost_estimate=pl.CostEstimate(flops=2400000000, bytes_accessed=16000000, transcendentals=0),
    )(info, *operands)


def grad_kernel(info_ref, x_ref, cot_ref, mine_ref, other_ref, out_ref):
    frames, block, chans = out_ref.shape
    half = chans // 2
    for kernel_ref, index in ((mine_ref, info_ref[0]), (other_ref, 1 - info_ref[0])):
        for a in range(3):

            def convolve(f, _, kernel_ref=kernel_ref, index=index, a=a):
                if a > 0:
                    total = out_ref[f, :, lanes(index, half)]
                else:
                    total = cot_ref[f, :, lanes(index, half)].astype(jnp.float32)
                for b in range(3):
                    piece = x_ref[2 - b, f, 2 - a : 4 - a].reshape(block, chans)
                    kernel = kernel_ref[a, b].reshape(chans, half)
                    total += jnp.dot(piece, kernel, preferred_element_type=jnp.float32)
                out_ref[f, :, lanes(index, half)] = total
                return 0

            lax.fori_loop(0, frames, convolve, 0)


def input_gradient(info, shifts, cotangent, k_mine, k_other):
    frames, rows, width, chans = cotangent.shape
    return pl.pallas_call(
        grad_kernel,
        out_shape=jax.ShapeDtypeStruct((frames, rows * width, chans), jnp.float32),
        in_specs=[SMEM] + [VMEM] * 4,
        out_specs=VMEM,
        compiler_params=PARAMS,
        cost_estimate=pl.CostEstimate(flops=3600000000, bytes_accessed=16000000, transcendentals=0),
    )(info, shifts, cotangent.reshape(frames, rows * width, chans), k_mine, k_other)


def kernel_unit(spatial_kernel, temporal_kernel, half):
    both = jnp.concatenate(
        [spatial_kernel.transpose(1, 0, 2), temporal_kernel.transpose(1, 0, 2)], axis=0
    )
    start = (3 * lax.axis_index("x"), 0, lax.axis_index("core") * half)
    unit = lax.dynamic_slice(both, start, (3, both.shape[1], half))
    return gathered(unit, "zh").transpose(1, 0, 2, 3)


def kernel_parts(unit, waited):
    lower = jnp.concatenate(ring_gather(unit[:, :2], "y"))
    upper = jnp.concatenate(ring_gather(unit[:, 2:], "x"))
    lower, lower_near = lower, exchange(lower, "x", 0)
    upper, upper_near = upper, exchange(upper, "y", 0)
    (lower_near, upper_near), waited = lax.optimization_barrier(((lower_near, upper_near), waited))
    lower = jnp.stack([lower, lower_near])
    upper = jnp.stack([upper, upper_near])
    lower_rest, upper_rest = exchange(lower, "x", 1), exchange(upper, "y", 1)
    mine = (lower, lower_rest, upper, upper_rest)
    return mine, tuple(swap(part) for part in mine), waited


def per_device(activations, cotangent, spatial_kernel, temporal_kernel):
    frames, rows, width, chans = activations.shape
    count = frames * rows * width
    half = chans // 2
    core = lax.axis_index("core").astype(jnp.int32).reshape(1)
    own = spatial_kernel.shape[0]
    infos = [
        jnp.concatenate([core ^ turn, slots_in("x", turn), slots_in("y", turn)])
        for turn in range(2)
    ]

    unit = kernel_unit(spatial_kernel, temporal_kernel, half)
    edges = (activations, cotangent)
    edges, unit = lax.optimization_barrier((edges, unit))
    x_wide = widened(edges[0], edges_of(edges[0], SPACE, 1), SPACE, 1)
    cot_pad = widened(edges[1], edges_of(edges[1], TM, 0), TM, 0)
    parts, parts_other, (x_wide, cot_pad) = kernel_parts(unit, (x_wide, cot_pad))
    x_pair = swap(lax.dynamic_slice_in_dim(x_wide, (1 - core[0]) * half, half, axis=3))
    shifts = column_shifts(x_wide)
    shifts_pair = column_shifts(x_pair)
    cot_turned = cot_pad.reshape((frames + 2) * rows * width, chans).T
    cot_turned_pair = swap(cot_turned)
    (shifts_pair, cot_turned_pair), parts_other = lax.optimization_barrier(
        ((shifts_pair, cot_turned_pair), parts_other)
    )

    k_mine, results = forward(infos, shifts, cot_pad, parts, parts_other)
    hid_mine, hid_other, slope_pre, turned, k_other = results
    turned_pair, hid_pair = swap(turned), swap(hid_other)
    slope_maps = slope_pre.reshape(frames, rows, width, chans)
    slope_edges = edges_of(slope_maps, SPACE, 1)
    operands = (
        turned,
        turned_pair,
        shifts,
        shifts_pair,
        cot_turned,
        cot_turned_pair,
        hid_mine.reshape(count, half),
        hid_pair.reshape(count, half),
    )
    info = jnp.concatenate([core, slots_of("x"), slots_of("y")])
    lower, sent_lower = weight_terms(0, own, info, *operands)
    info, sent_lower, slope_edges = lax.optimization_barrier((info, sent_lower, slope_edges))
    upper, sent_upper = weight_terms(1, own, info, *operands)
    slope_wide = widened(slope_maps, slope_edges, SPACE, 1)
    slope_wide, sent_upper = lax.optimization_barrier((slope_wide, sent_upper))
    grad = input_gradient(core, column_shifts(slope_wide), cotangent, k_mine, k_other)

    lower = ring_scatter(lower, sent_lower, "x", grad)
    upper = ring_scatter(upper, sent_upper, "y", grad)
    lower = ring_scatter(lower, lower[2:], "y")
    upper = ring_scatter(upper, upper[2:], "x")
    terms = jnp.concatenate([lower, upper], axis=1)
    terms = terms.reshape(3, 4, 2, own // 2, half).transpose(1, 2, 0, 3, 4)
    terms = scattered(terms.reshape(8, 3, own // 2, half), ("zh", "zl"))
    pixels = count * lax.axis_size(TM) * lax.axis_size(SPACE)
    terms = gathered(terms * (1.0 / math.sqrt(pixels)), TM)
    terms = terms.reshape(4, 2, 2, 3, own // 2, half).transpose(0, 3, 1, 4, 2, 5)
    spatial = terms[:3].reshape(9, own, chans).transpose(1, 0, 2)
    temporal = terms[3].reshape(3, own, chans).transpose(1, 0, 2)
    return grad.reshape(frames, rows, width, chans), spatial, temporal


def solution(mesh):
    split = Mesh(mesh.devices.reshape(4, 2, 2, 4, 4), TM + SPACE)
    maps = P(TM, SPACE, None, None)
    kernels = P(SPACE, None, None)
    return jax.shard_map(
        per_device,
        mesh=split,
        in_specs=(maps, maps, kernels, kernels),
        out_specs=(maps, kernels, kernels),
        check_vma=False,
    )
```

time: 242 us -> 198 us (0.82)
  matrix products: 38.5 us -> 0 us
  local copies, waits for them, and re-layouts: 36.2 us -> 10.6 us
  blocking collectives: 16.8 us -> 41.5 us
  waiting for transfers between devices: 28.5 us -> 45.4 us
  starting transfers between devices: 76.3 us -> 63.9 us
  other arithmetic: 19.4 us -> 7.67 us
  Pallas kernels: 23.5 us -> 27.5 us
    dot_general x18 -> x0, matrix products: 38.5 us -> none  [per_device(): jnp.dot(piece, kernel[tap], preferred_element_type=jnp.float32)]
    all_to_all x3 -> x0, starting transfers between devices: 26.7 us -> none  [scattered(): lax.all_to_all(block, axis, 0, 0, tiled=True).astype(jnp.float32)]
    ppermute x8 -> x16, waiting for transfers between devices: 0.47 us -> 25 us  [exchange(): return lax.ppermute(block, names, pairs)]
    ppermute x8 -> x16, starting transfers between devices: 10.8 us -> 29.8 us  [exchange(): return lax.ppermute(block, names, pairs)]
    all_to_all x0 -> x1, blocking collectives: none -> 15.9 us  [scattered(): lax.all_to_all(block, axis, 0, 0, tiled=True).astype(jnp.float32)]
    dynamic_update_slice x8 -> x0, local copies, waits for them, and re-layouts: 10.4 us -> none  [placed(): lax.dynamic_update_slice(target, jnp.expand_dims(block, dim), start)]
    all_to_all x1, blocking collectives: 16.8 us -> 25.6 us  [gathered(): return lax.all_to_all(spread, axis, 0, 0, tiled=True)]
    all_to_all x3 -> x1, starting transfers between devices: 16.7 us -> 9.01 us  [gathered(): return lax.all_to_all(spread, axis, 0, 0, tiled=True)]
  transfers between devices with their start and end apart: 25 -> 31, of which waited for: 10 -> 12; matrix products, arithmetic and copies ran while one was open for 30% -> 5% of each run, Pallas kernels for 7% -> 8%
where the time goes in v1:
time: 198 us
  starting transfers between devices  63.9 us (32%)
  waiting for transfers between devices  45.4 us (23%)
  blocking collectives  41.5 us (21%)
  Pallas kernels  27.5 us (14%)
  local copies, waits for them, and re-layouts  10.6 us (5%)
  other arithmetic  7.67 us (4%)
    ppermute x16, starting transfers between devices, exchange(): return lax.ppermute(block, names, pairs)  29.8 us
    all_to_all x1, blocking collectives, gathered(): return lax.all_to_all(spread, axis, 0, 0, tiled=True)  25.6 us
    ppermute x16, waiting for transfers between devices, exchange(): return lax.ppermute(block, names, pairs)  25 us
    all_to_all x1, blocking collectives, scattered(): lax.all_to_all(block, axis, 0, 0, tiled=True).astype(jnp.float32)  15.9 us
    ppermute x3, starting transfers between devices, edges_of(): high = lax.ppermute(lax.slice_in_dim(block, 0, 1, axis=dim), axis, backward)  15 us
    ppermute x8, starting transfers between devices, swap(): return lax.ppermute(block, 'core', PAIR)  9.38 us
    all_to_all x1, starting transfers between devices, gathered(): return lax.all_to_all(spread, axis, 0, 0, tiled=True)  9.01 us
    all_to_all x1, waiting for transfers between devices, gathered(): return lax.all_to_all(spread, axis, 0, 0, tiled=True)  7.61 us
  transfers between devices with their start and end apart: 31, of which 12 were waited for; matrix products, arithmetic and copies ran while one was open for 5% of the time, Pallas kernels for 8%

profile of v1, /device:TPU:1, one launch (start us, length us, event | category | flops | bytes accessed | tf_op | source)
XLA Modules:
  0.0 197.7 jit_solution(275042172187507491)
XLA Ops:
  0.6 0.9 fusion.14
  1.6 0.7 broadcast_in_dim.36
  2.2 9.0 %all-to-all-start = ((bf16[4,3,32,256]{3,2,1,0:T(8,128)(2,1)}), bf16[4,3,32,256]{3,2,1,0:T(8,128)(2,1)S(1)}, u32[]{:S(2)}, u32[]{:S(2)}) async-start(bf16[4,3,32,256]{3,2,1,0:T(8,128)(2,1)} %broadcast_in_dim.36), calls=%async_computation | async-start | bytes 393216 | tf_op jit(solution)/shard_map/all_to_all | solution.py:72
  11.4 7.6 %all-to-all-done = bf16[4,3,32,256]{3,2,1,0:T(8,128)(2,1)S(1)} async-done(((bf16[4,3,32,256]{3,2,1,0:T(8,128)(2,1)}), bf16[4,3,32,256]{3,2,1,0:T(8,128)(2,1)S(1)}, u32[]{:S(2)}, u32[]{:S(2)}) %all-to-all-start) | async-done | bytes 196640 | tf_op jit(solution)/shard_map/all_to_all | solution.py:72
  19.1 2.8 %collective-permute-start = (bf16[3,2,32,256]{3,2,1,0:T(8,128)(2,1)S(1)}, bf16[3,2,32,256]{3,2,1,0:T(8,128)(2,1)S(1)}, u32[]{:S(2)}, u32[]{:S(2)}) collective-permute-start(bf16[3,2,32,256]{3,2,1,0:T(8,128)(2,1)S(1)} %get-tuple-element.88), channel_id=1, source_target_pairs={{0,1},{1,0},{2,3},{3,2},{16,19},{17,18},{18,17},{19,16},{4,5},{5,4... | collective-permute-start | bytes 294920 | tf_op jit(solution)/shard_map/ppermute | solution.py:35
  21.9 2.5 %collective-permute-start.3 = (bf16[3,2,32,256]{3,2,1,0:T(8,128)(2,1)S(1)}, bf16[3,2,32,256]{3,2,1,0:T(8,128)(2,1)S(1)}, u32[]{:S(2)}, u32[]{:S(2)}) collective-permute-start(bf16[3,2,32,256]{3,2,1,0:T(8,128)(2,1)S(1)} %get-tuple-element.87), channel_id=1, source_target_pairs={{0,64},{64,0},{128,192},{192,128},{16,208},{80,144},{144,80},{208,... | collective-permute-start | bytes 294920 | tf_op jit(solution)/shard_map/ppermute | solution.py:35
  24.5 1.7 collective-permute-start.7
  26.3 0.3 collective-permute-done.3
  26.6 0.4 collective-permute-start.4
  27.1 7.6 %collective-permute-start.9 = (bf16[1,2,192,512]{3,2,1,0:T(8,128)(2,1)S(1)}, bf16[1,2,192,512]{3,2,1,0:T(8,128)(2,1)S(1)}, u32[]{:S(2)}, u32[]{:S(2)}) collective-permute-start(bf16[1,2,192,512]{3,2,1,0:T(8,128)(2,1)S(1)} %get-tuple-element.78), channel_id=1, source_target_pairs={{16,0},{32,16},{48,32},{64,48},{80,64},{96,80},{112,96},{128,112},... | collective-permute-start | bytes 1179656 | tf_op jit(solution)/shard_map/ppermute | solution.py:85
  34.7 3.1 %collective-permute-done.1 = bf16[2,3,2,32,256]{4,3,2,1,0:T(8,128)(2,1)S(1)} collective-permute-done((bf16[2,3,2,32,256]{4,3,2,1,0:T(8,128)(2,1)S(1)}, bf16[2,3,2,32,256]{4,3,2,1,0:T(8,128)(2,1)S(1)}, u32[]{:S(2)}, u32[]{:S(2)}) %collective-permute-start.1) | collective-permute-done | bytes 196640 | tf_op jit(solution)/shard_map/ppermute | solution.py:35
  37.8 0.6 collective-permute-start.8
  38.5 2.6 %collective-permute-start.2 = (bf16[4,3,2,32,256]{4,3,2,1,0:T(8,128)(2,1)S(1)}, bf16[4,3,2,32,256]{4,3,2,1,0:T(8,128)(2,1)S(1)}, u32[]{:S(2)}, u32[]{:S(2)}) collective-permute-start(bf16[4,3,2,32,256]{4,3,2,1,0:T(8,128)(2,1)S(1)} %get-tuple-element.84), channel_id=1, source_target_pairs={{0,64},{64,0},{128,192},{192,128},{16,208},{80,144},{144,80},{208,... | collective-permute-start | bytes 1179656 | tf_op jit(solution)/shard_map/ppermute | solution.py:35
  41.1 0.8 fusion.15
  41.9 2.4 %collective-permute-start.5 = (bf16[4,3,2,32,256]{4,3,2,1,0:T(8,128)(2,1)S(1)}, bf16[4,3,2,32,256]{4,3,2,1,0:T(8,128)(2,1)S(1)}, u32[]{:S(2)}, u32[]{:S(2)}) collective-permute-start(bf16[4,3,2,32,256]{4,3,2,1,0:T(8,128)(2,1)S(1)} %get-tuple-element.82), channel_id=1, source_target_pairs={{0,1},{1,0},{2,3},{3,2},{16,19},{17,18},{18,17},{19,16},{4,5},{5,4... | collective-permute-start | bytes 1179656 | tf_op jit(solution)/shard_map/ppermute | solution.py:35
  44.3 0.2 pad_maximum_fusion.3
  44.5 7.3 %collective-permute-done.9 = bf16[1,2,192,512]{3,2,1,0:T(8,128)(2,1)S(1)} collective-permute-done((bf16[1,2,192,512]{3,2,1,0:T(8,128)(2,1)S(1)}, bf16[1,2,192,512]{3,2,1,0:T(8,128)(2,1)S(1)}, u32[]{:S(2)}, u32[]{:S(2)}) %collective-permute-start.9) | collective-permute-done | bytes 393248 | tf_op jit(solution)/shard_map/ppermute | solution.py:85
  51.9 1.3 pad_maximum_fusion.4.cot_ref
  53.2 1.0 constant_dynamic-slice_fusion
  54.3 0.3 collective-permute-start.10
  54.6 1.7 copy.13
  56.4 0.3 collective-permute-start.11
  56.6 1.2 pad_maximum_fusion.6.refs_0_
  58.2 0.5 fusion.18
  58.7 4.3 %collective-permute-start.12 = (bf16[2,4,3,2,32,256]{5,4,3,2,1,0:T(8,128)(2,1)S(1)}, bf16[2,4,3,2,32,256]{5,4,3,2,1,0:T(8,128)(2,1)S(1)}, u32[]{:S(2)}, u32[]{:S(2)}) collective-permute-start(bf16[2,4,3,2,32,256]{5,4,3,2,1,0:T(8,128)(2,1)S(1)} %pad_maximum_fusion.6.refs_0_), channel_id=1, source_target_pairs={{0,16},{16,0},{1,17},{17,1},{2,18},{18,2},{3,19},{19,3},{4,20},{20... | collective-permute-start | bytes 2359304 | tf_op jit(solution)/shard_map/ppermute | solution.py:22
  63.1 0.5 pad_bitcast_fusion.2
  63.6 0.6 pad_maximum_fusion.x_ref
  64.2 0.3 collective-permute-start.15
  64.5 4.6 %collective-permute-done.13.refs_1_ = bf16[2,4,3,2,32,256]{5,4,3,2,1,0:T(8,128)(2,1)S(1)} collective-permute-done((bf16[2,4,3,2,32,256]{5,4,3,2,1,0:T(8,128)(2,1)S(1)}, bf16[2,4,3,2,32,256]{5,4,3,2,1,0:T(8,128)(2,1)S(1)}, u32[]{:S(2)}, u32[]{:S(2)}) %collective-permute-start.13) | collective-permute-done | bytes 786464 | tf_op jit(solution)/shard_map/ppermute | solution.py:35
  69.0 2.4 %collective-permute-start.14 = (bf16[2,4,3,2,32,256]{5,4,3,2,1,0:T(8,128)(2,1)S(1)}, bf16[2,4,3,2,32,256]{5,4,3,2,1,0:T(8,128)(2,1)S(1)}, u32[]{:S(2)}, u32[]{:S(2)}) collective-permute-start(bf16[2,4,3,2,32,256]{5,4,3,2,1,0:T(8,128)(2,1)S(1)} %collective-permute-done.13.refs_1_), channel_id=1, source_target_pairs={{0,16},{16,0},{1,17},{17,1},{2,18},{18,2},{3,19},{19,3},{4,20},{20... | collective-permute-start | bytes 2359304 | tf_op jit(solution)/shard_map/ppermute | solution.py:22
  71.4 1.2 collective-permute-start.17
  72.6 0.2 fusion.20
  72.9 0.2 pad_bitcast_fusion.4
  73.1 0.3 pad_maximum_fusion.2.x_pair_ref
  73.4 1.1 copy-done.1
  74.5 5.5 %shard_map.67 = (f32[2,384,512]{2,1,0:T(8,128)S(1)}, f32[2,384,256]{2,1,0:T(8,128)S(1)}, bf16[4,3,4,4,32,256]{5,4,3,2,1,0:T(8,128)(2,1)S(1)}) custom-call(s32[9]{0:T(128)S(1)} %concatenate.61.info_ref, bf16[3,2,4,192,512]{4,3,2,1,0:T(8,128)(2,1)S(1)} %pad_maximum_fusion.x_ref, bf16[4,2,192,512]{3,2,1,0:T(8,128)(2,1)S(1)} %copy-done.1, ...), custom_call_target="tpu_custom_call" | custom-call | flops 3200000000 | bytes 12000000 | tf_op jit(solution)/shard_map/pallas_call | solution.py:217
  80.1 7.6 %shard_map.68 = (bf16[2,384,256]{2,1,0:T(8,128)(2,1)S(1)}, bf16[2,384,256]{2,1,0:T(8,128)(2,1)S(1)}, bf16[2,384,512]{2,1,0:T(8,128)(2,1)S(1)}, bf16[512,768]{1,0...) custom-call(s32[9]{0:T(128)S(1)} %concatenate.51.info_ref, bf16[3,2,4,192,512]{4,3,2,1,0:T(8,128)(2,1)S(1)} %pad_maximum_fusion.x_ref, ...), custom_call_target="tpu_custom_call" | custom-call | flops 3200000000 | bytes 15000000 | tf_op jit(solution)/shard_map/pallas_call | solution.py:226
  87.8 0.5 collective-permute-start.19
  88.4 5.7 %collective-permute-start.21 = (bf16[2,1,192,512]{3,2,1,0:T(8,128)(2,1)S(1)}, bf16[2,1,192,512]{3,2,1,0:T(8,128)(2,1)S(1)}, u32[]{:S(2)}, u32[]{:S(2)}) collective-permute-start(bf16[2,1,192,512]{3,2,1,0:T(8,128)(2,1)S(1)} %get-tuple-element.73), channel_id=1, source_target_pairs={{1,0},{2,1},{3,2},{4,3},{5,4},{6,5},{7,6},{8,7},{9,8},{10,9},{11,1... | collective-permute-start | bytes 1179656 | tf_op jit(solution)/shard_map/ppermute | solution.py:85
  94.2 3.8 %shard_map.69 = (f32[4,4,3,2,32,256]{5,4,3,2,1,0:T(8,128)S(1)}, bf16[2,4,3,2,32,256]{5,4,3,2,1,0:T(8,128)(2,1)S(1)}) custom-call(s32[9]{0:T(128)S(1)} %pad_add_fusion.info_ref, bf16[512,768]{1,0:T(8,128)(2,1)S(1)} %get-tuple-element.49.turned_ref, bf16[512,768]{1,0:T(8,128)(2,1)S(1)} %collective-permute-done.18.turned_pair_ref, ...), custom_call_target="tpu_custom_call" | custom-call | flops 2400000000 | bytes 16000000 | tf_op jit(solution)/shard_map/pallas_call | solution.py:301
  98.0 5.5 %collective-permute-done.20 = bf16[2,1,192,512]{3,2,1,0:T(8,128)(2,1)S(1)} collective-permute-done((bf16[2,1,192,512]{3,2,1,0:T(8,128)(2,1)S(1)}, bf16[2,1,192,512]{3,2,1,0:T(8,128)(2,1)S(1)}, u32[]{:S(2)}, u32[]{:S(2)}) %collective-permute-start.20) | collective-permute-done | bytes 393248 | tf_op jit(solution)/shard_map/ppermute | solution.py:84
  103.7 3.8 %shard_map.70 = (f32[4,4,3,2,32,256]{5,4,3,2,1,0:T(8,128)S(1)}, bf16[2,4,3,2,32,256]{5,4,3,2,1,0:T(8,128)(2,1)S(1)}) custom-call(s32[9]{0:T(128)S(1)} %pad_add_fusion.info_ref, bf16[512,768]{1,0:T(8,128)(2,1)S(1)} %get-tuple-element.49.turned_ref, bf16[512,768]{1,0:T(8,128)(2,1)S(1)} %collective-permute-done.18.turned_pair_ref, ...), custom_call_target="tpu_custom_call" | custom-call | flops 2400000000 | bytes 16000000 | tf_op jit(solution)/shard_map/pallas_call | solution.py:301
  107.5 0.5 fusion.17
  108.2 3.9 %collective-permute-start.26 = (bf16[2,4,3,2,32,256]{5,4,3,2,1,0:T(8,128)(2,1)S(1)}, bf16[2,4,3,2,32,256]{5,4,3,2,1,0:T(8,128)(2,1)S(1)}, u32[]{:S(2)}, u32[]{:S(2)}) collective-permute-start(bf16[2,4,3,2,32,256]{5,4,3,2,1,0:T(8,128)(2,1)S(1)} %get-tuple-element.67), channel_id=1, source_target_pairs={{0,1},{1,0},{2,3},{3,2},{16,19},{17,18},{18,17},{19,16},{4,5},{5,4... | collective-permute-start | bytes 2359304 | tf_op jit(solution)/shard_map/ppermute | solution.py:35
  112.1 9.3 %collective-permute-start.22 = (bf16[2,4,3,2,32,256]{5,4,3,2,1,0:T(8,128)(2,1)S(1)}, bf16[2,4,3,2,32,256]{5,4,3,2,1,0:T(8,128)(2,1)S(1)}, u32[]{:S(2)}, u32[]{:S(2)}) collective-permute-start(bf16[2,4,3,2,32,256]{5,4,3,2,1,0:T(8,128)(2,1)S(1)} %get-tuple-element.64), channel_id=1, source_target_pairs={{0,64},{64,0},{128,192},{192,128},{16,208},{80,144},{144,80},{208,... | collective-permute-start | bytes 2359304 | tf_op jit(solution)/shard_map/ppermute | solution.py:35
  121.5 0.4 pad_bitcast_fusion.1
  121.9 0.6 pad_maximum_fusion.1.x_ref
  122.5 6.8 %shard_map.71 = f32[2,384,512]{2,1,0:T(8,128)} custom-call(s32[1]{0:T(128)} %bitcast.info_ref, bf16[3,2,4,192,512]{4,3,2,1,0:T(8,128)(2,1)S(1)} %pad_maximum_fusion.1.x_ref, bf16[2,384,512]{2,1,0:T(8,128)(2,1)S(1)} %bitcast.88, bf16[4,3,4,4,32,256]{5,4,3,2,1,0:T(8,128)(2,1)S(1)} %get-tuple-element.61.mine_ref, ...), custom_call_target="tpu_custom_call" | custom-call | flops 3600000000 | bytes 16000000 | tf_op jit(solution)/shard_map/pallas_call | solution.py:337
  129.7 1.1 collective-permute-done.22
  131.3 5.0 %collective-permute-done.27 = bf16[4,3,2,32,256]{4,3,2,1,0:T(8,128)(2,1)S(1)} collective-permute-done((bf16[4,3,2,32,256]{4,3,2,1,0:T(8,128)(2,1)S(1)}, bf16[4,3,2,32,256]{4,3,2,1,0:T(8,128)(2,1)S(1)}, u32[]{:S(2)}, u32[]{:S(2)}) %collective-permute-start.27) | collective-permute-done | bytes 393248 | tf_op jit(solution)/shard_map/ppermute | solution.py:35
  136.4 0.2 fusion.2
  136.6 2.0 collective-permute-start.28
  138.6 0.2 fusion.5
  138.8 2.8 %collective-permute-start.24 = (f32[2,3,2,32,256]{4,3,2,1,0:T(8,128)S(1)}, f32[2,3,2,32,256]{4,3,2,1,0:T(8,128)S(1)}, u32[]{:S(2)}, u32[]{:S(2)}) collective-permute-start(f32[2,3,2,32,256]{4,3,2,1,0:T(8,128)S(1)} %slice.143), channel_id=1, source_target_pairs={{0,1},{1,0},{2,3},{3,2},{16,19},{17,18},{18,17},{19,16},{4,5},{5,4... | collective-permute-start | bytes 1179656 | tf_op jit(solution)/shard_map/ppermute | solution.py:35
  141.6 3.9 %collective-permute-done.28 = f32[2,3,2,32,256]{4,3,2,1,0:T(8,128)S(1)} collective-permute-done((f32[2,3,2,32,256]{4,3,2,1,0:T(8,128)S(1)}, f32[2,3,2,32,256]{4,3,2,1,0:T(8,128)S(1)}, u32[]{:S(2)}, u32[]{:S(2)}) %collective-permute-start.28) | collective-permute-done | bytes 393248 | tf_op jit(solution)/shard_map/ppermute | solution.py:35
  145.5 0.6 collective-permute-start.29
  146.1 0.7 collective-permute-done.24
  146.9 3.6 %collective-permute-done.29 = f32[3,2,32,256]{3,2,1,0:T(8,128)S(1)} collective-permute-done((f32[3,2,32,256]{3,2,1,0:T(8,128)S(1)}, f32[3,2,32,256]{3,2,1,0:T(8,128)S(1)}, u32[]{:S(2)}, u32[]{:S(2)}) %collective-permute-start.29) | collective-permute-done | bytes 196640 | tf_op jit(solution)/shard_map/ppermute | solution.py:35
  150.5 2.7 %collective-permute-done.25 = f32[3,2,32,256]{3,2,1,0:T(8,128)S(1)} collective-permute-done((f32[3,2,32,256]{3,2,1,0:T(8,128)S(1)}, f32[3,2,32,256]{3,2,1,0:T(8,128)S(1)}, u32[]{:S(2)}, u32[]{:S(2)}) %collective-permute-start.25) | collective-permute-done | bytes 196640 | tf_op jit(solution)/shard_map/ppermute | solution.py:35
  153.3 15.9 %all_to_all.15 = f32[8,3,16,256]{3,2,1,0:T(8,128)S(1)} all-to-all(f32[8,3,16,256]{3,2,1,0:T(8,128)S(1)} %bitcast.102), channel_id=1, replica_groups=mesh['x'=4,'zl'=2,'core'=2,'zh'=4,'y'=4] {'zh','zl'}, dimensions={0} | all-to-all | bytes 786432 | tf_op jit(solution)/shard_map/all_to_all | solution.py:76
  169.3 25.6 %all_to_all.16 = f32[16,3,16,256]{3,2,1,0:T(8,128)S(1)} all-to-all(f32[16,3,16,256]{3,2,1,0:T(8,128)S(1)} %broadcast_in_dim.37), channel_id=1, replica_groups=mesh['x'=4,'zl'=2,'core'=2,'zh'=4,'y'=4] {'x','zl','core'}, dimensions={0} | all-to-all | bytes 1572864 | tf_op jit(solution)/shard_map/all_to_all | solution.py:72
  195.0 0.5 copy.15
  195.5 1.3 reshape.63
  196.9 0.8 reshape_squeeze.3
  (84 shorter events, 3.4 us)
Async XLA Ops:
  0.6 23.8 %copy-start.4 = (bf16[2,2,192,512]{3,2,1,0:T(8,128)(2,1)S(1)}, bf16[2,2,192,512]{3,2,1,0:T(8,128)(2,1)}, u32[]{:S(2)}) copy-start(bf16[2,2,192,512]{3,2,1,0:T(8,128)(2,1)} %param.4) | copy-start | bytes 2359300
  2.2 16.8 %all-to-all-start = ((bf16[4,3,32,256]{3,2,1,0:T(8,128)(2,1)}), bf16[4,3,32,256]{3,2,1,0:T(8,128)(2,1)S(1)}, u32[]{:S(2)}, u32[]{:S(2)}) async-start(bf16[4,3,32,256]{3,2,1,0:T(8,128)(2,1)} %broadcast_in_dim.36), calls=%async_computation | async-start | bytes 393216 | tf_op jit(solution)/shard_map/all_to_all | solution.py:72
  19.1 8.0 %copy-start = (bf16[2,2,192,512]{3,2,1,0:T(8,128)(2,1)S(1)}, bf16[2,2,192,512]{3,2,1,0:T(8,128)(2,1)}, u32[]{:S(2)}) copy-start(bf16[2,2,192,512]{3,2,1,0:T(8,128)(2,1)} %param.5) | copy-start | bytes 2359300
  19.1 7.1 %collective-permute-start = (bf16[3,2,32,256]{3,2,1,0:T(8,128)(2,1)S(1)}, bf16[3,2,32,256]{3,2,1,0:T(8,128)(2,1)S(1)}, u32[]{:S(2)}, u32[]{:S(2)}) collective-permute-start(bf16[3,2,32,256]{3,2,1,0:T(8,128)(2,1)S(1)} %get-tuple-element.88), channel_id=1, source_target_pairs={{0,1},{1,0},{2,3},{3,2},{16,19},{17,18},{18,17},{19,16},{4,5},{5,4... | collective-permute-start | bytes 294920 | tf_op jit(solution)/shard_map/ppermute | solution.py:35
  21.9 4.7 %collective-permute-start.3 = (bf16[3,2,32,256]{3,2,1,0:T(8,128)(2,1)S(1)}, bf16[3,2,32,256]{3,2,1,0:T(8,128)(2,1)S(1)}, u32[]{:S(2)}, u32[]{:S(2)}) collective-permute-start(bf16[3,2,32,256]{3,2,1,0:T(8,128)(2,1)S(1)} %get-tuple-element.87), channel_id=1, source_target_pairs={{0,64},{64,0},{128,192},{192,128},{16,208},{80,144},{144,80},{208,... | collective-permute-start | bytes 294920 | tf_op jit(solution)/shard_map/ppermute | solution.py:35
  24.5 17.4 %collective-permute-start.7 = (bf16[2,1,192,512]{3,2,1,0:T(8,128)(2,1)S(1)}, bf16[2,1,192,512]{3,2,1,0:T(8,128)(2,1)S(1)}, u32[]{:S(2)}, u32[]{:S(2)}) collective-permute-start(bf16[2,1,192,512]{3,2,1,0:T(8,128)(2,1)S(1)} %get-tuple-element.80), channel_id=1, source_target_pairs={{1,0},{2,1},{3,2},{4,3},{5,4},{6,5},{7,6},{8,7},{9,8},{10,9},{11,1... | collective-permute-start | bytes 1179656 | tf_op jit(solution)/shard_map/ppermute | solution.py:85
  26.2 18.0 %collective-permute-start.6 = (bf16[2,1,192,512]{3,2,1,0:T(8,128)(2,1)S(1)}, bf16[2,1,192,512]{3,2,1,0:T(8,128)(2,1)S(1)}, u32[]{:S(2)}, u32[]{:S(2)}) collective-permute-start(bf16[2,1,192,512]{3,2,1,0:T(8,128)(2,1)S(1)} %get-tuple-element.79), channel_id=1, source_target_pairs={{0,1},{1,2},{2,3},{3,4},{4,5},{5,6},{6,7},{7,8},{8,9},{9,10},{10,1... | collective-permute-start | bytes 1179656 | tf_op jit(solution)/shard_map/ppermute | solution.py:84
  26.2 11.6 %collective-permute-start.1 = (bf16[2,3,2,32,256]{4,3,2,1,0:T(8,128)(2,1)S(1)}, bf16[2,3,2,32,256]{4,3,2,1,0:T(8,128)(2,1)S(1)}, u32[]{:S(2)}, u32[]{:S(2)}) collective-permute-start(bf16[2,3,2,32,256]{4,3,2,1,0:T(8,128)(2,1)S(1)} %pad_maximum_fusion.11), channel_id=1, source_target_pairs={{0,3},{1,2},{2,1},{3,0},{16,17},{17,16},{18,19},{19,18},{4,7},{5,6... | collective-permute-start | bytes 589832 | tf_op jit(solution)/shard_map/ppermute | solution.py:35
  26.6 11.8 %collective-permute-start.4 = (bf16[2,3,2,32,256]{4,3,2,1,0:T(8,128)(2,1)S(1)}, bf16[2,3,2,32,256]{4,3,2,1,0:T(8,128)(2,1)S(1)}, u32[]{:S(2)}, u32[]{:S(2)}) collective-permute-start(bf16[2,3,2,32,256]{4,3,2,1,0:T(8,128)(2,1)S(1)} %pad_maximum_fusion.12), channel_id=1, source_target_pairs={{0,192},{64,128},{128,64},{192,0},{16,80},{80,16},{144,208},{208,1... | collective-permute-start | bytes 589832 | tf_op jit(solution)/shard_map/ppermute | solution.py:35
  27.1 24.7 %collective-permute-start.9 = (bf16[1,2,192,512]{3,2,1,0:T(8,128)(2,1)S(1)}, bf16[1,2,192,512]{3,2,1,0:T(8,128)(2,1)S(1)}, u32[]{:S(2)}, u32[]{:S(2)}) collective-permute-start(bf16[1,2,192,512]{3,2,1,0:T(8,128)(2,1)S(1)} %get-tuple-element.78), channel_id=1, source_target_pairs={{16,0},{32,16},{48,32},{64,48},{80,64},{96,80},{112,96},{128,112},... | collective-permute-start | bytes 1179656 | tf_op jit(solution)/shard_map/ppermute | solution.py:85
  37.8 14.0 %collective-permute-start.8 = (bf16[1,2,192,512]{3,2,1,0:T(8,128)(2,1)S(1)}, bf16[1,2,192,512]{3,2,1,0:T(8,128)(2,1)S(1)}, u32[]{:S(2)}, u32[]{:S(2)}) collective-permute-start(bf16[1,2,192,512]{3,2,1,0:T(8,128)(2,1)S(1)} %get-tuple-element.77), channel_id=1, source_target_pairs={{0,16},{16,32},{32,48},{48,64},{64,80},{80,96},{96,112},{112,128},... | collective-permute-start | bytes 1179656 | tf_op jit(solution)/shard_map/ppermute | solution.py:84
  38.5 14.7 %collective-permute-start.2 = (bf16[4,3,2,32,256]{4,3,2,1,0:T(8,128)(2,1)S(1)}, bf16[4,3,2,32,256]{4,3,2,1,0:T(8,128)(2,1)S(1)}, u32[]{:S(2)}, u32[]{:S(2)}) collective-permute-start(bf16[4,3,2,32,256]{4,3,2,1,0:T(8,128)(2,1)S(1)} %get-tuple-element.84), channel_id=1, source_target_pairs={{0,64},{64,0},{128,192},{192,128},{16,208},{80,144},{144,80},{208,... | collective-permute-start | bytes 1179656 | tf_op jit(solution)/shard_map/ppermute | solution.py:35
  41.9 11.3 %collective-permute-start.5 = (bf16[4,3,2,32,256]{4,3,2,1,0:T(8,128)(2,1)S(1)}, bf16[4,3,2,32,256]{4,3,2,1,0:T(8,128)(2,1)S(1)}, u32[]{:S(2)}, u32[]{:S(2)}) collective-permute-start(bf16[4,3,2,32,256]{4,3,2,1,0:T(8,128)(2,1)S(1)} %get-tuple-element.82), channel_id=1, source_target_pairs={{0,1},{1,0},{2,3},{3,2},{16,19},{17,18},{18,17},{19,16},{4,5},{5,4... | collective-permute-start | bytes 1179656 | tf_op jit(solution)/shard_map/ppermute | solution.py:35
  44.5 8.7 %copy-start.2 = (bf16[2,4,192,512]{3,2,1,0:T(8,128)(2,1)}, bf16[2,4,192,512]{3,2,1,0:T(8,128)(2,1)S(1)}, u32[]{:S(2)}) copy-start(bf16[2,4,192,512]{3,2,1,0:T(8,128)(2,1)S(1)} %pad_maximum_fusion.3) | copy-start | bytes 4718596
  53.2 1.4 copy-start.6
  53.2 1.4 copy-start.7
  54.3 9.9 %collective-permute-start.10 = (bf16[2,4,192,256]{3,2,1,0:T(8,128)(2,1)}, bf16[2,4,192,256]{3,2,1,0:T(8,128)(2,1)S(1)}, u32[]{:S(2)}, u32[]{:S(2)}) collective-permute-start(bf16[2,4,192,256]{3,2,1,0:T(8,128)(2,1)} %constant_dynamic-slice_fusion), channel_id=1, source_target_pairs={{0,16},{16,0},{1,17},{17,1},{2,18},{18,2},{3,19},{19,3},{4,20},{20... | collective-permute-start | bytes 2359304 | tf_op jit(solution)/shard_map/ppermute | solution.py:22
  56.3 1.6 copy-start.5
  56.4 1.6 copy-start.8
  56.4 23.7 %collective-permute-start.11 = (bf16[512,1536]{1,0:T(8,128)(2,1)S(1)}, bf16[512,1536]{1,0:T(8,128)(2,1)S(1)}, u32[]{:S(2)}, u32[]{:S(2)}) collective-permute-start(bf16[512,1536]{1,0:T(8,128)(2,1)S(1)} %bitcast.85), channel_id=1, source_target_pairs={{0,16},{16,0},{1,17},{17,1},{2,18},{18,2},{3,19},{19,3},{4,20},{20... | collective-permute-start | bytes 4718600 | tf_op jit(solution)/shard_map/ppermute | solution.py:22
  56.6 1.6 copy-start.3
  57.8 11.2 %collective-permute-start.13 = (bf16[2,4,3,2,32,256]{5,4,3,2,1,0:T(8,128)(2,1)S(1)}, bf16[2,4,3,2,32,256]{5,4,3,2,1,0:T(8,128)(2,1)S(1)}, u32[]{:S(2)}, u32[]{:S(2)}) collective-permute-start(bf16[2,4,3,2,32,256]{5,4,3,2,1,0:T(8,128)(2,1)S(1)} %pad_maximum_fusion.6.refs_0_), channel_id=1, source_target_pairs={{0,192},{64,128},{128,64},{192,0},{16,80},{80,16},{144,208},{208,1... | collective-permute-start | bytes 2359304 | tf_op jit(solution)/shard_map/ppermute | solution.py:35
  58.1 13.4 %collective-permute-start.16 = (bf16[2,4,3,2,32,256]{5,4,3,2,1,0:T(8,128)(2,1)S(1)}, bf16[2,4,3,2,32,256]{5,4,3,2,1,0:T(8,128)(2,1)S(1)}, u32[]{:S(2)}, u32[]{:S(2)}) collective-permute-start(bf16[2,4,3,2,32,256]{5,4,3,2,1,0:T(8,128)(2,1)S(1)} %pad_maximum_fusion.7.refs_2_), channel_id=1, source_target_pairs={{0,3},{1,2},{2,1},{3,0},{16,17},{17,16},{18,19},{19,18},{4,7},{5,6... | collective-permute-start | bytes 2359304 | tf_op jit(solution)/shard_map/ppermute | solution.py:35
  58.7 21.3 %collective-permute-start.12 = (bf16[2,4,3,2,32,256]{5,4,3,2,1,0:T(8,128)(2,1)S(1)}, bf16[2,4,3,2,32,256]{5,4,3,2,1,0:T(8,128)(2,1)S(1)}, u32[]{:S(2)}, u32[]{:S(2)}) collective-permute-start(bf16[2,4,3,2,32,256]{5,4,3,2,1,0:T(8,128)(2,1)S(1)} %pad_maximum_fusion.6.refs_0_), channel_id=1, source_target_pairs={{0,16},{16,0},{1,17},{17,1},{2,18},{18,2},{3,19},{19,3},{4,20},{20... | collective-permute-start | bytes 2359304 | tf_op jit(solution)/shard_map/ppermute | solution.py:22
  64.2 15.9 %collective-permute-start.15 = (bf16[2,4,3,2,32,256]{5,4,3,2,1,0:T(8,128)(2,1)S(1)}, bf16[2,4,3,2,32,256]{5,4,3,2,1,0:T(8,128)(2,1)S(1)}, u32[]{:S(2)}, u32[]{:S(2)}) collective-permute-start(bf16[2,4,3,2,32,256]{5,4,3,2,1,0:T(8,128)(2,1)S(1)} %pad_maximum_fusion.7.refs_2_), channel_id=1, source_target_pairs={{0,16},{16,0},{1,17},{17,1},{2,18},{18,2},{3,19},{19,3},{4,20},{20... | collective-permute-start | bytes 2359304 | tf_op jit(solution)/shard_map/ppermute | solution.py:22
  69.0 11.1 %collective-permute-start.14 = (bf16[2,4,3,2,32,256]{5,4,3,2,1,0:T(8,128)(2,1)S(1)}, bf16[2,4,3,2,32,256]{5,4,3,2,1,0:T(8,128)(2,1)S(1)}, u32[]{:S(2)}, u32[]{:S(2)}) collective-permute-start(bf16[2,4,3,2,32,256]{5,4,3,2,1,0:T(8,128)(2,1)S(1)} %collective-permute-done.13.refs_1_), channel_id=1, source_target_pairs={{0,16},{16,0},{1,17},{17,1},{2,18},{18,2},{3,19},{19,3},{4,20},{20... | collective-permute-start | bytes 2359304 | tf_op jit(solution)/shard_map/ppermute | solution.py:22
  71.4 8.7 %collective-permute-start.17 = (bf16[2,4,3,2,32,256]{5,4,3,2,1,0:T(8,128)(2,1)S(1)}, bf16[2,4,3,2,32,256]{5,4,3,2,1,0:T(8,128)(2,1)S(1)}, u32[]{:S(2)}, u32[]{:S(2)}) collective-permute-start(bf16[2,4,3,2,32,256]{5,4,3,2,1,0:T(8,128)(2,1)S(1)} %collective-permute-done.16.refs_3_), channel_id=1, source_target_pairs={{0,16},{16,0},{1,17},{17,1},{2,18},{18,2},{3,19},{19,3},{4,20},{20... | collective-permute-start | bytes 2359304 | tf_op jit(solution)/shard_map/ppermute | solution.py:22
  73.1 1.4 copy-start.1
  87.7 6.5 %collective-permute-start.18 = (bf16[512,768]{1,0:T(8,128)(2,1)S(1)}, bf16[512,768]{1,0:T(8,128)(2,1)S(1)}, u32[]{:S(2)}, u32[]{:S(2)}) collective-permute-start(bf16[512,768]{1,0:T(8,128)(2,1)S(1)} %get-tuple-element.49.turned_ref), channel_id=1, source_target_pairs={{0,16},{16,0},{1,17},{17,1},{2,18},{18,2},{3,19},{19,3},{4,20},{20... | collective-permute-start | bytes 2359304 | tf_op jit(solution)/shard_map/ppermute | solution.py:22
  87.8 6.4 %collective-permute-start.19 = (bf16[2,384,256]{2,1,0:T(8,128)(2,1)S(1)}, bf16[2,384,256]{2,1,0:T(8,128)(2,1)S(1)}, u32[]{:S(2)}, u32[]{:S(2)}) collective-permute-start(bf16[2,384,256]{2,1,0:T(8,128)(2,1)S(1)} %get-tuple-element.53), channel_id=1, source_target_pairs={{0,16},{16,0},{1,17},{17,1},{2,18},{18,2},{3,19},{19,3},{4,20},{20... | collective-permute-start | bytes 1179656 | tf_op jit(solution)/shard_map/ppermute | solution.py:22
  88.3 15.2 %collective-permute-start.20 = (bf16[2,1,192,512]{3,2,1,0:T(8,128)(2,1)S(1)}, bf16[2,1,192,512]{3,2,1,0:T(8,128)(2,1)S(1)}, u32[]{:S(2)}, u32[]{:S(2)}) collective-permute-start(bf16[2,1,192,512]{3,2,1,0:T(8,128)(2,1)S(1)} %get-tuple-element.74), channel_id=1, source_target_pairs={{0,1},{1,2},{2,3},{3,4},{4,5},{5,6},{6,7},{7,8},{8,9},{9,10},{10,1... | collective-permute-start | bytes 1179656 | tf_op jit(solution)/shard_map/ppermute | solution.py:84
  88.4 15.1 %collective-permute-start.21 = (bf16[2,1,192,512]{3,2,1,0:T(8,128)(2,1)S(1)}, bf16[2,1,192,512]{3,2,1,0:T(8,128)(2,1)S(1)}, u32[]{:S(2)}, u32[]{:S(2)}) collective-permute-start(bf16[2,1,192,512]{3,2,1,0:T(8,128)(2,1)S(1)} %get-tuple-element.73), channel_id=1, source_target_pairs={{1,0},{2,1},{3,2},{4,3},{5,4},{6,5},{7,6},{8,7},{9,8},{10,9},{11,1... | collective-permute-start | bytes 1179656 | tf_op jit(solution)/shard_map/ppermute | solution.py:85
  108.2 21.0 %collective-permute-start.26 = (bf16[2,4,3,2,32,256]{5,4,3,2,1,0:T(8,128)(2,1)S(1)}, bf16[2,4,3,2,32,256]{5,4,3,2,1,0:T(8,128)(2,1)S(1)}, u32[]{:S(2)}, u32[]{:S(2)}) collective-permute-start(bf16[2,4,3,2,32,256]{5,4,3,2,1,0:T(8,128)(2,1)S(1)} %get-tuple-element.67), channel_id=1, source_target_pairs={{0,1},{1,0},{2,3},{3,2},{16,19},{17,18},{18,17},{19,16},{4,5},{5,4... | collective-permute-start | bytes 2359304 | tf_op jit(solution)/shard_map/ppermute | solution.py:35
  112.1 18.7 %collective-permute-start.22 = (bf16[2,4,3,2,32,256]{5,4,3,2,1,0:T(8,128)(2,1)S(1)}, bf16[2,4,3,2,32,256]{5,4,3,2,1,0:T(8,128)(2,1)S(1)}, u32[]{:S(2)}, u32[]{:S(2)}) collective-permute-start(bf16[2,4,3,2,32,256]{5,4,3,2,1,0:T(8,128)(2,1)S(1)} %get-tuple-element.64), channel_id=1, source_target_pairs={{0,64},{64,0},{128,192},{192,128},{16,208},{80,144},{144,80},{208,... | collective-permute-start | bytes 2359304 | tf_op jit(solution)/shard_map/ppermute | solution.py:35
  129.6 6.7 %collective-permute-start.27 = (bf16[4,3,2,32,256]{4,3,2,1,0:T(8,128)(2,1)S(1)}, bf16[4,3,2,32,256]{4,3,2,1,0:T(8,128)(2,1)S(1)}, u32[]{:S(2)}, u32[]{:S(2)}) collective-permute-start(bf16[4,3,2,32,256]{4,3,2,1,0:T(8,128)(2,1)S(1)} %fusion.7), channel_id=1, source_target_pairs={{0,3},{1,2},{2,1},{3,0},{16,17},{17,16},{18,19},{19,18},{4,7},{5,6... | collective-permute-start | bytes 1179656 | tf_op jit(solution)/shard_map/ppermute | solution.py:35
  131.2 7.4 %collective-permute-start.23 = (bf16[4,3,2,32,256]{4,3,2,1,0:T(8,128)(2,1)S(1)}, bf16[4,3,2,32,256]{4,3,2,1,0:T(8,128)(2,1)S(1)}, u32[]{:S(2)}, u32[]{:S(2)}) collective-permute-start(bf16[4,3,2,32,256]{4,3,2,1,0:T(8,128)(2,1)S(1)} %fusion.6), channel_id=1, source_target_pairs={{0,192},{64,128},{128,64},{192,0},{16,80},{80,16},{144,208},{208,1... | collective-permute-start | bytes 1179656 | tf_op jit(solution)/shard_map/ppermute | solution.py:35
  136.6 8.9 %collective-permute-start.28 = (f32[2,3,2,32,256]{4,3,2,1,0:T(8,128)S(1)}, f32[2,3,2,32,256]{4,3,2,1,0:T(8,128)S(1)}, u32[]{:S(2)}, u32[]{:S(2)}) collective-permute-start(f32[2,3,2,32,256]{4,3,2,1,0:T(8,128)S(1)} %slice.150), channel_id=1, source_target_pairs={{0,64},{64,0},{128,192},{192,128},{16,208},{80,144},{144,80},{208,... | collective-permute-start | bytes 1179656 | tf_op jit(solution)/shard_map/ppermute | solution.py:35
  138.8 7.9 %collective-permute-start.24 = (f32[2,3,2,32,256]{4,3,2,1,0:T(8,128)S(1)}, f32[2,3,2,32,256]{4,3,2,1,0:T(8,128)S(1)}, u32[]{:S(2)}, u32[]{:S(2)}) collective-permute-start(f32[2,3,2,32,256]{4,3,2,1,0:T(8,128)S(1)} %slice.143), channel_id=1, source_target_pairs={{0,1},{1,0},{2,3},{3,2},{16,19},{17,18},{18,17},{19,16},{4,5},{5,4... | collective-permute-start | bytes 1179656 | tf_op jit(solution)/shard_map/ppermute | solution.py:35
  145.5 4.9 %collective-permute-start.29 = (f32[3,2,32,256]{3,2,1,0:T(8,128)S(1)}, f32[3,2,32,256]{3,2,1,0:T(8,128)S(1)}, u32[]{:S(2)}, u32[]{:S(2)}) collective-permute-start(f32[3,2,32,256]{3,2,1,0:T(8,128)S(1)} %fusion.8), channel_id=1, source_target_pairs={{0,192},{64,128},{128,64},{192,0},{16,80},{80,16},{144,208},{208,1... | collective-permute-start | bytes 589832 | tf_op jit(solution)/shard_map/ppermute | solution.py:35
  146.8 6.4 %collective-permute-start.25 = (f32[3,2,32,256]{3,2,1,0:T(8,128)S(1)}, f32[3,2,32,256]{3,2,1,0:T(8,128)S(1)}, u32[]{:S(2)}, u32[]{:S(2)}) collective-permute-start(f32[3,2,32,256]{3,2,1,0:T(8,128)S(1)} %fusion.11), channel_id=1, source_target_pairs={{0,3},{1,2},{2,1},{3,0},{16,17},{17,16},{18,19},{19,18},{4,7},{5,6... | collective-permute-start | bytes 589832 | tf_op jit(solution)/shard_map/ppermute | solution.py:35

commit v2 on v1

--- a/solution.py
+++ b/solution.py
@@ -350,19 +350,22 @@
     )
     start = (3 * lax.axis_index("x"), 0, lax.axis_index("core") * half)
     unit = lax.dynamic_slice(both, start, (3, both.shape[1], half))
-    return gathered(unit, "zh").transpose(1, 0, 2, 3)
+    p = lax.axis_index("zh")
+    slots = [unit]
+    for k in range(1, 4):
+        slots.append(lax.ppermute(unit, "zh", [(i, i ^ k) for i in range(4)]))
+    slots = [jnp.where(p & 1, slots[k ^ 1], slots[k]) for k in range(4)]
+    slots = [jnp.where(p & 2, slots[k ^ 2], slots[k]) for k in range(4)]
+    return jnp.stack(slots, axis=1)
 
 
 def kernel_parts(unit, waited):
     lower = jnp.concatenate(ring_gather(unit[:, :2], "y"))
     upper = jnp.concatenate(ring_gather(unit[:, 2:], "x"))
-    lower, lower_near = lower, exchange(lower, "x", 0)
-    upper, upper_near = upper, exchange(upper, "y", 0)
-    (lower_near, upper_near), waited = lax.optimization_barrier(((lower_near, upper_near), waited))
-    lower = jnp.stack([lower, lower_near])
-    upper = jnp.stack([upper, upper_near])
-    lower_rest, upper_rest = exchange(lower, "x", 1), exchange(upper, "y", 1)
-    mine = (lower, lower_rest, upper, upper_rest)
+    lower, lower_rest = ring_gather(lower, "x")
+    upper, upper_rest = ring_gather(upper, "y")
+    rest, waited = lax.optimization_barrier(((lower_rest, upper_rest), waited))
+    mine = (lower, rest[0], upper, rest[1])
     return mine, tuple(swap(part) for part in mine), waited
 
 
@@ -378,15 +381,14 @@
     ]
 
     unit = kernel_unit(spatial_kernel, temporal_kernel, half)
-    edges = (activations, cotangent)
-    edges, unit = lax.optimization_barrier((edges, unit))
-    x_wide = widened(edges[0], edges_of(edges[0], SPACE, 1), SPACE, 1)
-    cot_pad = widened(edges[1], edges_of(edges[1], TM, 0), TM, 0)
-    parts, parts_other, (x_wide, cot_pad) = kernel_parts(unit, (x_wide, cot_pad))
+    x_wide = widened(activations, edges_of(activations, SPACE, 1), SPACE, 1)
+    cot_pad = widened(cotangent, edges_of(cotangent, TM, 0), TM, 0)
     x_pair = swap(lax.dynamic_slice_in_dim(x_wide, (1 - core[0]) * half, half, axis=3))
     shifts = column_shifts(x_wide)
+    cot_turned = cot_pad.reshape((frames + 2) * rows * width, chans).T
+    waited = (shifts, cot_pad, cot_turned)
+    parts, parts_other, (shifts, cot_pad, cot_turned) = kernel_parts(unit, waited)
     shifts_pair = column_shifts(x_pair)
-    cot_turned = cot_pad.reshape((frames + 2) * rows * width, chans).T
     cot_turned_pair = swap(cot_turned)
     (shifts_pair, cot_turned_pair), parts_other = lax.optimization_barrier(
         ((shifts_pair, cot_turned_pair), parts_other)
@@ -409,10 +411,9 @@
     )
     info = jnp.concatenate([core, slots_of("x"), slots_of("y")])
     lower, sent_lower = weight_terms(0, own, info, *operands)
-    info, sent_lower, slope_edges = lax.optimization_barrier((info, sent_lower, slope_edges))
     upper, sent_upper = weight_terms(1, own, info, *operands)
+    slope_edges, _ = lax.optimization_barrier((slope_edges, (sent_lower, sent_upper)))
     slope_wide = widened(slope_maps, slope_edges, SPACE, 1)
-    slope_wide, sent_upper = lax.optimization_barrier((slope_wide, sent_upper))
     grad = input_gradient(core, column_shifts(slope_wide), cotangent, k_mine, k_other)
 
     lower = ring_scatter(lower, sent_lower, "x", grad)
@@ -423,8 +424,12 @@
     terms = terms.reshape(3, 4, 2, own // 2, half).transpose(1, 2, 0, 3, 4)
     terms = scattered(terms.reshape(8, 3, own // 2, half), ("zh", "zl"))
     pixels = count * lax.axis_size(TM) * lax.axis_size(SPACE)
-    terms = gathered(terms * (1.0 / math.sqrt(pixels)), TM)
-    terms = terms.reshape(4, 2, 2, 3, own // 2, half).transpose(0, 3, 1, 4, 2, 5)
+    terms = gathered(terms * (1.0 / math.sqrt(pixels)), ("x", "zl"))
+    came = swap(terms)
+    terms = jnp.concatenate(
+        [jnp.where(core[0] == 0, terms, came), jnp.where(core[0] == 0, came, terms)], axis=3
+    )
+    terms = terms.reshape(4, 2, 3, own // 2, chans).transpose(0, 2, 1, 3, 4)
     spatial = terms[:3].reshape(9, own, chans).transpose(1, 0, 2)
     temporal = terms[3].reshape(3, own, chans).transpose(1, 0, 2)
     return grad.reshape(frames, rows, width, chans), spatial, temporal

time: 198 us -> 185 us (0.934)
  blocking collectives: 41.5 us -> 25.3 us
  waiting for transfers between devices: 45.4 us -> 38.3 us
  other arithmetic: 7.67 us -> 14.2 us
  Pallas kernels: 27.5 us -> 30.1 us
  local copies, waits for them, and re-layouts: 10.6 us -> 12.9 us
    all_to_all x1, blocking collectives: 25.6 us -> 9.34 us  [gathered(): return lax.all_to_all(spread, axis, 0, 0, tiled=True)]
    ppermute x8 -> x9, starting transfers between devices: 9.38 us -> 21.8 us  [swap(): return lax.ppermute(block, 'core', PAIR)]
    ppermute x16, starting transfers between devices: 29.8 us -> 18.1 us  [exchange(): return lax.ppermute(block, names, pairs)]
    ppermute x16, waiting for transfers between devices: 25 us -> 36.2 us  [exchange(): return lax.ppermute(block, names, pairs)]
    ppermute x0 -> x3, starting transfers between devices: none -> 9.12 us  [kernel_unit(): slots.append(lax.ppermute(unit, 'zh', [(i, i ^ k) for i in range(4)]))]
    all_to_all x1 -> x0, starting transfers between devices: 9.01 us -> none  [gathered(): return lax.all_to_all(spread, axis, 0, 0, tiled=True)]
    all_to_all x1 -> x0, waiting for transfers between devices: 7.61 us -> none  [gathered(): return lax.all_to_all(spread, axis, 0, 0, tiled=True)]
    ppermute x3, waiting for transfers between devices: 7.27 us -> 0.66 us  [edges_of(): high = lax.ppermute(lax.slice_in_dim(block, 0, 1, axis=dim), axis, backward)]
  transfers between devices with their start and end apart: 31 -> 34, of which waited for: 12 -> 13; matrix products, arithmetic and copies ran while one was open for 5% -> 13% of each run, Pallas kernels for 8% -> 12%
where the time goes in v2:
time: 185 us
  starting transfers between devices  62.7 us (34%)
  waiting for transfers between devices  38.3 us (21%)
  Pallas kernels  30.1 us (16%)
  blocking collectives  25.3 us (14%)
  other arithmetic  14.2 us (8%)
  local copies, waits for them, and re-layouts  12.9 us (7%)
    ppermute x16, waiting for transfers between devices, exchange(): return lax.ppermute(block, names, pairs)  36.2 us
    ppermute x9, starting transfers between devices, swap(): return lax.ppermute(block, 'core', PAIR)  21.8 us
    ppermute x16, starting transfers between devices, exchange(): return lax.ppermute(block, names, pairs)  18.1 us
    all_to_all x1, blocking collectives, scattered(): lax.all_to_all(block, axis, 0, 0, tiled=True).astype(jnp.float32)  16 us
    ppermute x3, starting transfers between devices, edges_of(): high = lax.ppermute(lax.slice_in_dim(block, 0, 1, axis=dim), axis, backward)  11.8 us
    all_to_all x1, blocking collectives, gathered(): return lax.all_to_all(spread, axis, 0, 0, tiled=True)  9.34 us
    pallas_call x2, Pallas kernels, weight_terms(): pl.pallas_call(functools.partial(weight_kernel, upper), out_shape=(jax.Sh...  9.29 us
    ppermute x3, starting transfers between devices, kernel_unit(): slots.append(lax.ppermute(unit, 'zh', [(i, i ^ k) for i in range(4)]))  9.12 us
  transfers between devices with their start and end apart: 34, of which 13 were waited for; matrix products, arithmetic and copies ran while one was open for 13% of the time, Pallas kernels for 12%

profile of v2, /device:TPU:1, one launch (start us, length us, event | category | flops | bytes accessed | tf_op | source)
XLA Modules:
  0.0 184.8 jit_solution(8615151939662584204)
XLA Ops:
  0.6 0.8 fusion.14
  1.5 6.9 %collective-permute-start = (bf16[3,32,256]{2,1,0:T(8,128)(2,1)S(1)}, bf16[3,32,256]{2,1,0:T(8,128)(2,1)S(1)}, u32[]{:S(2)}, u32[]{:S(2)}) collective-permute-start(bf16[3,32,256]{2,1,0:T(8,128)(2,1)S(1)} %fusion.14), channel_id=1, source_target_pairs={{0,12},{4,8},{8,4},{12,0},{1,13},{5,9},{9,5},{13,1},{2,14},{6,10},... | collective-permute-start | bytes 147464 | tf_op jit(solution)/shard_map/ppermute | solution.py:356
  8.4 1.0 collective-permute-start.1
  9.4 1.2 collective-permute-start.2
  10.6 1.2 fusion.26
  11.8 6.0 %collective-permute-start.12 = (bf16[2,1,192,512]{3,2,1,0:T(8,128)(2,1)S(1)}, bf16[2,1,192,512]{3,2,1,0:T(8,128)(2,1)S(1)}, u32[]{:S(2)}, u32[]{:S(2)}) collective-permute-start(bf16[2,1,192,512]{3,2,1,0:T(8,128)(2,1)S(1)} %get-tuple-element.74), channel_id=1, source_target_pairs={{1,0},{2,1},{3,2},{4,3},{5,4},{6,5},{7,6},{8,7},{9,8},{10,9},{11,1... | collective-permute-start | bytes 1179656 | tf_op jit(solution)/shard_map/ppermute | solution.py:85
  17.9 2.6 %collective-permute-start.7 = (bf16[3,2,32,256]{3,2,1,0:T(8,128)(2,1)S(1)}, bf16[3,2,32,256]{3,2,1,0:T(8,128)(2,1)S(1)}, u32[]{:S(2)}, u32[]{:S(2)}) collective-permute-start(bf16[3,2,32,256]{3,2,1,0:T(8,128)(2,1)S(1)} %get-tuple-element.84), channel_id=1, source_target_pairs={{0,64},{64,0},{128,192},{192,128},{16,208},{80,144},{144,80},{208,... | collective-permute-start | bytes 294920 | tf_op jit(solution)/shard_map/ppermute | solution.py:35
  20.4 1.4 collective-permute-start.3
  21.8 0.8 collective-permute-done.7
  22.6 0.7 pad_maximum_fusion.13
  23.3 0.3 collective-permute-start.8
  23.6 6.6 %collective-permute-done.3 = bf16[3,2,32,256]{3,2,0,1:T(8,128)(2,1)S(1)} collective-permute-done((bf16[3,2,32,256]{3,2,0,1:T(8,128)(2,1)S(1)}, bf16[3,2,32,256]{3,2,0,1:T(8,128)(2,1)S(1)}, u32[]{:S(2)}, u32[]{:S(2)}) %collective-permute-start.3) | collective-permute-done | bytes 98336 | tf_op jit(solution)/shard_map/ppermute | solution.py:35
  30.2 0.7 pad_maximum_fusion.12
  31.1 1.8 collective-permute-start.13
  32.9 1.0 fusion.17
  33.9 2.2 %collective-permute-done.4 = bf16[2,3,2,32,256]{4,3,1,2,0:T(8,128)(2,1)} collective-permute-done((bf16[2,3,2,32,256]{4,3,1,2,0:T(8,128)(2,1)}, bf16[2,3,2,32,256]{4,3,1,2,0:T(8,128)(2,1)}, u32[]{:S(2)}, u32[]{:S(2)}) %collective-permute-start.4) | collective-permute-done | bytes 196640 | tf_op jit(solution)/shard_map/ppermute | solution.py:35
  36.0 1.0 fusion.18
  37.0 2.0 %collective-permute-start.5 = (bf16[4,3,2,32,256]{4,3,1,2,0:T(8,128)(2,1)S(1)}, bf16[4,3,2,32,256]{4,3,1,2,0:T(8,128)(2,1)S(1)}, u32[]{:S(2)}, u32[]{:S(2)}) collective-permute-start(bf16[4,3,2,32,256]{4,3,1,2,0:T(8,128)(2,1)S(1)} %get-tuple-element.78), channel_id=1, source_target_pairs={{0,64},{64,0},{128,192},{192,128},{16,208},{80,144},{144,80},{208,... | collective-permute-start | bytes 1179656 | tf_op jit(solution)/shard_map/ppermute | solution.py:35
  39.1 0.2 fusion.20
  39.4 0.5 fusion.22
  39.9 1.1 constant_dynamic-slice_fusion
  40.9 3.0 %collective-permute-start.15 = (bf16[2,4,192,256]{3,2,1,0:T(8,128)(2,1)}, bf16[2,4,192,256]{3,2,1,0:T(8,128)(2,1)}, u32[]{:S(2)}, u32[]{:S(2)}) collective-permute-start(bf16[2,4,192,256]{3,2,1,0:T(8,128)(2,1)} %constant_dynamic-slice_fusion), channel_id=1, source_target_pairs={{0,16},{16,0},{1,17},{17,1},{2,18},{18,2},{3,19},{19,3},{4,20},{20... | collective-permute-start | bytes 2359304 | tf_op jit(solution)/shard_map/ppermute | solution.py:22
  43.9 0.7 collective-permute-done.14
  44.6 1.0 broadcast_select_fusion
  45.8 1.4 collective-permute-done.5
  47.2 1.0 pad_maximum_fusion.6
  48.2 0.5 pad_bitcast_fusion.2
  48.8 2.5 %pad_maximum_fusion.x_ref = bf16[3,2,4,192,512]{4,3,2,1,0:T(8,128)(2,1)} fusion(bf16[1,2,4,192,512]{4,3,2,1,0:T(8,128)(2,1)S(1)} %get-tuple-element.87, bf16[1,2,4,192,512]{4,3,2,1,0:T(8,128)(2,1)S(1)} %get-tuple-element.63, bf16[1,2,4,192,512]{4,3,2,1,0:T(8,128)(2,1)S(1)} %get-tuple-element.88), kind=kLoop, calls=%fused_computation | loop fusion | flops 4718592 | bytes 9437184 | tf_op jit(solution)/shard_map/stack | solution.py:99
  51.3 1.3 pad_maximum_fusion.4.cot_ref
  52.6 1.7 copy.28
  54.3 2.7 %collective-permute-done.10.refs_3_ = bf16[2,4,3,2,32,256]{5,4,3,2,1,0:T(8,128)(2,1)} collective-permute-done((bf16[2,4,3,2,32,256]{5,4,3,2,1,0:T(8,128)(2,1)S(1)}, bf16[2,4,3,2,32,256]{5,4,3,2,1,0:T(8,128)(2,1)}, u32[]{:S(2)}, u32[]{:S(2)}) %collective-permute-start.10) | collective-permute-done | bytes 786464 | tf_op jit(solution)/shard_map/ppermute | solution.py:35
  57.0 2.6 %collective-permute-done.6 = bf16[2,4,3,2,32,256]{5,4,2,3,1,0:T(8,128)(2,1)} collective-permute-done((bf16[2,4,3,2,32,256]{5,4,2,3,1,0:T(8,128)(2,1)}, bf16[2,4,3,2,32,256]{5,4,2,3,1,0:T(8,128)(2,1)}, u32[]{:S(2)}, u32[]{:S(2)}) %collective-permute-start.6) | collective-permute-done | bytes 786464 | tf_op jit(solution)/shard_map/ppermute | solution.py:35
  59.6 4.9 %collective-permute-start.16 = (bf16[512,1536]{1,0:T(8,128)(2,1)S(1)}, bf16[512,1536]{1,0:T(8,128)(2,1)}, u32[]{:S(2)}, u32[]{:S(2)}) collective-permute-start(bf16[512,1536]{1,0:T(8,128)(2,1)S(1)} %bitcast.100), channel_id=1, source_target_pairs={{0,16},{16,0},{1,17},{17,1},{2,18},{18,2},{3,19},{19,3},{4,20},{20... | collective-permute-start | bytes 4718600 | tf_op jit(solution)/shard_map/ppermute | solution.py:22
  64.8 1.3 copy.29.refs_0_
  66.2 0.5 collective-permute-start.17
  66.8 0.4 collective-permute-start.20
  67.2 1.7 fusion.24
  69.2 1.4 pad_maximum_fusion.2.x_pair_ref
  70.6 1.3 copy.30.refs_1_
  71.9 0.3 copy-done.1
  72.2 6.4 %shard_map.67 = (f32[2,384,512]{2,1,0:T(8,128)S(1)}, f32[2,384,256]{2,1,0:T(8,128)S(1)}, bf16[4,3,4,4,32,256]{5,4,3,2,1,0:T(8,128)(2,1)S(1)}) custom-call(s32[9]{0:T(128)S(1)} %concatenate.65.info_ref, bf16[3,2,4,192,512]{4,3,2,1,0:T(8,128)(2,1)S(1)} %bitcast.99, bf16[4,2,192,512]{3,2,1,0:T(8,128)(2,1)S(1)} %copy-done.1, ...), custom_call_target="tpu_custom_call" | custom-call | flops 3200000000 | bytes 12000000 | tf_op jit(solution)/shard_map/pallas_call | solution.py:217
  78.8 7.6 %shard_map.68 = (bf16[2,384,256]{2,1,0:T(8,128)(2,1)S(1)}, bf16[2,384,256]{2,1,0:T(8,128)(2,1)S(1)}, bf16[2,384,512]{2,1,0:T(8,128)(2,1)S(1)}, bf16[512,768]{1,0...) custom-call(s32[9]{0:T(128)S(1)} %concatenate.55.info_ref, bf16[3,2,4,192,512]{4,3,2,1,0:T(8,128)(2,1)S(1)} %bitcast.99, ...), custom_call_target="tpu_custom_call" | custom-call | flops 3200000000 | bytes 15000000 | tf_op jit(solution)/shard_map/pallas_call | solution.py:226
  86.6 0.4 collective-permute-start.24
  87.2 5.7 %collective-permute-start.22 = (bf16[2,1,192,512]{3,2,1,0:T(8,128)(2,1)S(1)}, bf16[2,1,192,512]{3,2,1,0:T(8,128)(2,1)S(1)}, u32[]{:S(2)}, u32[]{:S(2)}) collective-permute-start(bf16[2,1,192,512]{3,2,1,0:T(8,128)(2,1)S(1)} %get-tuple-element.67), channel_id=1, source_target_pairs={{1,0},{2,1},{3,2},{4,3},{5,4},{6,5},{7,6},{8,7},{9,8},{10,9},{11,1... | collective-permute-start | bytes 1179656 | tf_op jit(solution)/shard_map/ppermute | solution.py:85
  92.9 4.6 %shard_map.69 = (f32[4,4,3,2,32,256]{5,4,3,2,1,0:T(8,128)S(1)}, bf16[2,4,3,2,32,256]{5,4,3,2,1,0:T(8,128)(2,1)S(1)}) custom-call(s32[9]{0:T(128)S(1)} %pad_add_fusion.info_ref, bf16[512,768]{1,0:T(8,128)(2,1)S(1)} %get-tuple-element.42.turned_ref, bf16[512,768]{1,0:T(8,128)(2,1)S(1)} %collective-permute-done.23.turned_pair_ref, ...), custom_call_target="tpu_custom_call" | custom-call | flops 2400000000 | bytes 16000000 | tf_op jit(solution)/shard_map/pallas_call | solution.py:301
  97.6 3.0 %collective-permute-start.25 = (bf16[2,4,3,2,32,256]{5,4,3,2,1,0:T(8,128)(2,1)S(1)}, bf16[2,4,3,2,32,256]{5,4,3,2,1,0:T(8,128)(2,1)S(1)}, u32[]{:S(2)}, u32[]{:S(2)}) collective-permute-start(bf16[2,4,3,2,32,256]{5,4,3,2,1,0:T(8,128)(2,1)S(1)} %get-tuple-element.47), channel_id=1, source_target_pairs={{0,64},{64,0},{128,192},{192,128},{16,208},{80,144},{144,80},{208,... | collective-permute-start | bytes 2359304 | tf_op jit(solution)/shard_map/ppermute | solution.py:35
  100.6 4.6 %shard_map.70 = (f32[4,4,3,2,32,256]{5,4,3,2,1,0:T(8,128)S(1)}, bf16[2,4,3,2,32,256]{5,4,3,2,1,0:T(8,128)(2,1)S(1)}) custom-call(s32[9]{0:T(128)S(1)} %pad_add_fusion.info_ref, bf16[512,768]{1,0:T(8,128)(2,1)S(1)} %get-tuple-element.42.turned_ref, bf16[512,768]{1,0:T(8,128)(2,1)S(1)} %collective-permute-done.23.turned_pair_ref, ...), custom_call_target="tpu_custom_call" | custom-call | flops 2400000000 | bytes 16000000 | tf_op jit(solution)/shard_map/pallas_call | solution.py:301
  105.7 0.4 fusion.21
  106.3 0.4 pad_bitcast_fusion.1
  106.7 0.6 pad_maximum_fusion.1.x_ref
  107.2 6.8 %shard_map.71 = f32[2,384,512]{2,1,0:T(8,128)} custom-call(s32[1]{0:T(128)} %bitcast.info_ref, bf16[3,2,4,192,512]{4,3,2,1,0:T(8,128)(2,1)S(1)} %pad_maximum_fusion.1.x_ref, bf16[2,384,512]{2,1,0:T(8,128)(2,1)S(1)} %bitcast.103, bf16[4,3,4,4,32,256]{5,4,3,2,1,0:T(8,128)(2,1)S(1)} %get-tuple-element.51.mine_ref, ...), custom_call_target="tpu_custom_call" | custom-call | flops 3600000000 | bytes 16000000 | tf_op jit(solution)/shard_map/pallas_call | solution.py:337
  114.4 5.7 %collective-permute-start.26 = (bf16[4,3,2,32,256]{4,3,2,1,0:T(8,128)(2,1)S(1)}, bf16[4,3,2,32,256]{4,3,2,1,0:T(8,128)(2,1)S(1)}, u32[]{:S(2)}, u32[]{:S(2)}) collective-permute-start(bf16[4,3,2,32,256]{4,3,2,1,0:T(8,128)(2,1)S(1)} %fusion.6), channel_id=1, source_target_pairs={{0,192},{64,128},{128,64},{192,0},{16,80},{80,16},{144,208},{208,1... | collective-permute-start | bytes 1179656 | tf_op jit(solution)/shard_map/ppermute | solution.py:35
  120.6 5.0 %collective-permute-done.26 = bf16[4,3,2,32,256]{4,3,2,1,0:T(8,128)(2,1)S(1)} collective-permute-done((bf16[4,3,2,32,256]{4,3,2,1,0:T(8,128)(2,1)S(1)}, bf16[4,3,2,32,256]{4,3,2,1,0:T(8,128)(2,1)S(1)}, u32[]{:S(2)}, u32[]{:S(2)}) %collective-permute-start.26) | collective-permute-done | bytes 393248 | tf_op jit(solution)/shard_map/ppermute | solution.py:35
  125.9 1.6 collective-permute-done.30
  127.7 2.6 %collective-permute-start.31 = (f32[2,3,2,32,256]{4,3,2,1,0:T(8,128)S(1)}, f32[2,3,2,32,256]{4,3,2,1,0:T(8,128)S(1)}, u32[]{:S(2)}, u32[]{:S(2)}) collective-permute-start(f32[2,3,2,32,256]{4,3,2,1,0:T(8,128)S(1)} %slice.150), channel_id=1, source_target_pairs={{0,64},{64,0},{128,192},{192,128},{16,208},{80,144},{144,80},{208,... | collective-permute-start | bytes 1179656 | tf_op jit(solution)/shard_map/ppermute | solution.py:35
  130.3 6.5 %collective-permute-done.27 = f32[2,3,2,32,256]{4,3,2,1,0:T(8,128)S(1)} collective-permute-done((f32[2,3,2,32,256]{4,3,2,1,0:T(8,128)S(1)}, f32[2,3,2,32,256]{4,3,2,1,0:T(8,128)S(1)}, u32[]{:S(2)}, u32[]{:S(2)}) %collective-permute-start.27) | collective-permute-done | bytes 393248 | tf_op jit(solution)/shard_map/ppermute | solution.py:35
  137.1 4.7 %collective-permute-done.28 = f32[3,2,32,256]{3,2,1,0:T(8,128)S(1)} collective-permute-done((f32[3,2,32,256]{3,2,1,0:T(8,128)S(1)}, f32[3,2,32,256]{3,2,1,0:T(8,128)S(1)}, u32[]{:S(2)}, u32[]{:S(2)}) %collective-permute-start.28) | collective-permute-done | bytes 196640 | tf_op jit(solution)/shard_map/ppermute | solution.py:35
  141.8 2.1 %collective-permute-done.32 = f32[3,2,32,256]{3,2,1,0:T(8,128)S(1)} collective-permute-done((f32[3,2,32,256]{3,2,1,0:T(8,128)S(1)}, f32[3,2,32,256]{3,2,1,0:T(8,128)S(1)}, u32[]{:S(2)}, u32[]{:S(2)}) %collective-permute-start.32) | collective-permute-done | bytes 196640 | tf_op jit(solution)/shard_map/ppermute | solution.py:35
  144.1 16.0 %all_to_all.10 = f32[8,3,16,256]{3,2,1,0:T(8,128)S(1)} all-to-all(f32[8,3,16,256]{3,2,1,0:T(8,128)S(1)} %bitcast.114), channel_id=1, replica_groups=mesh['x'=4,'zl'=2,'core'=2,'zh'=4,'y'=4] {'zh','zl'}, dimensions={0} | all-to-all | bytes 786432 | tf_op jit(solution)/shard_map/all_to_all | solution.py:76
  160.1 9.3 %all_to_all.11 = f32[8,3,16,256]{3,2,1,0:T(8,128)S(1)} all-to-all(f32[8,3,16,256]{3,2,1,0:T(8,128)S(1)} %broadcast_in_dim.30), channel_id=1, replica_groups=mesh['x'=4,'zl'=2,'core'=2,'zh'=4,'y'=4] {'x','zl'}, dimensions={0} | all-to-all | bytes 786432 | tf_op jit(solution)/shard_map/all_to_all | solution.py:72
  169.5 12.2 %collective-permute-start.33 = (f32[8,3,16,256]{3,2,1,0:T(8,128)S(1)}, f32[8,3,16,256]{3,2,1,0:T(8,128)S(1)}, u32[]{:S(2)}, u32[]{:S(2)}) collective-permute-start(f32[8,3,16,256]{3,2,1,0:T(8,128)S(1)} %all_to_all.11), channel_id=1, source_target_pairs={{0,16},{16,0},{1,17},{17,1},{2,18},{18,2},{3,19},{19,3},{4,20},{20... | collective-permute-start | bytes 1179656 | tf_op jit(solution)/shard_map/ppermute | solution.py:22
  181.6 1.3 collective-permute-done.33
  183.2 0.9 copy.34
  184.1 0.7 copy.35
  (88 shorter events, 4.1 us)
Async XLA Ops:
  1.5 29.4 %copy-start = (bf16[2,2,192,512]{3,2,1,0:T(8,128)(2,1)S(1)}, bf16[2,2,192,512]{3,2,1,0:T(8,128)(2,1)}, u32[]{:S(2)}) copy-start(bf16[2,2,192,512]{3,2,1,0:T(8,128)(2,1)} %param.5) | copy-start | bytes 2359300
  1.5 16.3 %collective-permute-start = (bf16[3,32,256]{2,1,0:T(8,128)(2,1)S(1)}, bf16[3,32,256]{2,1,0:T(8,128)(2,1)S(1)}, u32[]{:S(2)}, u32[]{:S(2)}) collective-permute-start(bf16[3,32,256]{2,1,0:T(8,128)(2,1)S(1)} %fusion.14), channel_id=1, source_target_pairs={{0,12},{4,8},{8,4},{12,0},{1,13},{5,9},{9,5},{13,1},{2,14},{6,10},... | collective-permute-start | bytes 147464 | tf_op jit(solution)/shard_map/ppermute | solution.py:356
  8.4 9.4 %collective-permute-start.1 = (bf16[3,32,256]{2,1,0:T(8,128)(2,1)S(1)}, bf16[3,32,256]{2,1,0:T(8,128)(2,1)S(1)}, u32[]{:S(2)}, u32[]{:S(2)}) collective-permute-start(bf16[3,32,256]{2,1,0:T(8,128)(2,1)S(1)} %fusion.14), channel_id=1, source_target_pairs={{0,8},{4,12},{8,0},{12,4},{1,9},{5,13},{9,1},{13,5},{2,10},{6,14},... | collective-permute-start | bytes 147464 | tf_op jit(solution)/shard_map/ppermute | solution.py:356
  9.4 8.4 %collective-permute-start.2 = (bf16[3,32,256]{2,1,0:T(8,128)(2,1)S(1)}, bf16[3,32,256]{2,1,0:T(8,128)(2,1)S(1)}, u32[]{:S(2)}, u32[]{:S(2)}) collective-permute-start(bf16[3,32,256]{2,1,0:T(8,128)(2,1)S(1)} %fusion.14), channel_id=1, source_target_pairs={{0,4},{4,0},{8,12},{12,8},{1,5},{5,1},{9,13},{13,9},{2,6},{6,2},{1... | collective-permute-start | bytes 147464 | tf_op jit(solution)/shard_map/ppermute | solution.py:356
  11.8 25.3 %collective-permute-start.12 = (bf16[2,1,192,512]{3,2,1,0:T(8,128)(2,1)S(1)}, bf16[2,1,192,512]{3,2,1,0:T(8,128)(2,1)S(1)}, u32[]{:S(2)}, u32[]{:S(2)}) collective-permute-start(bf16[2,1,192,512]{3,2,1,0:T(8,128)(2,1)S(1)} %get-tuple-element.74), channel_id=1, source_target_pairs={{1,0},{2,1},{3,2},{4,3},{5,4},{6,5},{7,6},{8,7},{9,8},{10,9},{11,1... | collective-permute-start | bytes 1179656 | tf_op jit(solution)/shard_map/ppermute | solution.py:85
  17.8 21.3 %collective-permute-start.11 = (bf16[2,1,192,512]{3,2,1,0:T(8,128)(2,1)S(1)}, bf16[2,1,192,512]{3,2,1,0:T(8,128)(2,1)S(1)}, u32[]{:S(2)}, u32[]{:S(2)}) collective-permute-start(bf16[2,1,192,512]{3,2,1,0:T(8,128)(2,1)S(1)} %get-tuple-element.73), channel_id=1, source_target_pairs={{0,1},{1,2},{2,3},{3,4},{4,5},{5,6},{6,7},{7,8},{8,9},{9,10},{10,1... | collective-permute-start | bytes 1179656 | tf_op jit(solution)/shard_map/ppermute | solution.py:84
  17.9 4.8 %collective-permute-start.7 = (bf16[3,2,32,256]{3,2,1,0:T(8,128)(2,1)S(1)}, bf16[3,2,32,256]{3,2,1,0:T(8,128)(2,1)S(1)}, u32[]{:S(2)}, u32[]{:S(2)}) collective-permute-start(bf16[3,2,32,256]{3,2,1,0:T(8,128)(2,1)S(1)} %get-tuple-element.84), channel_id=1, source_target_pairs={{0,64},{64,0},{128,192},{192,128},{16,208},{80,144},{144,80},{208,... | collective-permute-start | bytes 294920 | tf_op jit(solution)/shard_map/ppermute | solution.py:35
  20.4 9.8 %collective-permute-start.3 = (bf16[3,2,32,256]{3,2,0,1:T(8,128)(2,1)S(1)}, bf16[3,2,32,256]{3,2,0,1:T(8,128)(2,1)S(1)}, u32[]{:S(2)}, u32[]{:S(2)}) collective-permute-start(bf16[3,2,32,256]{3,2,0,1:T(8,128)(2,1)S(1)} %get-tuple-element.86), channel_id=1, source_target_pairs={{0,1},{1,0},{2,3},{3,2},{16,19},{17,18},{18,17},{19,16},{4,5},{5,4... | collective-permute-start | bytes 294920 | tf_op jit(solution)/shard_map/ppermute | solution.py:35
  23.3 7.8 %collective-permute-start.8 = (bf16[2,3,2,32,256]{4,3,2,1,0:T(8,128)(2,1)}, bf16[2,3,2,32,256]{4,3,2,1,0:T(8,128)(2,1)}, u32[]{:S(2)}, u32[]{:S(2)}) collective-permute-start(bf16[2,3,2,32,256]{4,3,2,1,0:T(8,128)(2,1)} %pad_maximum_fusion.13), channel_id=1, source_target_pairs={{0,192},{64,128},{128,64},{192,0},{16,80},{80,16},{144,208},{208,1... | collective-permute-start | bytes 589832 | tf_op jit(solution)/shard_map/ppermute | solution.py:35
  30.9 5.1 %collective-permute-start.4 = (bf16[2,3,2,32,256]{4,3,1,2,0:T(8,128)(2,1)}, bf16[2,3,2,32,256]{4,3,1,2,0:T(8,128)(2,1)}, u32[]{:S(2)}, u32[]{:S(2)}) collective-permute-start(bf16[2,3,2,32,256]{4,3,1,2,0:T(8,128)(2,1)} %pad_maximum_fusion.12), channel_id=1, source_target_pairs={{0,3},{1,2},{2,1},{3,0},{16,17},{17,16},{18,19},{19,18},{4,7},{5,6... | collective-permute-start | bytes 589832 | tf_op jit(solution)/shard_map/ppermute | solution.py:35
  31.0 13.6 %collective-permute-start.14 = (bf16[1,2,192,512]{3,2,1,0:T(8,128)(2,1)S(1)}, bf16[1,2,192,512]{3,2,1,0:T(8,128)(2,1)}, u32[]{:S(2)}, u32[]{:S(2)}) collective-permute-start(bf16[1,2,192,512]{3,2,1,0:T(8,128)(2,1)S(1)} %get-tuple-element.72), channel_id=1, source_target_pairs={{16,0},{32,16},{48,32},{64,48},{80,64},{96,80},{112,96},{128,112},... | collective-permute-start | bytes 1179656 | tf_op jit(solution)/shard_map/ppermute | solution.py:85
  31.1 17.6 %collective-permute-start.13 = (bf16[1,2,192,512]{3,2,1,0:T(8,128)(2,1)S(1)}, bf16[1,2,192,512]{3,2,1,0:T(8,128)(2,1)S(1)}, u32[]{:S(2)}, u32[]{:S(2)}) collective-permute-start(bf16[1,2,192,512]{3,2,1,0:T(8,128)(2,1)S(1)} %get-tuple-element.71), channel_id=1, source_target_pairs={{0,16},{16,32},{32,48},{48,64},{64,80},{80,96},{96,112},{112,128},... | collective-permute-start | bytes 1179656 | tf_op jit(solution)/shard_map/ppermute | solution.py:84
  33.9 5.3 %copy-start.2 = (bf16[2,2,192,512]{3,2,1,0:T(8,128)(2,1)S(1)}, bf16[2,2,192,512]{3,2,1,0:T(8,128)(2,1)}, u32[]{:S(2)}) copy-start(bf16[2,2,192,512]{3,2,1,0:T(8,128)(2,1)} %param.4) | copy-start | bytes 2359300
  36.0 9.5 %collective-permute-start.9 = (bf16[4,3,2,32,256]{4,3,2,1,0:T(8,128)(2,1)S(1)}, bf16[4,3,2,32,256]{4,3,2,1,0:T(8,128)(2,1)S(1)}, u32[]{:S(2)}, u32[]{:S(2)}) collective-permute-start(bf16[4,3,2,32,256]{4,3,2,1,0:T(8,128)(2,1)S(1)} %get-tuple-element.76), channel_id=1, source_target_pairs={{0,1},{1,0},{2,3},{3,2},{16,19},{17,18},{18,17},{19,16},{4,5},{5,4... | collective-permute-start | bytes 1179656 | tf_op jit(solution)/shard_map/ppermute | solution.py:35
  37.0 10.2 %collective-permute-start.5 = (bf16[4,3,2,32,256]{4,3,1,2,0:T(8,128)(2,1)S(1)}, bf16[4,3,2,32,256]{4,3,1,2,0:T(8,128)(2,1)S(1)}, u32[]{:S(2)}, u32[]{:S(2)}) collective-permute-start(bf16[4,3,2,32,256]{4,3,1,2,0:T(8,128)(2,1)S(1)} %get-tuple-element.78), channel_id=1, source_target_pairs={{0,64},{64,0},{128,192},{192,128},{16,208},{80,144},{144,80},{208,... | collective-permute-start | bytes 1179656 | tf_op jit(solution)/shard_map/ppermute | solution.py:35
  40.9 25.9 %collective-permute-start.15 = (bf16[2,4,192,256]{3,2,1,0:T(8,128)(2,1)}, bf16[2,4,192,256]{3,2,1,0:T(8,128)(2,1)}, u32[]{:S(2)}, u32[]{:S(2)}) collective-permute-start(bf16[2,4,192,256]{3,2,1,0:T(8,128)(2,1)} %constant_dynamic-slice_fusion), channel_id=1, source_target_pairs={{0,16},{16,0},{1,17},{17,1},{2,18},{18,2},{3,19},{19,3},{4,20},{20... | collective-permute-start | bytes 2359304 | tf_op jit(solution)/shard_map/ppermute | solution.py:22
  45.7 11.3 %collective-permute-start.10 = (bf16[2,4,3,2,32,256]{5,4,3,2,1,0:T(8,128)(2,1)S(1)}, bf16[2,4,3,2,32,256]{5,4,3,2,1,0:T(8,128)(2,1)}, u32[]{:S(2)}, u32[]{:S(2)}) collective-permute-start(bf16[2,4,3,2,32,256]{5,4,3,2,1,0:T(8,128)(2,1)S(1)} %pad_maximum_fusion.7.refs_2_), channel_id=1, source_target_pairs={{0,3},{1,2},{2,1},{3,0},{16,17},{17,16},{18,19},{19,18},{4,7},{5,6... | collective-permute-start | bytes 2359304 | tf_op jit(solution)/shard_map/ppermute | solution.py:35
  48.2 11.5 %collective-permute-start.6 = (bf16[2,4,3,2,32,256]{5,4,2,3,1,0:T(8,128)(2,1)}, bf16[2,4,3,2,32,256]{5,4,2,3,1,0:T(8,128)(2,1)}, u32[]{:S(2)}, u32[]{:S(2)}) collective-permute-start(bf16[2,4,3,2,32,256]{5,4,2,3,1,0:T(8,128)(2,1)} %pad_maximum_fusion.6), channel_id=1, source_target_pairs={{0,192},{64,128},{128,64},{192,0},{16,80},{80,16},{144,208},{208,1... | collective-permute-start | bytes 2359304 | tf_op jit(solution)/shard_map/ppermute | solution.py:35
  59.6 19.0 %collective-permute-start.16 = (bf16[512,1536]{1,0:T(8,128)(2,1)S(1)}, bf16[512,1536]{1,0:T(8,128)(2,1)}, u32[]{:S(2)}, u32[]{:S(2)}) collective-permute-start(bf16[512,1536]{1,0:T(8,128)(2,1)S(1)} %bitcast.100), channel_id=1, source_target_pairs={{0,16},{16,0},{1,17},{17,1},{2,18},{18,2},{3,19},{19,3},{4,20},{20... | collective-permute-start | bytes 4718600 | tf_op jit(solution)/shard_map/ppermute | solution.py:22
  64.8 7.1 %slice-start = ((s8[4718592]{0:T(1024)(128)(4,1)}), s8[4194304]{0:T(1024)(128)(4,1)S(1)}, s32[]{:S(2)}) async-start(s8[4718592]{0:T(1024)(128)(4,1)} %bitcast.98), calls=%async_computation.2 | async-start | bytes 8388608
  66.1 12.5 %collective-permute-start.19 = (bf16[2,4,3,2,32,256]{5,4,3,2,1,0:T(8,128)(2,1)S(1)}, bf16[2,4,3,2,32,256]{5,4,3,2,1,0:T(8,128)(2,1)S(1)}, u32[]{:S(2)}, u32[]{:S(2)}) collective-permute-start(bf16[2,4,3,2,32,256]{5,4,3,2,1,0:T(8,128)(2,1)S(1)} %pad_maximum_fusion.7.refs_2_), channel_id=1, source_target_pairs={{0,16},{16,0},{1,17},{17,1},{2,18},{18,2},{3,19},{19,3},{4,20},{20... | collective-permute-start | bytes 2359304 | tf_op jit(solution)/shard_map/ppermute | solution.py:22
  66.2 12.4 %collective-permute-start.17 = (bf16[2,4,3,2,32,256]{5,4,2,3,1,0:T(8,128)(2,1)}, bf16[2,4,3,2,32,256]{5,4,2,3,1,0:T(8,128)(2,1)S(1)}, u32[]{:S(2)}, u32[]{:S(2)}) collective-permute-start(bf16[2,4,3,2,32,256]{5,4,2,3,1,0:T(8,128)(2,1)} %pad_maximum_fusion.6), channel_id=1, source_target_pairs={{0,16},{16,0},{1,17},{17,1},{2,18},{18,2},{3,19},{19,3},{4,20},{20... | collective-permute-start | bytes 2359304 | tf_op jit(solution)/shard_map/ppermute | solution.py:22
  66.7 12.0 %collective-permute-start.18 = (bf16[2,4,3,2,32,256]{5,4,2,3,1,0:T(8,128)(2,1)}, bf16[2,4,3,2,32,256]{5,4,2,3,1,0:T(8,128)(2,1)S(1)}, u32[]{:S(2)}, u32[]{:S(2)}) collective-permute-start(bf16[2,4,3,2,32,256]{5,4,2,3,1,0:T(8,128)(2,1)} %collective-permute-done.6), channel_id=1, source_target_pairs={{0,16},{16,0},{1,17},{17,1},{2,18},{18,2},{3,19},{19,3},{4,20},{20... | collective-permute-start | bytes 2359304 | tf_op jit(solution)/shard_map/ppermute | solution.py:22
  66.8 11.9 %collective-permute-start.20 = (bf16[2,4,3,2,32,256]{5,4,3,2,1,0:T(8,128)(2,1)}, bf16[2,4,3,2,32,256]{5,4,3,2,1,0:T(8,128)(2,1)S(1)}, u32[]{:S(2)}, u32[]{:S(2)}) collective-permute-start(bf16[2,4,3,2,32,256]{5,4,3,2,1,0:T(8,128)(2,1)} %collective-permute-done.10.refs_3_), channel_id=1, source_target_pairs={{0,16},{16,0},{1,17},{17,1},{2,18},{18,2},{3,19},{19,3},{4,20},{20... | collective-permute-start | bytes 2359304 | tf_op jit(solution)/shard_map/ppermute | solution.py:22
  68.9 3.0 %slice-start.1 = ((s8[4718592]{0:T(1024)(128)(4,1)}), s8[524288]{0:T(1024)(128)(4,1)S(1)}, s32[]{:S(2)}) async-start(s8[4718592]{0:T(1024)(128)(4,1)} %bitcast.98), calls=%async_computation.3 | async-start | bytes 1048576
  70.5 1.6 copy-start.1
  86.4 6.5 %collective-permute-start.23 = (bf16[512,768]{1,0:T(8,128)(2,1)S(1)}, bf16[512,768]{1,0:T(8,128)(2,1)S(1)}, u32[]{:S(2)}, u32[]{:S(2)}) collective-permute-start(bf16[512,768]{1,0:T(8,128)(2,1)S(1)} %get-tuple-element.42.turned_ref), channel_id=1, source_target_pairs={{0,16},{16,0},{1,17},{17,1},{2,18},{18,2},{3,19},{19,3},{4,20},{20... | collective-permute-start | bytes 2359304 | tf_op jit(solution)/shard_map/ppermute | solution.py:22
  86.6 6.3 %collective-permute-start.24 = (bf16[2,384,256]{2,1,0:T(8,128)(2,1)S(1)}, bf16[2,384,256]{2,1,0:T(8,128)(2,1)S(1)}, u32[]{:S(2)}, u32[]{:S(2)}) collective-permute-start(bf16[2,384,256]{2,1,0:T(8,128)(2,1)S(1)} %get-tuple-element.46), channel_id=1, source_target_pairs={{0,16},{16,0},{1,17},{17,1},{2,18},{18,2},{3,19},{19,3},{4,20},{20... | collective-permute-start | bytes 1179656 | tf_op jit(solution)/shard_map/ppermute | solution.py:22
  87.1 18.2 %collective-permute-start.21 = (bf16[2,1,192,512]{3,2,1,0:T(8,128)(2,1)S(1)}, bf16[2,1,192,512]{3,2,1,0:T(8,128)(2,1)S(1)}, u32[]{:S(2)}, u32[]{:S(2)}) collective-permute-start(bf16[2,1,192,512]{3,2,1,0:T(8,128)(2,1)S(1)} %get-tuple-element.68), channel_id=1, source_target_pairs={{0,1},{1,2},{2,3},{3,4},{4,5},{5,6},{6,7},{7,8},{8,9},{9,10},{10,1... | collective-permute-start | bytes 1179656 | tf_op jit(solution)/shard_map/ppermute | solution.py:84
  87.2 18.2 %collective-permute-start.22 = (bf16[2,1,192,512]{3,2,1,0:T(8,128)(2,1)S(1)}, bf16[2,1,192,512]{3,2,1,0:T(8,128)(2,1)S(1)}, u32[]{:S(2)}, u32[]{:S(2)}) collective-permute-start(bf16[2,1,192,512]{3,2,1,0:T(8,128)(2,1)S(1)} %get-tuple-element.67), channel_id=1, source_target_pairs={{1,0},{2,1},{3,2},{4,3},{5,4},{6,5},{7,6},{8,7},{9,8},{10,9},{11,1... | collective-permute-start | bytes 1179656 | tf_op jit(solution)/shard_map/ppermute | solution.py:85
  97.6 16.5 %collective-permute-start.25 = (bf16[2,4,3,2,32,256]{5,4,3,2,1,0:T(8,128)(2,1)S(1)}, bf16[2,4,3,2,32,256]{5,4,3,2,1,0:T(8,128)(2,1)S(1)}, u32[]{:S(2)}, u32[]{:S(2)}) collective-permute-start(bf16[2,4,3,2,32,256]{5,4,3,2,1,0:T(8,128)(2,1)S(1)} %get-tuple-element.47), channel_id=1, source_target_pairs={{0,64},{64,0},{128,192},{192,128},{16,208},{80,144},{144,80},{208,... | collective-permute-start | bytes 2359304 | tf_op jit(solution)/shard_map/ppermute | solution.py:35
  105.3 14.8 %collective-permute-start.29 = (bf16[2,4,3,2,32,256]{5,4,3,2,1,0:T(8,128)(2,1)S(1)}, bf16[2,4,3,2,32,256]{5,4,3,2,1,0:T(8,128)(2,1)S(1)}, u32[]{:S(2)}, u32[]{:S(2)}) collective-permute-start(bf16[2,4,3,2,32,256]{5,4,3,2,1,0:T(8,128)(2,1)S(1)} %get-tuple-element.48), channel_id=1, source_target_pairs={{0,1},{1,0},{2,3},{3,2},{16,19},{17,18},{18,17},{19,16},{4,5},{5,4... | collective-permute-start | bytes 2359304 | tf_op jit(solution)/shard_map/ppermute | solution.py:35
  114.4 11.2 %collective-permute-start.26 = (bf16[4,3,2,32,256]{4,3,2,1,0:T(8,128)(2,1)S(1)}, bf16[4,3,2,32,256]{4,3,2,1,0:T(8,128)(2,1)S(1)}, u32[]{:S(2)}, u32[]{:S(2)}) collective-permute-start(bf16[4,3,2,32,256]{4,3,2,1,0:T(8,128)(2,1)S(1)} %fusion.6), channel_id=1, source_target_pairs={{0,192},{64,128},{128,64},{192,0},{16,80},{80,16},{144,208},{208,1... | collective-permute-start | bytes 1179656 | tf_op jit(solution)/shard_map/ppermute | solution.py:35
  120.5 7.0 %collective-permute-start.30 = (bf16[4,3,2,32,256]{4,3,2,1,0:T(8,128)(2,1)S(1)}, bf16[4,3,2,32,256]{4,3,2,1,0:T(8,128)(2,1)S(1)}, u32[]{:S(2)}, u32[]{:S(2)}) collective-permute-start(bf16[4,3,2,32,256]{4,3,2,1,0:T(8,128)(2,1)S(1)} %fusion.7), channel_id=1, source_target_pairs={{0,3},{1,2},{2,1},{3,0},{16,17},{17,16},{18,19},{19,18},{4,7},{5,6... | collective-permute-start | bytes 1179656 | tf_op jit(solution)/shard_map/ppermute | solution.py:35
  125.8 11.1 %collective-permute-start.27 = (f32[2,3,2,32,256]{4,3,2,1,0:T(8,128)S(1)}, f32[2,3,2,32,256]{4,3,2,1,0:T(8,128)S(1)}, u32[]{:S(2)}, u32[]{:S(2)}) collective-permute-start(f32[2,3,2,32,256]{4,3,2,1,0:T(8,128)S(1)} %slice.143), channel_id=1, source_target_pairs={{0,1},{1,0},{2,3},{3,2},{16,19},{17,18},{18,17},{19,16},{4,5},{5,4... | collective-permute-start | bytes 1179656 | tf_op jit(solution)/shard_map/ppermute | solution.py:35
  127.7 9.3 %collective-permute-start.31 = (f32[2,3,2,32,256]{4,3,2,1,0:T(8,128)S(1)}, f32[2,3,2,32,256]{4,3,2,1,0:T(8,128)S(1)}, u32[]{:S(2)}, u32[]{:S(2)}) collective-permute-start(f32[2,3,2,32,256]{4,3,2,1,0:T(8,128)S(1)} %slice.150), channel_id=1, source_target_pairs={{0,64},{64,0},{128,192},{192,128},{16,208},{80,144},{144,80},{208,... | collective-permute-start | bytes 1179656 | tf_op jit(solution)/shard_map/ppermute | solution.py:35
  136.9 4.9 %collective-permute-start.28 = (f32[3,2,32,256]{3,2,1,0:T(8,128)S(1)}, f32[3,2,32,256]{3,2,1,0:T(8,128)S(1)}, u32[]{:S(2)}, u32[]{:S(2)}) collective-permute-start(f32[3,2,32,256]{3,2,1,0:T(8,128)S(1)} %fusion.11), channel_id=1, source_target_pairs={{0,3},{1,2},{2,1},{3,0},{16,17},{17,16},{18,19},{19,18},{4,7},{5,6... | collective-permute-start | bytes 589832 | tf_op jit(solution)/shard_map/ppermute | solution.py:35
  137.0 6.9 %collective-permute-start.32 = (f32[3,2,32,256]{3,2,1,0:T(8,128)S(1)}, f32[3,2,32,256]{3,2,1,0:T(8,128)S(1)}, u32[]{:S(2)}, u32[]{:S(2)}) collective-permute-start(f32[3,2,32,256]{3,2,1,0:T(8,128)S(1)} %fusion.8), channel_id=1, source_target_pairs={{0,192},{64,128},{128,64},{192,0},{16,80},{80,16},{144,208},{208,1... | collective-permute-start | bytes 589832 | tf_op jit(solution)/shard_map/ppermute | solution.py:35
  169.5 13.5 %collective-permute-start.33 = (f32[8,3,16,256]{3,2,1,0:T(8,128)S(1)}, f32[8,3,16,256]{3,2,1,0:T(8,128)S(1)}, u32[]{:S(2)}, u32[]{:S(2)}) collective-permute-start(f32[8,3,16,256]{3,2,1,0:T(8,128)S(1)} %all_to_all.11), channel_id=1, source_target_pairs={{0,16},{16,0},{1,17},{17,1},{2,18},{18,2},{3,19},{19,3},{4,20},{20... | collective-permute-start | bytes 1179656 | tf_op jit(solution)/shard_map/ppermute | solution.py:22

commit v3 on v2

--- a/solution.py
+++ b/solution.py
@@ -53,10 +53,9 @@
     return jnp.stack([p, p ^ (1 + 2 * core), p ^ (3 - 2 * core), p ^ 2]).astype(jnp.int32)
 
 
-def ring_scatter(terms, sent, axis, waited=None):
+def ring_scatter(terms, sent, axis, waited):
     came = exchange(sent, axis, 0)
-    if waited is not None:
-        came, waited = lax.optimization_barrier((came, waited))
+    came, _ = lax.optimization_barrier((came, waited))
     came = came.astype(jnp.float32)
     passed = (terms[1] + came[1]).astype(sent.dtype)
     return terms[0] + came[0] + exchange(passed, axis, 1).astype(jnp.float32)
@@ -65,6 +64,23 @@
 def ring_gather(block, axis):
     pair = jnp.stack([block, exchange(block, axis, 0)])
     return pair, exchange(pair, axis, 1)
+
+
+def turned_by(axis):
+    return (lax.axis_index(axis) ^ jnp.arange(4)).astype(jnp.int32)
+
+
+def direct(blocks, axis):
+    came = {
+        k: lax.ppermute(blocks[k], axis, [(i, i ^ k) for i in range(4)]) for k in (2, 1, 3)
+    }
+    return [blocks[0], came[1], came[2], came[3]]
+
+
+def direct_scatter(terms, axis):
+    blocks = [terms[0]] + [terms[k].astype(jnp.bfloat16) for k in range(1, 4)]
+    first, *others = direct(blocks, axis)
+    return first + sum(block.astype(jnp.float32) for block in others)
 
 
 def gathered(block, axis):
@@ -115,11 +131,11 @@
         for j in range(2):
             slot = 2 * pair + j
             for t in range(4):
-                x, y = info_ref[1 + slot], info_ref[5 + t]
-                target = kernel_ref.at[x, :, pl.ds(0, 2), y]
+                x, y = info_ref[1 + slot], info_ref[13 + t]
+                target = kernel_ref.at[x, pl.ds(0, 2), :, y]
                 copies.append((parts[pair].at[j, t], target))
-                x, y = info_ref[1 + t], info_ref[5 + slot]
-                target = kernel_ref.at[x, :, pl.ds(2, 2), y]
+                x, y = info_ref[9 + t], info_ref[5 + slot]
+                target = kernel_ref.at[x, pl.ds(2, 2), :, y]
                 copies.append((parts[2 + pair].at[j, t], target))
     copies = [
         pltpu.make_async_copy(source, target, sems.at[i])
@@ -142,24 +158,27 @@
             total = start_ref[f]
         else:
             total = jnp.zeros((block, chans), jnp.float32)
-        for b in range(3):
-            piece = x_ref[b, f, a : a + 2, :, lanes(index, half)].reshape(block, half)
-            total += lax.dot_general(
-                piece,
-                kernel_ref[a, b].reshape(chans, half),
-                (((1,), (1,)), ((), ())),
-                preferred_element_type=jnp.float32,
-            )
+        pieces = [
+            x_ref[b, f, a : a + 2, :, lanes(index, half)].reshape(block, half) for b in range(3)
+        ]
+        kernels = [kernel_ref[a, :, b].reshape(chans, half) for b in range(3)]
+        total += lax.dot_general(
+            jnp.concatenate(pieces, axis=1),
+            jnp.concatenate(kernels, axis=1),
+            (((1,), (1,)), ((), ())),
+            preferred_element_type=jnp.float32,
+        )
         pre_ref[f] = total
         return 0
 
     def blend(f, _):
-        total = jnp.zeros((block, half), jnp.float32)
-        for k in range(3):
-            piece = cot_ref[2 - k + f].reshape(block, chans)
-            kernel = kernel_ref[3, k].reshape(chans, half)
-            total += jnp.dot(piece, kernel, preferred_element_type=jnp.float32)
-        slope_ref[f] = total
+        pieces = [cot_ref[2 - k + f].reshape(block, chans) for k in range(3)]
+        kernels = [kernel_ref[3, :, k].reshape(chans, half) for k in range(3)]
+        slope_ref[f] = jnp.dot(
+            jnp.concatenate(pieces, axis=1),
+            jnp.concatenate(kernels, axis=0),
+            preferred_element_type=jnp.float32,
+        )
         return 0
 
     for a in range(3):
@@ -212,7 +231,7 @@
     full = jax.ShapeDtypeStruct((frames, block, chans), jnp.float32)
     part = jax.ShapeDtypeStruct((frames, block, half), jnp.float32)
     hid = jax.ShapeDtypeStruct((frames, block, half), jnp.bfloat16)
-    kernel = jax.ShapeDtypeStruct((4, 3, 4, 4) + parts[0].shape[-2:], parts[0].dtype)
+    kernel = jax.ShapeDtypeStruct((4, 4, 3, 4) + parts[0].shape[-2:], parts[0].dtype)
     sems = pltpu.SemaphoreType.DMA((32,))
     pre, mine, k_mine = pl.pallas_call(
         first_kernel,
@@ -270,25 +289,32 @@
         for zh in range(2):
             for y in range(4):
                 row = (4 * zh + y) * own
-                slots = info_ref[1 + group], info_ref[5 + y]
-                slots = slots[::-1] if upper else slots
+                if upper:
+                    slots = info_ref[5 + y], info_ref[9 + group]
+                else:
+                    slots = info_ref[1 + group], info_ref[13 + y]
                 terms_ref[slots[0], slots[1], b, zh] = total[row : row + own]
 
     def spatial(a, _):
         for b in range(3):
-            piece = x_ref[b, :, pl.ds(a, 2), :, lanes(info_ref[0], half)].reshape(count, half)
-            total = jnp.dot(turned_ref[outs], piece, preferred_element_type=jnp.float32)
-            piece = x_pair_ref[b, :, pl.ds(a, 2)].reshape(count, half)
-            total += jnp.dot(turned_pair_ref[outs], piece, preferred_element_type=jnp.float32)
+            mine = x_ref[b, :, pl.ds(a, 2), :, lanes(info_ref[0], half)].reshape(count, half)
+            other = x_pair_ref[b, :, pl.ds(a, 2)].reshape(count, half)
+            total = jnp.dot(
+                jnp.concatenate([turned_ref[outs], turned_pair_ref[outs]], axis=1),
+                jnp.concatenate([mine, other], axis=0),
+                preferred_element_type=jnp.float32,
+            )
             keep(total, a, b)
         return 0
 
     lax.fori_loop(0, 3, spatial, 0)
     for k in range(3):
-        piece = cot_ref[outs, (2 - k) * block : (4 - k) * block]
-        total = jnp.dot(piece, hid_ref[...], preferred_element_type=jnp.float32)
-        piece = cot_pair_ref[outs, (2 - k) * block : (4 - k) * block]
-        total += jnp.dot(piece, hid_pair_ref[...], preferred_element_type=jnp.float32)
+        span = slice((2 - k) * block, (4 - k) * block)
+        total = jnp.dot(
+            jnp.concatenate([cot_ref[outs, span], cot_pair_ref[outs, span]], axis=1),
+            jnp.concatenate([hid_ref[...], hid_pair_ref[...]], axis=0),
+            preferred_element_type=jnp.float32,
+        )
         keep(total, 3, k)
     for slot in range(2):
         for i in range(4):
@@ -322,10 +348,13 @@
                     total = out_ref[f, :, lanes(index, half)]
                 else:
                     total = cot_ref[f, :, lanes(index, half)].astype(jnp.float32)
-                for b in range(3):
-                    piece = x_ref[2 - b, f, 2 - a : 4 - a].reshape(block, chans)
-                    kernel = kernel_ref[a, b].reshape(chans, half)
-                    total += jnp.dot(piece, kernel, preferred_element_type=jnp.float32)
+                pieces = [x_ref[2 - b, f, 2 - a : 4 - a].reshape(block, chans) for b in range(3)]
+                kernels = [kernel_ref[a, :, b].reshape(chans, half) for b in range(3)]
+                total += jnp.dot(
+                    jnp.concatenate(pieces, axis=1),
+                    jnp.concatenate(kernels, axis=0),
+                    preferred_element_type=jnp.float32,
+                )
                 out_ref[f, :, lanes(index, half)] = total
                 return 0
 
@@ -351,17 +380,16 @@
     start = (3 * lax.axis_index("x"), 0, lax.axis_index("core") * half)
     unit = lax.dynamic_slice(both, start, (3, both.shape[1], half))
     p = lax.axis_index("zh")
-    slots = [unit]
-    for k in range(1, 4):
-        slots.append(lax.ppermute(unit, "zh", [(i, i ^ k) for i in range(4)]))
+    slots = direct([unit] * 4, "zh")
     slots = [jnp.where(p & 1, slots[k ^ 1], slots[k]) for k in range(4)]
     slots = [jnp.where(p & 2, slots[k ^ 2], slots[k]) for k in range(4)]
-    return jnp.stack(slots, axis=1)
+    return jnp.stack(slots[:2]), jnp.stack(slots[2:])
 
 
 def kernel_parts(unit, waited):
-    lower = jnp.concatenate(ring_gather(unit[:, :2], "y"))
-    upper = jnp.concatenate(ring_gather(unit[:, 2:], "x"))
+    lower, upper = unit
+    lower = jnp.stack(direct([lower] * 4, "y"))
+    upper = jnp.stack(direct([upper] * 4, "x"))
     lower, lower_rest = ring_gather(lower, "x")
     upper, upper_rest = ring_gather(upper, "y")
     rest, waited = lax.optimization_barrier(((lower_rest, upper_rest), waited))
@@ -376,7 +404,15 @@
     core = lax.axis_index("core").astype(jnp.int32).reshape(1)
     own = spatial_kernel.shape[0]
     infos = [
-        jnp.concatenate([core ^ turn, slots_in("x", turn), slots_in("y", turn)])
+        jnp.concatenate(
+            [
+                core ^ turn,
+                slots_in("x", turn),
+                slots_in("y", turn),
+                turned_by("x"),
+                turned_by("y"),
+            ]
+        )
         for turn in range(2)
     ]
 
@@ -388,15 +424,14 @@
     cot_turned = cot_pad.reshape((frames + 2) * rows * width, chans).T
     waited = (shifts, cot_pad, cot_turned)
     parts, parts_other, (shifts, cot_pad, cot_turned) = kernel_parts(unit, waited)
-    shifts_pair = column_shifts(x_pair)
     cot_turned_pair = swap(cot_turned)
-    (shifts_pair, cot_turned_pair), parts_other = lax.optimization_barrier(
-        ((shifts_pair, cot_turned_pair), parts_other)
-    )
+    cot_turned_pair, parts_other = lax.optimization_barrier((cot_turned_pair, parts_other))
 
     k_mine, results = forward(infos, shifts, cot_pad, parts, parts_other)
     hid_mine, hid_other, slope_pre, turned, k_other = results
     turned_pair, hid_pair = swap(turned), swap(hid_other)
+    x_pair, _ = lax.optimization_barrier((x_pair, turned))
+    shifts_pair = column_shifts(x_pair)
     slope_maps = slope_pre.reshape(frames, rows, width, chans)
     slope_edges = edges_of(slope_maps, SPACE, 1)
     operands = (
@@ -409,7 +444,9 @@
         hid_mine.reshape(count, half),
         hid_pair.reshape(count, half),
     )
-    info = jnp.concatenate([core, slots_of("x"), slots_of("y")])
+    info = jnp.concatenate(
+        [core, slots_of("x"), slots_of("y"), turned_by("x"), turned_by("y")]
+    )
     lower, sent_lower = weight_terms(0, own, info, *operands)
     upper, sent_upper = weight_terms(1, own, info, *operands)
     slope_edges, _ = lax.optimization_barrier((slope_edges, (sent_lower, sent_upper)))
@@ -418,8 +455,8 @@
 
     lower = ring_scatter(lower, sent_lower, "x", grad)
     upper = ring_scatter(upper, sent_upper, "y", grad)
-    lower = ring_scatter(lower, lower[2:], "y")
-    upper = ring_scatter(upper, upper[2:], "x")
+    lower = direct_scatter(lower, "y")
+    upper = direct_scatter(upper, "x")
     terms = jnp.concatenate([lower, upper], axis=1)
     terms = terms.reshape(3, 4, 2, own // 2, half).transpose(1, 2, 0, 3, 4)
     terms = scattered(terms.reshape(8, 3, own // 2, half), ("zh", "zl"))

time: 185 us -> 201 us (1.086); the launches traced: 185 us -> 197 us
  starting transfers between devices: 62.7 us -> 74.3 us
  waiting for transfers between devices: 38.3 us -> 27.9 us
  blocking collectives: 25.3 us -> 28.6 us
  other arithmetic: 14.2 us -> 17.3 us
  local copies, waits for them, and re-layouts: 12.9 us -> 15.5 us
    ppermute x16 -> x8, waiting for transfers between devices: 36.2 us -> 14.6 us  [exchange(): return lax.ppermute(block, names, pairs)]
    ppermute x3 -> x15, starting transfers between devices: 9.12 us -> 22.4 us  [direct(): lax.ppermute(blocks[k], axis, [(i, i ^ k) for i in range(4)])]
    ppermute x3, starting transfers between devices: 11.8 us -> 24 us  [edges_of(): high = lax.ppermute(lax.slice_in_dim(block, 0, 1, axis=dim), axis, backward)]
    ppermute x16 -> x8, starting transfers between devices: 18.1 us -> 7.01 us  [exchange(): return lax.ppermute(block, names, pairs)]
    ppermute x3 -> x15, waiting for transfers between devices: 0.01 us -> 10.6 us  [direct(): lax.ppermute(blocks[k], axis, [(i, i ^ k) for i in range(4)])]
    ppermute x9, starting transfers between devices: 21.8 us -> 18.3 us  [swap(): return lax.ppermute(block, 'core', PAIR)]
    unnamed x10 -> x18, local copies, waits for them, and re-layouts: 0.32 us -> 3.77 us
    all_to_all x1, blocking collectives: 16 us -> 19.1 us  [scattered(): lax.all_to_all(block, axis, 0, 0, tiled=True).astype(jnp.float32)]
  transfers between devices with their start and end apart: 34 -> 38, of which waited for: 13 -> 12; matrix products, arithmetic and copies ran while one was open for 13% -> 13% of each run, Pallas kernels for 12% -> 16%
where the time goes in v3:
time: 201 us; the launch traced here: 197 us
  starting transfers between devices  74.3 us (37%)
  Pallas kernels  31.9 us (16%)
  blocking collectives  28.6 us (14%)
  waiting for transfers between devices  27.9 us (14%)
  other arithmetic  17.3 us (9%)
  local copies, waits for them, and re-layouts  15.5 us (8%)
    ppermute x3, starting transfers between devices, edges_of(): high = lax.ppermute(lax.slice_in_dim(block, 0, 1, axis=dim), axis, backward)  24 us
    ppermute x15, starting transfers between devices, direct(): lax.ppermute(blocks[k], axis, [(i, i ^ k) for i in range(4)])  22.4 us
    all_to_all x1, blocking collectives, scattered(): lax.all_to_all(block, axis, 0, 0, tiled=True).astype(jnp.float32)  19.1 us
    ppermute x9, starting transfers between devices, swap(): return lax.ppermute(block, 'core', PAIR)  18.3 us
    ppermute x8, waiting for transfers between devices, exchange(): return lax.ppermute(block, names, pairs)  14.6 us
    ppermute x15, waiting for transfers between devices, direct(): lax.ppermute(blocks[k], axis, [(i, i ^ k) for i in range(4)])  10.6 us
    all_to_all x1, blocking collectives, gathered(): return lax.all_to_all(spread, axis, 0, 0, tiled=True)  9.46 us
    pallas_call x2, Pallas kernels, weight_terms(): pl.pallas_call(functools.partial(weight_kernel, upper), out_shape=(jax.Sh...  9.32 us
  transfers between devices with their start and end apart: 38, of which 12 were waited for; matrix products, arithmetic and copies ran while one was open for 13% of the time, Pallas kernels for 16%

profile of v3, /device:TPU:1, one launch (start us, length us, event | category | flops | bytes accessed | tf_op | source)
XLA Modules:
  0.0 197.0 jit_solution(3545252415506772698)
XLA Ops:
  0.6 0.9 fusion.10
  1.6 6.9 %collective-permute-start = (bf16[3,32,256]{2,1,0:T(8,128)(2,1)S(1)}, bf16[3,32,256]{2,1,0:T(8,128)(2,1)S(1)}, u32[]{:S(2)}, u32[]{:S(2)}) collective-permute-start(bf16[3,32,256]{2,1,0:T(8,128)(2,1)S(1)} %fusion.10), channel_id=1, source_target_pairs={{0,12},{4,8},{8,4},{12,0},{1,13},{5,9},{9,5},{13,1},{2,14},{6,10},... | collective-permute-start | bytes 147464 | tf_op jit(solution)/shard_map/ppermute | solution.py:75
  8.5 1.0 collective-permute-start.1
  9.5 1.2 collective-permute-start.2
  10.7 1.2 fusion.26
  11.8 6.0 %collective-permute-start.14 = (bf16[2,1,192,512]{3,2,1,0:T(8,128)(2,1)S(1)}, bf16[2,1,192,512]{3,2,1,0:T(8,128)(2,1)S(1)}, u32[]{:S(2)}, u32[]{:S(2)}) collective-permute-start(bf16[2,1,192,512]{3,2,1,0:T(8,128)(2,1)S(1)} %get-tuple-element.78), channel_id=1, source_target_pairs={{1,0},{2,1},{3,2},{4,3},{5,4},{6,5},{7,6},{8,7},{9,8},{10,9},{11,1... | collective-permute-start | bytes 1179656 | tf_op jit(solution)/shard_map/ppermute | solution.py:101
  17.9 0.8 fusion.25
  18.7 1.3 collective-permute-start.8
  20.0 2.5 %collective-permute-start.9 = (bf16[2,3,32,256]{3,2,1,0:T(8,128)(2,1)S(1)}, bf16[2,3,32,256]{3,2,1,0:T(8,128)(2,1)S(1)}, u32[]{:S(2)}, u32[]{:S(2)}) collective-permute-start(bf16[2,3,32,256]{3,2,1,0:T(8,128)(2,1)S(1)} %get-tuple-element.94), channel_id=1, source_target_pairs={{0,128},{64,192},{128,0},{192,64},{1,129},{65,193},{129,1},{193,65... | collective-permute-start | bytes 294920 | tf_op jit(solution)/shard_map/ppermute | solution.py:75
  22.8 2.7 %collective-permute-done.9 = bf16[2,3,32,256]{3,2,1,0:T(8,128)(2,1)S(1)} collective-permute-done((bf16[2,3,32,256]{3,2,1,0:T(8,128)(2,1)S(1)}, bf16[2,3,32,256]{3,2,1,0:T(8,128)(2,1)S(1)}, u32[]{:S(2)}, u32[]{:S(2)}) %collective-permute-start.9) | collective-permute-done | bytes 98336 | tf_op jit(solution)/shard_map/ppermute | solution.py:75
  25.6 2.9 %collective-permute-done.10 = bf16[2,3,32,256]{3,2,1,0:T(8,128)(2,1)S(1)} collective-permute-done((bf16[2,3,32,256]{3,2,1,0:T(8,128)(2,1)S(1)}, bf16[2,3,32,256]{3,2,1,0:T(8,128)(2,1)S(1)}, u32[]{:S(2)}, u32[]{:S(2)}) %collective-permute-start.10) | collective-permute-done | bytes 98336 | tf_op jit(solution)/shard_map/ppermute | solution.py:75
  28.5 1.3 collective-permute-start.5
  29.8 1.0 fusion.13
  30.8 2.4 %collective-permute-start.16 = (bf16[1,2,192,512]{3,2,1,0:T(8,128)(2,1)}, bf16[1,2,192,512]{3,2,1,0:T(8,128)(2,1)S(1)}, u32[]{:S(2)}, u32[]{:S(2)}) collective-permute-start(bf16[1,2,192,512]{3,2,1,0:T(8,128)(2,1)} %get-tuple-element.76), channel_id=1, source_target_pairs={{16,0},{32,16},{48,32},{64,48},{80,64},{96,80},{112,96},{128,112},... | collective-permute-start | bytes 1179656 | tf_op jit(solution)/shard_map/ppermute | solution.py:101
  33.2 2.6 %collective-permute-start.15 = (bf16[1,2,192,512]{3,2,1,0:T(8,128)(2,1)S(1)}, bf16[1,2,192,512]{3,2,1,0:T(8,128)(2,1)S(1)}, u32[]{:S(2)}, u32[]{:S(2)}) collective-permute-start(bf16[1,2,192,512]{3,2,1,0:T(8,128)(2,1)S(1)} %get-tuple-element.75), channel_id=1, source_target_pairs={{0,16},{16,32},{32,48},{48,64},{64,80},{80,96},{96,112},{112,128},... | collective-permute-start | bytes 1179656 | tf_op jit(solution)/shard_map/ppermute | solution.py:100
  35.8 2.0 %collective-permute-done.5 = bf16[2,3,32,256]{3,2,1,0:T(8,128)(2,1)S(1)} collective-permute-done((bf16[2,3,32,256]{3,2,1,0:T(8,128)(2,1)S(1)}, bf16[2,3,32,256]{3,2,1,0:T(8,128)(2,1)S(1)}, u32[]{:S(2)}, u32[]{:S(2)}) %collective-permute-start.5) | collective-permute-done | bytes 98336 | tf_op jit(solution)/shard_map/ppermute | solution.py:75
  37.8 2.7 %collective-permute-start.11 = (bf16[4,2,3,32,256]{4,3,2,1,0:T(8,128)(2,1)}, bf16[4,2,3,32,256]{4,3,2,1,0:T(8,128)(2,1)}, u32[]{:S(2)}, u32[]{:S(2)}) collective-permute-start(bf16[4,2,3,32,256]{4,3,2,1,0:T(8,128)(2,1)} %get-tuple-element.86), channel_id=1, source_target_pairs={{0,1},{1,0},{2,3},{3,2},{16,19},{17,18},{18,17},{19,16},{4,5},{5,4... | collective-permute-start | bytes 1179656 | tf_op jit(solution)/shard_map/ppermute | solution.py:35
  40.5 0.9 fusion.14
  41.5 2.0 %collective-permute-start.6 = (bf16[4,2,3,32,256]{4,3,2,1,0:T(8,128)(2,1)}, bf16[4,2,3,32,256]{4,3,2,1,0:T(8,128)(2,1)}, u32[]{:S(2)}, u32[]{:S(2)}) collective-permute-start(bf16[4,2,3,32,256]{4,3,2,1,0:T(8,128)(2,1)} %get-tuple-element.88), channel_id=1, source_target_pairs={{0,64},{64,0},{128,192},{192,128},{16,208},{80,144},{144,80},{208,... | collective-permute-start | bytes 1179656 | tf_op jit(solution)/shard_map/ppermute | solution.py:35
  43.7 1.3 pad_maximum_fusion.4.cot_ref
  45.0 1.7 copy.12
  46.7 1.4 fusion.16
  48.2 2.4 %pad_maximum_fusion.7.refs_2_ = bf16[2,4,2,3,32,256]{5,4,3,2,1,0:T(8,128)(2,1)} fusion(bf16[1,4,2,3,32,256]{5,4,3,2,1,0:T(8,128)(2,1)} %bitcast.26, bf16[1,4,2,3,32,256]{5,4,3,2,1,0:T(8,128)(2,1)S(1)} %copy-done.5), kind=kLoop, calls=%fused_computation.21 | loop fusion | flops 393216 | bytes 1572864 | tf_op jit(solution)/shard_map/stack | solution.py:65
  50.5 0.3 collective-permute-done.6
  50.9 2.0 pad_maximum_fusion.6.refs_0_
  53.1 0.5 fusion.22
  53.6 0.5 pad_bitcast_fusion.2
  54.1 2.5 %pad_maximum_fusion.x_ref = bf16[3,2,4,192,512]{4,3,2,1,0:T(8,128)(2,1)} fusion(bf16[1,2,4,192,512]{4,3,2,1,0:T(8,128)(2,1)S(1)} %get-tuple-element.99, bf16[1,2,4,192,512]{4,3,2,1,0:T(8,128)(2,1)S(1)} %get-tuple-element.67, bf16[1,2,4,192,512]{4,3,2,1,0:T(8,128)(2,1)S(1)} %get-tuple-element.100), kind=kLoop, calls=%fused_computation | loop fusion | flops 4718592 | bytes 9437184 | tf_op jit(solution)/shard_map/stack | solution.py:115
  56.6 5.4 %collective-permute-done.12.refs_3_ = bf16[2,4,2,3,32,256]{5,4,3,2,1,0:T(8,128)(2,1)} collective-permute-done((bf16[2,4,2,3,32,256]{5,4,3,2,1,0:T(8,128)(2,1)}, bf16[2,4,2,3,32,256]{5,4,3,2,1,0:T(8,128)(2,1)}, u32[]{:S(2)}, u32[]{:S(2)}) %collective-permute-start.12) | collective-permute-done | bytes 786464 | tf_op jit(solution)/shard_map/ppermute | solution.py:35
  62.0 2.5 %collective-permute-done.7.refs_1_ = bf16[2,4,2,3,32,256]{5,4,3,2,1,0:T(8,128)(2,1)} collective-permute-done((bf16[2,4,2,3,32,256]{5,4,3,2,1,0:T(8,128)(2,1)}, bf16[2,4,2,3,32,256]{5,4,3,2,1,0:T(8,128)(2,1)}, u32[]{:S(2)}, u32[]{:S(2)}) %collective-permute-start.7) | collective-permute-done | bytes 786464 | tf_op jit(solution)/shard_map/ppermute | solution.py:35
  64.5 7.6 %collective-permute-start.17 = (bf16[512,1536]{1,0:T(8,128)(2,1)S(1)}, bf16[512,1536]{1,0:T(8,128)(2,1)}, u32[]{:S(2)}, u32[]{:S(2)}) collective-permute-start(bf16[512,1536]{1,0:T(8,128)(2,1)S(1)} %bitcast.112), channel_id=1, source_target_pairs={{0,16},{16,0},{1,17},{17,1},{2,18},{18,2},{3,19},{19,3},{4,20},{20... | collective-permute-start | bytes 4718600 | tf_op jit(solution)/shard_map/ppermute | solution.py:22
  72.1 0.5 collective-permute-start.18
  72.6 0.5 collective-permute-start.21
  73.1 2.1 %constant_dynamic-slice_fusion = bf16[2,4,192,256]{3,2,1,0:T(8,128)(2,1)} fusion(bf16[2,4,192,512]{3,2,1,0:T(8,128)(2,1)} %copy-done.4, s32[]{:T(128)S(6)} %select_n.141), kind=kLoop, calls=%fused_computation.68 | loop fusion | bytes 1572868 | tf_op jit(solution)/shard_map/dynamic_slice | solution.py:422
  75.3 1.2 collective-permute-done.20.refs_2_
  76.9 2.3 %copy-done = bf16[3,2,4,192,512]{4,3,2,1,0:T(8,128)(2,1)S(1)} copy-done((bf16[3,2,4,192,512]{4,3,2,1,0:T(8,128)(2,1)S(1)}, bf16[3,2,4,192,512]{4,3,2,1,0:T(8,128)(2,1)}, u32[]{:S(2)}) %copy-start) | copy-done | bytes 4718616
  79.2 1.4 copy-done.2
  80.6 7.0 %shard_map.67 = (f32[2,384,512]{2,1,0:T(8,128)S(1)}, f32[2,384,256]{2,1,0:T(8,128)S(1)}, bf16[4,4,3,4,32,256]{5,4,3,2,1,0:T(8,128)(2,1)S(1)}) custom-call(s32[17]{0:T(128)S(1)} %concatenate.51.info_ref, bf16[3,2,4,192,512]{4,3,2,1,0:T(8,128)(2,1)S(1)} %copy-done, bf16[4,2,192,512]{3,2,1,0:T(8,128)(2,1)S(1)} %copy-done.2, ...), custom_call_target="tpu_custom_call" | custom-call | flops 3200000000 | bytes 12000000 | tf_op jit(solution)/shard_map/pallas_call | solution.py:236
  87.7 8.7 %shard_map.68 = (bf16[2,384,256]{2,1,0:T(8,128)(2,1)S(1)}, bf16[2,384,256]{2,1,0:T(8,128)(2,1)S(1)}, bf16[2,384,512]{2,1,0:T(8,128)(2,1)S(1)}, bf16[512,768]{1,0...) custom-call(s32[17]{0:T(128)S(1)} %concatenate.45.info_ref, bf16[3,2,4,192,512]{4,3,2,1,0:T(8,128)(2,1)S(1)} %bitcast.111, ...), custom_call_target="tpu_custom_call" | custom-call | flops 3200000000 | bytes 15000000 | tf_op jit(solution)/shard_map/pallas_call | solution.py:245
  96.4 0.5 collective-permute-start.24
  97.2 15.6 %collective-permute-start.23 = (bf16[2,1,192,512]{3,2,1,0:T(8,128)(2,1)S(1)}, bf16[2,1,192,512]{3,2,1,0:T(8,128)(2,1)S(1)}, u32[]{:S(2)}, u32[]{:S(2)}) collective-permute-start(bf16[2,1,192,512]{3,2,1,0:T(8,128)(2,1)S(1)} %get-tuple-element.73), channel_id=1, source_target_pairs={{1,0},{2,1},{3,2},{4,3},{5,4},{6,5},{7,6},{8,7},{9,8},{10,9},{11,1... | collective-permute-start | bytes 1179656 | tf_op jit(solution)/shard_map/ppermute | solution.py:101
  112.8 1.6 fusion.23
  114.6 1.4 pad_maximum_fusion.2.x_pair_ref
  116.0 4.7 %shard_map.69 = (f32[4,4,3,2,32,256]{5,4,3,2,1,0:T(8,128)S(1)}, bf16[2,4,3,2,32,256]{5,4,3,2,1,0:T(8,128)(2,1)S(1)}) custom-call(s32[17]{0:T(128)S(1)} %concatenate.52.info_ref, bf16[512,768]{1,0:T(8,128)(2,1)S(1)} %get-tuple-element.42.turned_ref, bf16[512,768]{1,0:T(8,128)(2,1)S(1)} %collective-permute-done.24.turned_pair_ref, ...), custom_call_target="tpu_custom_call" | custom-call | flops 2400000000 | bytes 16000000 | tf_op jit(solution)/shard_map/pallas_call | solution.py:327
  120.7 1.8 collective-permute-start.27
  122.4 4.7 %shard_map.70 = (f32[4,4,3,2,32,256]{5,4,3,2,1,0:T(8,128)S(1)}, bf16[2,4,3,2,32,256]{5,4,3,2,1,0:T(8,128)(2,1)S(1)}) custom-call(s32[17]{0:T(128)S(1)} %concatenate.52.info_ref, bf16[512,768]{1,0:T(8,128)(2,1)S(1)} %get-tuple-element.42.turned_ref, bf16[512,768]{1,0:T(8,128)(2,1)S(1)} %collective-permute-done.24.turned_pair_ref, ...), custom_call_target="tpu_custom_call" | custom-call | flops 2400000000 | bytes 16000000 | tf_op jit(solution)/shard_map/pallas_call | solution.py:327
  127.5 0.5 fusion.21
  128.2 0.4 pad_bitcast_fusion.1
  128.6 0.6 pad_maximum_fusion.1.x_ref
  129.2 6.8 %shard_map.71 = f32[2,384,512]{2,1,0:T(8,128)} custom-call(s32[1]{0:T(128)} %bitcast.info_ref, bf16[3,2,4,192,512]{4,3,2,1,0:T(8,128)(2,1)S(1)} %pad_maximum_fusion.1.x_ref, bf16[2,384,512]{2,1,0:T(8,128)(2,1)S(1)} %bitcast.115, bf16[4,4,3,4,32,256]{5,4,3,2,1,0:T(8,128)(2,1)S(1)} %get-tuple-element.51.mine_ref, ...), custom_call_target="tpu_custom_call" | custom-call | flops 3600000000 | bytes 16000000 | tf_op jit(solution)/shard_map/pallas_call | solution.py:366
  136.0 1.3 convert_element_type.66
  137.6 1.6 collective-permute-done.32
  139.7 4.8 %collective-permute-done.28 = bf16[4,3,2,32,256]{4,3,2,1,0:T(8,128)(2,1)S(1)} collective-permute-done((bf16[4,3,2,32,256]{4,3,2,1,0:T(8,128)(2,1)S(1)}, bf16[4,3,2,32,256]{4,3,2,1,0:T(8,128)(2,1)S(1)}, u32[]{:S(2)}, u32[]{:S(2)}) %collective-permute-start.28) | collective-permute-done | bytes 393248 | tf_op jit(solution)/shard_map/ppermute | solution.py:35
  144.8 3.8 %collective-permute-start.30 = (bf16[3,2,32,256]{3,2,1,0:T(8,128)(2,1)S(1)}, bf16[3,2,32,256]{3,2,1,0:T(8,128)(2,1)S(1)}, u32[]{:S(2)}, u32[]{:S(2)}) collective-permute-start(bf16[3,2,32,256]{3,2,1,0:T(8,128)(2,1)S(1)} %get-tuple-element.81), channel_id=1, source_target_pairs={{0,2},{1,3},{2,0},{3,1},{4,6},{5,7},{6,4},{7,5},{8,10},{9,11},{10,... | collective-permute-start | bytes 294920 | tf_op jit(solution)/shard_map/ppermute | solution.py:75
  149.0 2.2 %collective-permute-start.35 = (bf16[3,2,32,256]{3,2,1,0:T(8,128)(2,1)S(1)}, bf16[3,2,32,256]{3,2,1,0:T(8,128)(2,1)S(1)}, u32[]{:S(2)}, u32[]{:S(2)}) collective-permute-start(bf16[3,2,32,256]{3,2,1,0:T(8,128)(2,1)S(1)} %get-tuple-element.84), channel_id=1, source_target_pairs={{0,128},{64,192},{128,0},{192,64},{1,129},{65,193},{129,1},{193,65... | collective-permute-start | bytes 294920 | tf_op jit(solution)/shard_map/ppermute | solution.py:75
  151.2 1.7 collective-permute-start.36
  152.9 1.5 collective-permute-done.31
  154.4 1.4 collective-permute-done.36
  156.0 19.1 %all_to_all.10 = f32[8,3,16,256]{3,2,1,0:T(8,128)S(1)} all-to-all(f32[8,3,16,256]{3,2,1,0:T(8,128)S(1)} %bitcast.126), channel_id=1, replica_groups=mesh['x'=4,'zl'=2,'core'=2,'zh'=4,'y'=4] {'zh','zl'}, dimensions={0} | all-to-all | bytes 786432 | tf_op jit(solution)/shard_map/all_to_all | solution.py:92
  175.2 9.5 %all_to_all.11 = f32[8,3,16,256]{3,2,1,0:T(8,128)S(1)} all-to-all(f32[8,3,16,256]{3,2,1,0:T(8,128)S(1)} %broadcast_in_dim.30), channel_id=1, replica_groups=mesh['x'=4,'zl'=2,'core'=2,'zh'=4,'y'=4] {'x','zl'}, dimensions={0} | all-to-all | bytes 786432 | tf_op jit(solution)/shard_map/all_to_all | solution.py:88
  184.7 8.9 %collective-permute-start.37 = (f32[8,3,16,256]{3,2,1,0:T(8,128)S(1)}, f32[8,3,16,256]{3,2,1,0:T(8,128)S(1)}, u32[]{:S(2)}, u32[]{:S(2)}) collective-permute-start(f32[8,3,16,256]{3,2,1,0:T(8,128)S(1)} %all_to_all.11), channel_id=1, source_target_pairs={{0,16},{16,0},{1,17},{17,1},{2,18},{18,2},{3,19},{19,3},{4,20},{20... | collective-permute-start | bytes 1179656 | tf_op jit(solution)/shard_map/ppermute | solution.py:22
  193.6 1.3 collective-permute-done.37
  195.2 0.9 copy.14
  196.1 0.7 copy.15
  (98 shorter events, 4.1 us)
Async XLA Ops:
  0.6 17.2 %copy-start.1 = (bf16[2,2,192,512]{3,2,1,0:T(8,128)(2,1)S(1)}, bf16[2,2,192,512]{3,2,1,0:T(8,128)(2,1)}, u32[]{:S(2)}) copy-start(bf16[2,2,192,512]{3,2,1,0:T(8,128)(2,1)} %param.5) | copy-start | bytes 2359300
  1.6 17.1 %collective-permute-start = (bf16[3,32,256]{2,1,0:T(8,128)(2,1)S(1)}, bf16[3,32,256]{2,1,0:T(8,128)(2,1)S(1)}, u32[]{:S(2)}, u32[]{:S(2)}) collective-permute-start(bf16[3,32,256]{2,1,0:T(8,128)(2,1)S(1)} %fusion.10), channel_id=1, source_target_pairs={{0,12},{4,8},{8,4},{12,0},{1,13},{5,9},{9,5},{13,1},{2,14},{6,10},... | collective-permute-start | bytes 147464 | tf_op jit(solution)/shard_map/ppermute | solution.py:75
  8.5 10.2 %collective-permute-start.1 = (bf16[3,32,256]{2,1,0:T(8,128)(2,1)S(1)}, bf16[3,32,256]{2,1,0:T(8,128)(2,1)S(1)}, u32[]{:S(2)}, u32[]{:S(2)}) collective-permute-start(bf16[3,32,256]{2,1,0:T(8,128)(2,1)S(1)} %fusion.10), channel_id=1, source_target_pairs={{0,8},{4,12},{8,0},{12,4},{1,9},{5,13},{9,1},{13,5},{2,10},{6,14},... | collective-permute-start | bytes 147464 | tf_op jit(solution)/shard_map/ppermute | solution.py:75
  9.5 9.2 %collective-permute-start.2 = (bf16[3,32,256]{2,1,0:T(8,128)(2,1)S(1)}, bf16[3,32,256]{2,1,0:T(8,128)(2,1)S(1)}, u32[]{:S(2)}, u32[]{:S(2)}) collective-permute-start(bf16[3,32,256]{2,1,0:T(8,128)(2,1)S(1)} %fusion.10), channel_id=1, source_target_pairs={{0,4},{4,0},{8,12},{12,8},{1,5},{5,1},{9,13},{13,9},{2,6},{6,2},{1... | collective-permute-start | bytes 147464 | tf_op jit(solution)/shard_map/ppermute | solution.py:75
  11.8 29.6 %collective-permute-start.14 = (bf16[2,1,192,512]{3,2,1,0:T(8,128)(2,1)S(1)}, bf16[2,1,192,512]{3,2,1,0:T(8,128)(2,1)S(1)}, u32[]{:S(2)}, u32[]{:S(2)}) collective-permute-start(bf16[2,1,192,512]{3,2,1,0:T(8,128)(2,1)S(1)} %get-tuple-element.78), channel_id=1, source_target_pairs={{1,0},{2,1},{3,2},{4,3},{5,4},{6,5},{7,6},{8,7},{9,8},{10,9},{11,1... | collective-permute-start | bytes 1179656 | tf_op jit(solution)/shard_map/ppermute | solution.py:101
  17.8 25.7 %collective-permute-start.13 = (bf16[2,1,192,512]{3,2,1,0:T(8,128)(2,1)S(1)}, bf16[2,1,192,512]{3,2,1,0:T(8,128)(2,1)S(1)}, u32[]{:S(2)}, u32[]{:S(2)}) collective-permute-start(bf16[2,1,192,512]{3,2,1,0:T(8,128)(2,1)S(1)} %get-tuple-element.77), channel_id=1, source_target_pairs={{0,1},{1,2},{2,3},{3,4},{4,5},{5,6},{6,7},{7,8},{8,9},{9,10},{10,1... | collective-permute-start | bytes 1179656 | tf_op jit(solution)/shard_map/ppermute | solution.py:100
  18.7 4.0 %collective-permute-start.8 = (bf16[2,3,32,256]{3,2,1,0:T(8,128)(2,1)S(1)}, bf16[2,3,32,256]{3,2,1,0:T(8,128)(2,1)S(1)}, u32[]{:S(2)}, u32[]{:S(2)}) collective-permute-start(bf16[2,3,32,256]{3,2,1,0:T(8,128)(2,1)S(1)} %get-tuple-element.94), channel_id=1, source_target_pairs={{0,64},{64,0},{128,192},{192,128},{1,65},{65,1},{129,193},{193,129... | collective-permute-start | bytes 294920 | tf_op jit(solution)/shard_map/ppermute | solution.py:75
  20.0 5.5 %collective-permute-start.9 = (bf16[2,3,32,256]{3,2,1,0:T(8,128)(2,1)S(1)}, bf16[2,3,32,256]{3,2,1,0:T(8,128)(2,1)S(1)}, u32[]{:S(2)}, u32[]{:S(2)}) collective-permute-start(bf16[2,3,32,256]{3,2,1,0:T(8,128)(2,1)S(1)} %get-tuple-element.94), channel_id=1, source_target_pairs={{0,128},{64,192},{128,0},{192,64},{1,129},{65,193},{129,1},{193,65... | collective-permute-start | bytes 294920 | tf_op jit(solution)/shard_map/ppermute | solution.py:75
  22.5 6.0 %collective-permute-start.10 = (bf16[2,3,32,256]{3,2,1,0:T(8,128)(2,1)S(1)}, bf16[2,3,32,256]{3,2,1,0:T(8,128)(2,1)S(1)}, u32[]{:S(2)}, u32[]{:S(2)}) collective-permute-start(bf16[2,3,32,256]{3,2,1,0:T(8,128)(2,1)S(1)} %get-tuple-element.94), channel_id=1, source_target_pairs={{0,192},{64,128},{128,64},{192,0},{1,193},{65,129},{129,65},{193,1... | collective-permute-start | bytes 294920 | tf_op jit(solution)/shard_map/ppermute | solution.py:75
  22.7 8.1 %collective-permute-start.3 = (bf16[2,3,32,256]{3,2,1,0:T(8,128)(2,1)S(1)}, bf16[2,3,32,256]{3,2,1,0:T(8,128)(2,1)S(1)}, u32[]{:S(2)}, u32[]{:S(2)}) collective-permute-start(bf16[2,3,32,256]{3,2,1,0:T(8,128)(2,1)S(1)} %get-tuple-element.96), channel_id=1, source_target_pairs={{0,1},{1,0},{2,3},{3,2},{4,5},{5,4},{6,7},{7,6},{8,9},{9,8},{10,11... | collective-permute-start | bytes 294920 | tf_op jit(solution)/shard_map/ppermute | solution.py:75
  25.5 7.7 %collective-permute-start.4 = (bf16[2,3,32,256]{3,2,1,0:T(8,128)(2,1)S(1)}, bf16[2,3,32,256]{3,2,1,0:T(8,128)(2,1)S(1)}, u32[]{:S(2)}, u32[]{:S(2)}) collective-permute-start(bf16[2,3,32,256]{3,2,1,0:T(8,128)(2,1)S(1)} %get-tuple-element.96), channel_id=1, source_target_pairs={{0,2},{1,3},{2,0},{3,1},{4,6},{5,7},{6,4},{7,5},{8,10},{9,11},{10,... | collective-permute-start | bytes 294920 | tf_op jit(solution)/shard_map/ppermute | solution.py:75
  28.5 9.3 %collective-permute-start.5 = (bf16[2,3,32,256]{3,2,1,0:T(8,128)(2,1)S(1)}, bf16[2,3,32,256]{3,2,1,0:T(8,128)(2,1)S(1)}, u32[]{:S(2)}, u32[]{:S(2)}) collective-permute-start(bf16[2,3,32,256]{3,2,1,0:T(8,128)(2,1)S(1)} %get-tuple-element.96), channel_id=1, source_target_pairs={{0,3},{1,2},{2,1},{3,0},{4,7},{5,6},{6,5},{7,4},{8,11},{9,10},{10,... | collective-permute-start | bytes 294920 | tf_op jit(solution)/shard_map/ppermute | solution.py:75
  30.8 12.8 %collective-permute-start.16 = (bf16[1,2,192,512]{3,2,1,0:T(8,128)(2,1)}, bf16[1,2,192,512]{3,2,1,0:T(8,128)(2,1)S(1)}, u32[]{:S(2)}, u32[]{:S(2)}) collective-permute-start(bf16[1,2,192,512]{3,2,1,0:T(8,128)(2,1)} %get-tuple-element.76), channel_id=1, source_target_pairs={{16,0},{32,16},{48,32},{64,48},{80,64},{96,80},{112,96},{128,112},... | collective-permute-start | bytes 1179656 | tf_op jit(solution)/shard_map/ppermute | solution.py:101
  33.2 10.4 %collective-permute-start.15 = (bf16[1,2,192,512]{3,2,1,0:T(8,128)(2,1)S(1)}, bf16[1,2,192,512]{3,2,1,0:T(8,128)(2,1)S(1)}, u32[]{:S(2)}, u32[]{:S(2)}) collective-permute-start(bf16[1,2,192,512]{3,2,1,0:T(8,128)(2,1)S(1)} %get-tuple-element.75), channel_id=1, source_target_pairs={{0,16},{16,32},{32,48},{48,64},{64,80},{80,96},{96,112},{112,128},... | collective-permute-start | bytes 1179656 | tf_op jit(solution)/shard_map/ppermute | solution.py:100
  37.8 10.4 %collective-permute-start.11 = (bf16[4,2,3,32,256]{4,3,2,1,0:T(8,128)(2,1)}, bf16[4,2,3,32,256]{4,3,2,1,0:T(8,128)(2,1)}, u32[]{:S(2)}, u32[]{:S(2)}) collective-permute-start(bf16[4,2,3,32,256]{4,3,2,1,0:T(8,128)(2,1)} %get-tuple-element.86), channel_id=1, source_target_pairs={{0,1},{1,0},{2,3},{3,2},{16,19},{17,18},{18,17},{19,16},{4,5},{5,4... | collective-permute-start | bytes 1179656 | tf_op jit(solution)/shard_map/ppermute | solution.py:35
  41.5 9.4 %collective-permute-start.6 = (bf16[4,2,3,32,256]{4,3,2,1,0:T(8,128)(2,1)}, bf16[4,2,3,32,256]{4,3,2,1,0:T(8,128)(2,1)}, u32[]{:S(2)}, u32[]{:S(2)}) collective-permute-start(bf16[4,2,3,32,256]{4,3,2,1,0:T(8,128)(2,1)} %get-tuple-element.88), channel_id=1, source_target_pairs={{0,64},{64,0},{128,192},{192,128},{16,208},{80,144},{144,80},{208,... | collective-permute-start | bytes 1179656 | tf_op jit(solution)/shard_map/ppermute | solution.py:35
  46.7 1.5 copy-start.5
  48.1 5.4 %copy-start.4 = (bf16[2,4,192,512]{3,2,1,0:T(8,128)(2,1)}, bf16[2,4,192,512]{3,2,1,0:T(8,128)(2,1)S(1)}, u32[]{:S(2)}) copy-start(bf16[2,4,192,512]{3,2,1,0:T(8,128)(2,1)S(1)} %get-tuple-element.68) | copy-start | bytes 4718596
  48.1 2.7 %copy-start.6 = (bf16[1,4,2,3,32,256]{5,4,3,2,1,0:T(8,128)(2,1)S(1)}, bf16[1,4,2,3,32,256]{5,4,3,2,1,0:T(8,128)(2,1)}, u32[]{:S(2)}) copy-start(bf16[1,4,2,3,32,256]{5,4,3,2,1,0:T(8,128)(2,1)} %get-tuple-element.87) | copy-start | bytes 1179652
  50.5 11.5 %collective-permute-start.12 = (bf16[2,4,2,3,32,256]{5,4,3,2,1,0:T(8,128)(2,1)}, bf16[2,4,2,3,32,256]{5,4,3,2,1,0:T(8,128)(2,1)}, u32[]{:S(2)}, u32[]{:S(2)}) collective-permute-start(bf16[2,4,2,3,32,256]{5,4,3,2,1,0:T(8,128)(2,1)} %pad_maximum_fusion.7.refs_2_), channel_id=1, source_target_pairs={{0,3},{1,2},{2,1},{3,0},{16,17},{17,16},{18,19},{19,18},{4,7},{5,6... | collective-permute-start | bytes 2359304 | tf_op jit(solution)/shard_map/ppermute | solution.py:35
  52.8 11.7 %collective-permute-start.7 = (bf16[2,4,2,3,32,256]{5,4,3,2,1,0:T(8,128)(2,1)}, bf16[2,4,2,3,32,256]{5,4,3,2,1,0:T(8,128)(2,1)}, u32[]{:S(2)}, u32[]{:S(2)}) collective-permute-start(bf16[2,4,2,3,32,256]{5,4,3,2,1,0:T(8,128)(2,1)} %pad_maximum_fusion.6.refs_0_), channel_id=1, source_target_pairs={{0,192},{64,128},{128,64},{192,0},{16,80},{80,16},{144,208},{208,1... | collective-permute-start | bytes 2359304 | tf_op jit(solution)/shard_map/ppermute | solution.py:35
  64.5 23.2 %collective-permute-start.17 = (bf16[512,1536]{1,0:T(8,128)(2,1)S(1)}, bf16[512,1536]{1,0:T(8,128)(2,1)}, u32[]{:S(2)}, u32[]{:S(2)}) collective-permute-start(bf16[512,1536]{1,0:T(8,128)(2,1)S(1)} %bitcast.112), channel_id=1, source_target_pairs={{0,16},{16,0},{1,17},{17,1},{2,18},{18,2},{3,19},{19,3},{4,20},{20... | collective-permute-start | bytes 4718600 | tf_op jit(solution)/shard_map/ppermute | solution.py:22
  72.1 4.4 %collective-permute-start.20 = (bf16[2,4,2,3,32,256]{5,4,3,2,1,0:T(8,128)(2,1)}, bf16[2,4,2,3,32,256]{5,4,3,2,1,0:T(8,128)(2,1)}, u32[]{:S(2)}, u32[]{:S(2)}) collective-permute-start(bf16[2,4,2,3,32,256]{5,4,3,2,1,0:T(8,128)(2,1)} %pad_maximum_fusion.7.refs_2_), channel_id=1, source_target_pairs={{0,16},{16,0},{1,17},{17,1},{2,18},{18,2},{3,19},{19,3},{4,20},{20... | collective-permute-start | bytes 2359304 | tf_op jit(solution)/shard_map/ppermute | solution.py:22
  72.1 15.5 %collective-permute-start.18 = (bf16[2,4,2,3,32,256]{5,4,3,2,1,0:T(8,128)(2,1)}, bf16[2,4,2,3,32,256]{5,4,3,2,1,0:T(8,128)(2,1)}, u32[]{:S(2)}, u32[]{:S(2)}) collective-permute-start(bf16[2,4,2,3,32,256]{5,4,3,2,1,0:T(8,128)(2,1)} %pad_maximum_fusion.6.refs_0_), channel_id=1, source_target_pairs={{0,16},{16,0},{1,17},{17,1},{2,18},{18,2},{3,19},{19,3},{4,20},{20... | collective-permute-start | bytes 2359304 | tf_op jit(solution)/shard_map/ppermute | solution.py:22
  72.6 15.0 %collective-permute-start.19 = (bf16[2,4,2,3,32,256]{5,4,3,2,1,0:T(8,128)(2,1)}, bf16[2,4,2,3,32,256]{5,4,3,2,1,0:T(8,128)(2,1)}, u32[]{:S(2)}, u32[]{:S(2)}) collective-permute-start(bf16[2,4,2,3,32,256]{5,4,3,2,1,0:T(8,128)(2,1)} %collective-permute-done.7.refs_1_), channel_id=1, source_target_pairs={{0,16},{16,0},{1,17},{17,1},{2,18},{18,2},{3,19},{19,3},{4,20},{20... | collective-permute-start | bytes 2359304 | tf_op jit(solution)/shard_map/ppermute | solution.py:22
  72.6 15.0 %collective-permute-start.21 = (bf16[2,4,2,3,32,256]{5,4,3,2,1,0:T(8,128)(2,1)}, bf16[2,4,2,3,32,256]{5,4,3,2,1,0:T(8,128)(2,1)}, u32[]{:S(2)}, u32[]{:S(2)}) collective-permute-start(bf16[2,4,2,3,32,256]{5,4,3,2,1,0:T(8,128)(2,1)} %collective-permute-done.12.refs_3_), channel_id=1, source_target_pairs={{0,16},{16,0},{1,17},{17,1},{2,18},{18,2},{3,19},{19,3},{4,20},{20... | collective-permute-start | bytes 2359304 | tf_op jit(solution)/shard_map/ppermute | solution.py:22
  73.1 14.5 %slice-start = ((s8[4718592]{0:T(1024)(128)(4,1)}), s8[524288]{0:T(1024)(128)(4,1)S(1)}, s32[]{:S(2)}) async-start(s8[4718592]{0:T(1024)(128)(4,1)} %bitcast.110), calls=%async_computation.2 | async-start | bytes 1048576
  76.5 20.4 %collective-permute-start.25 = (bf16[2,4,192,256]{3,2,1,0:T(8,128)(2,1)}, bf16[2,4,192,256]{3,2,1,0:T(8,128)(2,1)}, u32[]{:S(2)}, u32[]{:S(2)}) collective-permute-start(bf16[2,4,192,256]{3,2,1,0:T(8,128)(2,1)} %constant_dynamic-slice_fusion), channel_id=1, source_target_pairs={{0,16},{16,0},{1,17},{17,1},{2,18},{18,2},{3,19},{19,3},{4,20},{20... | collective-permute-start | bytes 2359304 | tf_op jit(solution)/shard_map/ppermute | solution.py:22
  76.9 2.3 %copy-start = (bf16[3,2,4,192,512]{4,3,2,1,0:T(8,128)(2,1)S(1)}, bf16[3,2,4,192,512]{4,3,2,1,0:T(8,128)(2,1)}, u32[]{:S(2)}) copy-start(bf16[3,2,4,192,512]{4,3,2,1,0:T(8,128)(2,1)} %pad_maximum_fusion.x_ref) | copy-start | bytes 14155780
  79.2 1.4 copy-start.2
  80.6 7.0 %slice-start.1 = ((s8[4718592]{0:T(1024)(128)(4,1)}), s8[4194304]{0:T(1024)(128)(4,1)S(1)}, s32[]{:S(2)}) async-start(s8[4718592]{0:T(1024)(128)(4,1)} %bitcast.110), calls=%async_computation.3 | async-start | bytes 8388608
  80.6 7.1 %copy-start.3 = (bf16[4,2,192,512]{3,2,1,0:T(8,128)(2,1)S(1)}, bf16[4,2,192,512]{3,2,1,0:T(8,128)(2,1)}, u32[]{:S(2)}) copy-start(bf16[4,2,192,512]{3,2,1,0:T(8,128)(2,1)} %pad_maximum_fusion.4.cot_ref) | copy-start | bytes 4718596
  96.4 19.6 %collective-permute-start.24 = (bf16[512,768]{1,0:T(8,128)(2,1)S(1)}, bf16[512,768]{1,0:T(8,128)(2,1)S(1)}, u32[]{:S(2)}, u32[]{:S(2)}) collective-permute-start(bf16[512,768]{1,0:T(8,128)(2,1)S(1)} %get-tuple-element.42.turned_ref), channel_id=1, source_target_pairs={{0,16},{16,0},{1,17},{17,1},{2,18},{18,2},{3,19},{19,3},{4,20},{20... | collective-permute-start | bytes 2359304 | tf_op jit(solution)/shard_map/ppermute | solution.py:22
  96.9 19.1 %collective-permute-start.26 = (bf16[2,384,256]{2,1,0:T(8,128)(2,1)S(1)}, bf16[2,384,256]{2,1,0:T(8,128)(2,1)S(1)}, u32[]{:S(2)}, u32[]{:S(2)}) collective-permute-start(bf16[2,384,256]{2,1,0:T(8,128)(2,1)S(1)} %get-tuple-element.46), channel_id=1, source_target_pairs={{0,16},{16,0},{1,17},{17,1},{2,18},{18,2},{3,19},{19,3},{4,20},{20... | collective-permute-start | bytes 1179656 | tf_op jit(solution)/shard_map/ppermute | solution.py:22
  97.1 30.1 %collective-permute-start.22 = (bf16[2,1,192,512]{3,2,1,0:T(8,128)(2,1)S(1)}, bf16[2,1,192,512]{3,2,1,0:T(8,128)(2,1)S(1)}, u32[]{:S(2)}, u32[]{:S(2)}) collective-permute-start(bf16[2,1,192,512]{3,2,1,0:T(8,128)(2,1)S(1)} %get-tuple-element.74), channel_id=1, source_target_pairs={{0,1},{1,2},{2,3},{3,4},{4,5},{5,6},{6,7},{7,8},{8,9},{9,10},{10,1... | collective-permute-start | bytes 1179656 | tf_op jit(solution)/shard_map/ppermute | solution.py:100
  97.2 30.0 %collective-permute-start.23 = (bf16[2,1,192,512]{3,2,1,0:T(8,128)(2,1)S(1)}, bf16[2,1,192,512]{3,2,1,0:T(8,128)(2,1)S(1)}, u32[]{:S(2)}, u32[]{:S(2)}) collective-permute-start(bf16[2,1,192,512]{3,2,1,0:T(8,128)(2,1)S(1)} %get-tuple-element.73), channel_id=1, source_target_pairs={{1,0},{2,1},{3,2},{4,3},{5,4},{6,5},{7,6},{8,7},{9,8},{10,9},{11,1... | collective-permute-start | bytes 1179656 | tf_op jit(solution)/shard_map/ppermute | solution.py:101
  120.7 15.3 %collective-permute-start.27 = (bf16[2,4,3,2,32,256]{5,4,3,2,1,0:T(8,128)(2,1)S(1)}, bf16[2,4,3,2,32,256]{5,4,3,2,1,0:T(8,128)(2,1)}, u32[]{:S(2)}, u32[]{:S(2)}) collective-permute-start(bf16[2,4,3,2,32,256]{5,4,3,2,1,0:T(8,128)(2,1)S(1)} %get-tuple-element.47), channel_id=1, source_target_pairs={{0,64},{64,0},{128,192},{192,128},{16,208},{80,144},{144,80},{208,... | collective-permute-start | bytes 2359304 | tf_op jit(solution)/shard_map/ppermute | solution.py:35
  127.1 12.1 %collective-permute-start.32 = (bf16[2,4,3,2,32,256]{5,4,3,2,1,0:T(8,128)(2,1)S(1)}, bf16[2,4,3,2,32,256]{5,4,3,2,1,0:T(8,128)(2,1)S(1)}, u32[]{:S(2)}, u32[]{:S(2)}) collective-permute-start(bf16[2,4,3,2,32,256]{5,4,3,2,1,0:T(8,128)(2,1)S(1)} %get-tuple-element.48), channel_id=1, source_target_pairs={{0,1},{1,0},{2,3},{3,2},{16,19},{17,18},{18,17},{19,16},{4,5},{5,4... | collective-permute-start | bytes 2359304 | tf_op jit(solution)/shard_map/ppermute | solution.py:35
  137.5 7.0 %collective-permute-start.28 = (bf16[4,3,2,32,256]{4,3,2,1,0:T(8,128)(2,1)S(1)}, bf16[4,3,2,32,256]{4,3,2,1,0:T(8,128)(2,1)S(1)}, u32[]{:S(2)}, u32[]{:S(2)}) collective-permute-start(bf16[4,3,2,32,256]{4,3,2,1,0:T(8,128)(2,1)S(1)} %fusion.6), channel_id=1, source_target_pairs={{0,192},{64,128},{128,64},{192,0},{16,80},{80,16},{144,208},{208,1... | collective-permute-start | bytes 1179656 | tf_op jit(solution)/shard_map/ppermute | solution.py:35
  139.6 9.1 %collective-permute-start.33 = (bf16[4,3,2,32,256]{4,3,2,1,0:T(8,128)(2,1)S(1)}, bf16[4,3,2,32,256]{4,3,2,1,0:T(8,128)(2,1)S(1)}, u32[]{:S(2)}, u32[]{:S(2)}) collective-permute-start(bf16[4,3,2,32,256]{4,3,2,1,0:T(8,128)(2,1)S(1)} %fusion.7), channel_id=1, source_target_pairs={{0,3},{1,2},{2,1},{3,0},{16,17},{17,16},{18,19},{19,18},{4,7},{5,6... | collective-permute-start | bytes 1179656 | tf_op jit(solution)/shard_map/ppermute | solution.py:35
  144.7 6.5 %collective-permute-start.29 = (bf16[3,2,32,256]{3,2,1,0:T(8,128)(2,1)S(1)}, bf16[3,2,32,256]{3,2,1,0:T(8,128)(2,1)S(1)}, u32[]{:S(2)}, u32[]{:S(2)}) collective-permute-start(bf16[3,2,32,256]{3,2,1,0:T(8,128)(2,1)S(1)} %get-tuple-element.79), channel_id=1, source_target_pairs={{0,1},{1,0},{2,3},{3,2},{4,5},{5,4},{6,7},{7,6},{8,9},{9,8},{10,11... | collective-permute-start | bytes 294920 | tf_op jit(solution)/shard_map/ppermute | solution.py:75
  144.8 8.0 %collective-permute-start.30 = (bf16[3,2,32,256]{3,2,1,0:T(8,128)(2,1)S(1)}, bf16[3,2,32,256]{3,2,1,0:T(8,128)(2,1)S(1)}, u32[]{:S(2)}, u32[]{:S(2)}) collective-permute-start(bf16[3,2,32,256]{3,2,1,0:T(8,128)(2,1)S(1)} %get-tuple-element.81), channel_id=1, source_target_pairs={{0,2},{1,3},{2,0},{3,1},{4,6},{5,7},{6,4},{7,5},{8,10},{9,11},{10,... | collective-permute-start | bytes 294920 | tf_op jit(solution)/shard_map/ppermute | solution.py:75
  148.6 5.7 %collective-permute-start.31 = (bf16[3,2,32,256]{3,2,1,0:T(8,128)(2,1)S(1)}, bf16[3,2,32,256]{3,2,1,0:T(8,128)(2,1)S(1)}, u32[]{:S(2)}, u32[]{:S(2)}) collective-permute-start(bf16[3,2,32,256]{3,2,1,0:T(8,128)(2,1)S(1)} %get-tuple-element.80), channel_id=1, source_target_pairs={{0,3},{1,2},{2,1},{3,0},{4,7},{5,6},{6,5},{7,4},{8,11},{9,10},{10,... | collective-permute-start | bytes 294920 | tf_op jit(solution)/shard_map/ppermute | solution.py:75
  148.9 5.5 %collective-permute-start.34 = (bf16[3,2,32,256]{3,2,1,0:T(8,128)(2,1)S(1)}, bf16[3,2,32,256]{3,2,1,0:T(8,128)(2,1)S(1)}, u32[]{:S(2)}, u32[]{:S(2)}) collective-permute-start(bf16[3,2,32,256]{3,2,1,0:T(8,128)(2,1)S(1)} %get-tuple-element.82), channel_id=1, source_target_pairs={{0,64},{64,0},{128,192},{192,128},{1,65},{65,1},{129,193},{193,129... | collective-permute-start | bytes 294920 | tf_op jit(solution)/shard_map/ppermute | solution.py:75
  149.0 5.4 %collective-permute-start.35 = (bf16[3,2,32,256]{3,2,1,0:T(8,128)(2,1)S(1)}, bf16[3,2,32,256]{3,2,1,0:T(8,128)(2,1)S(1)}, u32[]{:S(2)}, u32[]{:S(2)}) collective-permute-start(bf16[3,2,32,256]{3,2,1,0:T(8,128)(2,1)S(1)} %get-tuple-element.84), channel_id=1, source_target_pairs={{0,128},{64,192},{128,0},{192,64},{1,129},{65,193},{129,1},{193,65... | collective-permute-start | bytes 294920 | tf_op jit(solution)/shard_map/ppermute | solution.py:75
  151.2 4.7 %collective-permute-start.36 = (bf16[3,2,32,256]{3,2,1,0:T(8,128)(2,1)S(1)}, bf16[3,2,32,256]{3,2,1,0:T(8,128)(2,1)S(1)}, u32[]{:S(2)}, u32[]{:S(2)}) collective-permute-start(bf16[3,2,32,256]{3,2,1,0:T(8,128)(2,1)S(1)} %get-tuple-element.83), channel_id=1, source_target_pairs={{0,192},{64,128},{128,64},{192,0},{1,193},{65,129},{129,65},{193,1... | collective-permute-start | bytes 294920 | tf_op jit(solution)/shard_map/ppermute | solution.py:75
  184.7 10.3 %collective-permute-start.37 = (f32[8,3,16,256]{3,2,1,0:T(8,128)S(1)}, f32[8,3,16,256]{3,2,1,0:T(8,128)S(1)}, u32[]{:S(2)}, u32[]{:S(2)}) collective-permute-start(f32[8,3,16,256]{3,2,1,0:T(8,128)S(1)} %all_to_all.11), channel_id=1, source_target_pairs={{0,16},{16,0},{1,17},{17,1},{2,18},{18,2},{3,19},{19,3},{4,20},{20... | collective-permute-start | bytes 1179656 | tf_op jit(solution)/shard_map/ppermute | solution.py:22

commit v4 on v2

--- a/solution.py
+++ b/solution.py
@@ -15,7 +15,7 @@
 VMEM = pl.BlockSpec(memory_space=pltpu.VMEM)
 ANY = pl.BlockSpec(memory_space=pl.ANY)
 SMEM = pl.BlockSpec(memory_space=pltpu.SMEM)
-PARAMS = pltpu.CompilerParams(vmem_limit_bytes=24 * 1024 * 1024)
+PARAMS = pltpu.CompilerParams(vmem_limit_bytes=12 * 1024 * 1024)
 
 
 def swap(block):
@@ -53,13 +53,14 @@
     return jnp.stack([p, p ^ (1 + 2 * core), p ^ (3 - 2 * core), p ^ 2]).astype(jnp.int32)
 
 
-def ring_scatter(terms, sent, axis, waited=None):
+def widen(block):
+    return block.astype(jnp.float32)
+
+
+def ring_scatter(terms, sent, axis):
     came = exchange(sent, axis, 0)
-    if waited is not None:
-        came, waited = lax.optimization_barrier((came, waited))
-    came = came.astype(jnp.float32)
-    passed = (terms[1] + came[1]).astype(sent.dtype)
-    return terms[0] + came[0] + exchange(passed, axis, 1).astype(jnp.float32)
+    passed = (terms[1] + widen(came[1])).astype(sent.dtype)
+    return terms[0] + widen(came[0]) + widen(exchange(passed, axis, 1))
 
 
 def ring_gather(block, axis):
@@ -116,10 +117,10 @@
             slot = 2 * pair + j
             for t in range(4):
                 x, y = info_ref[1 + slot], info_ref[5 + t]
-                target = kernel_ref.at[x, :, pl.ds(0, 2), y]
+                target = kernel_ref.at[x, pl.ds(0, 2), :, y]
                 copies.append((parts[pair].at[j, t], target))
                 x, y = info_ref[1 + t], info_ref[5 + slot]
-                target = kernel_ref.at[x, :, pl.ds(2, 2), y]
+                target = kernel_ref.at[x, pl.ds(2, 2), :, y]
                 copies.append((parts[2 + pair].at[j, t], target))
     copies = [
         pltpu.make_async_copy(source, target, sems.at[i])
@@ -146,7 +147,7 @@
             piece = x_ref[b, f, a : a + 2, :, lanes(index, half)].reshape(block, half)
             total += lax.dot_general(
                 piece,
-                kernel_ref[a, b].reshape(chans, half),
+                kernel_ref[a, :, b].reshape(chans, half),
                 (((1,), (1,)), ((), ())),
                 preferred_element_type=jnp.float32,
             )
@@ -157,7 +158,7 @@
         total = jnp.zeros((block, half), jnp.float32)
         for k in range(3):
             piece = cot_ref[2 - k + f].reshape(block, chans)
-            kernel = kernel_ref[3, k].reshape(chans, half)
+            kernel = kernel_ref[3, :, k].reshape(chans, half)
             total += jnp.dot(piece, kernel, preferred_element_type=jnp.float32)
         slope_ref[f] = total
         return 0
@@ -212,7 +213,7 @@
     full = jax.ShapeDtypeStruct((frames, block, chans), jnp.float32)
     part = jax.ShapeDtypeStruct((frames, block, half), jnp.float32)
     hid = jax.ShapeDtypeStruct((frames, block, half), jnp.bfloat16)
-    kernel = jax.ShapeDtypeStruct((4, 3, 4, 4) + parts[0].shape[-2:], parts[0].dtype)
+    kernel = jax.ShapeDtypeStruct((4, 4, 3, 4) + parts[0].shape[-2:], parts[0].dtype)
     sems = pltpu.SemaphoreType.DMA((32,))
     pre, mine, k_mine = pl.pallas_call(
         first_kernel,
@@ -311,37 +312,39 @@
     )(info, *operands)
 
 
-def grad_kernel(info_ref, x_ref, cot_ref, mine_ref, other_ref, out_ref):
-    frames, block, chans = out_ref.shape
+def grad_kernel(f, info_ref, x_ref, cot_ref, mine_ref, other_ref, *refs):
+    out_ref = refs[-1]
+    block, chans = out_ref.shape[1:]
     half = chans // 2
     for kernel_ref, index in ((mine_ref, info_ref[0]), (other_ref, 1 - info_ref[0])):
-        for a in range(3):
-
-            def convolve(f, _, kernel_ref=kernel_ref, index=index, a=a):
-                if a > 0:
-                    total = out_ref[f, :, lanes(index, half)]
-                else:
-                    total = cot_ref[f, :, lanes(index, half)].astype(jnp.float32)
-                for b in range(3):
-                    piece = x_ref[2 - b, f, 2 - a : 4 - a].reshape(block, chans)
-                    kernel = kernel_ref[a, b].reshape(chans, half)
-                    total += jnp.dot(piece, kernel, preferred_element_type=jnp.float32)
-                out_ref[f, :, lanes(index, half)] = total
-                return 0
-
-            lax.fori_loop(0, frames, convolve, 0)
-
-
-def input_gradient(info, shifts, cotangent, k_mine, k_other):
+
+        def convolve(a, _, kernel_ref=kernel_ref, index=index):
+            total = out_ref[0, :, lanes(index, half)]
+            for b in range(3):
+                piece = x_ref[2 - b, f, pl.ds(2 - a, 2)].reshape(block, chans)
+                kernel = kernel_ref[a, :, b].reshape(chans, half)
+                total += jnp.dot(piece, kernel, preferred_element_type=jnp.float32)
+            out_ref[0, :, lanes(index, half)] = total
+            return 0
+
+        out_ref[0, :, lanes(index, half)] = cot_ref[f, :, lanes(index, half)].astype(jnp.float32)
+        lax.fori_loop(0, 3, convolve, 0)
+
+
+def input_gradient(f, info, shifts, cotangent, k_mine, k_other, earlier=()):
     frames, rows, width, chans = cotangent.shape
+    block = pl.BlockSpec((1, rows * width, chans), lambda i: (f, 0, 0))
+    whole = [pl.BlockSpec(memory_space=pltpu.VMEM)] * 4
     return pl.pallas_call(
-        grad_kernel,
+        functools.partial(grad_kernel, f),
+        grid=(1,),
         out_shape=jax.ShapeDtypeStruct((frames, rows * width, chans), jnp.float32),
-        in_specs=[SMEM] + [VMEM] * 4,
-        out_specs=VMEM,
+        in_specs=[SMEM] + whole + [ANY] * len(earlier),
+        out_specs=block,
+        input_output_aliases={5: 0} if earlier else {},
         compiler_params=PARAMS,
-        cost_estimate=pl.CostEstimate(flops=3600000000, bytes_accessed=16000000, transcendentals=0),
-    )(info, shifts, cotangent.reshape(frames, rows * width, chans), k_mine, k_other)
+        cost_estimate=pl.CostEstimate(flops=1800000000, bytes_accessed=8000000, transcendentals=0),
+    )(info, shifts, cotangent.reshape(frames, rows * width, chans), k_mine, k_other, *earlier)
 
 
 def kernel_unit(spatial_kernel, temporal_kernel, half):
@@ -356,12 +359,12 @@
         slots.append(lax.ppermute(unit, "zh", [(i, i ^ k) for i in range(4)]))
     slots = [jnp.where(p & 1, slots[k ^ 1], slots[k]) for k in range(4)]
     slots = [jnp.where(p & 2, slots[k ^ 2], slots[k]) for k in range(4)]
-    return jnp.stack(slots, axis=1)
+    return jnp.stack(slots[:2]), jnp.stack(slots[2:])
 
 
 def kernel_parts(unit, waited):
-    lower = jnp.concatenate(ring_gather(unit[:, :2], "y"))
-    upper = jnp.concatenate(ring_gather(unit[:, 2:], "x"))
+    lower = jnp.concatenate(ring_gather(unit[0], "y"))
+    upper = jnp.concatenate(ring_gather(unit[1], "x"))
     lower, lower_rest = ring_gather(lower, "x")
     upper, upper_rest = ring_gather(upper, "y")
     rest, waited = lax.optimization_barrier(((lower_rest, upper_rest), waited))
@@ -388,15 +391,14 @@
     cot_turned = cot_pad.reshape((frames + 2) * rows * width, chans).T
     waited = (shifts, cot_pad, cot_turned)
     parts, parts_other, (shifts, cot_pad, cot_turned) = kernel_parts(unit, waited)
-    shifts_pair = column_shifts(x_pair)
     cot_turned_pair = swap(cot_turned)
-    (shifts_pair, cot_turned_pair), parts_other = lax.optimization_barrier(
-        ((shifts_pair, cot_turned_pair), parts_other)
-    )
+    cot_turned_pair, parts_other = lax.optimization_barrier((cot_turned_pair, parts_other))
 
     k_mine, results = forward(infos, shifts, cot_pad, parts, parts_other)
     hid_mine, hid_other, slope_pre, turned, k_other = results
     turned_pair, hid_pair = swap(turned), swap(hid_other)
+    x_pair, _ = lax.optimization_barrier((x_pair, turned))
+    shifts_pair = column_shifts(x_pair)
     slope_maps = slope_pre.reshape(frames, rows, width, chans)
     slope_edges = edges_of(slope_maps, SPACE, 1)
     operands = (
@@ -414,15 +416,32 @@
     upper, sent_upper = weight_terms(1, own, info, *operands)
     slope_edges, _ = lax.optimization_barrier((slope_edges, (sent_lower, sent_upper)))
     slope_wide = widened(slope_maps, slope_edges, SPACE, 1)
-    grad = input_gradient(core, column_shifts(slope_wide), cotangent, k_mine, k_other)
-
-    lower = ring_scatter(lower, sent_lower, "x", grad)
-    upper = ring_scatter(upper, sent_upper, "y", grad)
-    lower = ring_scatter(lower, lower[2:], "y")
-    upper = ring_scatter(upper, upper[2:], "x")
+    shifts_slope = column_shifts(slope_wide)
+    grad = input_gradient(0, core, shifts_slope, cotangent, k_mine, k_other)
+
+    came_lower = exchange(sent_lower, "x", 0)
+    came_upper = exchange(sent_upper, "y", 0)
+    came_lower, grad = lax.optimization_barrier((came_lower, grad))
+    passed = (lower[1] + widen(came_lower[1])).astype(jnp.bfloat16)
+    info, _ = lax.optimization_barrier((core, passed))
+    grad = input_gradient(1, info, shifts_slope, cotangent, k_mine, k_other, (grad,))
+    last_lower = exchange(passed, "x", 1)
+    came_upper, grad = lax.optimization_barrier((came_upper, grad))
+    passed = (upper[1] + widen(came_upper[1])).astype(jnp.bfloat16)
+    last_upper = exchange(passed, "y", 1)
+
+    def total(terms, came, last, slots):
+        return terms[0, slots] + widen(came[0, slots]) + widen(last[slots])
+
+    keep, send = slice(0, 2), slice(2, 4)
+    sent_lower = total(lower, came_lower, last_lower, send)
+    sent_upper = total(upper, came_upper, last_upper, send)
+    lower = ring_scatter(total(lower, came_lower, last_lower, keep), sent_lower, "y")
+    upper = ring_scatter(total(upper, came_upper, last_upper, keep), sent_upper, "x")
     terms = jnp.concatenate([lower, upper], axis=1)
     terms = terms.reshape(3, 4, 2, own // 2, half).transpose(1, 2, 0, 3, 4)
-    terms = scattered(terms.reshape(8, 3, own // 2, half), ("zh", "zl"))
+    terms = terms.reshape(8, 3, own // 2, half).astype(jnp.bfloat16)
+    terms = scattered(terms, ("zh", "zl"))
     pixels = count * lax.axis_size(TM) * lax.axis_size(SPACE)
     terms = gathered(terms * (1.0 / math.sqrt(pixels)), ("x", "zl"))
     came = swap(terms)

time: 185 us -> 191 us (1.032)
  other arithmetic: 14.2 us -> 18.6 us
  waiting for transfers between devices: 38.3 us -> 42.5 us
  blocking collectives: 25.3 us -> 22.7 us
  Pallas kernels: 30.1 us -> 32.3 us
    ppermute x3, waiting for transfers between devices: 0.66 us -> 6.27 us  [edges_of(): high = lax.ppermute(lax.slice_in_dim(block, 0, 1, axis=dim), axis, backward)]
    all_to_all x1, blocking collectives: 16 us -> 11 us  [scattered(): lax.all_to_all(block, axis, 0, 0, tiled=True).astype(jnp.float32)]
    ppermute x16, waiting for transfers between devices: 36.2 us -> 32 us  [exchange(): return lax.ppermute(block, names, pairs)]
    another operation x8, other arithmetic: 4.43 us -> 8.61 us  [ring_gather(): pair = jnp.stack([block, exchange(block, axis, 0)])]
    ppermute x9, waiting for transfers between devices: 1.37 us -> 4.27 us  [swap(): return lax.ppermute(block, 'core', PAIR)]
    all_to_all x1, blocking collectives: 9.34 us -> 11.7 us  [gathered(): return lax.all_to_all(spread, axis, 0, 0, tiled=True)]
    unnamed x10 -> x16, local copies, waits for them, and re-layouts: 0.32 us -> 2.41 us
    pallas_call x1 -> x2, Pallas kernels: 6.82 us -> 7.55 us  [input_gradient(): pl.pallas_call(functools.partial(grad_kernel, f), grid=(1,), out_shape=ja...]
  transfers between devices with their start and end apart: 34 -> 34, of which waited for: 13 -> 14; matrix products, arithmetic and copies ran while one was open for 13% -> 13% of each run, Pallas kernels for 12% -> 17%
where the time goes in v4:
time: 191 us; the launch traced here: 190 us
  starting transfers between devices  61.4 us (32%)
  waiting for transfers between devices  42.5 us (22%)
  Pallas kernels  32.3 us (17%)
  blocking collectives  22.7 us (12%)
  other arithmetic  18.6 us (10%)
  local copies, waits for them, and re-layouts  11.2 us (6%)
    ppermute x16, waiting for transfers between devices, exchange(): return lax.ppermute(block, names, pairs)  32 us
    ppermute x9, starting transfers between devices, swap(): return lax.ppermute(block, 'core', PAIR)  20.8 us
    ppermute x16, starting transfers between devices, exchange(): return lax.ppermute(block, names, pairs)  17.8 us
    ppermute x3, starting transfers between devices, edges_of(): high = lax.ppermute(lax.slice_in_dim(block, 0, 1, axis=dim), axis, backward)  11.8 us
    all_to_all x1, blocking collectives, gathered(): return lax.all_to_all(spread, axis, 0, 0, tiled=True)  11.7 us
    all_to_all x1, blocking collectives, scattered(): lax.all_to_all(block, axis, 0, 0, tiled=True).astype(jnp.float32)  11 us
    pallas_call x2, Pallas kernels, weight_terms(): pl.pallas_call(functools.partial(weight_kernel, upper), out_shape=(jax.Sh...  9.29 us
    ppermute x3, starting transfers between devices, kernel_unit(): slots.append(lax.ppermute(unit, 'zh', [(i, i ^ k) for i in range(4)]))  9.12 us
  transfers between devices with their start and end apart: 34, of which 14 were waited for; matrix products, arithmetic and copies ran while one was open for 13% of the time, Pallas kernels for 17%

profile of v4, /device:TPU:1, one launch (start us, length us, event | category | flops | bytes accessed | tf_op | source)
XLA Modules:
  0.0 189.9 jit_solution(8682660561468454360)
XLA Ops:
  0.6 0.8 fusion.10
  1.5 6.9 %collective-permute-start = (bf16[3,32,256]{2,1,0:T(8,128)(2,1)S(1)}, bf16[3,32,256]{2,1,0:T(8,128)(2,1)S(1)}, u32[]{:S(2)}, u32[]{:S(2)}) collective-permute-start(bf16[3,32,256]{2,1,0:T(8,128)(2,1)S(1)} %fusion.10), channel_id=1, source_target_pairs={{0,12},{4,8},{8,4},{12,0},{1,13},{5,9},{9,5},{13,1},{2,14},{6,10},... | collective-permute-start | bytes 147464 | tf_op jit(solution)/shard_map/ppermute | solution.py:359
  8.4 1.0 collective-permute-start.1
  9.4 1.2 collective-permute-start.2
  10.6 1.2 fusion.22
  11.8 6.0 %collective-permute-start.12 = (bf16[2,1,192,512]{3,2,1,0:T(8,128)(2,1)S(1)}, bf16[2,1,192,512]{3,2,1,0:T(8,128)(2,1)S(1)}, u32[]{:S(2)}, u32[]{:S(2)}) collective-permute-start(bf16[2,1,192,512]{3,2,1,0:T(8,128)(2,1)S(1)} %get-tuple-element.84), channel_id=1, source_target_pairs={{1,0},{2,1},{3,2},{4,3},{5,4},{6,5},{7,6},{8,7},{9,8},{10,9},{11,1... | collective-permute-start | bytes 1179656 | tf_op jit(solution)/shard_map/ppermute | solution.py:86
  17.9 2.6 %collective-permute-start.7 = (bf16[2,3,32,256]{3,2,1,0:T(8,128)(2,1)S(1)}, bf16[2,3,32,256]{3,2,1,0:T(8,128)(2,1)S(1)}, u32[]{:S(2)}, u32[]{:S(2)}) collective-permute-start(bf16[2,3,32,256]{3,2,1,0:T(8,128)(2,1)S(1)} %get-tuple-element.94), channel_id=1, source_target_pairs={{0,64},{64,0},{128,192},{192,128},{16,208},{80,144},{144,80},{208,... | collective-permute-start | bytes 294920 | tf_op jit(solution)/shard_map/ppermute | solution.py:35
  20.4 1.4 collective-permute-start.3
  21.8 0.8 collective-permute-done.7
  22.6 0.7 pad_maximum_fusion.12
  23.6 6.6 %collective-permute-done.3 = bf16[2,3,32,256]{3,2,1,0:T(8,128)(2,1)S(1)} collective-permute-done((bf16[2,3,32,256]{3,2,1,0:T(8,128)(2,1)S(1)}, bf16[2,3,32,256]{3,2,1,0:T(8,128)(2,1)S(1)}, u32[]{:S(2)}, u32[]{:S(2)}) %collective-permute-start.3) | collective-permute-done | bytes 98336 | tf_op jit(solution)/shard_map/ppermute | solution.py:35
  30.2 0.7 pad_maximum_fusion.11
  31.1 1.8 collective-permute-start.13
  32.9 1.9 fusion.13
  34.7 1.3 collective-permute-done.4
  36.0 1.9 fusion.14
  37.9 2.7 %collective-permute-start.5 = (bf16[4,2,3,32,256]{4,3,2,1,0:T(8,128)(2,1)}, bf16[4,2,3,32,256]{4,3,2,1,0:T(8,128)(2,1)}, u32[]{:S(2)}, u32[]{:S(2)}) collective-permute-start(bf16[4,2,3,32,256]{4,3,2,1,0:T(8,128)(2,1)} %get-tuple-element.88), channel_id=1, source_target_pairs={{0,64},{64,0},{128,192},{192,128},{16,208},{80,144},{144,80},{208,... | collective-permute-start | bytes 1179656 | tf_op jit(solution)/shard_map/ppermute | solution.py:35
  40.6 0.8 broadcast_select_fusion.5
  41.4 3.2 %collective-permute-done.14 = bf16[1,2,192,512]{3,2,1,0:T(8,128)(2,1)} collective-permute-done((bf16[1,2,192,512]{3,2,1,0:T(8,128)(2,1)S(1)}, bf16[1,2,192,512]{3,2,1,0:T(8,128)(2,1)}, u32[]{:S(2)}, u32[]{:S(2)}) %collective-permute-start.14) | collective-permute-done | bytes 393248 | tf_op jit(solution)/shard_map/ppermute | solution.py:86
  44.7 1.0 broadcast_select_fusion
  45.7 1.3 pad_maximum_fusion.4.cot_ref
  47.1 1.8 copy.13
  48.9 1.3 fusion.16
  50.2 1.5 pad_maximum_fusion.7.refs_2_
  51.9 2.0 %pad_maximum_fusion.6.refs_0_ = bf16[2,4,2,3,32,256]{5,4,3,2,1,0:T(8,128)(2,1)} fusion(bf16[1,4,2,3,32,256]{5,4,3,2,1,0:T(8,128)(2,1)} %bitcast.16, bf16[1,4,2,3,32,256]{5,4,3,2,1,0:T(8,128)(2,1)S(1)} %copy-done.7), kind=kLoop, calls=%fused_computation.10 | loop fusion | flops 393216 | bytes 1572864 | tf_op jit(solution)/shard_map/stack | solution.py:67
  53.8 1.2 collective-permute-start.6
  55.0 0.5 fusion.18
  55.5 0.5 pad_bitcast_fusion.2
  56.1 2.5 %pad_maximum_fusion.x_ref = bf16[3,2,4,192,512]{4,3,2,1,0:T(8,128)(2,1)} fusion(bf16[1,2,4,192,512]{4,3,2,1,0:T(8,128)(2,1)S(1)} %get-tuple-element.97, bf16[1,2,4,192,512]{4,3,2,1,0:T(8,128)(2,1)S(1)} %get-tuple-element.73, bf16[1,2,4,192,512]{4,3,2,1,0:T(8,128)(2,1)S(1)} %get-tuple-element.98), kind=kLoop, calls=%fused_computation | loop fusion | flops 4718592 | bytes 9437184 | tf_op jit(solution)/shard_map/stack | solution.py:100
  58.5 4.5 %collective-permute-done.10.refs_3_ = bf16[2,4,2,3,32,256]{5,4,3,2,1,0:T(8,128)(2,1)} collective-permute-done((bf16[2,4,2,3,32,256]{5,4,3,2,1,0:T(8,128)(2,1)S(1)}, bf16[2,4,2,3,32,256]{5,4,3,2,1,0:T(8,128)(2,1)}, u32[]{:S(2)}, u32[]{:S(2)}) %collective-permute-start.10) | collective-permute-done | bytes 786464 | tf_op jit(solution)/shard_map/ppermute | solution.py:35
  63.0 2.2 %collective-permute-done.6.refs_1_ = bf16[2,4,2,3,32,256]{5,4,3,2,1,0:T(8,128)(2,1)} collective-permute-done((bf16[2,4,2,3,32,256]{5,4,3,2,1,0:T(8,128)(2,1)}, bf16[2,4,2,3,32,256]{5,4,3,2,1,0:T(8,128)(2,1)}, u32[]{:S(2)}, u32[]{:S(2)}) %collective-permute-start.6) | collective-permute-done | bytes 786464 | tf_op jit(solution)/shard_map/ppermute | solution.py:35
  65.3 6.2 %collective-permute-start.15 = (bf16[512,1536]{1,0:T(8,128)(2,1)S(1)}, bf16[512,1536]{1,0:T(8,128)(2,1)}, u32[]{:S(2)}, u32[]{:S(2)}) collective-permute-start(bf16[512,1536]{1,0:T(8,128)(2,1)S(1)} %bitcast.100), channel_id=1, source_target_pairs={{0,16},{16,0},{1,17},{17,1},{2,18},{18,2},{3,19},{19,3},{4,20},{20... | collective-permute-start | bytes 4718600 | tf_op jit(solution)/shard_map/ppermute | solution.py:22
  71.5 0.5 collective-permute-start.16
  72.0 0.5 collective-permute-start.19
  72.7 1.3 constant_dynamic-slice_fusion
  74.0 2.9 %collective-permute-done.18.refs_2_ = bf16[2,4,2,3,32,256]{5,4,3,2,1,0:T(8,128)(2,1)} collective-permute-done((bf16[2,4,2,3,32,256]{5,4,3,2,1,0:T(8,128)(2,1)S(1)}, bf16[2,4,2,3,32,256]{5,4,3,2,1,0:T(8,128)(2,1)}, u32[]{:S(2)}, u32[]{:S(2)}) %collective-permute-start.18) | collective-permute-done | bytes 786464 | tf_op jit(solution)/shard_map/ppermute | solution.py:22
  76.9 0.4 collective-permute-start.21
  77.4 2.3 %copy-done = bf16[3,2,4,192,512]{4,3,2,1,0:T(8,128)(2,1)S(1)} copy-done((bf16[3,2,4,192,512]{4,3,2,1,0:T(8,128)(2,1)S(1)}, bf16[3,2,4,192,512]{4,3,2,1,0:T(8,128)(2,1)}, u32[]{:S(2)}) %copy-start) | copy-done | bytes 4718616
  79.7 6.7 %shard_map.67 = (f32[2,384,512]{2,1,0:T(8,128)S(1)}, f32[2,384,256]{2,1,0:T(8,128)S(1)}, bf16[4,4,3,4,32,256]{5,4,3,2,1,0:T(8,128)(2,1)S(1)}) custom-call(s32[9]{0:T(128)S(1)} %concatenate.63.info_ref, bf16[3,2,4,192,512]{4,3,2,1,0:T(8,128)(2,1)S(1)} %copy-done, bf16[4,2,192,512]{3,2,1,0:T(8,128)(2,1)S(1)} %copy-done.3, ...), custom_call_target="tpu_custom_call" | custom-call | flops 3200000000 | bytes 12000000 | tf_op jit(solution)/shard_map/pallas_call | solution.py:218
  86.5 8.7 %shard_map.68 = (bf16[2,384,256]{2,1,0:T(8,128)(2,1)S(1)}, bf16[2,384,256]{2,1,0:T(8,128)(2,1)S(1)}, bf16[2,384,512]{2,1,0:T(8,128)(2,1)S(1)}, bf16[512,768]{1,0...) custom-call(s32[9]{0:T(128)S(1)} %concatenate.55.info_ref, bf16[3,2,4,192,512]{4,3,2,1,0:T(8,128)(2,1)S(1)} %copy-done.1, ...), custom_call_target="tpu_custom_call" | custom-call | flops 3200000000 | bytes 15000000 | tf_op jit(solution)/shard_map/pallas_call | solution.py:227
  96.0 5.7 %collective-permute-start.26 = (bf16[2,1,192,512]{3,2,1,0:T(8,128)(2,1)S(1)}, bf16[2,1,192,512]{3,2,1,0:T(8,128)(2,1)S(1)}, u32[]{:S(2)}, u32[]{:S(2)}) collective-permute-start(bf16[2,1,192,512]{3,2,1,0:T(8,128)(2,1)S(1)} %get-tuple-element.77), channel_id=1, source_target_pairs={{1,0},{2,1},{3,2},{4,3},{5,4},{6,5},{7,6},{8,7},{9,8},{10,9},{11,1... | collective-permute-start | bytes 1179656 | tf_op jit(solution)/shard_map/ppermute | solution.py:86
  102.5 4.6 %shard_map.70 = (f32[4,4,3,2,32,256]{5,4,3,2,1,0:T(8,128)S(1)}, bf16[2,4,3,2,32,256]{5,4,3,2,1,0:T(8,128)(2,1)S(1)}) custom-call(s32[9]{0:T(128)S(1)} %pad_add_fusion.info_ref, bf16[512,768]{1,0:T(8,128)(2,1)S(1)} %get-tuple-element.44.turned_ref, bf16[512,768]{1,0:T(8,128)(2,1)S(1)} %collective-permute-done.20.turned_pair_ref, ...), custom_call_target="tpu_custom_call" | custom-call | flops 2400000000 | bytes 16000000 | tf_op jit(solution)/shard_map/pallas_call | solution.py:302
  107.1 3.3 %collective-permute-start.24 = (bf16[2,4,3,2,32,256]{5,4,3,2,1,0:T(8,128)(2,1)S(1)}, bf16[2,4,3,2,32,256]{5,4,3,2,1,0:T(8,128)(2,1)S(1)}, u32[]{:S(2)}, u32[]{:S(2)}) collective-permute-start(bf16[2,4,3,2,32,256]{5,4,3,2,1,0:T(8,128)(2,1)S(1)} %get-tuple-element.51), channel_id=1, source_target_pairs={{0,64},{64,0},{128,192},{192,128},{16,208},{80,144},{144,80},{208,... | collective-permute-start | bytes 2359304 | tf_op jit(solution)/shard_map/ppermute | solution.py:35
  110.4 4.6 %shard_map.69 = (f32[4,4,3,2,32,256]{5,4,3,2,1,0:T(8,128)S(1)}, bf16[2,4,3,2,32,256]{5,4,3,2,1,0:T(8,128)(2,1)S(1)}) custom-call(s32[9]{0:T(128)S(1)} %pad_add_fusion.info_ref, bf16[512,768]{1,0:T(8,128)(2,1)S(1)} %get-tuple-element.44.turned_ref, bf16[512,768]{1,0:T(8,128)(2,1)S(1)} %collective-permute-done.20.turned_pair_ref, ...), custom_call_target="tpu_custom_call" | custom-call | flops 2400000000 | bytes 16000000 | tf_op jit(solution)/shard_map/pallas_call | solution.py:302
  115.2 3.0 %collective-permute-done.26 = bf16[2,1,192,512]{3,2,1,0:T(8,128)(2,1)S(1)} collective-permute-done((bf16[2,1,192,512]{3,2,1,0:T(8,128)(2,1)S(1)}, bf16[2,1,192,512]{3,2,1,0:T(8,128)(2,1)S(1)}, u32[]{:S(2)}, u32[]{:S(2)}) %collective-permute-start.26) | collective-permute-done | bytes 393248 | tf_op jit(solution)/shard_map/ppermute | solution.py:86
  118.5 0.5 fusion.17
  119.2 0.4 pad_bitcast_fusion.1
  119.6 0.6 pad_maximum_fusion.1.x_ref
  120.1 3.8 %shard_map.71.refs_0_ = f32[2,384,512]{2,1,0:T(8,128)} custom-call(s32[1]{0:T(128)} %bitcast.info_ref, bf16[3,2,4,192,512]{4,3,2,1,0:T(8,128)(2,1)S(1)} %pad_maximum_fusion.1.x_ref, bf16[2,384,512]{2,1,0:T(8,128)(2,1)S(1)} %bitcast.103, bf16[4,4,3,4,32,256]{5,4,3,2,1,0:T(8,128)(2,1)S(1)} %get-tuple-element.55.mine_ref, ...), custom_call_target="tpu_custom_call" | custom-call | flops 1800000000 | bytes 8000000 | tf_op jit(solution)/shard_map/pallas_call | solution.py:338
  124.1 1.4 collective-permute-start.27
  125.4 3.8 %shard_map.72 = f32[2,384,512]{2,1,0:T(8,128)} custom-call(s32[1]{0:T(128)} %bitcast.info_ref, bf16[3,2,4,192,512]{4,3,2,1,0:T(8,128)(2,1)S(1)} %pad_maximum_fusion.1.x_ref, bf16[2,384,512]{2,1,0:T(8,128)(2,1)S(1)} %bitcast.104, bf16[4,4,3,4,32,256]{5,4,3,2,1,0:T(8,128)(2,1)S(1)} %get-tuple-element.55.mine_ref, ...), custom_call_target="tpu_custom_call", output_to_operand_aliasing={{}: (5, {})} | custom-call | flops 1800000000 | bytes 8000000 | tf_op jit(solution)/shard_map/pallas_call | solution.py:338
  129.5 1.6 collective-permute-done.27
  131.3 4.7 %collective-permute-done.30 = bf16[4,3,2,32,256]{4,3,2,1,0:T(8,128)(2,1)S(1)} collective-permute-done((bf16[4,3,2,32,256]{4,3,2,1,0:T(8,128)(2,1)S(1)}, bf16[4,3,2,32,256]{4,3,2,1,0:T(8,128)(2,1)S(1)}, u32[]{:S(2)}, u32[]{:S(2)}) %collective-permute-start.30) | collective-permute-done | bytes 393248 | tf_op jit(solution)/shard_map/ppermute | solution.py:35
  136.2 3.0 %collective-permute-start.31 = (f32[2,3,2,32,256]{4,3,2,1,0:T(8,128)S(1)}, f32[2,3,2,32,256]{4,3,2,1,0:T(8,128)S(1)}, u32[]{:S(2)}, u32[]{:S(2)}) collective-permute-start(f32[2,3,2,32,256]{4,3,2,1,0:T(8,128)S(1)} %get-tuple-element.66), channel_id=1, source_target_pairs={{0,64},{64,0},{128,192},{192,128},{16,208},{80,144},{144,80},{208,... | collective-permute-start | bytes 1179656 | tf_op jit(solution)/shard_map/ppermute | solution.py:35
  139.2 1.9 collective-permute-done.28
  141.2 3.1 %collective-permute-done.31 = f32[2,3,2,32,256]{4,3,2,1,0:T(8,128)S(1)} collective-permute-done((f32[2,3,2,32,256]{4,3,2,1,0:T(8,128)S(1)}, f32[2,3,2,32,256]{4,3,2,1,0:T(8,128)S(1)}, u32[]{:S(2)}, u32[]{:S(2)}) %collective-permute-start.31) | collective-permute-done | bytes 393248 | tf_op jit(solution)/shard_map/ppermute | solution.py:35
  144.4 1.6 collective-permute-start.32
  146.1 5.2 %collective-permute-done.32 = f32[3,2,32,256]{3,2,1,0:T(8,128)S(1)} collective-permute-done((f32[3,2,32,256]{3,2,1,0:T(8,128)S(1)}, f32[3,2,32,256]{3,2,1,0:T(8,128)S(1)}, u32[]{:S(2)}, u32[]{:S(2)}) %collective-permute-start.32) | collective-permute-done | bytes 196640 | tf_op jit(solution)/shard_map/ppermute | solution.py:35
  151.3 11.0 %all_to_all.10 = bf16[8,3,16,256]{3,2,1,0:T(8,128)(2,1)S(1)} all-to-all(bf16[8,3,16,256]{3,2,1,0:T(8,128)(2,1)S(1)} %bitcast.117), channel_id=1, replica_groups=mesh['x'=4,'zl'=2,'core'=2,'zh'=4,'y'=4] {'zh','zl'}, dimensions={0} | all-to-all | bytes 393216 | tf_op jit(solution)/shard_map/all_to_all | solution.py:77
  162.4 11.7 %all_to_all.11 = f32[8,3,16,256]{3,2,1,0:T(8,128)S(1)} all-to-all(f32[8,3,16,256]{3,2,1,0:T(8,128)S(1)} %broadcast_in_dim.30), channel_id=1, replica_groups=mesh['x'=4,'zl'=2,'core'=2,'zh'=4,'y'=4] {'x','zl'}, dimensions={0} | all-to-all | bytes 786432 | tf_op jit(solution)/shard_map/all_to_all | solution.py:73
  174.1 12.6 %collective-permute-start.33 = (f32[8,3,16,256]{3,2,1,0:T(8,128)S(1)}, f32[8,3,16,256]{3,2,1,0:T(8,128)S(1)}, u32[]{:S(2)}, u32[]{:S(2)}) collective-permute-start(f32[8,3,16,256]{3,2,1,0:T(8,128)S(1)} %all_to_all.11), channel_id=1, source_target_pairs={{0,16},{16,0},{1,17},{17,1},{2,18},{18,2},{3,19},{19,3},{4,20},{20... | collective-permute-start | bytes 1179656 | tf_op jit(solution)/shard_map/ppermute | solution.py:22
  186.7 1.3 collective-permute-done.33
  188.4 0.9 copy.15
  189.2 0.7 copy.16
  (87 shorter events, 4.4 us)
Async XLA Ops:
  1.5 29.4 %copy-start.2 = (bf16[2,2,192,512]{3,2,1,0:T(8,128)(2,1)S(1)}, bf16[2,2,192,512]{3,2,1,0:T(8,128)(2,1)}, u32[]{:S(2)}) copy-start(bf16[2,2,192,512]{3,2,1,0:T(8,128)(2,1)} %param.5) | copy-start | bytes 2359300
  1.5 16.3 %collective-permute-start = (bf16[3,32,256]{2,1,0:T(8,128)(2,1)S(1)}, bf16[3,32,256]{2,1,0:T(8,128)(2,1)S(1)}, u32[]{:S(2)}, u32[]{:S(2)}) collective-permute-start(bf16[3,32,256]{2,1,0:T(8,128)(2,1)S(1)} %fusion.10), channel_id=1, source_target_pairs={{0,12},{4,8},{8,4},{12,0},{1,13},{5,9},{9,5},{13,1},{2,14},{6,10},... | collective-permute-start | bytes 147464 | tf_op jit(solution)/shard_map/ppermute | solution.py:359
  8.4 9.4 %collective-permute-start.1 = (bf16[3,32,256]{2,1,0:T(8,128)(2,1)S(1)}, bf16[3,32,256]{2,1,0:T(8,128)(2,1)S(1)}, u32[]{:S(2)}, u32[]{:S(2)}) collective-permute-start(bf16[3,32,256]{2,1,0:T(8,128)(2,1)S(1)} %fusion.10), channel_id=1, source_target_pairs={{0,8},{4,12},{8,0},{12,4},{1,9},{5,13},{9,1},{13,5},{2,10},{6,14},... | collective-permute-start | bytes 147464 | tf_op jit(solution)/shard_map/ppermute | solution.py:359
  9.4 8.4 %collective-permute-start.2 = (bf16[3,32,256]{2,1,0:T(8,128)(2,1)S(1)}, bf16[3,32,256]{2,1,0:T(8,128)(2,1)S(1)}, u32[]{:S(2)}, u32[]{:S(2)}) collective-permute-start(bf16[3,32,256]{2,1,0:T(8,128)(2,1)S(1)} %fusion.10), channel_id=1, source_target_pairs={{0,4},{4,0},{8,12},{12,8},{1,5},{5,1},{9,13},{13,9},{2,6},{6,2},{1... | collective-permute-start | bytes 147464 | tf_op jit(solution)/shard_map/ppermute | solution.py:359
  11.8 26.2 %collective-permute-start.12 = (bf16[2,1,192,512]{3,2,1,0:T(8,128)(2,1)S(1)}, bf16[2,1,192,512]{3,2,1,0:T(8,128)(2,1)S(1)}, u32[]{:S(2)}, u32[]{:S(2)}) collective-permute-start(bf16[2,1,192,512]{3,2,1,0:T(8,128)(2,1)S(1)} %get-tuple-element.84), channel_id=1, source_target_pairs={{1,0},{2,1},{3,2},{4,3},{5,4},{6,5},{7,6},{8,7},{9,8},{10,9},{11,1... | collective-permute-start | bytes 1179656 | tf_op jit(solution)/shard_map/ppermute | solution.py:86
  17.8 22.9 %collective-permute-start.11 = (bf16[2,1,192,512]{3,2,1,0:T(8,128)(2,1)S(1)}, bf16[2,1,192,512]{3,2,1,0:T(8,128)(2,1)S(1)}, u32[]{:S(2)}, u32[]{:S(2)}) collective-permute-start(bf16[2,1,192,512]{3,2,1,0:T(8,128)(2,1)S(1)} %get-tuple-element.83), channel_id=1, source_target_pairs={{0,1},{1,2},{2,3},{3,4},{4,5},{5,6},{6,7},{7,8},{8,9},{9,10},{10,1... | collective-permute-start | bytes 1179656 | tf_op jit(solution)/shard_map/ppermute | solution.py:85
  17.9 4.8 %collective-permute-start.7 = (bf16[2,3,32,256]{3,2,1,0:T(8,128)(2,1)S(1)}, bf16[2,3,32,256]{3,2,1,0:T(8,128)(2,1)S(1)}, u32[]{:S(2)}, u32[]{:S(2)}) collective-permute-start(bf16[2,3,32,256]{3,2,1,0:T(8,128)(2,1)S(1)} %get-tuple-element.94), channel_id=1, source_target_pairs={{0,64},{64,0},{128,192},{192,128},{16,208},{80,144},{144,80},{208,... | collective-permute-start | bytes 294920 | tf_op jit(solution)/shard_map/ppermute | solution.py:35
  20.4 9.8 %collective-permute-start.3 = (bf16[2,3,32,256]{3,2,1,0:T(8,128)(2,1)S(1)}, bf16[2,3,32,256]{3,2,1,0:T(8,128)(2,1)S(1)}, u32[]{:S(2)}, u32[]{:S(2)}) collective-permute-start(bf16[2,3,32,256]{3,2,1,0:T(8,128)(2,1)S(1)} %get-tuple-element.96), channel_id=1, source_target_pairs={{0,1},{1,0},{2,3},{3,2},{16,19},{17,18},{18,17},{19,16},{4,5},{5,4... | collective-permute-start | bytes 294920 | tf_op jit(solution)/shard_map/ppermute | solution.py:35
  23.3 7.8 %collective-permute-start.8 = (bf16[2,2,3,32,256]{4,3,2,1,0:T(8,128)(2,1)}, bf16[2,2,3,32,256]{4,3,2,1,0:T(8,128)(2,1)}, u32[]{:S(2)}, u32[]{:S(2)}) collective-permute-start(bf16[2,2,3,32,256]{4,3,2,1,0:T(8,128)(2,1)} %pad_maximum_fusion.12), channel_id=1, source_target_pairs={{0,192},{64,128},{128,64},{192,0},{16,80},{80,16},{144,208},{208,1... | collective-permute-start | bytes 589832 | tf_op jit(solution)/shard_map/ppermute | solution.py:35
  30.9 5.1 %collective-permute-start.4 = (bf16[2,2,3,32,256]{4,3,2,1,0:T(8,128)(2,1)}, bf16[2,2,3,32,256]{4,3,2,1,0:T(8,128)(2,1)}, u32[]{:S(2)}, u32[]{:S(2)}) collective-permute-start(bf16[2,2,3,32,256]{4,3,2,1,0:T(8,128)(2,1)} %pad_maximum_fusion.11), channel_id=1, source_target_pairs={{0,3},{1,2},{2,1},{3,0},{16,17},{17,16},{18,19},{19,18},{4,7},{5,6... | collective-permute-start | bytes 589832 | tf_op jit(solution)/shard_map/ppermute | solution.py:35
  31.0 13.7 %collective-permute-start.14 = (bf16[1,2,192,512]{3,2,1,0:T(8,128)(2,1)S(1)}, bf16[1,2,192,512]{3,2,1,0:T(8,128)(2,1)}, u32[]{:S(2)}, u32[]{:S(2)}) collective-permute-start(bf16[1,2,192,512]{3,2,1,0:T(8,128)(2,1)S(1)} %get-tuple-element.82), channel_id=1, source_target_pairs={{16,0},{32,16},{48,32},{64,48},{80,64},{96,80},{112,96},{128,112},... | collective-permute-start | bytes 1179656 | tf_op jit(solution)/shard_map/ppermute | solution.py:86
  31.1 14.6 %collective-permute-start.13 = (bf16[1,2,192,512]{3,2,1,0:T(8,128)(2,1)S(1)}, bf16[1,2,192,512]{3,2,1,0:T(8,128)(2,1)S(1)}, u32[]{:S(2)}, u32[]{:S(2)}) collective-permute-start(bf16[1,2,192,512]{3,2,1,0:T(8,128)(2,1)S(1)} %get-tuple-element.81), channel_id=1, source_target_pairs={{0,16},{16,32},{32,48},{48,64},{64,80},{80,96},{96,112},{112,128},... | collective-permute-start | bytes 1179656 | tf_op jit(solution)/shard_map/ppermute | solution.py:85
  36.0 14.1 %collective-permute-start.9 = (bf16[4,2,3,32,256]{4,3,2,1,0:T(8,128)(2,1)}, bf16[4,2,3,32,256]{4,3,2,1,0:T(8,128)(2,1)}, u32[]{:S(2)}, u32[]{:S(2)}) collective-permute-start(bf16[4,2,3,32,256]{4,3,2,1,0:T(8,128)(2,1)} %get-tuple-element.86), channel_id=1, source_target_pairs={{0,1},{1,0},{2,3},{3,2},{16,19},{17,18},{18,17},{19,16},{4,5},{5,4... | collective-permute-start | bytes 1179656 | tf_op jit(solution)/shard_map/ppermute | solution.py:35
  37.9 13.9 %collective-permute-start.5 = (bf16[4,2,3,32,256]{4,3,2,1,0:T(8,128)(2,1)}, bf16[4,2,3,32,256]{4,3,2,1,0:T(8,128)(2,1)}, u32[]{:S(2)}, u32[]{:S(2)}) collective-permute-start(bf16[4,2,3,32,256]{4,3,2,1,0:T(8,128)(2,1)} %get-tuple-element.88), channel_id=1, source_target_pairs={{0,64},{64,0},{128,192},{192,128},{16,208},{80,144},{144,80},{208,... | collective-permute-start | bytes 1179656 | tf_op jit(solution)/shard_map/ppermute | solution.py:35
  47.1 1.8 copy-start.5
  48.9 1.3 copy-start.6
  50.2 4.9 %copy-start.4 = (bf16[2,4,192,512]{3,2,1,0:T(8,128)(2,1)}, bf16[2,4,192,512]{3,2,1,0:T(8,128)(2,1)S(1)}, u32[]{:S(2)}) copy-start(bf16[2,4,192,512]{3,2,1,0:T(8,128)(2,1)S(1)} %get-tuple-element.74) | copy-start | bytes 4718596
  50.2 1.7 copy-start.7
  51.7 11.3 %collective-permute-start.10 = (bf16[2,4,2,3,32,256]{5,4,3,2,1,0:T(8,128)(2,1)S(1)}, bf16[2,4,2,3,32,256]{5,4,3,2,1,0:T(8,128)(2,1)}, u32[]{:S(2)}, u32[]{:S(2)}) collective-permute-start(bf16[2,4,2,3,32,256]{5,4,3,2,1,0:T(8,128)(2,1)S(1)} %pad_maximum_fusion.7.refs_2_), channel_id=1, source_target_pairs={{0,3},{1,2},{2,1},{3,0},{16,17},{17,16},{18,19},{19,18},{4,7},{5,6... | collective-permute-start | bytes 2359304 | tf_op jit(solution)/shard_map/ppermute | solution.py:35
  53.8 11.5 %collective-permute-start.6 = (bf16[2,4,2,3,32,256]{5,4,3,2,1,0:T(8,128)(2,1)}, bf16[2,4,2,3,32,256]{5,4,3,2,1,0:T(8,128)(2,1)}, u32[]{:S(2)}, u32[]{:S(2)}) collective-permute-start(bf16[2,4,2,3,32,256]{5,4,3,2,1,0:T(8,128)(2,1)} %pad_maximum_fusion.6.refs_0_), channel_id=1, source_target_pairs={{0,192},{64,128},{128,64},{192,0},{16,80},{80,16},{144,208},{208,1... | collective-permute-start | bytes 2359304 | tf_op jit(solution)/shard_map/ppermute | solution.py:35
  65.3 21.2 %collective-permute-start.15 = (bf16[512,1536]{1,0:T(8,128)(2,1)S(1)}, bf16[512,1536]{1,0:T(8,128)(2,1)}, u32[]{:S(2)}, u32[]{:S(2)}) collective-permute-start(bf16[512,1536]{1,0:T(8,128)(2,1)S(1)} %bitcast.100), channel_id=1, source_target_pairs={{0,16},{16,0},{1,17},{17,1},{2,18},{18,2},{3,19},{19,3},{4,20},{20... | collective-permute-start | bytes 4718600 | tf_op jit(solution)/shard_map/ppermute | solution.py:22
  71.5 5.4 %collective-permute-start.18 = (bf16[2,4,2,3,32,256]{5,4,3,2,1,0:T(8,128)(2,1)S(1)}, bf16[2,4,2,3,32,256]{5,4,3,2,1,0:T(8,128)(2,1)}, u32[]{:S(2)}, u32[]{:S(2)}) collective-permute-start(bf16[2,4,2,3,32,256]{5,4,3,2,1,0:T(8,128)(2,1)S(1)} %pad_maximum_fusion.7.refs_2_), channel_id=1, source_target_pairs={{0,16},{16,0},{1,17},{17,1},{2,18},{18,2},{3,19},{19,3},{4,20},{20... | collective-permute-start | bytes 2359304 | tf_op jit(solution)/shard_map/ppermute | solution.py:22
  71.5 15.0 %collective-permute-start.16 = (bf16[2,4,2,3,32,256]{5,4,3,2,1,0:T(8,128)(2,1)}, bf16[2,4,2,3,32,256]{5,4,3,2,1,0:T(8,128)(2,1)}, u32[]{:S(2)}, u32[]{:S(2)}) collective-permute-start(bf16[2,4,2,3,32,256]{5,4,3,2,1,0:T(8,128)(2,1)} %pad_maximum_fusion.6.refs_0_), channel_id=1, source_target_pairs={{0,16},{16,0},{1,17},{17,1},{2,18},{18,2},{3,19},{19,3},{4,20},{20... | collective-permute-start | bytes 2359304 | tf_op jit(solution)/shard_map/ppermute | solution.py:22
  72.0 14.5 %collective-permute-start.17 = (bf16[2,4,2,3,32,256]{5,4,3,2,1,0:T(8,128)(2,1)}, bf16[2,4,2,3,32,256]{5,4,3,2,1,0:T(8,128)(2,1)}, u32[]{:S(2)}, u32[]{:S(2)}) collective-permute-start(bf16[2,4,2,3,32,256]{5,4,3,2,1,0:T(8,128)(2,1)} %collective-permute-done.6.refs_1_), channel_id=1, source_target_pairs={{0,16},{16,0},{1,17},{17,1},{2,18},{18,2},{3,19},{19,3},{4,20},{20... | collective-permute-start | bytes 2359304 | tf_op jit(solution)/shard_map/ppermute | solution.py:22
  72.0 14.5 %collective-permute-start.19 = (bf16[2,4,2,3,32,256]{5,4,3,2,1,0:T(8,128)(2,1)}, bf16[2,4,2,3,32,256]{5,4,3,2,1,0:T(8,128)(2,1)}, u32[]{:S(2)}, u32[]{:S(2)}) collective-permute-start(bf16[2,4,2,3,32,256]{5,4,3,2,1,0:T(8,128)(2,1)} %collective-permute-done.10.refs_3_), channel_id=1, source_target_pairs={{0,16},{16,0},{1,17},{17,1},{2,18},{18,2},{3,19},{19,3},{4,20},{20... | collective-permute-start | bytes 2359304 | tf_op jit(solution)/shard_map/ppermute | solution.py:22
  72.7 4.7 %copy-start.3 = (bf16[4,2,192,512]{3,2,1,0:T(8,128)(2,1)S(1)}, bf16[4,2,192,512]{3,2,1,0:T(8,128)(2,1)}, u32[]{:S(2)}) copy-start(bf16[4,2,192,512]{3,2,1,0:T(8,128)(2,1)} %pad_maximum_fusion.4.cot_ref) | copy-start | bytes 4718596
  76.9 18.6 %collective-permute-start.21 = (bf16[2,4,192,256]{3,2,1,0:T(8,128)(2,1)S(1)}, bf16[2,4,192,256]{3,2,1,0:T(8,128)(2,1)S(1)}, u32[]{:S(2)}, u32[]{:S(2)}) collective-permute-start(bf16[2,4,192,256]{3,2,1,0:T(8,128)(2,1)S(1)} %constant_dynamic-slice_fusion), channel_id=1, source_target_pairs={{0,16},{16,0},{1,17},{17,1},{2,18},{18,2},{3,19},{19,3},{4,20},{20... | collective-permute-start | bytes 2359304 | tf_op jit(solution)/shard_map/ppermute | solution.py:22
  77.4 2.3 %copy-start = (bf16[3,2,4,192,512]{4,3,2,1,0:T(8,128)(2,1)S(1)}, bf16[3,2,4,192,512]{4,3,2,1,0:T(8,128)(2,1)}, u32[]{:S(2)}) copy-start(bf16[3,2,4,192,512]{4,3,2,1,0:T(8,128)(2,1)} %pad_maximum_fusion.x_ref) | copy-start | bytes 14155780
  79.7 6.8 %copy-start.1 = (bf16[3,2,4,192,512]{4,3,2,1,0:T(8,128)(2,1)S(1)}, bf16[3,2,4,192,512]{4,3,2,1,0:T(8,128)(2,1)}, u32[]{:S(2)}) copy-start(bf16[3,2,4,192,512]{4,3,2,1,0:T(8,128)(2,1)} %pad_maximum_fusion.x_ref) | copy-start | bytes 14155780
  95.2 7.2 %collective-permute-start.20 = (bf16[512,768]{1,0:T(8,128)(2,1)S(1)}, bf16[512,768]{1,0:T(8,128)(2,1)S(1)}, u32[]{:S(2)}, u32[]{:S(2)}) collective-permute-start(bf16[512,768]{1,0:T(8,128)(2,1)S(1)} %get-tuple-element.44.turned_ref), channel_id=1, source_target_pairs={{0,16},{16,0},{1,17},{17,1},{2,18},{18,2},{3,19},{19,3},{4,20},{20... | collective-permute-start | bytes 2359304 | tf_op jit(solution)/shard_map/ppermute | solution.py:22
  95.5 7.0 %collective-permute-start.22 = (bf16[2,384,256]{2,1,0:T(8,128)(2,1)S(1)}, bf16[2,384,256]{2,1,0:T(8,128)(2,1)S(1)}, u32[]{:S(2)}, u32[]{:S(2)}) collective-permute-start(bf16[2,384,256]{2,1,0:T(8,128)(2,1)S(1)} %get-tuple-element.48), channel_id=1, source_target_pairs={{0,16},{16,0},{1,17},{17,1},{2,18},{18,2},{3,19},{19,3},{4,20},{20... | collective-permute-start | bytes 1179656 | tf_op jit(solution)/shard_map/ppermute | solution.py:22
  95.9 19.3 %collective-permute-start.25 = (bf16[2,1,192,512]{3,2,1,0:T(8,128)(2,1)S(1)}, bf16[2,1,192,512]{3,2,1,0:T(8,128)(2,1)S(1)}, u32[]{:S(2)}, u32[]{:S(2)}) collective-permute-start(bf16[2,1,192,512]{3,2,1,0:T(8,128)(2,1)S(1)} %get-tuple-element.78), channel_id=1, source_target_pairs={{0,1},{1,2},{2,3},{3,4},{4,5},{5,6},{6,7},{7,8},{8,9},{9,10},{10,1... | collective-permute-start | bytes 1179656 | tf_op jit(solution)/shard_map/ppermute | solution.py:85
  96.0 22.2 %collective-permute-start.26 = (bf16[2,1,192,512]{3,2,1,0:T(8,128)(2,1)S(1)}, bf16[2,1,192,512]{3,2,1,0:T(8,128)(2,1)S(1)}, u32[]{:S(2)}, u32[]{:S(2)}) collective-permute-start(bf16[2,1,192,512]{3,2,1,0:T(8,128)(2,1)S(1)} %get-tuple-element.77), channel_id=1, source_target_pairs={{1,0},{2,1},{3,2},{4,3},{5,4},{6,5},{7,6},{8,7},{9,8},{10,9},{11,1... | collective-permute-start | bytes 1179656 | tf_op jit(solution)/shard_map/ppermute | solution.py:86
  107.1 16.8 %collective-permute-start.24 = (bf16[2,4,3,2,32,256]{5,4,3,2,1,0:T(8,128)(2,1)S(1)}, bf16[2,4,3,2,32,256]{5,4,3,2,1,0:T(8,128)(2,1)S(1)}, u32[]{:S(2)}, u32[]{:S(2)}) collective-permute-start(bf16[2,4,3,2,32,256]{5,4,3,2,1,0:T(8,128)(2,1)S(1)} %get-tuple-element.51), channel_id=1, source_target_pairs={{0,64},{64,0},{128,192},{192,128},{16,208},{80,144},{144,80},{208,... | collective-permute-start | bytes 2359304 | tf_op jit(solution)/shard_map/ppermute | solution.py:35
  115.1 14.2 %collective-permute-start.23 = (bf16[2,4,3,2,32,256]{5,4,3,2,1,0:T(8,128)(2,1)S(1)}, bf16[2,4,3,2,32,256]{5,4,3,2,1,0:T(8,128)(2,1)S(1)}, u32[]{:S(2)}, u32[]{:S(2)}) collective-permute-start(bf16[2,4,3,2,32,256]{5,4,3,2,1,0:T(8,128)(2,1)S(1)} %get-tuple-element.49), channel_id=1, source_target_pairs={{0,1},{1,0},{2,3},{3,2},{16,19},{17,18},{18,17},{19,16},{4,5},{5,4... | collective-permute-start | bytes 2359304 | tf_op jit(solution)/shard_map/ppermute | solution.py:35
  124.1 7.0 %collective-permute-start.27 = (bf16[4,3,2,32,256]{4,3,2,1,0:T(8,128)(2,1)S(1)}, bf16[4,3,2,32,256]{4,3,2,1,0:T(8,128)(2,1)S(1)}, u32[]{:S(2)}, u32[]{:S(2)}) collective-permute-start(bf16[4,3,2,32,256]{4,3,2,1,0:T(8,128)(2,1)S(1)} %fusion), channel_id=1, source_target_pairs={{0,192},{64,128},{128,64},{192,0},{16,80},{80,16},{144,208},{208,1... | collective-permute-start | bytes 1179656 | tf_op jit(solution)/shard_map/ppermute | solution.py:35
  129.4 6.7 %collective-permute-start.30 = (bf16[4,3,2,32,256]{4,3,2,1,0:T(8,128)(2,1)S(1)}, bf16[4,3,2,32,256]{4,3,2,1,0:T(8,128)(2,1)S(1)}, u32[]{:S(2)}, u32[]{:S(2)}) collective-permute-start(bf16[4,3,2,32,256]{4,3,2,1,0:T(8,128)(2,1)S(1)} %fusion.1), channel_id=1, source_target_pairs={{0,3},{1,2},{2,1},{3,0},{16,17},{17,16},{18,19},{19,18},{4,7},{5,6... | collective-permute-start | bytes 1179656 | tf_op jit(solution)/shard_map/ppermute | solution.py:35
  131.2 9.9 %collective-permute-start.28 = (f32[2,3,2,32,256]{4,3,2,1,0:T(8,128)S(1)}, f32[2,3,2,32,256]{4,3,2,1,0:T(8,128)S(1)}, u32[]{:S(2)}, u32[]{:S(2)}) collective-permute-start(f32[2,3,2,32,256]{4,3,2,1,0:T(8,128)S(1)} %get-tuple-element.64), channel_id=1, source_target_pairs={{0,1},{1,0},{2,3},{3,2},{16,19},{17,18},{18,17},{19,16},{4,5},{5,4... | collective-permute-start | bytes 1179656 | tf_op jit(solution)/shard_map/ppermute | solution.py:35
  136.2 8.1 %collective-permute-start.31 = (f32[2,3,2,32,256]{4,3,2,1,0:T(8,128)S(1)}, f32[2,3,2,32,256]{4,3,2,1,0:T(8,128)S(1)}, u32[]{:S(2)}, u32[]{:S(2)}) collective-permute-start(f32[2,3,2,32,256]{4,3,2,1,0:T(8,128)S(1)} %get-tuple-element.66), channel_id=1, source_target_pairs={{0,64},{64,0},{128,192},{192,128},{16,208},{80,144},{144,80},{208,... | collective-permute-start | bytes 1179656 | tf_op jit(solution)/shard_map/ppermute | solution.py:35
  141.1 4.9 %collective-permute-start.29 = (f32[3,2,32,256]{3,2,1,0:T(8,128)S(1)}, f32[3,2,32,256]{3,2,1,0:T(8,128)S(1)}, u32[]{:S(2)}, u32[]{:S(2)}) collective-permute-start(f32[3,2,32,256]{3,2,1,0:T(8,128)S(1)} %fusion.6), channel_id=1, source_target_pairs={{0,3},{1,2},{2,1},{3,0},{16,17},{17,16},{18,19},{19,18},{4,7},{5,6... | collective-permute-start | bytes 589832 | tf_op jit(solution)/shard_map/ppermute | solution.py:35
  144.4 6.8 %collective-permute-start.32 = (f32[3,2,32,256]{3,2,1,0:T(8,128)S(1)}, f32[3,2,32,256]{3,2,1,0:T(8,128)S(1)}, u32[]{:S(2)}, u32[]{:S(2)}) collective-permute-start(f32[3,2,32,256]{3,2,1,0:T(8,128)S(1)} %fusion.2), channel_id=1, source_target_pairs={{0,192},{64,128},{128,64},{192,0},{16,80},{80,16},{144,208},{208,1... | collective-permute-start | bytes 589832 | tf_op jit(solution)/shard_map/ppermute | solution.py:35
  174.1 14.0 %collective-permute-start.33 = (f32[8,3,16,256]{3,2,1,0:T(8,128)S(1)}, f32[8,3,16,256]{3,2,1,0:T(8,128)S(1)}, u32[]{:S(2)}, u32[]{:S(2)}) collective-permute-start(f32[8,3,16,256]{3,2,1,0:T(8,128)S(1)} %all_to_all.11), channel_id=1, source_target_pairs={{0,16},{16,0},{1,17},{17,1},{2,18},{18,2},{3,19},{19,3},{4,20},{20... | collective-permute-start | bytes 1179656 | tf_op jit(solution)/shard_map/ppermute | solution.py:22

commit v5 on v4

--- a/solution.py
+++ b/solution.py
@@ -97,13 +97,9 @@
 
 def column_shifts(maps):
     edge = jnp.zeros_like(maps[:, :, :1])
-    return jnp.stack(
-        [
-            jnp.concatenate([edge, maps[:, :, :-1]], axis=2),
-            maps,
-            jnp.concatenate([maps[:, :, 1:], edge], axis=2),
-        ]
-    )
+    left = jnp.concatenate([edge, maps[:, :, :-1]], axis=2)
+    right = jnp.concatenate([maps[:, :, 1:], edge], axis=2)
+    return left, maps, right
 
 
 def lanes(index, half):
@@ -112,16 +108,12 @@
 
 def assemble(info_ref, parts, kernel_ref, sems):
     copies = []
-    for pair in range(2):
-        for j in range(2):
-            slot = 2 * pair + j
-            for t in range(4):
-                x, y = info_ref[1 + slot], info_ref[5 + t]
-                target = kernel_ref.at[x, pl.ds(0, 2), :, y]
-                copies.append((parts[pair].at[j, t], target))
-                x, y = info_ref[1 + t], info_ref[5 + slot]
-                target = kernel_ref.at[x, pl.ds(2, 2), :, y]
-                copies.append((parts[2 + pair].at[j, t], target))
+    for slot in range(4):
+        for t in range(4):
+            x, y = info_ref[1 + slot], info_ref[5 + t]
+            copies.append((parts[slot].at[t], kernel_ref.at[x, pl.ds(0, 2), :, y]))
+            x, y = info_ref[1 + t], info_ref[5 + slot]
+            copies.append((parts[4 + slot].at[t], kernel_ref.at[x, pl.ds(2, 2), :, y]))
     copies = [
         pltpu.make_async_copy(source, target, sems.at[i])
         for i, (source, target) in enumerate(copies)
@@ -132,7 +124,7 @@
         copy.wait()
 
 
-def add_terms(index, x_ref, cot_ref, kernel_ref, pre_ref, slope_ref, start_ref):
+def add_terms(index, x_refs, cot_ref, kernel_ref, pre_ref, slope_ref, start_ref):
     frames, block, chans = pre_ref.shape
     half = chans // 2
 
@@ -144,7 +136,7 @@
         else:
             total = jnp.zeros((block, chans), jnp.float32)
         for b in range(3):
-            piece = x_ref[b, f, a : a + 2, :, lanes(index, half)].reshape(block, half)
+            piece = x_refs[b][f, a : a + 2, :, lanes(index, half)].reshape(block, half)
             total += lax.dot_general(
                 piece,
                 kernel_ref[a, :, b].reshape(chans, half),
@@ -168,19 +160,20 @@
     lax.fori_loop(0, frames, blend, 0)
 
 
-def first_kernel(info_ref, x_ref, cot_ref, *refs):
-    parts, (pre_ref, slope_ref, kernel_ref, sems) = refs[:4], refs[4:]
+def first_kernel(info_ref, *refs):
+    x_refs, cot_ref, parts, refs = refs[:3], refs[3], refs[4:12], refs[12:]
+    pre_ref, slope_ref, kernel_ref, sems = refs
     assemble(info_ref, parts, kernel_ref, sems)
-    add_terms(info_ref[0], x_ref, cot_ref, kernel_ref, pre_ref, slope_ref, None)
-
-
-def second_kernel(info_ref, x_ref, cot_ref, *refs):
-    parts, (start_ref, mine_ref), refs = refs[:4], refs[4:6], refs[6:]
-    hid_mine_ref, hid_other_ref, slope_ref, turned_ref, kernel_ref = refs[:5]
-    pre_ref, other_ref, work_ref, sems = refs[5:]
+    add_terms(info_ref[0], x_refs, cot_ref, kernel_ref, pre_ref, slope_ref, None)
+
+
+def second_kernel(info_ref, *refs):
+    x_refs, cot_ref, parts, refs = refs[:3], refs[3], refs[4:12], refs[12:]
+    start_ref, mine_ref, hid_mine_ref, hid_other_ref, slope_ref, turned_ref = refs[:6]
+    kernel_ref, pre_ref, other_ref, work_ref, sems = refs[6:]
     assemble(info_ref, parts, kernel_ref, sems)
     other = info_ref[0]
-    add_terms(other, x_ref, cot_ref, kernel_ref, pre_ref, other_ref, start_ref)
+    add_terms(other, x_refs, cot_ref, kernel_ref, pre_ref, other_ref, start_ref)
     frames, block, chans = pre_ref.shape
     half = chans // 2
     part = 32
@@ -207,7 +200,7 @@
 
 
 def forward(infos, shifts, cot_pad, parts, parts_other):
-    frames, _, width, chans = shifts.shape[1:]
+    frames, _, width, chans = shifts[0].shape
     block = 2 * width
     half = chans // 2
     full = jax.ShapeDtypeStruct((frames, block, chans), jnp.float32)
@@ -218,12 +211,12 @@
     pre, mine, k_mine = pl.pallas_call(
         first_kernel,
         out_shape=(full, part, kernel),
-        in_specs=[SMEM, VMEM, VMEM] + [ANY] * 4,
+        in_specs=[SMEM] + [VMEM] * 4 + [ANY] * 8,
         out_specs=(VMEM,) * 3,
         scratch_shapes=[sems],
         compiler_params=PARAMS,
         cost_estimate=pl.CostEstimate(flops=3200000000, bytes_accessed=12000000, transcendentals=0),
-    )(infos[0], shifts, cot_pad, *parts)
+    )(infos[0], *shifts, cot_pad, *parts)
     results = pl.pallas_call(
         second_kernel,
         out_shape=(
@@ -233,7 +226,7 @@
             jax.ShapeDtypeStruct((chans, frames * block), jnp.bfloat16),
             kernel,
         ),
-        in_specs=[SMEM, VMEM, VMEM] + [ANY] * 4 + [VMEM] * 2,
+        in_specs=[SMEM] + [VMEM] * 4 + [ANY] * 8 + [VMEM] * 2,
         out_specs=(VMEM,) * 5,
         scratch_shapes=[
             pltpu.VMEM(full.shape, jnp.float32),
@@ -243,25 +236,14 @@
         ],
         compiler_params=PARAMS,
         cost_estimate=pl.CostEstimate(flops=3200000000, bytes_accessed=15000000, transcendentals=0),
-    )(infos[1], shifts, cot_pad, *parts_other, pre, mine)
+    )(infos[1], *shifts, cot_pad, *parts_other, pre, mine)
     return k_mine, results
 
 
-def weight_kernel(
-    upper,
-    info_ref,
-    turned_ref,
-    turned_pair_ref,
-    x_ref,
-    x_pair_ref,
-    cot_ref,
-    cot_pair_ref,
-    hid_ref,
-    hid_pair_ref,
-    terms_ref,
-    sent_ref,
-):
-    half = x_pair_ref.shape[-1]
+def weight_kernel(upper, info_ref, turned_ref, turned_pair_ref, *refs):
+    x_refs, x_pair_refs, refs = refs[:3], refs[3:6], refs[6:]
+    cot_ref, cot_pair_ref, hid_ref, hid_pair_ref, terms_ref, sent_ref = refs
+    half = hid_ref.shape[-1]
     count = turned_ref.shape[1]
     block = count // 2
     own = terms_ref.shape[-2]
@@ -277,9 +259,9 @@
 
     def spatial(a, _):
         for b in range(3):
-            piece = x_ref[b, :, pl.ds(a, 2), :, lanes(info_ref[0], half)].reshape(count, half)
+            piece = x_refs[b][:, pl.ds(a, 2), :, lanes(info_ref[0], half)].reshape(count, half)
             total = jnp.dot(turned_ref[outs], piece, preferred_element_type=jnp.float32)
-            piece = x_pair_ref[b, :, pl.ds(a, 2)].reshape(count, half)
+            piece = x_pair_refs[b][:, pl.ds(a, 2)].reshape(count, half)
             total += jnp.dot(turned_pair_ref[outs], piece, preferred_element_type=jnp.float32)
             keep(total, a, b)
         return 0
@@ -305,15 +287,15 @@
             jax.ShapeDtypeStruct(shape, jnp.float32),
             jax.ShapeDtypeStruct((2,) + shape[1:], jnp.bfloat16),
         ),
-        in_specs=[SMEM] + [VMEM] * 8,
+        in_specs=[SMEM] + [VMEM] * 12,
         out_specs=(VMEM, VMEM),
         compiler_params=PARAMS,
         cost_estimate=pl.CostEstimate(flops=2400000000, bytes_accessed=16000000, transcendentals=0),
     )(info, *operands)
 
 
-def grad_kernel(f, info_ref, x_ref, cot_ref, mine_ref, other_ref, *refs):
-    out_ref = refs[-1]
+def grad_kernel(f, info_ref, *refs):
+    x_refs, cot_ref, mine_ref, other_ref, out_ref = refs[:3], *refs[3:6], refs[-1]
     block, chans = out_ref.shape[1:]
     half = chans // 2
     for kernel_ref, index in ((mine_ref, info_ref[0]), (other_ref, 1 - info_ref[0])):
@@ -321,7 +303,7 @@
         def convolve(a, _, kernel_ref=kernel_ref, index=index):
             total = out_ref[0, :, lanes(index, half)]
             for b in range(3):
-                piece = x_ref[2 - b, f, pl.ds(2 - a, 2)].reshape(block, chans)
+                piece = x_refs[2 - b][f, pl.ds(2 - a, 2)].reshape(block, chans)
                 kernel = kernel_ref[a, :, b].reshape(chans, half)
                 total += jnp.dot(piece, kernel, preferred_element_type=jnp.float32)
             out_ref[0, :, lanes(index, half)] = total
@@ -334,17 +316,17 @@
 def input_gradient(f, info, shifts, cotangent, k_mine, k_other, earlier=()):
     frames, rows, width, chans = cotangent.shape
     block = pl.BlockSpec((1, rows * width, chans), lambda i: (f, 0, 0))
-    whole = [pl.BlockSpec(memory_space=pltpu.VMEM)] * 4
+    whole = [pl.BlockSpec(memory_space=pltpu.VMEM)] * 6
     return pl.pallas_call(
         functools.partial(grad_kernel, f),
         grid=(1,),
         out_shape=jax.ShapeDtypeStruct((frames, rows * width, chans), jnp.float32),
         in_specs=[SMEM] + whole + [ANY] * len(earlier),
         out_specs=block,
-        input_output_aliases={5: 0} if earlier else {},
+        input_output_aliases={7: 0} if earlier else {},
         compiler_params=PARAMS,
         cost_estimate=pl.CostEstimate(flops=1800000000, bytes_accessed=8000000, transcendentals=0),
-    )(info, shifts, cotangent.reshape(frames, rows * width, chans), k_mine, k_other, *earlier)
+    )(info, *shifts, cotangent.reshape(frames, rows * width, chans), k_mine, k_other, *earlier)
 
 
 def kernel_unit(spatial_kernel, temporal_kernel, half):
@@ -362,14 +344,15 @@
     return jnp.stack(slots[:2]), jnp.stack(slots[2:])
 
 
-def kernel_parts(unit, waited):
+def kernel_parts(unit, ready):
     lower = jnp.concatenate(ring_gather(unit[0], "y"))
     upper = jnp.concatenate(ring_gather(unit[1], "x"))
-    lower, lower_rest = ring_gather(lower, "x")
-    upper, upper_rest = ring_gather(upper, "y")
-    rest, waited = lax.optimization_barrier(((lower_rest, upper_rest), waited))
-    mine = (lower, rest[0], upper, rest[1])
-    return mine, tuple(swap(part) for part in mine), waited
+    near = exchange(lower, "x", 0), exchange(upper, "y", 0)
+    second = exchange(lower, "x", 1), exchange(upper, "y", 1)
+    near, second, ready = lax.optimization_barrier((near, second, ready))
+    far = exchange(near[0], "x", 1), exchange(near[1], "y", 1)
+    parts = (lower, near[0], second[0], far[0], upper, near[1], second[1], far[1])
+    return parts, ready
 
 
 def per_device(activations, cotangent, spatial_kernel, temporal_kernel):
@@ -384,13 +367,17 @@
     ]
 
     unit = kernel_unit(spatial_kernel, temporal_kernel, half)
-    x_wide = widened(activations, edges_of(activations, SPACE, 1), SPACE, 1)
-    cot_pad = widened(cotangent, edges_of(cotangent, TM, 0), TM, 0)
-    x_pair = swap(lax.dynamic_slice_in_dim(x_wide, (1 - core[0]) * half, half, axis=3))
+    edges = edges_of(activations, SPACE, 1), edges_of(cotangent, TM, 0)
+    x_wide = widened(activations, edges[0], SPACE, 1)
+    x_other = lax.dynamic_slice_in_dim(x_wide, (1 - core[0]) * half, half, axis=3)
     shifts = column_shifts(x_wide)
+    cot_pad = widened(cotangent, edges[1], TM, 0)
     cot_turned = cot_pad.reshape((frames + 2) * rows * width, chans).T
-    waited = (shifts, cot_pad, cot_turned)
-    parts, parts_other, (shifts, cot_pad, cot_turned) = kernel_parts(unit, waited)
+    ready = (shifts, cot_pad, cot_turned, x_other)
+    parts, ready = kernel_parts(unit, ready)
+    shifts, cot_pad, cot_turned, x_other = ready
+    parts_other = tuple(swap(part) for part in parts)
+    x_pair = swap(x_other)
     cot_turned_pair = swap(cot_turned)
     cot_turned_pair, parts_other = lax.optimization_barrier((cot_turned_pair, parts_other))
 
@@ -404,8 +391,8 @@
     operands = (
         turned,
         turned_pair,
-        shifts,
-        shifts_pair,
+        *shifts,
+        *shifts_pair,
         cot_turned,
         cot_turned_pair,
         hid_mine.reshape(count, half),

time: 191 us -> 195 us (1.021)
  other arithmetic: 18.6 us -> 5.56 us
  starting transfers between devices: 61.4 us -> 72.2 us
  local copies, waits for them, and re-layouts: 11.2 us -> 20.9 us
  waiting for transfers between devices: 42.5 us -> 39.7 us
    ppermute x16 -> x18, waiting for transfers between devices: 32 us -> 17.1 us  [exchange(): return lax.ppermute(block, names, pairs)]
    ppermute x3, waiting for transfers between devices: 0.01 us -> 10.3 us  [edges_of(): lax.ppermute(lax.slice_in_dim(block, size - 1, size, axis=dim), axis, for...]
    another operation x8 -> x4, other arithmetic: 8.61 us -> 0.07 us  [ring_gather(): pair = jnp.stack([block, exchange(block, axis, 0)])]
    unnamed x16 -> x40, local copies, waits for them, and re-layouts: 2.41 us -> 10.4 us
    ppermute x9 -> x13, starting transfers between devices: 20.8 us -> 26.4 us  [swap(): return lax.ppermute(block, 'core', PAIR)]
    another operation x7 -> x2, other arithmetic: 4.88 us -> 0.09 us  [the longest x5 4.78 us: column_shifts(): jnp.stack([jnp.concatenate([edge, maps[:, :, :-1]], axis=2), maps, jnp.co...]
    ppermute x16 -> x18, starting transfers between devices: 17.8 us -> 21.6 us  [exchange(): return lax.ppermute(block, names, pairs)]
    concatenate x0 -> x6, local copies, waits for them, and re-layouts: none -> 3.67 us  [the longest x3 2.14 us: column_shifts(): left = jnp.concatenate([edge, maps[:, :, :-1]], axis=2)]
  transfers between devices with their start and end apart: 34 -> 40, of which waited for: 14 -> 14; matrix products, arithmetic and copies ran while one was open for 13% -> 7% of each run, Pallas kernels for 17% -> 16%
where the time goes in v5:
time: 195 us
  starting transfers between devices  72.2 us (37%)
  waiting for transfers between devices  39.7 us (20%)
  Pallas kernels  31.9 us (16%)
  blocking collectives  23.2 us (12%)
  local copies, waits for them, and re-layouts  20.9 us (11%)
  other arithmetic  5.56 us (3%)
    ppermute x13, starting transfers between devices, swap(): return lax.ppermute(block, 'core', PAIR)  26.4 us
    ppermute x18, starting transfers between devices, exchange(): return lax.ppermute(block, names, pairs)  21.6 us
    ppermute x18, waiting for transfers between devices, exchange(): return lax.ppermute(block, names, pairs)  17.1 us
    all_to_all x1, blocking collectives, scattered(): lax.all_to_all(block, axis, 0, 0, tiled=True).astype(jnp.float32)  12.2 us
    ppermute x3, starting transfers between devices, edges_of(): high = lax.ppermute(lax.slice_in_dim(block, 0, 1, axis=dim), axis, backward)  11.3 us
    all_to_all x1, blocking collectives, gathered(): return lax.all_to_all(spread, axis, 0, 0, tiled=True)  11.1 us
    unnamed x40, local copies, waits for them, and re-layouts  10.4 us
    ppermute x3, waiting for transfers between devices, edges_of(): lax.ppermute(lax.slice_in_dim(block, size - 1, size, axis=dim), axis, for...  10.3 us
  transfers between devices with their start and end apart: 40, of which 14 were waited for; matrix products, arithmetic and copies ran while one was open for 7% of the time, Pallas kernels for 16%

profile of v5, /device:TPU:1, one launch (start us, length us, event | category | flops | bytes accessed | tf_op | source)
XLA Modules:
  0.0 194.8 jit_solution(7541890170335104213)
XLA Ops:
  0.6 0.8 fusion.10
  1.5 6.9 %collective-permute-start = (bf16[3,32,256]{2,1,0:T(8,128)(2,1)S(1)}, bf16[3,32,256]{2,1,0:T(8,128)(2,1)S(1)}, u32[]{:S(2)}, u32[]{:S(2)}) collective-permute-start(bf16[3,32,256]{2,1,0:T(8,128)(2,1)S(1)} %fusion.10), channel_id=1, source_target_pairs={{0,12},{4,8},{8,4},{12,0},{1,13},{5,9},{9,5},{13,1},{2,14},{6,10},... | collective-permute-start | bytes 147464 | tf_op jit(solution)/shard_map/ppermute | solution.py:341
  8.4 1.0 collective-permute-start.1
  9.4 1.2 collective-permute-start.2
  10.6 1.2 fusion.17
  11.8 1.3 collective-permute-start.14
  13.1 2.7 %collective-permute-done.1 = bf16[3,32,256]{2,1,0:T(8,128)(2,1)S(1)} collective-permute-done((bf16[3,32,256]{2,1,0:T(8,128)(2,1)S(1)}, bf16[3,32,256]{2,1,0:T(8,128)(2,1)S(1)}, u32[]{:S(2)}, u32[]{:S(2)}) %collective-permute-start.1) | collective-permute-done | bytes 49184 | tf_op jit(solution)/shard_map/ppermute | solution.py:341
  15.8 2.6 %collective-permute-start.6 = (bf16[2,3,32,256]{3,2,1,0:T(8,128)(2,1)S(1)}, bf16[2,3,32,256]{3,2,1,0:T(8,128)(2,1)S(1)}, u32[]{:S(2)}, u32[]{:S(2)}) collective-permute-start(bf16[2,3,32,256]{3,2,1,0:T(8,128)(2,1)S(1)} %get-tuple-element.104), channel_id=1, source_target_pairs={{0,64},{64,0},{128,192},{192,128},{16,208},{80,144},{144,80},{208,... | collective-permute-start | bytes 294920 | tf_op jit(solution)/shard_map/ppermute | solution.py:35
  18.4 2.8 %collective-permute-start.3 = (bf16[2,3,32,256]{3,2,1,0:T(8,128)(2,1)S(1)}, bf16[2,3,32,256]{3,2,1,0:T(8,128)(2,1)S(1)}, u32[]{:S(2)}, u32[]{:S(2)}) collective-permute-start(bf16[2,3,32,256]{3,2,1,0:T(8,128)(2,1)S(1)} %get-tuple-element.106), channel_id=1, source_target_pairs={{0,1},{1,0},{2,3},{3,2},{16,19},{17,18},{18,17},{19,16},{4,5},{5,4... | collective-permute-start | bytes 294920 | tf_op jit(solution)/shard_map/ppermute | solution.py:35
  21.3 1.9 collective-permute-done.3
  23.6 0.9 fusion.18
  24.6 4.3 %collective-permute-start.12 = (bf16[2,1,192,512]{3,2,1,0:T(8,128)(2,1)}, bf16[2,1,192,512]{3,2,1,0:T(8,128)(2,1)}, u32[]{:S(2)}, u32[]{:S(2)}) collective-permute-start(bf16[2,1,192,512]{3,2,1,0:T(8,128)(2,1)} %get-tuple-element.98), channel_id=1, source_target_pairs={{1,0},{2,1},{3,2},{4,3},{5,4},{6,5},{7,6},{8,7},{9,8},{10,9},{11,1... | collective-permute-start | bytes 1179656 | tf_op jit(solution)/shard_map/ppermute | solution.py:86
  28.9 3.8 %collective-permute-start.13 = (bf16[1,2,192,512]{3,2,1,0:T(8,128)(2,1)S(1)}, bf16[1,2,192,512]{3,2,1,0:T(8,128)(2,1)S(1)}, u32[]{:S(2)}, u32[]{:S(2)}) collective-permute-start(bf16[1,2,192,512]{3,2,1,0:T(8,128)(2,1)S(1)} %get-tuple-element.95), channel_id=1, source_target_pairs={{0,16},{16,32},{32,48},{48,64},{64,80},{80,96},{96,112},{112,128},... | collective-permute-start | bytes 1179656 | tf_op jit(solution)/shard_map/ppermute | solution.py:85
  32.7 1.0 pad_maximum_fusion.5.refs_8_
  33.7 0.8 pad_maximum_fusion.4.refs_4_
  34.5 2.7 %collective-permute-start.8 = (bf16[4,2,3,32,256]{4,3,2,1,0:T(8,128)(2,1)S(1)}, bf16[4,2,3,32,256]{4,3,2,1,0:T(8,128)(2,1)}, u32[]{:S(2)}, u32[]{:S(2)}) collective-permute-start(bf16[4,2,3,32,256]{4,3,2,1,0:T(8,128)(2,1)S(1)} %pad_maximum_fusion.5.refs_8_), channel_id=1, source_target_pairs={{0,1},{1,0},{2,3},{3,2},{16,19},{17,18},{18,17},{19,16},{4,5},{5,4... | collective-permute-start | bytes 1179656 | tf_op jit(solution)/shard_map/ppermute | solution.py:35
  37.4 1.4 collective-permute-start.5
  39.0 0.7 copy.13
  40.2 1.1 broadcast_select_fusion.3
  41.3 10.2 %collective-permute-done.11 = bf16[2,1,192,512]{3,2,1,0:T(8,128)(2,1)} collective-permute-done((bf16[2,1,192,512]{3,2,1,0:T(8,128)(2,1)}, bf16[2,1,192,512]{3,2,1,0:T(8,128)(2,1)}, u32[]{:S(2)}, u32[]{:S(2)}) %collective-permute-start.11) | collective-permute-done | bytes 393248 | tf_op jit(solution)/shard_map/ppermute | solution.py:85
  52.2 1.5 concatenate.60.refs_0_
  53.8 1.3 concatenate.61.refs_2_
  55.1 0.9 constant_dynamic-slice_fusion
  56.0 8.7 %collective-permute-start.15 = (bf16[512,1536]{1,0:T(8,128)(2,1)S(1)}, bf16[512,1536]{1,0:T(8,128)(2,1)}, u32[]{:S(2)}, u32[]{:S(2)}) collective-permute-start(bf16[512,1536]{1,0:T(8,128)(2,1)S(1)} %bitcast.77), channel_id=1, source_target_pairs={{0,16},{16,0},{1,17},{17,1},{2,18},{18,2},{3,19},{19,3},{4,20},{20... | collective-permute-start | bytes 4718600 | tf_op jit(solution)/shard_map/ppermute | solution.py:22
  64.8 0.5 collective-permute-start.16
  65.3 3.5 %collective-permute-done.21.refs_8_ = bf16[4,2,3,32,256]{4,3,2,1,0:T(8,128)(2,1)S(1)} collective-permute-done((bf16[4,2,3,32,256]{4,3,2,1,0:T(8,128)(2,1)S(1)}, bf16[4,2,3,32,256]{4,3,2,1,0:T(8,128)(2,1)S(1)}, u32[]{:S(2)}, u32[]{:S(2)}) %collective-permute-start.21) | collective-permute-done | bytes 393248 | tf_op jit(solution)/shard_map/ppermute | solution.py:22
  68.8 0.8 copy-done.10
  69.7 0.7 copy-done.12
  70.8 0.7 copy-done.8
  71.6 0.9 collective-permute-done.19.refs_7_
  72.5 2.1 %collective-permute-start.22 = (bf16[4,2,3,32,256]{4,3,2,1,0:T(8,128)(2,1)}, bf16[4,2,3,32,256]{4,3,2,1,0:T(8,128)(2,1)}, u32[]{:S(2)}, u32[]{:S(2)}) collective-permute-start(bf16[4,2,3,32,256]{4,3,2,1,0:T(8,128)(2,1)} %collective-permute-done.8.refs_9_), channel_id=1, source_target_pairs={{0,16},{16,0},{1,17},{17,1},{2,18},{18,2},{3,19},{19,3},{4,20},{20... | collective-permute-start | bytes 1179656 | tf_op jit(solution)/shard_map/ppermute | solution.py:22
  74.6 0.8 collective-permute-start.23
  75.4 0.8 copy-done.14
  76.1 0.7 copy-done.16
  77.7 1.4 copy-done
  79.1 1.4 copy-done.2
  80.5 1.4 copy-done.7
  81.9 1.0 copy-done.9
  82.9 6.5 %shard_map.67 = (f32[2,384,512]{2,1,0:T(8,128)S(1)}, f32[2,384,256]{2,1,0:T(8,128)S(1)}, bf16[4,4,3,4,32,256]{5,4,3,2,1,0:T(8,128)(2,1)S(1)}) custom-call(s32[9]{0:T(128)S(1)} %concatenate.63.info_ref, bf16[2,4,192,512]{3,2,1,0:T(8,128)(2,1)S(1)} %copy-done, bf16[2,4,192,512]{3,2,1,0:T(8,128)(2,1)S(1)} %pad_maximum_fusion.refs_1_, ...), custom_call_target="tpu_custom_call" | custom-call | flops 3200000000 | bytes 12000000 | tf_op jit(solution)/shard_map/pallas_call | solution.py:211
  89.5 8.5 %shard_map.68 = (bf16[2,384,256]{2,1,0:T(8,128)(2,1)S(1)}, bf16[2,384,256]{2,1,0:T(8,128)(2,1)S(1)}, bf16[2,384,512]{2,1,0:T(8,128)(2,1)S(1)}, bf16[512,768]{1,0...) custom-call(s32[9]{0:T(128)S(1)} %concatenate.55.info_ref, bf16[2,4,192,512]{3,2,1,0:T(8,128)(2,1)S(1)} %copy-done, ...), custom_call_target="tpu_custom_call" | custom-call | flops 3200000000 | bytes 15000000 | tf_op jit(solution)/shard_map/pallas_call | solution.py:220
  98.0 0.6 collective-permute-start.26
  99.5 5.7 %collective-permute-start.32 = (bf16[2,1,192,512]{3,2,1,0:T(8,128)(2,1)S(1)}, bf16[2,1,192,512]{3,2,1,0:T(8,128)(2,1)S(1)}, u32[]{:S(2)}, u32[]{:S(2)}) collective-permute-start(bf16[2,1,192,512]{3,2,1,0:T(8,128)(2,1)S(1)} %get-tuple-element.91), channel_id=1, source_target_pairs={{1,0},{2,1},{3,2},{4,3},{5,4},{6,5},{7,6},{8,7},{9,8},{10,9},{11,1... | collective-permute-start | bytes 1179656 | tf_op jit(solution)/shard_map/ppermute | solution.py:86
  105.2 4.7 %shard_map.70 = (f32[4,4,3,2,32,256]{5,4,3,2,1,0:T(8,128)S(1)}, bf16[2,4,3,2,32,256]{5,4,3,2,1,0:T(8,128)(2,1)S(1)}) custom-call(s32[9]{0:T(128)S(1)} %pad_add_fusion.info_ref, bf16[512,768]{1,0:T(8,128)(2,1)S(1)} %get-tuple-element.61.turned_ref, bf16[512,768]{1,0:T(8,128)(2,1)S(1)} %collective-permute-done.26.turned_pair_ref, ...), custom_call_target="tpu_custom_call" | custom-call | flops 2400000000 | bytes 16000000 | tf_op jit(solution)/shard_map/pallas_call | solution.py:284
  109.9 2.2 %collective-permute-start.30 = (bf16[2,4,3,2,32,256]{5,4,3,2,1,0:T(8,128)(2,1)S(1)}, bf16[2,4,3,2,32,256]{5,4,3,2,1,0:T(8,128)(2,1)S(1)}, u32[]{:S(2)}, u32[]{:S(2)}) collective-permute-start(bf16[2,4,3,2,32,256]{5,4,3,2,1,0:T(8,128)(2,1)S(1)} %get-tuple-element.69), channel_id=1, source_target_pairs={{0,64},{64,0},{128,192},{192,128},{16,208},{80,144},{144,80},{208,... | collective-permute-start | bytes 2359304 | tf_op jit(solution)/shard_map/ppermute | solution.py:35
  112.1 4.7 %shard_map.69 = (f32[4,4,3,2,32,256]{5,4,3,2,1,0:T(8,128)S(1)}, bf16[2,4,3,2,32,256]{5,4,3,2,1,0:T(8,128)(2,1)S(1)}) custom-call(s32[9]{0:T(128)S(1)} %pad_add_fusion.info_ref, bf16[512,768]{1,0:T(8,128)(2,1)S(1)} %get-tuple-element.61.turned_ref, bf16[512,768]{1,0:T(8,128)(2,1)S(1)} %collective-permute-done.26.turned_pair_ref, ...), custom_call_target="tpu_custom_call" | custom-call | flops 2400000000 | bytes 16000000 | tf_op jit(solution)/shard_map/pallas_call | solution.py:284
  116.9 4.7 %collective-permute-done.32 = bf16[2,1,192,512]{3,2,1,0:T(8,128)(2,1)S(1)} collective-permute-done((bf16[2,1,192,512]{3,2,1,0:T(8,128)(2,1)S(1)}, bf16[2,1,192,512]{3,2,1,0:T(8,128)(2,1)S(1)}, u32[]{:S(2)}, u32[]{:S(2)}) %collective-permute-start.32) | collective-permute-done | bytes 393248 | tf_op jit(solution)/shard_map/ppermute | solution.py:86
  121.9 0.5 fusion.13
  123.0 1.0 copy-done.5
  123.9 3.8 %shard_map.71.refs_6_ = f32[2,384,512]{2,1,0:T(8,128)} custom-call(s32[1]{0:T(128)} %bitcast.info_ref, bf16[2,4,192,512]{3,2,1,0:T(8,128)(2,1)S(1)} %concatenate.67.refs_0_, bf16[2,4,192,512]{3,2,1,0:T(8,128)(2,1)S(1)} %pad_maximum_fusion.2.refs_1_, bf16[2,4,192,512]{3,2,1,0:T(8,128)(2,1)S(1)} %concatenate.68.refs_2_, bf16[2,384,512]{2,1,0:T(8,128)(2,1)S(1)} %bitcast.80, ...), custom_call_target="tpu_custom_call" | custom-call | flops 1800000000 | bytes 8000000 | tf_op jit(solution)/shard_map/pallas_call | solution.py:320
  127.9 3.8 %shard_map.72 = f32[2,384,512]{2,1,0:T(8,128)} custom-call(s32[1]{0:T(128)} %bitcast.info_ref, bf16[2,4,192,512]{3,2,1,0:T(8,128)(2,1)S(1)} %concatenate.67.refs_0_, bf16[2,4,192,512]{3,2,1,0:T(8,128)(2,1)S(1)} %pad_maximum_fusion.2.refs_1_, bf16[2,4,192,512]{3,2,1,0:T(8,128)(2,1)S(1)} %concatenate.68.refs_2_, ...), custom_call_target="tpu_custom_call", output_to_operand_aliasing={{}: (7, {})} | custom-call | flops 1800000000 | bytes 8000000 | tf_op jit(solution)/shard_map/pallas_call | solution.py:320
  132.0 2.9 %collective-permute-done.33 = bf16[4,3,2,32,256]{4,3,2,1,0:T(8,128)(2,1)S(1)} collective-permute-done((bf16[4,3,2,32,256]{4,3,2,1,0:T(8,128)(2,1)S(1)}, bf16[4,3,2,32,256]{4,3,2,1,0:T(8,128)(2,1)S(1)}, u32[]{:S(2)}, u32[]{:S(2)}) %collective-permute-start.33) | collective-permute-done | bytes 393248 | tf_op jit(solution)/shard_map/ppermute | solution.py:35
  135.0 2.7 %collective-permute-start.34 = (f32[2,3,2,32,256]{4,3,2,1,0:T(8,128)S(1)}, f32[2,3,2,32,256]{4,3,2,1,0:T(8,128)S(1)}, u32[]{:S(2)}, u32[]{:S(2)}) collective-permute-start(f32[2,3,2,32,256]{4,3,2,1,0:T(8,128)S(1)} %get-tuple-element.82), channel_id=1, source_target_pairs={{0,1},{1,0},{2,3},{3,2},{16,19},{17,18},{18,17},{19,16},{4,5},{5,4... | collective-permute-start | bytes 1179656 | tf_op jit(solution)/shard_map/ppermute | solution.py:35
  137.7 0.9 collective-permute-done.36
  138.7 3.8 %collective-permute-start.37 = (f32[2,3,2,32,256]{4,3,2,1,0:T(8,128)S(1)}, f32[2,3,2,32,256]{4,3,2,1,0:T(8,128)S(1)}, u32[]{:S(2)}, u32[]{:S(2)}) collective-permute-start(f32[2,3,2,32,256]{4,3,2,1,0:T(8,128)S(1)} %get-tuple-element.84), channel_id=1, source_target_pairs={{0,64},{64,0},{128,192},{192,128},{16,208},{80,144},{144,80},{208,... | collective-permute-start | bytes 1179656 | tf_op jit(solution)/shard_map/ppermute | solution.py:35
  142.5 3.3 %collective-permute-done.34 = f32[2,3,2,32,256]{4,3,2,1,0:T(8,128)S(1)} collective-permute-done((f32[2,3,2,32,256]{4,3,2,1,0:T(8,128)S(1)}, f32[2,3,2,32,256]{4,3,2,1,0:T(8,128)S(1)}, u32[]{:S(2)}, u32[]{:S(2)}) %collective-permute-start.34) | collective-permute-done | bytes 393248 | tf_op jit(solution)/shard_map/ppermute | solution.py:35
  146.0 1.7 collective-permute-done.37
  147.7 2.5 %collective-permute-start.38 = (f32[3,2,32,256]{3,2,1,0:T(8,128)S(1)}, f32[3,2,32,256]{3,2,1,0:T(8,128)S(1)}, u32[]{:S(2)}, u32[]{:S(2)}) collective-permute-start(f32[3,2,32,256]{3,2,1,0:T(8,128)S(1)} %fusion.2), channel_id=1, source_target_pairs={{0,192},{64,128},{128,64},{192,0},{16,80},{80,16},{144,208},{208,1... | collective-permute-start | bytes 589832 | tf_op jit(solution)/shard_map/ppermute | solution.py:35
  150.5 5.1 %collective-permute-done.38 = f32[3,2,32,256]{3,2,1,0:T(8,128)S(1)} collective-permute-done((f32[3,2,32,256]{3,2,1,0:T(8,128)S(1)}, f32[3,2,32,256]{3,2,1,0:T(8,128)S(1)}, u32[]{:S(2)}, u32[]{:S(2)}) %collective-permute-start.38) | collective-permute-done | bytes 196640 | tf_op jit(solution)/shard_map/ppermute | solution.py:35
  155.8 12.2 %all_to_all.10 = bf16[8,3,16,256]{3,2,1,0:T(8,128)(2,1)S(1)} all-to-all(bf16[8,3,16,256]{3,2,1,0:T(8,128)(2,1)S(1)} %bitcast.93), channel_id=1, replica_groups=mesh['x'=4,'zl'=2,'core'=2,'zh'=4,'y'=4] {'zh','zl'}, dimensions={0} | all-to-all | bytes 393216 | tf_op jit(solution)/shard_map/all_to_all | solution.py:77
  168.0 11.1 %all_to_all.11 = f32[8,3,16,256]{3,2,1,0:T(8,128)S(1)} all-to-all(f32[8,3,16,256]{3,2,1,0:T(8,128)S(1)} %broadcast_in_dim.30), channel_id=1, replica_groups=mesh['x'=4,'zl'=2,'core'=2,'zh'=4,'y'=4] {'x','zl'}, dimensions={0} | all-to-all | bytes 786432 | tf_op jit(solution)/shard_map/all_to_all | solution.py:73
  179.1 12.5 %collective-permute-start.39 = (f32[8,3,16,256]{3,2,1,0:T(8,128)S(1)}, f32[8,3,16,256]{3,2,1,0:T(8,128)S(1)}, u32[]{:S(2)}, u32[]{:S(2)}) collective-permute-start(f32[8,3,16,256]{3,2,1,0:T(8,128)S(1)} %all_to_all.11), channel_id=1, source_target_pairs={{0,16},{16,0},{1,17},{17,1},{2,18},{18,2},{3,19},{19,3},{4,20},{20... | collective-permute-start | bytes 1179656 | tf_op jit(solution)/shard_map/ppermute | solution.py:22
  191.6 1.3 collective-permute-done.39
  193.2 0.9 copy.15
  194.1 0.7 copy.16
  (119 shorter events, 6.9 us)
Async XLA Ops:
  1.5 22.2 %copy-start.18 = (bf16[2,2,192,512]{3,2,1,0:T(8,128)(2,1)S(1)}, bf16[2,2,192,512]{3,2,1,0:T(8,128)(2,1)}, u32[]{:S(2)}) copy-start(bf16[2,2,192,512]{3,2,1,0:T(8,128)(2,1)} %param.4) | copy-start | bytes 2359300
  1.5 11.6 %collective-permute-start = (bf16[3,32,256]{2,1,0:T(8,128)(2,1)S(1)}, bf16[3,32,256]{2,1,0:T(8,128)(2,1)S(1)}, u32[]{:S(2)}, u32[]{:S(2)}) collective-permute-start(bf16[3,32,256]{2,1,0:T(8,128)(2,1)S(1)} %fusion.10), channel_id=1, source_target_pairs={{0,12},{4,8},{8,4},{12,0},{1,13},{5,9},{9,5},{13,1},{2,14},{6,10},... | collective-permute-start | bytes 147464 | tf_op jit(solution)/shard_map/ppermute | solution.py:341
  8.4 7.3 %collective-permute-start.1 = (bf16[3,32,256]{2,1,0:T(8,128)(2,1)S(1)}, bf16[3,32,256]{2,1,0:T(8,128)(2,1)S(1)}, u32[]{:S(2)}, u32[]{:S(2)}) collective-permute-start(bf16[3,32,256]{2,1,0:T(8,128)(2,1)S(1)} %fusion.10), channel_id=1, source_target_pairs={{0,8},{4,12},{8,0},{12,4},{1,9},{5,13},{9,1},{13,5},{2,10},{6,14},... | collective-permute-start | bytes 147464 | tf_op jit(solution)/shard_map/ppermute | solution.py:341
  9.4 6.3 %collective-permute-start.2 = (bf16[3,32,256]{2,1,0:T(8,128)(2,1)S(1)}, bf16[3,32,256]{2,1,0:T(8,128)(2,1)S(1)}, u32[]{:S(2)}, u32[]{:S(2)}) collective-permute-start(bf16[3,32,256]{2,1,0:T(8,128)(2,1)S(1)} %fusion.10), channel_id=1, source_target_pairs={{0,4},{4,0},{8,12},{12,8},{1,5},{5,1},{9,13},{13,9},{2,6},{6,2},{1... | collective-permute-start | bytes 147464 | tf_op jit(solution)/shard_map/ppermute | solution.py:341
  11.8 22.8 %collective-permute-start.14 = (bf16[1,2,192,512]{3,2,1,0:T(8,128)(2,1)S(1)}, bf16[1,2,192,512]{3,2,1,0:T(8,128)(2,1)S(1)}, u32[]{:S(2)}, u32[]{:S(2)}) collective-permute-start(bf16[1,2,192,512]{3,2,1,0:T(8,128)(2,1)S(1)} %get-tuple-element.96), channel_id=1, source_target_pairs={{16,0},{32,16},{48,32},{64,48},{80,64},{96,80},{112,96},{128,112},... | collective-permute-start | bytes 1179656 | tf_op jit(solution)/shard_map/ppermute | solution.py:86
  15.8 5.4 %collective-permute-start.6 = (bf16[2,3,32,256]{3,2,1,0:T(8,128)(2,1)S(1)}, bf16[2,3,32,256]{3,2,1,0:T(8,128)(2,1)S(1)}, u32[]{:S(2)}, u32[]{:S(2)}) collective-permute-start(bf16[2,3,32,256]{3,2,1,0:T(8,128)(2,1)S(1)} %get-tuple-element.104), channel_id=1, source_target_pairs={{0,64},{64,0},{128,192},{192,128},{16,208},{80,144},{144,80},{208,... | collective-permute-start | bytes 294920 | tf_op jit(solution)/shard_map/ppermute | solution.py:35
  18.4 4.8 %collective-permute-start.3 = (bf16[2,3,32,256]{3,2,1,0:T(8,128)(2,1)S(1)}, bf16[2,3,32,256]{3,2,1,0:T(8,128)(2,1)S(1)}, u32[]{:S(2)}, u32[]{:S(2)}) collective-permute-start(bf16[2,3,32,256]{3,2,1,0:T(8,128)(2,1)S(1)} %get-tuple-element.106), channel_id=1, source_target_pairs={{0,1},{1,0},{2,3},{3,2},{16,19},{17,18},{18,17},{19,16},{4,5},{5,4... | collective-permute-start | bytes 294920 | tf_op jit(solution)/shard_map/ppermute | solution.py:35
  21.2 7.6 %collective-permute-start.7 = (bf16[2,2,3,32,256]{4,3,2,1,0:T(8,128)(2,1)S(1)}, bf16[2,2,3,32,256]{4,3,2,1,0:T(8,128)(2,1)}, u32[]{:S(2)}, u32[]{:S(2)}) collective-permute-start(bf16[2,2,3,32,256]{4,3,2,1,0:T(8,128)(2,1)S(1)} %pad_maximum_fusion.7), channel_id=1, source_target_pairs={{0,192},{64,128},{128,64},{192,0},{16,80},{80,16},{144,208},{208,1... | collective-permute-start | bytes 589832 | tf_op jit(solution)/shard_map/ppermute | solution.py:35
  23.2 10.4 %collective-permute-start.4 = (bf16[2,2,3,32,256]{4,3,2,1,0:T(8,128)(2,1)S(1)}, bf16[2,2,3,32,256]{4,3,2,1,0:T(8,128)(2,1)S(1)}, u32[]{:S(2)}, u32[]{:S(2)}) collective-permute-start(bf16[2,2,3,32,256]{4,3,2,1,0:T(8,128)(2,1)S(1)} %pad_maximum_fusion.6), channel_id=1, source_target_pairs={{0,3},{1,2},{2,1},{3,0},{16,17},{17,16},{18,19},{19,18},{4,7},{5,6... | collective-permute-start | bytes 589832 | tf_op jit(solution)/shard_map/ppermute | solution.py:35
  24.6 15.6 %collective-permute-start.12 = (bf16[2,1,192,512]{3,2,1,0:T(8,128)(2,1)}, bf16[2,1,192,512]{3,2,1,0:T(8,128)(2,1)}, u32[]{:S(2)}, u32[]{:S(2)}) collective-permute-start(bf16[2,1,192,512]{3,2,1,0:T(8,128)(2,1)} %get-tuple-element.98), channel_id=1, source_target_pairs={{1,0},{2,1},{3,2},{4,3},{5,4},{6,5},{7,6},{8,7},{9,8},{10,9},{11,1... | collective-permute-start | bytes 1179656 | tf_op jit(solution)/shard_map/ppermute | solution.py:86
  28.8 22.7 %collective-permute-start.11 = (bf16[2,1,192,512]{3,2,1,0:T(8,128)(2,1)}, bf16[2,1,192,512]{3,2,1,0:T(8,128)(2,1)}, u32[]{:S(2)}, u32[]{:S(2)}) collective-permute-start(bf16[2,1,192,512]{3,2,1,0:T(8,128)(2,1)} %get-tuple-element.97), channel_id=1, source_target_pairs={{0,1},{1,2},{2,3},{3,4},{4,5},{5,6},{6,7},{7,8},{8,9},{9,10},{10,1... | collective-permute-start | bytes 1179656 | tf_op jit(solution)/shard_map/ppermute | solution.py:85
  28.8 9.9 %copy-start.4 = (bf16[2,2,192,512]{3,2,1,0:T(8,128)(2,1)S(1)}, bf16[2,2,192,512]{3,2,1,0:T(8,128)(2,1)}, u32[]{:S(2)}) copy-start(bf16[2,2,192,512]{3,2,1,0:T(8,128)(2,1)} %param.5) | copy-start | bytes 2359300
  28.9 8.5 %collective-permute-start.13 = (bf16[1,2,192,512]{3,2,1,0:T(8,128)(2,1)S(1)}, bf16[1,2,192,512]{3,2,1,0:T(8,128)(2,1)S(1)}, u32[]{:S(2)}, u32[]{:S(2)}) collective-permute-start(bf16[1,2,192,512]{3,2,1,0:T(8,128)(2,1)S(1)} %get-tuple-element.95), channel_id=1, source_target_pairs={{0,16},{16,32},{32,48},{48,64},{64,80},{80,96},{96,112},{112,128},... | collective-permute-start | bytes 1179656 | tf_op jit(solution)/shard_map/ppermute | solution.py:85
  33.6 22.4 %collective-permute-start.10 = (bf16[4,2,3,32,256]{4,3,2,1,0:T(8,128)(2,1)S(1)}, bf16[4,2,3,32,256]{4,3,2,1,0:T(8,128)(2,1)}, u32[]{:S(2)}, u32[]{:S(2)}) collective-permute-start(bf16[4,2,3,32,256]{4,3,2,1,0:T(8,128)(2,1)S(1)} %pad_maximum_fusion.5.refs_8_), channel_id=1, source_target_pairs={{0,3},{1,2},{2,1},{3,0},{16,17},{17,16},{18,19},{19,18},{4,7},{5,6... | collective-permute-start | bytes 1179656 | tf_op jit(solution)/shard_map/ppermute | solution.py:35
  34.5 21.5 %collective-permute-start.8 = (bf16[4,2,3,32,256]{4,3,2,1,0:T(8,128)(2,1)S(1)}, bf16[4,2,3,32,256]{4,3,2,1,0:T(8,128)(2,1)}, u32[]{:S(2)}, u32[]{:S(2)}) collective-permute-start(bf16[4,2,3,32,256]{4,3,2,1,0:T(8,128)(2,1)S(1)} %pad_maximum_fusion.5.refs_8_), channel_id=1, source_target_pairs={{0,1},{1,0},{2,3},{3,2},{16,19},{17,18},{18,17},{19,16},{4,5},{5,4... | collective-permute-start | bytes 1179656 | tf_op jit(solution)/shard_map/ppermute | solution.py:35
  37.4 18.6 %collective-permute-start.5 = (bf16[4,2,3,32,256]{4,3,2,1,0:T(8,128)(2,1)}, bf16[4,2,3,32,256]{4,3,2,1,0:T(8,128)(2,1)}, u32[]{:S(2)}, u32[]{:S(2)}) collective-permute-start(bf16[4,2,3,32,256]{4,3,2,1,0:T(8,128)(2,1)} %pad_maximum_fusion.4.refs_4_), channel_id=1, source_target_pairs={{0,64},{64,0},{128,192},{192,128},{16,208},{80,144},{144,80},{208,... | collective-permute-start | bytes 1179656 | tf_op jit(solution)/shard_map/ppermute | solution.py:35
  39.0 1.2 copy-start.6
  40.2 11.4 %copy-start.19 = (bf16[2,2,192,512]{3,2,1,0:T(8,128)(2,1)S(1)}, bf16[2,2,192,512]{3,2,1,0:T(8,128)(2,1)}, u32[]{:S(2)}) copy-start(bf16[2,2,192,512]{3,2,1,0:T(8,128)(2,1)} %param.4) | copy-start | bytes 2359300
  40.2 15.9 %collective-permute-start.9 = (bf16[4,2,3,32,256]{4,3,2,1,0:T(8,128)(2,1)}, bf16[4,2,3,32,256]{4,3,2,1,0:T(8,128)(2,1)S(1)}, u32[]{:S(2)}, u32[]{:S(2)}) collective-permute-start(bf16[4,2,3,32,256]{4,3,2,1,0:T(8,128)(2,1)} %pad_maximum_fusion.4.refs_4_), channel_id=1, source_target_pairs={{0,192},{64,128},{128,64},{192,0},{16,80},{80,16},{144,208},{208,1... | collective-permute-start | bytes 1179656 | tf_op jit(solution)/shard_map/ppermute | solution.py:35
  56.0 33.4 %collective-permute-start.15 = (bf16[512,1536]{1,0:T(8,128)(2,1)S(1)}, bf16[512,1536]{1,0:T(8,128)(2,1)}, u32[]{:S(2)}, u32[]{:S(2)}) collective-permute-start(bf16[512,1536]{1,0:T(8,128)(2,1)S(1)} %bitcast.77), channel_id=1, source_target_pairs={{0,16},{16,0},{1,17},{17,1},{2,18},{18,2},{3,19},{19,3},{4,20},{20... | collective-permute-start | bytes 4718600 | tf_op jit(solution)/shard_map/ppermute | solution.py:22
  64.8 4.0 %collective-permute-start.21 = (bf16[4,2,3,32,256]{4,3,2,1,0:T(8,128)(2,1)S(1)}, bf16[4,2,3,32,256]{4,3,2,1,0:T(8,128)(2,1)S(1)}, u32[]{:S(2)}, u32[]{:S(2)}) collective-permute-start(bf16[4,2,3,32,256]{4,3,2,1,0:T(8,128)(2,1)S(1)} %pad_maximum_fusion.5.refs_8_), channel_id=1, source_target_pairs={{0,16},{16,0},{1,17},{17,1},{2,18},{18,2},{3,19},{19,3},{4,20},{20... | collective-permute-start | bytes 1179656 | tf_op jit(solution)/shard_map/ppermute | solution.py:22
  64.8 4.9 %collective-permute-start.16 = (bf16[4,2,3,32,256]{4,3,2,1,0:T(8,128)(2,1)}, bf16[4,2,3,32,256]{4,3,2,1,0:T(8,128)(2,1)S(1)}, u32[]{:S(2)}, u32[]{:S(2)}) collective-permute-start(bf16[4,2,3,32,256]{4,3,2,1,0:T(8,128)(2,1)} %pad_maximum_fusion.4.refs_4_), channel_id=1, source_target_pairs={{0,16},{16,0},{1,17},{17,1},{2,18},{18,2},{3,19},{19,3},{4,20},{20... | collective-permute-start | bytes 1179656 | tf_op jit(solution)/shard_map/ppermute | solution.py:22
  65.3 7.2 %collective-permute-start.19 = (bf16[4,2,3,32,256]{4,3,2,1,0:T(8,128)(2,1)}, bf16[4,2,3,32,256]{4,3,2,1,0:T(8,128)(2,1)}, u32[]{:S(2)}, u32[]{:S(2)}) collective-permute-start(bf16[4,2,3,32,256]{4,3,2,1,0:T(8,128)(2,1)} %collective-permute-done.5.refs_5_), channel_id=1, source_target_pairs={{0,192},{64,128},{128,64},{192,0},{16,80},{80,16},{144,208},{208,1... | collective-permute-start | bytes 1179656 | tf_op jit(solution)/shard_map/ppermute | solution.py:35
  65.3 9.3 %collective-permute-start.24 = (bf16[4,2,3,32,256]{4,3,2,1,0:T(8,128)(2,1)}, bf16[4,2,3,32,256]{4,3,2,1,0:T(8,128)(2,1)}, u32[]{:S(2)}, u32[]{:S(2)}) collective-permute-start(bf16[4,2,3,32,256]{4,3,2,1,0:T(8,128)(2,1)} %collective-permute-done.8.refs_9_), channel_id=1, source_target_pairs={{0,3},{1,2},{2,1},{3,0},{16,17},{17,16},{18,19},{19,18},{4,7},{5,6... | collective-permute-start | bytes 1179656 | tf_op jit(solution)/shard_map/ppermute | solution.py:35
  68.8 0.8 copy-start.10
  69.6 5.8 %collective-permute-start.17 = (bf16[4,2,3,32,256]{4,3,2,1,0:T(8,128)(2,1)}, bf16[4,2,3,32,256]{4,3,2,1,0:T(8,128)(2,1)S(1)}, u32[]{:S(2)}, u32[]{:S(2)}) collective-permute-start(bf16[4,2,3,32,256]{4,3,2,1,0:T(8,128)(2,1)} %collective-permute-done.5.refs_5_), channel_id=1, source_target_pairs={{0,16},{16,0},{1,17},{17,1},{2,18},{18,2},{3,19},{19,3},{4,20},{20... | collective-permute-start | bytes 1179656 | tf_op jit(solution)/shard_map/ppermute | solution.py:22
  69.7 0.7 copy-start.12
  70.4 5.7 %collective-permute-start.18 = (bf16[4,2,3,32,256]{4,3,2,1,0:T(8,128)(2,1)S(1)}, bf16[4,2,3,32,256]{4,3,2,1,0:T(8,128)(2,1)S(1)}, u32[]{:S(2)}, u32[]{:S(2)}) collective-permute-start(bf16[4,2,3,32,256]{4,3,2,1,0:T(8,128)(2,1)S(1)} %collective-permute-done.9.refs_6_), channel_id=1, source_target_pairs={{0,16},{16,0},{1,17},{17,1},{2,18},{18,2},{3,19},{19,3},{4,20},{20... | collective-permute-start | bytes 1179656 | tf_op jit(solution)/shard_map/ppermute | solution.py:22
  70.8 0.8 copy-start.8
  72.5 5.1 %collective-permute-start.22 = (bf16[4,2,3,32,256]{4,3,2,1,0:T(8,128)(2,1)}, bf16[4,2,3,32,256]{4,3,2,1,0:T(8,128)(2,1)}, u32[]{:S(2)}, u32[]{:S(2)}) collective-permute-start(bf16[4,2,3,32,256]{4,3,2,1,0:T(8,128)(2,1)} %collective-permute-done.8.refs_9_), channel_id=1, source_target_pairs={{0,16},{16,0},{1,17},{17,1},{2,18},{18,2},{3,19},{19,3},{4,20},{20... | collective-permute-start | bytes 1179656 | tf_op jit(solution)/shard_map/ppermute | solution.py:22
  74.6 14.9 %collective-permute-start.23 = (bf16[4,2,3,32,256]{4,3,2,1,0:T(8,128)(2,1)}, bf16[4,2,3,32,256]{4,3,2,1,0:T(8,128)(2,1)}, u32[]{:S(2)}, u32[]{:S(2)}) collective-permute-start(bf16[4,2,3,32,256]{4,3,2,1,0:T(8,128)(2,1)} %collective-permute-done.10.refs_10_), channel_id=1, source_target_pairs={{0,16},{16,0},{1,17},{17,1},{2,18},{18,2},{3,19},{19,3},{4,20},{20... | collective-permute-start | bytes 1179656 | tf_op jit(solution)/shard_map/ppermute | solution.py:22
  75.4 0.8 copy-start.14
  76.1 13.3 %collective-permute-start.20 = (bf16[4,2,3,32,256]{4,3,2,1,0:T(8,128)(2,1)}, bf16[4,2,3,32,256]{4,3,2,1,0:T(8,128)(2,1)}, u32[]{:S(2)}, u32[]{:S(2)}) collective-permute-start(bf16[4,2,3,32,256]{4,3,2,1,0:T(8,128)(2,1)} %collective-permute-done.19.refs_7_), channel_id=1, source_target_pairs={{0,16},{16,0},{1,17},{17,1},{2,18},{18,2},{3,19},{19,3},{4,20},{20... | collective-permute-start | bytes 1179656 | tf_op jit(solution)/shard_map/ppermute | solution.py:22
  76.1 0.7 copy-start.16
  76.9 12.6 %collective-permute-start.25 = (bf16[4,2,3,32,256]{4,3,2,1,0:T(8,128)(2,1)}, bf16[4,2,3,32,256]{4,3,2,1,0:T(8,128)(2,1)}, u32[]{:S(2)}, u32[]{:S(2)}) collective-permute-start(bf16[4,2,3,32,256]{4,3,2,1,0:T(8,128)(2,1)} %collective-permute-done.24.refs_11_), channel_id=1, source_target_pairs={{0,16},{16,0},{1,17},{17,1},{2,18},{18,2},{3,19},{19,3},{4,20},{20... | collective-permute-start | bytes 1179656 | tf_op jit(solution)/shard_map/ppermute | solution.py:22
  77.6 21.2 %collective-permute-start.27 = (bf16[2,4,192,256]{3,2,1,0:T(8,128)(2,1)}, bf16[2,4,192,256]{3,2,1,0:T(8,128)(2,1)S(1)}, u32[]{:S(2)}, u32[]{:S(2)}) collective-permute-start(bf16[2,4,192,256]{3,2,1,0:T(8,128)(2,1)} %constant_dynamic-slice_fusion), channel_id=1, source_target_pairs={{0,16},{16,0},{1,17},{17,1},{2,18},{18,2},{3,19},{19,3},{4,20},{20... | collective-permute-start | bytes 2359304 | tf_op jit(solution)/shard_map/ppermute | solution.py:22
  77.7 1.4 copy-start
  79.1 1.4 copy-start.2
  80.5 1.4 copy-start.7
  81.9 1.0 copy-start.9
  82.9 6.6 %copy-start.11 = (bf16[4,2,3,32,256]{4,3,2,1,0:T(8,128)(2,1)S(1)}, bf16[4,2,3,32,256]{4,3,2,1,0:T(8,128)(2,1)}, u32[]{:S(2)}) copy-start(bf16[4,2,3,32,256]{4,3,2,1,0:T(8,128)(2,1)} %copy-done.10) | copy-start | bytes 1179652
  82.9 6.6 %copy-start.13 = (bf16[4,2,3,32,256]{4,3,2,1,0:T(8,128)(2,1)S(1)}, bf16[4,2,3,32,256]{4,3,2,1,0:T(8,128)(2,1)}, u32[]{:S(2)}) copy-start(bf16[4,2,3,32,256]{4,3,2,1,0:T(8,128)(2,1)} %copy-done.12) | copy-start | bytes 1179652
  82.9 6.6 %copy-start.15 = (bf16[4,2,3,32,256]{4,3,2,1,0:T(8,128)(2,1)S(1)}, bf16[4,2,3,32,256]{4,3,2,1,0:T(8,128)(2,1)}, u32[]{:S(2)}) copy-start(bf16[4,2,3,32,256]{4,3,2,1,0:T(8,128)(2,1)} %copy-done.14) | copy-start | bytes 1179652
  82.9 6.6 %copy-start.17 = (bf16[4,2,3,32,256]{4,3,2,1,0:T(8,128)(2,1)S(1)}, bf16[4,2,3,32,256]{4,3,2,1,0:T(8,128)(2,1)}, u32[]{:S(2)}) copy-start(bf16[4,2,3,32,256]{4,3,2,1,0:T(8,128)(2,1)} %copy-done.16) | copy-start | bytes 1179652
  98.0 7.1 %collective-permute-start.26 = (bf16[512,768]{1,0:T(8,128)(2,1)S(1)}, bf16[512,768]{1,0:T(8,128)(2,1)S(1)}, u32[]{:S(2)}, u32[]{:S(2)}) collective-permute-start(bf16[512,768]{1,0:T(8,128)(2,1)S(1)} %get-tuple-element.61.turned_ref), channel_id=1, source_target_pairs={{0,16},{16,0},{1,17},{17,1},{2,18},{18,2},{3,19},{19,3},{4,20},{20... | collective-permute-start | bytes 2359304 | tf_op jit(solution)/shard_map/ppermute | solution.py:22
  98.7 6.4 %collective-permute-start.28 = (bf16[2,384,256]{2,1,0:T(8,128)(2,1)S(1)}, bf16[2,384,256]{2,1,0:T(8,128)(2,1)S(1)}, u32[]{:S(2)}, u32[]{:S(2)}) collective-permute-start(bf16[2,384,256]{2,1,0:T(8,128)(2,1)S(1)} %get-tuple-element.66), channel_id=1, source_target_pairs={{0,16},{16,0},{1,17},{17,1},{2,18},{18,2},{3,19},{19,3},{4,20},{20... | collective-permute-start | bytes 1179656 | tf_op jit(solution)/shard_map/ppermute | solution.py:22
  99.2 5.9 %copy-start.1 = (bf16[2,4,192,512]{3,2,1,0:T(8,128)(2,1)S(1)}, bf16[2,4,192,512]{3,2,1,0:T(8,128)(2,1)}, u32[]{:S(2)}) copy-start(bf16[2,4,192,512]{3,2,1,0:T(8,128)(2,1)} %concatenate.60.refs_0_) | copy-start | bytes 4718596
  99.3 5.9 %copy-start.3 = (bf16[2,4,192,512]{3,2,1,0:T(8,128)(2,1)S(1)}, bf16[2,4,192,512]{3,2,1,0:T(8,128)(2,1)}, u32[]{:S(2)}) copy-start(bf16[2,4,192,512]{3,2,1,0:T(8,128)(2,1)} %concatenate.61.refs_2_) | copy-start | bytes 4718596
  99.4 17.5 %collective-permute-start.31 = (bf16[2,1,192,512]{3,2,1,0:T(8,128)(2,1)S(1)}, bf16[2,1,192,512]{3,2,1,0:T(8,128)(2,1)S(1)}, u32[]{:S(2)}, u32[]{:S(2)}) collective-permute-start(bf16[2,1,192,512]{3,2,1,0:T(8,128)(2,1)S(1)} %get-tuple-element.92), channel_id=1, source_target_pairs={{0,1},{1,2},{2,3},{3,4},{4,5},{5,6},{6,7},{7,8},{8,9},{9,10},{10,1... | collective-permute-start | bytes 1179656 | tf_op jit(solution)/shard_map/ppermute | solution.py:85
  99.5 22.1 %collective-permute-start.32 = (bf16[2,1,192,512]{3,2,1,0:T(8,128)(2,1)S(1)}, bf16[2,1,192,512]{3,2,1,0:T(8,128)(2,1)S(1)}, u32[]{:S(2)}, u32[]{:S(2)}) collective-permute-start(bf16[2,1,192,512]{3,2,1,0:T(8,128)(2,1)S(1)} %get-tuple-element.91), channel_id=1, source_target_pairs={{1,0},{2,1},{3,2},{4,3},{5,4},{6,5},{7,6},{8,7},{9,8},{10,9},{11,1... | collective-permute-start | bytes 1179656 | tf_op jit(solution)/shard_map/ppermute | solution.py:86
  109.9 17.8 %collective-permute-start.30 = (bf16[2,4,3,2,32,256]{5,4,3,2,1,0:T(8,128)(2,1)S(1)}, bf16[2,4,3,2,32,256]{5,4,3,2,1,0:T(8,128)(2,1)S(1)}, u32[]{:S(2)}, u32[]{:S(2)}) collective-permute-start(bf16[2,4,3,2,32,256]{5,4,3,2,1,0:T(8,128)(2,1)S(1)} %get-tuple-element.69), channel_id=1, source_target_pairs={{0,64},{64,0},{128,192},{192,128},{16,208},{80,144},{144,80},{208,... | collective-permute-start | bytes 2359304 | tf_op jit(solution)/shard_map/ppermute | solution.py:35
  116.8 15.0 %collective-permute-start.29 = (bf16[2,4,3,2,32,256]{5,4,3,2,1,0:T(8,128)(2,1)S(1)}, bf16[2,4,3,2,32,256]{5,4,3,2,1,0:T(8,128)(2,1)S(1)}, u32[]{:S(2)}, u32[]{:S(2)}) collective-permute-start(bf16[2,4,3,2,32,256]{5,4,3,2,1,0:T(8,128)(2,1)S(1)} %get-tuple-element.67), channel_id=1, source_target_pairs={{0,1},{1,0},{2,3},{3,2},{16,19},{17,18},{18,17},{19,16},{4,5},{5,4... | collective-permute-start | bytes 2359304 | tf_op jit(solution)/shard_map/ppermute | solution.py:35
  122.8 1.1 copy-start.5
  127.8 7.0 %collective-permute-start.33 = (bf16[4,3,2,32,256]{4,3,2,1,0:T(8,128)(2,1)S(1)}, bf16[4,3,2,32,256]{4,3,2,1,0:T(8,128)(2,1)S(1)}, u32[]{:S(2)}, u32[]{:S(2)}) collective-permute-start(bf16[4,3,2,32,256]{4,3,2,1,0:T(8,128)(2,1)S(1)} %fusion), channel_id=1, source_target_pairs={{0,192},{64,128},{128,64},{192,0},{16,80},{80,16},{144,208},{208,1... | collective-permute-start | bytes 1179656 | tf_op jit(solution)/shard_map/ppermute | solution.py:35
  131.9 6.7 %collective-permute-start.36 = (bf16[4,3,2,32,256]{4,3,2,1,0:T(8,128)(2,1)S(1)}, bf16[4,3,2,32,256]{4,3,2,1,0:T(8,128)(2,1)S(1)}, u32[]{:S(2)}, u32[]{:S(2)}) collective-permute-start(bf16[4,3,2,32,256]{4,3,2,1,0:T(8,128)(2,1)S(1)} %fusion.1), channel_id=1, source_target_pairs={{0,3},{1,2},{2,1},{3,0},{16,17},{17,16},{18,19},{19,18},{4,7},{5,6... | collective-permute-start | bytes 1179656 | tf_op jit(solution)/shard_map/ppermute | solution.py:35
  135.0 10.8 %collective-permute-start.34 = (f32[2,3,2,32,256]{4,3,2,1,0:T(8,128)S(1)}, f32[2,3,2,32,256]{4,3,2,1,0:T(8,128)S(1)}, u32[]{:S(2)}, u32[]{:S(2)}) collective-permute-start(f32[2,3,2,32,256]{4,3,2,1,0:T(8,128)S(1)} %get-tuple-element.82), channel_id=1, source_target_pairs={{0,1},{1,0},{2,3},{3,2},{16,19},{17,18},{18,17},{19,16},{4,5},{5,4... | collective-permute-start | bytes 1179656 | tf_op jit(solution)/shard_map/ppermute | solution.py:35
  138.7 8.9 %collective-permute-start.37 = (f32[2,3,2,32,256]{4,3,2,1,0:T(8,128)S(1)}, f32[2,3,2,32,256]{4,3,2,1,0:T(8,128)S(1)}, u32[]{:S(2)}, u32[]{:S(2)}) collective-permute-start(f32[2,3,2,32,256]{4,3,2,1,0:T(8,128)S(1)} %get-tuple-element.84), channel_id=1, source_target_pairs={{0,64},{64,0},{128,192},{192,128},{16,208},{80,144},{144,80},{208,... | collective-permute-start | bytes 1179656 | tf_op jit(solution)/shard_map/ppermute | solution.py:35
  145.9 4.6 %collective-permute-start.35 = (f32[3,2,32,256]{3,2,1,0:T(8,128)S(1)}, f32[3,2,32,256]{3,2,1,0:T(8,128)S(1)}, u32[]{:S(2)}, u32[]{:S(2)}) collective-permute-start(f32[3,2,32,256]{3,2,1,0:T(8,128)S(1)} %fusion.6), channel_id=1, source_target_pairs={{0,3},{1,2},{2,1},{3,0},{16,17},{17,16},{18,19},{19,18},{4,7},{5,6... | collective-permute-start | bytes 589832 | tf_op jit(solution)/shard_map/ppermute | solution.py:35
  147.7 8.0 %collective-permute-start.38 = (f32[3,2,32,256]{3,2,1,0:T(8,128)S(1)}, f32[3,2,32,256]{3,2,1,0:T(8,128)S(1)}, u32[]{:S(2)}, u32[]{:S(2)}) collective-permute-start(f32[3,2,32,256]{3,2,1,0:T(8,128)S(1)} %fusion.2), channel_id=1, source_target_pairs={{0,192},{64,128},{128,64},{192,0},{16,80},{80,16},{144,208},{208,1... | collective-permute-start | bytes 589832 | tf_op jit(solution)/shard_map/ppermute | solution.py:35
  179.1 13.8 %collective-permute-start.39 = (f32[8,3,16,256]{3,2,1,0:T(8,128)S(1)}, f32[8,3,16,256]{3,2,1,0:T(8,128)S(1)}, u32[]{:S(2)}, u32[]{:S(2)}) collective-permute-start(f32[8,3,16,256]{3,2,1,0:T(8,128)S(1)} %all_to_all.11), channel_id=1, source_target_pairs={{0,16},{16,0},{1,17},{17,1},{2,18},{18,2},{3,19},{19,3},{4,20},{20... | collective-permute-start | bytes 1179656 | tf_op jit(solution)/shard_map/ppermute | solution.py:22

commit v6 on v5

--- a/solution.py
+++ b/solution.py
@@ -111,9 +111,11 @@
     for slot in range(4):
         for t in range(4):
             x, y = info_ref[1 + slot], info_ref[5 + t]
-            copies.append((parts[slot].at[t], kernel_ref.at[x, pl.ds(0, 2), :, y]))
+            source = parts[slot // 2].at[slot % 2, t]
+            copies.append((source, kernel_ref.at[x, pl.ds(0, 2), :, y]))
             x, y = info_ref[1 + t], info_ref[5 + slot]
-            copies.append((parts[4 + slot].at[t], kernel_ref.at[x, pl.ds(2, 2), :, y]))
+            source = parts[2 + slot // 2].at[slot % 2, t]
+            copies.append((source, kernel_ref.at[x, pl.ds(2, 2), :, y]))
     copies = [
         pltpu.make_async_copy(source, target, sems.at[i])
         for i, (source, target) in enumerate(copies)
@@ -161,14 +163,19 @@
 
 
 def first_kernel(info_ref, *refs):
-    x_refs, cot_ref, parts, refs = refs[:3], refs[3], refs[4:12], refs[12:]
-    pre_ref, slope_ref, kernel_ref, sems = refs
+    x_refs, cot_ref, parts, refs = refs[:3], refs[3], refs[4:8], refs[8:]
+    pre_ref, slope_ref, kernel_ref, turned_ref, part_ref, sems = refs
     assemble(info_ref, parts, kernel_ref, sems)
     add_terms(info_ref[0], x_refs, cot_ref, kernel_ref, pre_ref, slope_ref, None)
+    block, chans = pre_ref.shape[1:]
+    for i in range(cot_ref.shape[0]):
+        turned_ref[:, i * block : (i + 1) * block] = cot_ref[i].reshape(block, chans).T
+    for f in range(part_ref.shape[0]):
+        part_ref[f] = x_refs[1][f, :, :, lanes(1 - info_ref[0], chans // 2)]
 
 
 def second_kernel(info_ref, *refs):
-    x_refs, cot_ref, parts, refs = refs[:3], refs[3], refs[4:12], refs[12:]
+    x_refs, cot_ref, parts, refs = refs[:3], refs[3], refs[4:8], refs[8:]
     start_ref, mine_ref, hid_mine_ref, hid_other_ref, slope_ref, turned_ref = refs[:6]
     kernel_ref, pre_ref, other_ref, work_ref, sems = refs[6:]
     assemble(info_ref, parts, kernel_ref, sems)
@@ -208,15 +215,18 @@
     hid = jax.ShapeDtypeStruct((frames, block, half), jnp.bfloat16)
     kernel = jax.ShapeDtypeStruct((4, 4, 3, 4) + parts[0].shape[-2:], parts[0].dtype)
     sems = pltpu.SemaphoreType.DMA((32,))
-    pre, mine, k_mine = pl.pallas_call(
+    turned = jax.ShapeDtypeStruct((chans, (frames + 2) * block), jnp.bfloat16)
+    x_half = jax.ShapeDtypeStruct(shifts[0].shape[:3] + (half,), jnp.bfloat16)
+    pre, mine, k_mine, cot_turned, x_other = pl.pallas_call(
         first_kernel,
-        out_shape=(full, part, kernel),
-        in_specs=[SMEM] + [VMEM] * 4 + [ANY] * 8,
-        out_specs=(VMEM,) * 3,
+        out_shape=(full, part, kernel, turned, x_half),
+        in_specs=[SMEM] + [VMEM] * 4 + [ANY] * 4,
+        out_specs=(VMEM,) * 5,
         scratch_shapes=[sems],
         compiler_params=PARAMS,
         cost_estimate=pl.CostEstimate(flops=3200000000, bytes_accessed=12000000, transcendentals=0),
     )(infos[0], *shifts, cot_pad, *parts)
+    cot_turned_pair, x_pair = swap(cot_turned), swap(x_other)
     results = pl.pallas_call(
         second_kernel,
         out_shape=(
@@ -226,7 +236,7 @@
             jax.ShapeDtypeStruct((chans, frames * block), jnp.bfloat16),
             kernel,
         ),
-        in_specs=[SMEM] + [VMEM] * 4 + [ANY] * 8 + [VMEM] * 2,
+        in_specs=[SMEM] + [VMEM] * 4 + [ANY] * 4 + [VMEM] * 2,
         out_specs=(VMEM,) * 5,
         scratch_shapes=[
             pltpu.VMEM(full.shape, jnp.float32),
@@ -237,7 +247,7 @@
         compiler_params=PARAMS,
         cost_estimate=pl.CostEstimate(flops=3200000000, bytes_accessed=15000000, transcendentals=0),
     )(infos[1], *shifts, cot_pad, *parts_other, pre, mine)
-    return k_mine, results
+    return k_mine, (cot_turned, cot_turned_pair, x_pair), results
 
 
 def weight_kernel(upper, info_ref, turned_ref, turned_pair_ref, *refs):
@@ -347,12 +357,10 @@
 def kernel_parts(unit, ready):
     lower = jnp.concatenate(ring_gather(unit[0], "y"))
     upper = jnp.concatenate(ring_gather(unit[1], "x"))
-    near = exchange(lower, "x", 0), exchange(upper, "y", 0)
-    second = exchange(lower, "x", 1), exchange(upper, "y", 1)
-    near, second, ready = lax.optimization_barrier((near, second, ready))
-    far = exchange(near[0], "x", 1), exchange(near[1], "y", 1)
-    parts = (lower, near[0], second[0], far[0], upper, near[1], second[1], far[1])
-    return parts, ready
+    lower, lower_rest = ring_gather(lower, "x")
+    upper, upper_rest = ring_gather(upper, "y")
+    rest, ready = lax.optimization_barrier(((lower_rest, upper_rest), ready))
+    return (lower, rest[0], upper, rest[1]), ready
 
 
 def per_device(activations, cotangent, spatial_kernel, temporal_kernel):
@@ -369,19 +377,12 @@
     unit = kernel_unit(spatial_kernel, temporal_kernel, half)
     edges = edges_of(activations, SPACE, 1), edges_of(cotangent, TM, 0)
     x_wide = widened(activations, edges[0], SPACE, 1)
-    x_other = lax.dynamic_slice_in_dim(x_wide, (1 - core[0]) * half, half, axis=3)
     shifts = column_shifts(x_wide)
     cot_pad = widened(cotangent, edges[1], TM, 0)
-    cot_turned = cot_pad.reshape((frames + 2) * rows * width, chans).T
-    ready = (shifts, cot_pad, cot_turned, x_other)
-    parts, ready = kernel_parts(unit, ready)
-    shifts, cot_pad, cot_turned, x_other = ready
+    parts, (shifts, cot_pad) = kernel_parts(unit, (shifts, cot_pad))
     parts_other = tuple(swap(part) for part in parts)
-    x_pair = swap(x_other)
-    cot_turned_pair = swap(cot_turned)
-    cot_turned_pair, parts_other = lax.optimization_barrier((cot_turned_pair, parts_other))
-
-    k_mine, results = forward(infos, shifts, cot_pad, parts, parts_other)
+    k_mine, swapped, results = forward(infos, shifts, cot_pad, parts, parts_other)
+    cot_turned, cot_turned_pair, x_pair = swapped
     hid_mine, hid_other, slope_pre, turned, k_other = results
     turned_pair, hid_pair = swap(turned), swap(hid_other)
     x_pair, _ = lax.optimization_barrier((x_pair, turned))

time: 195 us -> 197 us (1.010)
  starting transfers between devices: 72.2 us -> 59.9 us
  waiting for transfers between devices: 39.7 us -> 48.4 us
  Pallas kernels: 31.9 us -> 35.6 us
  blocking collectives: 23.2 us -> 20.6 us
  other arithmetic: 5.56 us -> 8.03 us
    ppermute x3, waiting for transfers between devices: 10.3 us -> 22 us  [edges_of(): lax.ppermute(lax.slice_in_dim(block, size - 1, size, axis=dim), axis, for...]
    ppermute x18 -> x16, waiting for transfers between devices: 17.1 us -> 25 us  [exchange(): return lax.ppermute(block, names, pairs)]
    ppermute x13 -> x9, starting transfers between devices: 26.4 us -> 18.7 us  [swap(): return lax.ppermute(block, 'core', PAIR)]
    ppermute x18 -> x16, starting transfers between devices: 21.6 us -> 16.2 us  [exchange(): return lax.ppermute(block, names, pairs)]
    ppermute x3, waiting for transfers between devices: 4.73 us -> 0.01 us  [edges_of(): high = lax.ppermute(lax.slice_in_dim(block, 0, 1, axis=dim), axis, backward)]
    ppermute x3, starting transfers between devices: 11.3 us -> 15.4 us  [edges_of(): high = lax.ppermute(lax.slice_in_dim(block, 0, 1, axis=dim), axis, backward)]
    ppermute x13 -> x9, waiting for transfers between devices: 4.89 us -> 1.37 us  [swap(): return lax.ppermute(block, 'core', PAIR)]
    ppermute x3, starting transfers between devices: 3.89 us -> 0.47 us  [edges_of(): lax.ppermute(lax.slice_in_dim(block, size - 1, size, axis=dim), axis, for...]
  transfers between devices with their start and end apart: 40 -> 34, of which waited for: 14 -> 13; matrix products, arithmetic and copies ran while one was open for 7% -> 7% of each run, Pallas kernels for 16% -> 18%
where the time goes in v6:
time: 197 us; the launch traced here: 196 us
  starting transfers between devices  59.9 us (30%)
  waiting for transfers between devices  48.4 us (25%)
  Pallas kernels  35.6 us (18%)
  local copies, waits for them, and re-layouts  22.5 us (11%)
  blocking collectives  20.6 us (10%)
  other arithmetic  8.03 us (4%)
    ppermute x16, waiting for transfers between devices, exchange(): return lax.ppermute(block, names, pairs)  25 us
    ppermute x3, waiting for transfers between devices, edges_of(): lax.ppermute(lax.slice_in_dim(block, size - 1, size, axis=dim), axis, for...  22 us
    ppermute x9, starting transfers between devices, swap(): return lax.ppermute(block, 'core', PAIR)  18.7 us
    ppermute x16, starting transfers between devices, exchange(): return lax.ppermute(block, names, pairs)  16.2 us
    ppermute x3, starting transfers between devices, edges_of(): high = lax.ppermute(lax.slice_in_dim(block, 0, 1, axis=dim), axis, backward)  15.4 us
    unnamed x30, local copies, waits for them, and re-layouts  13.5 us
    all_to_all x1, blocking collectives, scattered(): lax.all_to_all(block, axis, 0, 0, tiled=True).astype(jnp.float32)  11 us
    pallas_call x2, Pallas kernels, weight_terms(): pl.pallas_call(functools.partial(weight_kernel, upper), out_shape=(jax.Sh...  10.8 us
  transfers between devices with their start and end apart: 34, of which 13 were waited for; matrix products, arithmetic and copies ran while one was open for 7% of the time, Pallas kernels for 18%

profile of v6, /device:TPU:1, one launch (start us, length us, event | category | flops | bytes accessed | tf_op | source)
XLA Modules:
  0.0 196.3 jit_solution(9008435399205168035)
XLA Ops:
  0.6 0.8 fusion.10
  1.5 6.9 %collective-permute-start = (bf16[3,32,256]{2,1,0:T(8,128)(2,1)S(1)}, bf16[3,32,256]{2,1,0:T(8,128)(2,1)S(1)}, u32[]{:S(2)}, u32[]{:S(2)}) collective-permute-start(bf16[3,32,256]{2,1,0:T(8,128)(2,1)S(1)} %fusion.10), channel_id=1, source_target_pairs={{0,12},{4,8},{8,4},{12,0},{1,13},{5,9},{9,5},{13,1},{2,14},{6,10},... | collective-permute-start | bytes 147464 | tf_op jit(solution)/shard_map/ppermute | solution.py:351
  8.4 1.0 collective-permute-start.1
  9.4 1.2 collective-permute-start.2
  10.6 1.2 fusion.20
  11.8 6.0 %collective-permute-start.12 = (bf16[2,1,192,512]{3,2,1,0:T(8,128)(2,1)S(1)}, bf16[2,1,192,512]{3,2,1,0:T(8,128)(2,1)S(1)}, u32[]{:S(2)}, u32[]{:S(2)}) collective-permute-start(bf16[2,1,192,512]{3,2,1,0:T(8,128)(2,1)S(1)} %get-tuple-element.76), channel_id=1, source_target_pairs={{1,0},{2,1},{3,2},{4,3},{5,4},{6,5},{7,6},{8,7},{9,8},{10,9},{11,1... | collective-permute-start | bytes 1179656 | tf_op jit(solution)/shard_map/ppermute | solution.py:86
  17.8 2.6 %collective-permute-start.7 = (bf16[2,3,32,256]{3,2,1,0:T(8,128)(2,1)S(1)}, bf16[2,3,32,256]{3,2,1,0:T(8,128)(2,1)S(1)}, u32[]{:S(2)}, u32[]{:S(2)}) collective-permute-start(bf16[2,3,32,256]{3,2,1,0:T(8,128)(2,1)S(1)} %get-tuple-element.86), channel_id=1, source_target_pairs={{0,64},{64,0},{128,192},{192,128},{16,208},{80,144},{144,80},{208,... | collective-permute-start | bytes 294920 | tf_op jit(solution)/shard_map/ppermute | solution.py:35
  20.4 0.8 collective-permute-start.3
  21.2 1.4 collective-permute-done.7
  23.0 2.2 %collective-permute-done.3 = bf16[2,3,32,256]{3,2,1,0:T(8,128)(2,1)S(1)} collective-permute-done((bf16[2,3,32,256]{3,2,1,0:T(8,128)(2,1)S(1)}, bf16[2,3,32,256]{3,2,1,0:T(8,128)(2,1)S(1)}, u32[]{:S(2)}, u32[]{:S(2)}) %collective-permute-start.3) | collective-permute-done | bytes 98336 | tf_op jit(solution)/shard_map/ppermute | solution.py:35
  25.3 0.8 fusion.19
  26.2 3.7 %collective-permute-start.14 = (bf16[1,2,192,512]{3,2,1,0:T(8,128)(2,1)}, bf16[1,2,192,512]{3,2,1,0:T(8,128)(2,1)}, u32[]{:S(2)}, u32[]{:S(2)}) collective-permute-start(bf16[1,2,192,512]{3,2,1,0:T(8,128)(2,1)} %get-tuple-element.74), channel_id=1, source_target_pairs={{16,0},{32,16},{48,32},{64,48},{80,64},{96,80},{112,96},{128,112},... | collective-permute-start | bytes 1179656 | tf_op jit(solution)/shard_map/ppermute | solution.py:86
  30.4 3.5 %collective-permute-start.9 = (bf16[4,2,3,32,256]{4,3,2,1,0:T(8,128)(2,1)S(1)}, bf16[4,2,3,32,256]{4,3,2,1,0:T(8,128)(2,1)S(1)}, u32[]{:S(2)}, u32[]{:S(2)}) collective-permute-start(bf16[4,2,3,32,256]{4,3,2,1,0:T(8,128)(2,1)S(1)} %get-tuple-element.78), channel_id=1, source_target_pairs={{0,1},{1,0},{2,3},{3,2},{16,19},{17,18},{18,17},{19,16},{4,5},{5,4... | collective-permute-start | bytes 1179656 | tf_op jit(solution)/shard_map/ppermute | solution.py:35
  33.9 1.1 collective-permute-start.5
  35.1 22.0 %collective-permute-done.11 = bf16[2,1,192,512]{3,2,1,0:T(8,128)(2,1)S(1)} collective-permute-done((bf16[2,1,192,512]{3,2,1,0:T(8,128)(2,1)S(1)}, bf16[2,1,192,512]{3,2,1,0:T(8,128)(2,1)S(1)}, u32[]{:S(2)}, u32[]{:S(2)}) %collective-permute-start.11) | collective-permute-done | bytes 393248 | tf_op jit(solution)/shard_map/ppermute | solution.py:85
  57.3 1.0 pad_maximum_fusion.4.refs_6_
  58.3 1.0 pad_maximum_fusion.3.refs_4_
  59.3 1.8 collective-permute-start.6
  61.1 0.5 fusion.16
  62.0 1.3 concatenate.61.refs_2_
  63.2 1.1 broadcast_select_fusion
  64.3 1.0 broadcast_select_fusion.1
  65.4 2.0 %collective-permute-start.17 = (bf16[2,4,2,3,32,256]{5,4,3,2,1,0:T(8,128)(2,1)}, bf16[2,4,2,3,32,256]{5,4,3,2,1,0:T(8,128)(2,1)}, u32[]{:S(2)}, u32[]{:S(2)}) collective-permute-start(bf16[2,4,2,3,32,256]{5,4,3,2,1,0:T(8,128)(2,1)} %pad_maximum_fusion.4.refs_6_), channel_id=1, source_target_pairs={{0,16},{16,0},{1,17},{17,1},{2,18},{18,2},{3,19},{19,3},{4,20},{20... | collective-permute-start | bytes 2359304 | tf_op jit(solution)/shard_map/ppermute | solution.py:22
  67.4 1.4 pad_maximum_fusion.1.refs_3_
  68.8 0.9 collective-permute-done.10.refs_7_
  69.7 1.3 collective-permute-done.6.refs_5_
  71.1 4.2 %collective-permute-start.16 = (bf16[2,4,2,3,32,256]{5,4,3,2,1,0:T(8,128)(2,1)}, bf16[2,4,2,3,32,256]{5,4,3,2,1,0:T(8,128)(2,1)}, u32[]{:S(2)}, u32[]{:S(2)}) collective-permute-start(bf16[2,4,2,3,32,256]{5,4,3,2,1,0:T(8,128)(2,1)} %collective-permute-done.6.refs_5_), channel_id=1, source_target_pairs={{0,16},{16,0},{1,17},{17,1},{2,18},{18,2},{3,19},{19,3},{4,20},{20... | collective-permute-start | bytes 2359304 | tf_op jit(solution)/shard_map/ppermute | solution.py:22
  75.3 1.4 copy-done
  76.8 1.4 copy-done.8
  78.2 8.6 %shard_map.67 = (f32[2,384,512]{2,1,0:T(8,128)S(1)}, f32[2,384,256]{2,1,0:T(8,128)S(1)}, bf16[4,4,3,4,32,256]{5,4,3,2,1,0:T(8,128)(2,1)S(1)}, bf16[512,1536]{1,0:T(8,128)(2,1)}, bf16[2,4,192,256]{3,2,1,0:T(8,128)(2,1)}) custom-call(s32[9]{0:T(128)S(1)} %concatenate.63.info_ref, bf16[2,4,192,512]{3,2,1,0:T(8,128)(2,1)S(1)} %concatenate.60.refs_0_, ...), custom_call_target="tpu_custom_call" | custom-call | flops 3200000000 | bytes 12000000 | tf_op jit(solution)/shard_map/pallas_call | solution.py:220
  86.8 1.6 copy-done.6
  88.4 1.2 copy-done.10
  89.6 0.9 copy-done.12
  90.4 0.5 collective-permute-start.21
  91.1 1.4 copy-done.1
  92.5 1.4 copy-done.9
  93.9 1.4 copy-done.11
  95.3 1.1 copy-done.13
  96.4 8.7 %shard_map.68 = (bf16[2,384,256]{2,1,0:T(8,128)(2,1)S(1)}, bf16[2,384,256]{2,1,0:T(8,128)(2,1)S(1)}, bf16[2,384,512]{2,1,0:T(8,128)(2,1)S(1)}, bf16[512,768]{1,0...) custom-call(s32[9]{0:T(128)S(1)} %concatenate.55.info_ref, bf16[2,4,192,512]{3,2,1,0:T(8,128)(2,1)S(1)} %concatenate.60.refs_0_, ...), custom_call_target="tpu_custom_call" | custom-call | flops 3200000000 | bytes 15000000 | tf_op jit(solution)/shard_map/pallas_call | solution.py:230
  105.2 0.6 collective-permute-start.19
  105.9 1.7 fusion.18
  108.1 5.7 %collective-permute-start.26 = (bf16[2,1,192,512]{3,2,1,0:T(8,128)(2,1)S(1)}, bf16[2,1,192,512]{3,2,1,0:T(8,128)(2,1)S(1)}, u32[]{:S(2)}, u32[]{:S(2)}) collective-permute-start(bf16[2,1,192,512]{3,2,1,0:T(8,128)(2,1)S(1)} %get-tuple-element.69), channel_id=1, source_target_pairs={{1,0},{2,1},{3,2},{4,3},{5,4},{6,5},{7,6},{8,7},{9,8},{10,9},{11,1... | collective-permute-start | bytes 1179656 | tf_op jit(solution)/shard_map/ppermute | solution.py:86
  113.8 5.4 %shard_map.70 = (f32[4,4,3,2,32,256]{5,4,3,2,1,0:T(8,128)S(1)}, bf16[2,4,3,2,32,256]{5,4,3,2,1,0:T(8,128)(2,1)S(1)}) custom-call(s32[9]{0:T(128)S(1)} %pad_add_fusion.info_ref, bf16[512,768]{1,0:T(8,128)(2,1)S(1)} %get-tuple-element.39.turned_ref, bf16[512,768]{1,0:T(8,128)(2,1)S(1)} %collective-permute-done.19.turned_pair_ref, ...), custom_call_target="tpu_custom_call" | custom-call | flops 2400000000 | bytes 16000000 | tf_op jit(solution)/shard_map/pallas_call | solution.py:294
  119.2 2.3 %collective-permute-start.24 = (bf16[2,4,3,2,32,256]{5,4,3,2,1,0:T(8,128)(2,1)S(1)}, bf16[2,4,3,2,32,256]{5,4,3,2,1,0:T(8,128)(2,1)S(1)}, u32[]{:S(2)}, u32[]{:S(2)}) collective-permute-start(bf16[2,4,3,2,32,256]{5,4,3,2,1,0:T(8,128)(2,1)S(1)} %get-tuple-element.47), channel_id=1, source_target_pairs={{0,64},{64,0},{128,192},{192,128},{16,208},{80,144},{144,80},{208,... | collective-permute-start | bytes 2359304 | tf_op jit(solution)/shard_map/ppermute | solution.py:35
  121.5 5.4 %shard_map.69 = (f32[4,4,3,2,32,256]{5,4,3,2,1,0:T(8,128)S(1)}, bf16[2,4,3,2,32,256]{5,4,3,2,1,0:T(8,128)(2,1)S(1)}) custom-call(s32[9]{0:T(128)S(1)} %pad_add_fusion.info_ref, bf16[512,768]{1,0:T(8,128)(2,1)S(1)} %get-tuple-element.39.turned_ref, bf16[512,768]{1,0:T(8,128)(2,1)S(1)} %collective-permute-done.19.turned_pair_ref, ...), custom_call_target="tpu_custom_call" | custom-call | flops 2400000000 | bytes 16000000 | tf_op jit(solution)/shard_map/pallas_call | solution.py:294
  127.2 0.5 fusion.15
  128.3 1.3 copy-done.7
  129.9 3.8 %shard_map.71.refs_6_ = f32[2,384,512]{2,1,0:T(8,128)} custom-call(s32[1]{0:T(128)} %bitcast.info_ref, bf16[2,4,192,512]{3,2,1,0:T(8,128)(2,1)S(1)} %concatenate.67.refs_0_, bf16[2,4,192,512]{3,2,1,0:T(8,128)(2,1)S(1)} %pad_maximum_fusion.2.refs_1_, bf16[2,4,192,512]{3,2,1,0:T(8,128)(2,1)S(1)} %concatenate.68.refs_2_, bf16[2,384,512]{2,1,0:T(8,128)(2,1)S(1)} %bitcast.81, ...), custom_call_target="tpu_custom_call" | custom-call | flops 1800000000 | bytes 8000000 | tf_op jit(solution)/shard_map/pallas_call | solution.py:330
  133.9 3.8 %shard_map.72 = f32[2,384,512]{2,1,0:T(8,128)} custom-call(s32[1]{0:T(128)} %bitcast.info_ref, bf16[2,4,192,512]{3,2,1,0:T(8,128)(2,1)S(1)} %concatenate.67.refs_0_, bf16[2,4,192,512]{3,2,1,0:T(8,128)(2,1)S(1)} %pad_maximum_fusion.2.refs_1_, bf16[2,4,192,512]{3,2,1,0:T(8,128)(2,1)S(1)} %concatenate.68.refs_2_, ...), custom_call_target="tpu_custom_call", output_to_operand_aliasing={{}: (7, {})} | custom-call | flops 1800000000 | bytes 8000000 | tf_op jit(solution)/shard_map/pallas_call | solution.py:330
  137.7 1.6 collective-permute-done.23
  139.5 1.3 collective-permute-done.27
  141.0 2.7 %collective-permute-start.28 = (f32[2,3,2,32,256]{4,3,2,1,0:T(8,128)S(1)}, f32[2,3,2,32,256]{4,3,2,1,0:T(8,128)S(1)}, u32[]{:S(2)}, u32[]{:S(2)}) collective-permute-start(f32[2,3,2,32,256]{4,3,2,1,0:T(8,128)S(1)} %get-tuple-element.60), channel_id=1, source_target_pairs={{0,1},{1,0},{2,3},{3,2},{16,19},{17,18},{18,17},{19,16},{4,5},{5,4... | collective-permute-start | bytes 1179656 | tf_op jit(solution)/shard_map/ppermute | solution.py:35
  143.8 3.6 %collective-permute-done.30 = bf16[4,3,2,32,256]{4,3,2,1,0:T(8,128)(2,1)S(1)} collective-permute-done((bf16[4,3,2,32,256]{4,3,2,1,0:T(8,128)(2,1)S(1)}, bf16[4,3,2,32,256]{4,3,2,1,0:T(8,128)(2,1)S(1)}, u32[]{:S(2)}, u32[]{:S(2)}) %collective-permute-start.30) | collective-permute-done | bytes 393248 | tf_op jit(solution)/shard_map/ppermute | solution.py:35
  147.7 4.1 %collective-permute-done.28 = f32[2,3,2,32,256]{4,3,2,1,0:T(8,128)S(1)} collective-permute-done((f32[2,3,2,32,256]{4,3,2,1,0:T(8,128)S(1)}, f32[2,3,2,32,256]{4,3,2,1,0:T(8,128)S(1)}, u32[]{:S(2)}, u32[]{:S(2)}) %collective-permute-start.28) | collective-permute-done | bytes 393248 | tf_op jit(solution)/shard_map/ppermute | solution.py:35
  151.8 0.5 collective-permute-start.29
  152.3 3.2 %collective-permute-done.31 = f32[2,3,2,32,256]{4,3,2,1,0:T(8,128)S(1)} collective-permute-done((f32[2,3,2,32,256]{4,3,2,1,0:T(8,128)S(1)}, f32[2,3,2,32,256]{4,3,2,1,0:T(8,128)S(1)}, u32[]{:S(2)}, u32[]{:S(2)}) %collective-permute-start.31) | collective-permute-done | bytes 393248 | tf_op jit(solution)/shard_map/ppermute | solution.py:35
  155.6 1.1 collective-permute-done.29
  156.8 4.3 %collective-permute-done.32 = f32[3,2,32,256]{3,2,1,0:T(8,128)S(1)} collective-permute-done((f32[3,2,32,256]{3,2,1,0:T(8,128)S(1)}, f32[3,2,32,256]{3,2,1,0:T(8,128)S(1)}, u32[]{:S(2)}, u32[]{:S(2)}) %collective-permute-start.32) | collective-permute-done | bytes 196640 | tf_op jit(solution)/shard_map/ppermute | solution.py:35
  161.1 11.0 %all_to_all.10 = bf16[8,3,16,256]{3,2,1,0:T(8,128)(2,1)S(1)} all-to-all(bf16[8,3,16,256]{3,2,1,0:T(8,128)(2,1)S(1)} %bitcast.93), channel_id=1, replica_groups=mesh['x'=4,'zl'=2,'core'=2,'zh'=4,'y'=4] {'zh','zl'}, dimensions={0} | all-to-all | bytes 393216 | tf_op jit(solution)/shard_map/all_to_all | solution.py:77
  172.2 9.6 %all_to_all.11 = f32[8,3,16,256]{3,2,1,0:T(8,128)S(1)} all-to-all(f32[8,3,16,256]{3,2,1,0:T(8,128)S(1)} %broadcast_in_dim.30), channel_id=1, replica_groups=mesh['x'=4,'zl'=2,'core'=2,'zh'=4,'y'=4] {'x','zl'}, dimensions={0} | all-to-all | bytes 786432 | tf_op jit(solution)/shard_map/all_to_all | solution.py:73
  181.8 11.3 %collective-permute-start.33 = (f32[8,3,16,256]{3,2,1,0:T(8,128)S(1)}, f32[8,3,16,256]{3,2,1,0:T(8,128)S(1)}, u32[]{:S(2)}, u32[]{:S(2)}) collective-permute-start(f32[8,3,16,256]{3,2,1,0:T(8,128)S(1)} %all_to_all.11), channel_id=1, source_target_pairs={{0,16},{16,0},{1,17},{17,1},{2,18},{18,2},{3,19},{19,3},{4,20},{20... | collective-permute-start | bytes 1179656 | tf_op jit(solution)/shard_map/ppermute | solution.py:22
  193.1 1.3 collective-permute-done.33
  194.7 0.9 copy.11
  195.6 0.7 copy.12
  (96 shorter events, 5.2 us)
Async XLA Ops:
  1.5 23.9 %copy-start.3 = (bf16[2,2,192,512]{3,2,1,0:T(8,128)(2,1)S(1)}, bf16[2,2,192,512]{3,2,1,0:T(8,128)(2,1)}, u32[]{:S(2)}) copy-start(bf16[2,2,192,512]{3,2,1,0:T(8,128)(2,1)} %param.5) | copy-start | bytes 2359300
  1.5 16.3 %collective-permute-start = (bf16[3,32,256]{2,1,0:T(8,128)(2,1)S(1)}, bf16[3,32,256]{2,1,0:T(8,128)(2,1)S(1)}, u32[]{:S(2)}, u32[]{:S(2)}) collective-permute-start(bf16[3,32,256]{2,1,0:T(8,128)(2,1)S(1)} %fusion.10), channel_id=1, source_target_pairs={{0,12},{4,8},{8,4},{12,0},{1,13},{5,9},{9,5},{13,1},{2,14},{6,10},... | collective-permute-start | bytes 147464 | tf_op jit(solution)/shard_map/ppermute | solution.py:351
  8.4 9.4 %collective-permute-start.1 = (bf16[3,32,256]{2,1,0:T(8,128)(2,1)S(1)}, bf16[3,32,256]{2,1,0:T(8,128)(2,1)S(1)}, u32[]{:S(2)}, u32[]{:S(2)}) collective-permute-start(bf16[3,32,256]{2,1,0:T(8,128)(2,1)S(1)} %fusion.10), channel_id=1, source_target_pairs={{0,8},{4,12},{8,0},{12,4},{1,9},{5,13},{9,1},{13,5},{2,10},{6,14},... | collective-permute-start | bytes 147464 | tf_op jit(solution)/shard_map/ppermute | solution.py:351
  9.4 8.4 %collective-permute-start.2 = (bf16[3,32,256]{2,1,0:T(8,128)(2,1)S(1)}, bf16[3,32,256]{2,1,0:T(8,128)(2,1)S(1)}, u32[]{:S(2)}, u32[]{:S(2)}) collective-permute-start(bf16[3,32,256]{2,1,0:T(8,128)(2,1)S(1)} %fusion.10), channel_id=1, source_target_pairs={{0,4},{4,0},{8,12},{12,8},{1,5},{5,1},{9,13},{13,9},{2,6},{6,2},{1... | collective-permute-start | bytes 147464 | tf_op jit(solution)/shard_map/ppermute | solution.py:351
  11.8 22.2 %collective-permute-start.12 = (bf16[2,1,192,512]{3,2,1,0:T(8,128)(2,1)S(1)}, bf16[2,1,192,512]{3,2,1,0:T(8,128)(2,1)S(1)}, u32[]{:S(2)}, u32[]{:S(2)}) collective-permute-start(bf16[2,1,192,512]{3,2,1,0:T(8,128)(2,1)S(1)} %get-tuple-element.76), channel_id=1, source_target_pairs={{1,0},{2,1},{3,2},{4,3},{5,4},{6,5},{7,6},{8,7},{9,8},{10,9},{11,1... | collective-permute-start | bytes 1179656 | tf_op jit(solution)/shard_map/ppermute | solution.py:86
  17.8 4.8 %collective-permute-start.7 = (bf16[2,3,32,256]{3,2,1,0:T(8,128)(2,1)S(1)}, bf16[2,3,32,256]{3,2,1,0:T(8,128)(2,1)S(1)}, u32[]{:S(2)}, u32[]{:S(2)}) collective-permute-start(bf16[2,3,32,256]{3,2,1,0:T(8,128)(2,1)S(1)} %get-tuple-element.86), channel_id=1, source_target_pairs={{0,64},{64,0},{128,192},{192,128},{16,208},{80,144},{144,80},{208,... | collective-permute-start | bytes 294920 | tf_op jit(solution)/shard_map/ppermute | solution.py:35
  20.4 4.8 %collective-permute-start.3 = (bf16[2,3,32,256]{3,2,1,0:T(8,128)(2,1)S(1)}, bf16[2,3,32,256]{3,2,1,0:T(8,128)(2,1)S(1)}, u32[]{:S(2)}, u32[]{:S(2)}) collective-permute-start(bf16[2,3,32,256]{3,2,1,0:T(8,128)(2,1)S(1)} %get-tuple-element.88), channel_id=1, source_target_pairs={{0,1},{1,0},{2,3},{3,2},{16,19},{17,18},{18,17},{19,16},{4,5},{5,4... | collective-permute-start | bytes 294920 | tf_op jit(solution)/shard_map/ppermute | solution.py:35
  22.6 7.6 %collective-permute-start.8 = (bf16[2,2,3,32,256]{4,3,2,1,0:T(8,128)(2,1)S(1)}, bf16[2,2,3,32,256]{4,3,2,1,0:T(8,128)(2,1)S(1)}, u32[]{:S(2)}, u32[]{:S(2)}) collective-permute-start(bf16[2,2,3,32,256]{4,3,2,1,0:T(8,128)(2,1)S(1)} %pad_maximum_fusion.9), channel_id=1, source_target_pairs={{0,192},{64,128},{128,64},{192,0},{16,80},{80,16},{144,208},{208,1... | collective-permute-start | bytes 589832 | tf_op jit(solution)/shard_map/ppermute | solution.py:35
  25.2 5.1 %collective-permute-start.4 = (bf16[2,2,3,32,256]{4,3,2,1,0:T(8,128)(2,1)S(1)}, bf16[2,2,3,32,256]{4,3,2,1,0:T(8,128)(2,1)S(1)}, u32[]{:S(2)}, u32[]{:S(2)}) collective-permute-start(bf16[2,2,3,32,256]{4,3,2,1,0:T(8,128)(2,1)S(1)} %pad_maximum_fusion.8), channel_id=1, source_target_pairs={{0,3},{1,2},{2,1},{3,0},{16,17},{17,16},{18,19},{19,18},{4,7},{5,6... | collective-permute-start | bytes 589832 | tf_op jit(solution)/shard_map/ppermute | solution.py:35
  26.2 37.1 %collective-permute-start.14 = (bf16[1,2,192,512]{3,2,1,0:T(8,128)(2,1)}, bf16[1,2,192,512]{3,2,1,0:T(8,128)(2,1)}, u32[]{:S(2)}, u32[]{:S(2)}) collective-permute-start(bf16[1,2,192,512]{3,2,1,0:T(8,128)(2,1)} %get-tuple-element.74), channel_id=1, source_target_pairs={{16,0},{32,16},{48,32},{64,48},{80,64},{96,80},{112,96},{128,112},... | collective-permute-start | bytes 1179656 | tf_op jit(solution)/shard_map/ppermute | solution.py:86
  29.9 34.4 %collective-permute-start.13 = (bf16[1,2,192,512]{3,2,1,0:T(8,128)(2,1)S(1)}, bf16[1,2,192,512]{3,2,1,0:T(8,128)(2,1)}, u32[]{:S(2)}, u32[]{:S(2)}) collective-permute-start(bf16[1,2,192,512]{3,2,1,0:T(8,128)(2,1)S(1)} %get-tuple-element.73), channel_id=1, source_target_pairs={{0,16},{16,32},{32,48},{48,64},{64,80},{80,96},{96,112},{112,128},... | collective-permute-start | bytes 1179656 | tf_op jit(solution)/shard_map/ppermute | solution.py:85
  30.3 26.8 %collective-permute-start.11 = (bf16[2,1,192,512]{3,2,1,0:T(8,128)(2,1)S(1)}, bf16[2,1,192,512]{3,2,1,0:T(8,128)(2,1)S(1)}, u32[]{:S(2)}, u32[]{:S(2)}) collective-permute-start(bf16[2,1,192,512]{3,2,1,0:T(8,128)(2,1)S(1)} %get-tuple-element.75), channel_id=1, source_target_pairs={{0,1},{1,2},{2,3},{3,4},{4,5},{5,6},{6,7},{7,8},{8,9},{9,10},{10,1... | collective-permute-start | bytes 1179656 | tf_op jit(solution)/shard_map/ppermute | solution.py:85
  30.3 26.8 %copy-start.14 = (bf16[2,2,192,512]{3,2,1,0:T(8,128)(2,1)S(1)}, bf16[2,2,192,512]{3,2,1,0:T(8,128)(2,1)}, u32[]{:S(2)}) copy-start(bf16[2,2,192,512]{3,2,1,0:T(8,128)(2,1)} %param.4) | copy-start | bytes 2359300
  30.4 27.0 %collective-permute-start.9 = (bf16[4,2,3,32,256]{4,3,2,1,0:T(8,128)(2,1)S(1)}, bf16[4,2,3,32,256]{4,3,2,1,0:T(8,128)(2,1)S(1)}, u32[]{:S(2)}, u32[]{:S(2)}) collective-permute-start(bf16[4,2,3,32,256]{4,3,2,1,0:T(8,128)(2,1)S(1)} %get-tuple-element.78), channel_id=1, source_target_pairs={{0,1},{1,0},{2,3},{3,2},{16,19},{17,18},{18,17},{19,16},{4,5},{5,4... | collective-permute-start | bytes 1179656 | tf_op jit(solution)/shard_map/ppermute | solution.py:35
  33.9 24.4 %collective-permute-start.5 = (bf16[4,2,3,32,256]{4,3,2,1,0:T(8,128)(2,1)S(1)}, bf16[4,2,3,32,256]{4,3,2,1,0:T(8,128)(2,1)S(1)}, u32[]{:S(2)}, u32[]{:S(2)}) collective-permute-start(bf16[4,2,3,32,256]{4,3,2,1,0:T(8,128)(2,1)S(1)} %get-tuple-element.80), channel_id=1, source_target_pairs={{0,64},{64,0},{128,192},{192,128},{16,208},{80,144},{144,80},{208,... | collective-permute-start | bytes 1179656 | tf_op jit(solution)/shard_map/ppermute | solution.py:35
  58.3 11.5 %collective-permute-start.10 = (bf16[2,4,2,3,32,256]{5,4,3,2,1,0:T(8,128)(2,1)}, bf16[2,4,2,3,32,256]{5,4,3,2,1,0:T(8,128)(2,1)}, u32[]{:S(2)}, u32[]{:S(2)}) collective-permute-start(bf16[2,4,2,3,32,256]{5,4,3,2,1,0:T(8,128)(2,1)} %pad_maximum_fusion.4.refs_6_), channel_id=1, source_target_pairs={{0,3},{1,2},{2,1},{3,0},{16,17},{17,16},{18,19},{19,18},{4,7},{5,6... | collective-permute-start | bytes 2359304 | tf_op jit(solution)/shard_map/ppermute | solution.py:35
  59.3 11.8 %collective-permute-start.6 = (bf16[2,4,2,3,32,256]{5,4,3,2,1,0:T(8,128)(2,1)}, bf16[2,4,2,3,32,256]{5,4,3,2,1,0:T(8,128)(2,1)}, u32[]{:S(2)}, u32[]{:S(2)}) collective-permute-start(bf16[2,4,2,3,32,256]{5,4,3,2,1,0:T(8,128)(2,1)} %pad_maximum_fusion.3.refs_4_), channel_id=1, source_target_pairs={{0,192},{64,128},{128,64},{192,0},{16,80},{80,16},{144,208},{208,1... | collective-permute-start | bytes 2359304 | tf_op jit(solution)/shard_map/ppermute | solution.py:35
  63.2 4.2 %copy-start.4 = (bf16[2,2,192,512]{3,2,1,0:T(8,128)(2,1)S(1)}, bf16[2,2,192,512]{3,2,1,0:T(8,128)(2,1)}, u32[]{:S(2)}) copy-start(bf16[2,2,192,512]{3,2,1,0:T(8,128)(2,1)} %param.5) | copy-start | bytes 2359300
  65.4 25.6 %collective-permute-start.17 = (bf16[2,4,2,3,32,256]{5,4,3,2,1,0:T(8,128)(2,1)}, bf16[2,4,2,3,32,256]{5,4,3,2,1,0:T(8,128)(2,1)}, u32[]{:S(2)}, u32[]{:S(2)}) collective-permute-start(bf16[2,4,2,3,32,256]{5,4,3,2,1,0:T(8,128)(2,1)} %pad_maximum_fusion.4.refs_6_), channel_id=1, source_target_pairs={{0,16},{16,0},{1,17},{17,1},{2,18},{18,2},{3,19},{19,3},{4,20},{20... | collective-permute-start | bytes 2359304 | tf_op jit(solution)/shard_map/ppermute | solution.py:22
  68.8 22.3 %collective-permute-start.15 = (bf16[2,4,2,3,32,256]{5,4,3,2,1,0:T(8,128)(2,1)}, bf16[2,4,2,3,32,256]{5,4,3,2,1,0:T(8,128)(2,1)}, u32[]{:S(2)}, u32[]{:S(2)}) collective-permute-start(bf16[2,4,2,3,32,256]{5,4,3,2,1,0:T(8,128)(2,1)} %pad_maximum_fusion.3.refs_4_), channel_id=1, source_target_pairs={{0,16},{16,0},{1,17},{17,1},{2,18},{18,2},{3,19},{19,3},{4,20},{20... | collective-permute-start | bytes 2359304 | tf_op jit(solution)/shard_map/ppermute | solution.py:22
  71.1 20.0 %collective-permute-start.16 = (bf16[2,4,2,3,32,256]{5,4,3,2,1,0:T(8,128)(2,1)}, bf16[2,4,2,3,32,256]{5,4,3,2,1,0:T(8,128)(2,1)}, u32[]{:S(2)}, u32[]{:S(2)}) collective-permute-start(bf16[2,4,2,3,32,256]{5,4,3,2,1,0:T(8,128)(2,1)} %collective-permute-done.6.refs_5_), channel_id=1, source_target_pairs={{0,16},{16,0},{1,17},{17,1},{2,18},{18,2},{3,19},{19,3},{4,20},{20... | collective-permute-start | bytes 2359304 | tf_op jit(solution)/shard_map/ppermute | solution.py:22
  75.3 15.8 %collective-permute-start.18 = (bf16[2,4,2,3,32,256]{5,4,3,2,1,0:T(8,128)(2,1)}, bf16[2,4,2,3,32,256]{5,4,3,2,1,0:T(8,128)(2,1)}, u32[]{:S(2)}, u32[]{:S(2)}) collective-permute-start(bf16[2,4,2,3,32,256]{5,4,3,2,1,0:T(8,128)(2,1)} %collective-permute-done.10.refs_7_), channel_id=1, source_target_pairs={{0,16},{16,0},{1,17},{17,1},{2,18},{18,2},{3,19},{19,3},{4,20},{20... | collective-permute-start | bytes 2359304 | tf_op jit(solution)/shard_map/ppermute | solution.py:22
  75.3 1.4 copy-start
  76.8 1.4 copy-start.8
  86.8 1.6 copy-start.6
  88.4 1.2 copy-start.10
  89.6 0.9 copy-start.12
  90.4 23.3 %collective-permute-start.21 = (bf16[512,1536]{1,0:T(8,128)(2,1)}, bf16[512,1536]{1,0:T(8,128)(2,1)}, u32[]{:S(2)}, u32[]{:S(2)}) collective-permute-start(bf16[512,1536]{1,0:T(8,128)(2,1)} %get-tuple-element.42.refs_6_), channel_id=1, source_target_pairs={{0,16},{16,0},{1,17},{17,1},{2,18},{18,2},{3,19},{19,3},{4,20},{20... | collective-permute-start | bytes 4718600 | tf_op jit(solution)/shard_map/ppermute | solution.py:22
  91.0 14.9 %collective-permute-start.20 = (bf16[2,4,192,256]{3,2,1,0:T(8,128)(2,1)}, bf16[2,4,192,256]{3,2,1,0:T(8,128)(2,1)}, u32[]{:S(2)}, u32[]{:S(2)}) collective-permute-start(bf16[2,4,192,256]{3,2,1,0:T(8,128)(2,1)} %get-tuple-element.40), channel_id=1, source_target_pairs={{0,16},{16,0},{1,17},{17,1},{2,18},{18,2},{3,19},{19,3},{4,20},{20... | collective-permute-start | bytes 2359304 | tf_op jit(solution)/shard_map/ppermute | solution.py:22
  91.1 1.4 copy-start.1
  92.5 1.4 copy-start.9
  93.9 1.4 copy-start.11
  95.3 1.1 copy-start.13
  105.2 8.6 %collective-permute-start.19 = (bf16[512,768]{1,0:T(8,128)(2,1)S(1)}, bf16[512,768]{1,0:T(8,128)(2,1)S(1)}, u32[]{:S(2)}, u32[]{:S(2)}) collective-permute-start(bf16[512,768]{1,0:T(8,128)(2,1)S(1)} %get-tuple-element.39.turned_ref), channel_id=1, source_target_pairs={{0,16},{16,0},{1,17},{17,1},{2,18},{18,2},{3,19},{19,3},{4,20},{20... | collective-permute-start | bytes 2359304 | tf_op jit(solution)/shard_map/ppermute | solution.py:22
  105.9 7.9 %collective-permute-start.22 = (bf16[2,384,256]{2,1,0:T(8,128)(2,1)S(1)}, bf16[2,384,256]{2,1,0:T(8,128)(2,1)S(1)}, u32[]{:S(2)}, u32[]{:S(2)}) collective-permute-start(bf16[2,384,256]{2,1,0:T(8,128)(2,1)S(1)} %get-tuple-element.44), channel_id=1, source_target_pairs={{0,16},{16,0},{1,17},{17,1},{2,18},{18,2},{3,19},{19,3},{4,20},{20... | collective-permute-start | bytes 1179656 | tf_op jit(solution)/shard_map/ppermute | solution.py:22
  107.9 5.9 %copy-start.2 = (bf16[2,4,192,512]{3,2,1,0:T(8,128)(2,1)S(1)}, bf16[2,4,192,512]{3,2,1,0:T(8,128)(2,1)}, u32[]{:S(2)}) copy-start(bf16[2,4,192,512]{3,2,1,0:T(8,128)(2,1)} %concatenate.61.refs_2_) | copy-start | bytes 4718596
  108.0 18.9 %collective-permute-start.25 = (bf16[2,1,192,512]{3,2,1,0:T(8,128)(2,1)S(1)}, bf16[2,1,192,512]{3,2,1,0:T(8,128)(2,1)S(1)}, u32[]{:S(2)}, u32[]{:S(2)}) collective-permute-start(bf16[2,1,192,512]{3,2,1,0:T(8,128)(2,1)S(1)} %get-tuple-element.70), channel_id=1, source_target_pairs={{0,1},{1,2},{2,3},{3,4},{4,5},{5,6},{6,7},{7,8},{8,9},{9,10},{10,1... | collective-permute-start | bytes 1179656 | tf_op jit(solution)/shard_map/ppermute | solution.py:85
  108.1 18.9 %collective-permute-start.26 = (bf16[2,1,192,512]{3,2,1,0:T(8,128)(2,1)S(1)}, bf16[2,1,192,512]{3,2,1,0:T(8,128)(2,1)S(1)}, u32[]{:S(2)}, u32[]{:S(2)}) collective-permute-start(bf16[2,1,192,512]{3,2,1,0:T(8,128)(2,1)S(1)} %get-tuple-element.69), channel_id=1, source_target_pairs={{1,0},{2,1},{3,2},{4,3},{5,4},{6,5},{7,6},{8,7},{9,8},{10,9},{11,1... | collective-permute-start | bytes 1179656 | tf_op jit(solution)/shard_map/ppermute | solution.py:86
  119.2 14.5 %collective-permute-start.24 = (bf16[2,4,3,2,32,256]{5,4,3,2,1,0:T(8,128)(2,1)S(1)}, bf16[2,4,3,2,32,256]{5,4,3,2,1,0:T(8,128)(2,1)S(1)}, u32[]{:S(2)}, u32[]{:S(2)}) collective-permute-start(bf16[2,4,3,2,32,256]{5,4,3,2,1,0:T(8,128)(2,1)S(1)} %get-tuple-element.47), channel_id=1, source_target_pairs={{0,64},{64,0},{128,192},{192,128},{16,208},{80,144},{144,80},{208,... | collective-permute-start | bytes 2359304 | tf_op jit(solution)/shard_map/ppermute | solution.py:35
  126.9 12.4 %collective-permute-start.23 = (bf16[2,4,3,2,32,256]{5,4,3,2,1,0:T(8,128)(2,1)S(1)}, bf16[2,4,3,2,32,256]{5,4,3,2,1,0:T(8,128)(2,1)S(1)}, u32[]{:S(2)}, u32[]{:S(2)}) collective-permute-start(bf16[2,4,3,2,32,256]{5,4,3,2,1,0:T(8,128)(2,1)S(1)} %get-tuple-element.45), channel_id=1, source_target_pairs={{0,1},{1,0},{2,3},{3,2},{16,19},{17,18},{18,17},{19,16},{4,5},{5,4... | collective-permute-start | bytes 2359304 | tf_op jit(solution)/shard_map/ppermute | solution.py:35
  127.7 1.9 copy-start.7
  128.2 1.8 copy-start.5
  133.8 7.0 %collective-permute-start.27 = (bf16[4,3,2,32,256]{4,3,2,1,0:T(8,128)(2,1)S(1)}, bf16[4,3,2,32,256]{4,3,2,1,0:T(8,128)(2,1)S(1)}, u32[]{:S(2)}, u32[]{:S(2)}) collective-permute-start(bf16[4,3,2,32,256]{4,3,2,1,0:T(8,128)(2,1)S(1)} %fusion), channel_id=1, source_target_pairs={{0,192},{64,128},{128,64},{192,0},{16,80},{80,16},{144,208},{208,1... | collective-permute-start | bytes 1179656 | tf_op jit(solution)/shard_map/ppermute | solution.py:35
  139.4 8.0 %collective-permute-start.30 = (bf16[4,3,2,32,256]{4,3,2,1,0:T(8,128)(2,1)S(1)}, bf16[4,3,2,32,256]{4,3,2,1,0:T(8,128)(2,1)S(1)}, u32[]{:S(2)}, u32[]{:S(2)}) collective-permute-start(bf16[4,3,2,32,256]{4,3,2,1,0:T(8,128)(2,1)S(1)} %fusion.1), channel_id=1, source_target_pairs={{0,3},{1,2},{2,1},{3,0},{16,17},{17,16},{18,19},{19,18},{4,7},{5,6... | collective-permute-start | bytes 1179656 | tf_op jit(solution)/shard_map/ppermute | solution.py:35
  141.0 10.8 %collective-permute-start.28 = (f32[2,3,2,32,256]{4,3,2,1,0:T(8,128)S(1)}, f32[2,3,2,32,256]{4,3,2,1,0:T(8,128)S(1)}, u32[]{:S(2)}, u32[]{:S(2)}) collective-permute-start(f32[2,3,2,32,256]{4,3,2,1,0:T(8,128)S(1)} %get-tuple-element.60), channel_id=1, source_target_pairs={{0,1},{1,0},{2,3},{3,2},{16,19},{17,18},{18,17},{19,16},{4,5},{5,4... | collective-permute-start | bytes 1179656 | tf_op jit(solution)/shard_map/ppermute | solution.py:35
  147.6 7.9 %collective-permute-start.31 = (f32[2,3,2,32,256]{4,3,2,1,0:T(8,128)S(1)}, f32[2,3,2,32,256]{4,3,2,1,0:T(8,128)S(1)}, u32[]{:S(2)}, u32[]{:S(2)}) collective-permute-start(f32[2,3,2,32,256]{4,3,2,1,0:T(8,128)S(1)} %get-tuple-element.62), channel_id=1, source_target_pairs={{0,64},{64,0},{128,192},{192,128},{16,208},{80,144},{144,80},{208,... | collective-permute-start | bytes 1179656 | tf_op jit(solution)/shard_map/ppermute | solution.py:35
  151.8 4.9 %collective-permute-start.29 = (f32[3,2,32,256]{3,2,1,0:T(8,128)S(1)}, f32[3,2,32,256]{3,2,1,0:T(8,128)S(1)}, u32[]{:S(2)}, u32[]{:S(2)}) collective-permute-start(f32[3,2,32,256]{3,2,1,0:T(8,128)S(1)} %fusion.6), channel_id=1, source_target_pairs={{0,3},{1,2},{2,1},{3,0},{16,17},{17,16},{18,19},{19,18},{4,7},{5,6... | collective-permute-start | bytes 589832 | tf_op jit(solution)/shard_map/ppermute | solution.py:35
  155.5 5.5 %collective-permute-start.32 = (f32[3,2,32,256]{3,2,1,0:T(8,128)S(1)}, f32[3,2,32,256]{3,2,1,0:T(8,128)S(1)}, u32[]{:S(2)}, u32[]{:S(2)}) collective-permute-start(f32[3,2,32,256]{3,2,1,0:T(8,128)S(1)} %fusion.2), channel_id=1, source_target_pairs={{0,192},{64,128},{128,64},{192,0},{16,80},{80,16},{144,208},{208,1... | collective-permute-start | bytes 589832 | tf_op jit(solution)/shard_map/ppermute | solution.py:35
  181.8 12.6 %collective-permute-start.33 = (f32[8,3,16,256]{3,2,1,0:T(8,128)S(1)}, f32[8,3,16,256]{3,2,1,0:T(8,128)S(1)}, u32[]{:S(2)}, u32[]{:S(2)}) collective-permute-start(f32[8,3,16,256]{3,2,1,0:T(8,128)S(1)} %all_to_all.11), channel_id=1, source_target_pairs={{0,16},{16,0},{1,17},{17,1},{2,18},{18,2},{3,19},{19,3},{4,20},{20... | collective-permute-start | bytes 1179656 | tf_op jit(solution)/shard_map/ppermute | solution.py:22

commit v7 on v4

--- a/solution.py
+++ b/solution.py
@@ -15,7 +15,7 @@
 VMEM = pl.BlockSpec(memory_space=pltpu.VMEM)
 ANY = pl.BlockSpec(memory_space=pl.ANY)
 SMEM = pl.BlockSpec(memory_space=pltpu.SMEM)
-PARAMS = pltpu.CompilerParams(vmem_limit_bytes=12 * 1024 * 1024)
+PARAMS = pltpu.CompilerParams(vmem_limit_bytes=24 * 1024 * 1024)
 
 
 def swap(block):
@@ -389,8 +389,9 @@
     x_pair = swap(lax.dynamic_slice_in_dim(x_wide, (1 - core[0]) * half, half, axis=3))
     shifts = column_shifts(x_wide)
     cot_turned = cot_pad.reshape((frames + 2) * rows * width, chans).T
-    waited = (shifts, cot_pad, cot_turned)
-    parts, parts_other, (shifts, cot_pad, cot_turned) = kernel_parts(unit, waited)
+    waited = (shifts, cot_pad, cot_turned, x_pair)
+    parts, parts_other, waited = kernel_parts(unit, waited)
+    shifts, cot_pad, cot_turned, x_pair = waited
     cot_turned_pair = swap(cot_turned)
     cot_turned_pair, parts_other = lax.optimization_barrier((cot_turned_pair, parts_other))
 
@@ -414,21 +415,11 @@
     info = jnp.concatenate([core, slots_of("x"), slots_of("y")])
     lower, sent_lower = weight_terms(0, own, info, *operands)
     upper, sent_upper = weight_terms(1, own, info, *operands)
-    slope_edges, _ = lax.optimization_barrier((slope_edges, (sent_lower, sent_upper)))
-    slope_wide = widened(slope_maps, slope_edges, SPACE, 1)
-    shifts_slope = column_shifts(slope_wide)
-    grad = input_gradient(0, core, shifts_slope, cotangent, k_mine, k_other)
-
     came_lower = exchange(sent_lower, "x", 0)
     came_upper = exchange(sent_upper, "y", 0)
-    came_lower, grad = lax.optimization_barrier((came_lower, grad))
-    passed = (lower[1] + widen(came_lower[1])).astype(jnp.bfloat16)
-    info, _ = lax.optimization_barrier((core, passed))
-    grad = input_gradient(1, info, shifts_slope, cotangent, k_mine, k_other, (grad,))
-    last_lower = exchange(passed, "x", 1)
-    came_upper, grad = lax.optimization_barrier((came_upper, grad))
-    passed = (upper[1] + widen(came_upper[1])).astype(jnp.bfloat16)
-    last_upper = exchange(passed, "y", 1)
+    passed_lower = (lower[1] + widen(came_lower[1])).astype(jnp.bfloat16)
+    passed_upper = (upper[1] + widen(came_upper[1])).astype(jnp.bfloat16)
+    last_lower, last_upper = exchange(passed_lower, "x", 1), exchange(passed_upper, "y", 1)
 
     def total(terms, came, last, slots):
         return terms[0, slots] + widen(came[0, slots]) + widen(last[slots])
@@ -441,9 +432,19 @@
     terms = jnp.concatenate([lower, upper], axis=1)
     terms = terms.reshape(3, 4, 2, own // 2, half).transpose(1, 2, 0, 3, 4)
     terms = terms.reshape(8, 3, own // 2, half).astype(jnp.bfloat16)
-    terms = scattered(terms, ("zh", "zl"))
+
+    slope_edges, _ = lax.optimization_barrier((slope_edges, terms))
+    slope_wide = widened(slope_maps, slope_edges, SPACE, 1)
+    shifts_slope = column_shifts(slope_wide)
+    grad = input_gradient(0, core, shifts_slope, cotangent, k_mine, k_other)
+    terms = lax.all_to_all(terms, ("zh", "zl"), 0, 0, tiled=True)
+    terms, grad = lax.optimization_barrier((terms, grad))
     pixels = count * lax.axis_size(TM) * lax.axis_size(SPACE)
-    terms = gathered(terms * (1.0 / math.sqrt(pixels)), ("x", "zl"))
+    terms = jnp.sum(widen(terms), axis=0) * (1.0 / math.sqrt(pixels))
+    info, _ = lax.optimization_barrier((core, terms))
+    grad = input_gradient(1, info, shifts_slope, cotangent, k_mine, k_other, (grad,))
+    terms = gathered(terms, ("x", "zl"))
+    terms, grad = lax.optimization_barrier((terms, grad))
     came = swap(terms)
     terms = jnp.concatenate(
         [jnp.where(core[0] == 0, terms, came), jnp.where(core[0] == 0, came, terms)], axis=3

time: 191 us -> 188 us (0.984)
  blocking collectives: 22.7 us -> 0 us
  local copies, waits for them, and re-layouts: 11.2 us -> 29.9 us
    all_to_all x2 -> x0, blocking collectives: 22.7 us -> none  [the longest x1 11.7 us: gathered(): return lax.all_to_all(spread, axis, 0, 0, tiled=True)]
    unnamed x16 -> x38, local copies, waits for them, and re-layouts: 2.41 us -> 17.5 us
    all_to_all x0 -> x2, starting transfers between devices: none -> 12.8 us  [the longest x1 9.46 us: gathered(): return lax.all_to_all(spread, axis, 0, 0, tiled=True)]
    ppermute x16, waiting for transfers between devices: 32 us -> 42.4 us  [exchange(): return lax.ppermute(block, names, pairs)]
    ppermute x9, starting transfers between devices: 20.8 us -> 13.8 us  [swap(): return lax.ppermute(block, 'core', PAIR)]
    ppermute x3, waiting for transfers between devices: 6.27 us -> 0.01 us  [edges_of(): high = lax.ppermute(lax.slice_in_dim(block, 0, 1, axis=dim), axis, backward)]
    ppermute x16, starting transfers between devices: 17.8 us -> 12.9 us  [exchange(): return lax.ppermute(block, names, pairs)]
    ppermute x9, waiting for transfers between devices: 4.27 us -> 1.37 us  [swap(): return lax.ppermute(block, 'core', PAIR)]
  transfers between devices with their start and end apart: 34 -> 36, of which waited for: 14 -> 11; matrix products, arithmetic and copies ran while one was open for 13% -> 14% of each run, Pallas kernels for 17% -> 10%
where the time goes in v7:
time: 188 us; the launch traced here: 187 us
  starting transfers between devices  62.2 us (33%)
  waiting for transfers between devices  43.8 us (23%)
  Pallas kernels  32.4 us (17%)
  local copies, waits for them, and re-layouts  29.9 us (16%)
  other arithmetic  17.9 us (10%)
    ppermute x16, waiting for transfers between devices, exchange(): return lax.ppermute(block, names, pairs)  42.4 us
    unnamed x38, local copies, waits for them, and re-layouts  17.5 us
    ppermute x9, starting transfers between devices, swap(): return lax.ppermute(block, 'core', PAIR)  13.8 us
    ppermute x16, starting transfers between devices, exchange(): return lax.ppermute(block, names, pairs)  12.9 us
    ppermute x3, starting transfers between devices, edges_of(): high = lax.ppermute(lax.slice_in_dim(block, 0, 1, axis=dim), axis, backward)  11.4 us
    all_to_all x1, starting transfers between devices, gathered(): return lax.all_to_all(spread, axis, 0, 0, tiled=True)  9.46 us
    pallas_call x2, Pallas kernels, weight_terms(): pl.pallas_call(functools.partial(weight_kernel, upper), out_shape=(jax.Sh...  9.31 us
    ppermute x3, starting transfers between devices, kernel_unit(): slots.append(lax.ppermute(unit, 'zh', [(i, i ^ k) for i in range(4)]))  9.12 us
  transfers between devices with their start and end apart: 36, of which 11 were waited for; matrix products, arithmetic and copies ran while one was open for 14% of the time, Pallas kernels for 10%

profile of v7, /device:TPU:1, one launch (start us, length us, event | category | flops | bytes accessed | tf_op | source)
XLA Modules:
  0.0 187.4 jit_solution(17404370553266058664)
XLA Ops:
  0.6 0.8 fusion.10
  1.5 6.9 %collective-permute-start = (bf16[3,32,256]{2,1,0:T(8,128)(2,1)S(1)}, bf16[3,32,256]{2,1,0:T(8,128)(2,1)S(1)}, u32[]{:S(2)}, u32[]{:S(2)}) collective-permute-start(bf16[3,32,256]{2,1,0:T(8,128)(2,1)S(1)} %fusion.10), channel_id=1, source_target_pairs={{0,12},{4,8},{8,4},{12,0},{1,13},{5,9},{9,5},{13,1},{2,14},{6,10},... | collective-permute-start | bytes 147464 | tf_op jit(solution)/shard_map/ppermute | solution.py:359
  8.4 1.0 collective-permute-start.1
  9.4 1.2 collective-permute-start.2
  10.6 1.2 fusion.22
  11.8 6.0 %collective-permute-start.12 = (bf16[2,1,192,512]{3,2,1,0:T(8,128)(2,1)S(1)}, bf16[2,1,192,512]{3,2,1,0:T(8,128)(2,1)S(1)}, u32[]{:S(2)}, u32[]{:S(2)}) collective-permute-start(bf16[2,1,192,512]{3,2,1,0:T(8,128)(2,1)S(1)} %get-tuple-element.84), channel_id=1, source_target_pairs={{1,0},{2,1},{3,2},{4,3},{5,4},{6,5},{7,6},{8,7},{9,8},{10,9},{11,1... | collective-permute-start | bytes 1179656 | tf_op jit(solution)/shard_map/ppermute | solution.py:86
  17.9 2.6 %collective-permute-start.7 = (bf16[2,3,32,256]{3,2,1,0:T(8,128)(2,1)S(1)}, bf16[2,3,32,256]{3,2,1,0:T(8,128)(2,1)S(1)}, u32[]{:S(2)}, u32[]{:S(2)}) collective-permute-start(bf16[2,3,32,256]{3,2,1,0:T(8,128)(2,1)S(1)} %get-tuple-element.94), channel_id=1, source_target_pairs={{0,64},{64,0},{128,192},{192,128},{16,208},{80,144},{144,80},{208,... | collective-permute-start | bytes 294920 | tf_op jit(solution)/shard_map/ppermute | solution.py:35
  20.4 1.4 collective-permute-start.3
  21.8 0.8 collective-permute-done.7
  23.0 7.1 %collective-permute-done.3 = bf16[2,3,32,256]{3,2,1,0:T(8,128)(2,1)S(1)} collective-permute-done((bf16[2,3,32,256]{3,2,1,0:T(8,128)(2,1)S(1)}, bf16[2,3,32,256]{3,2,1,0:T(8,128)(2,1)S(1)}, u32[]{:S(2)}, u32[]{:S(2)}) %collective-permute-start.3) | collective-permute-done | bytes 98336 | tf_op jit(solution)/shard_map/ppermute | solution.py:35
  30.1 0.7 pad_maximum_fusion.11
  30.8 0.8 fusion.21
  31.6 0.7 copy-done.18
  32.3 1.7 collective-permute-start.13
  34.1 1.8 fusion.13
  36.2 1.9 fusion.14
  38.1 3.6 %collective-permute-start.5 = (bf16[4,2,3,32,256]{4,3,2,1,0:T(8,128)(2,1)}, bf16[4,2,3,32,256]{4,3,2,1,0:T(8,128)(2,1)}, u32[]{:S(2)}, u32[]{:S(2)}) collective-permute-start(bf16[4,2,3,32,256]{4,3,2,1,0:T(8,128)(2,1)} %get-tuple-element.88), channel_id=1, source_target_pairs={{0,64},{64,0},{128,192},{192,128},{16,208},{80,144},{144,80},{208,... | collective-permute-start | bytes 1179656 | tf_op jit(solution)/shard_map/ppermute | solution.py:35
  41.8 1.4 fusion.16
  43.2 1.0 constant_dynamic-slice_fusion
  44.2 0.6 collective-permute-start.15
  44.8 1.0 broadcast_select_fusion
  45.9 1.3 pad_maximum_fusion.4.cot_ref
  47.2 1.7 copy.13
  49.0 1.2 pad_maximum_fusion.7.refs_2_
  50.8 1.9 %pad_maximum_fusion.6.refs_0_ = bf16[2,4,2,3,32,256]{5,4,3,2,1,0:T(8,128)(2,1)} fusion(bf16[1,4,2,3,32,256]{5,4,3,2,1,0:T(8,128)(2,1)} %bitcast.16, bf16[1,4,2,3,32,256]{5,4,3,2,1,0:T(8,128)(2,1)S(1)} %copy-done.17), kind=kLoop, calls=%fused_computation.10 | loop fusion | flops 393216 | bytes 1572864 | tf_op jit(solution)/shard_map/stack | solution.py:67
  52.7 0.6 collective-permute-start.6
  54.4 0.8 copy-done.15
  55.3 2.4 %pad_maximum_fusion.x_ref = bf16[3,2,4,192,512]{4,3,2,1,0:T(8,128)(2,1)} fusion(bf16[1,2,4,192,512]{4,3,2,1,0:T(8,128)(2,1)S(1)} %get-tuple-element.97, bf16[1,2,4,192,512]{4,3,2,1,0:T(8,128)(2,1)S(1)} %copy-done.15, bf16[1,2,4,192,512]{4,3,2,1,0:T(8,128)(2,1)S(1)} %get-tuple-element.98), kind=kLoop, calls=%fused_computation | loop fusion | flops 4718592 | bytes 9437184 | tf_op jit(solution)/shard_map/stack | solution.py:100
  57.7 3.9 %collective-permute-done.10.refs_3_ = bf16[2,4,2,3,32,256]{5,4,3,2,1,0:T(8,128)(2,1)} collective-permute-done((bf16[2,4,2,3,32,256]{5,4,3,2,1,0:T(8,128)(2,1)S(1)}, bf16[2,4,2,3,32,256]{5,4,3,2,1,0:T(8,128)(2,1)}, u32[]{:S(2)}, u32[]{:S(2)}) %collective-permute-start.10) | collective-permute-done | bytes 786464 | tf_op jit(solution)/shard_map/ppermute | solution.py:35
  61.5 2.6 %collective-permute-done.6.refs_1_ = bf16[2,4,2,3,32,256]{5,4,3,2,1,0:T(8,128)(2,1)} collective-permute-done((bf16[2,4,2,3,32,256]{5,4,3,2,1,0:T(8,128)(2,1)}, bf16[2,4,2,3,32,256]{5,4,3,2,1,0:T(8,128)(2,1)}, u32[]{:S(2)}, u32[]{:S(2)}) %collective-permute-start.6) | collective-permute-done | bytes 786464 | tf_op jit(solution)/shard_map/ppermute | solution.py:35
  64.2 6.2 %collective-permute-start.16 = (bf16[512,1536]{1,0:T(8,128)(2,1)S(1)}, bf16[512,1536]{1,0:T(8,128)(2,1)}, u32[]{:S(2)}, u32[]{:S(2)}) collective-permute-start(bf16[512,1536]{1,0:T(8,128)(2,1)S(1)} %bitcast.100), channel_id=1, source_target_pairs={{0,16},{16,0},{1,17},{17,1},{2,18},{18,2},{3,19},{19,3},{4,20},{20... | collective-permute-start | bytes 4718600 | tf_op jit(solution)/shard_map/ppermute | solution.py:22
  71.5 2.3 %copy-done = bf16[3,2,4,192,512]{4,3,2,1,0:T(8,128)(2,1)S(1)} copy-done((bf16[3,2,4,192,512]{4,3,2,1,0:T(8,128)(2,1)S(1)}, bf16[3,2,4,192,512]{4,3,2,1,0:T(8,128)(2,1)}, u32[]{:S(2)}) %copy-start) | copy-done | bytes 4718616
  73.9 1.4 copy-done.11
  75.3 6.8 %shard_map.67 = (f32[2,384,512]{2,1,0:T(8,128)S(1)}, f32[2,384,256]{2,1,0:T(8,128)S(1)}, bf16[4,4,3,4,32,256]{5,4,3,2,1,0:T(8,128)(2,1)S(1)}) custom-call(s32[9]{0:T(128)S(1)} %concatenate.63.info_ref, bf16[3,2,4,192,512]{4,3,2,1,0:T(8,128)(2,1)S(1)} %copy-done, bf16[4,2,192,512]{3,2,1,0:T(8,128)(2,1)S(1)} %copy-done.11, ...), custom_call_target="tpu_custom_call" | custom-call | flops 3200000000 | bytes 12000000 | tf_op jit(solution)/shard_map/pallas_call | solution.py:218
  82.1 1.7 copy-done.5
  83.9 8.7 %shard_map.68 = (bf16[2,384,256]{2,1,0:T(8,128)(2,1)S(1)}, bf16[2,384,256]{2,1,0:T(8,128)(2,1)S(1)}, bf16[2,384,512]{2,1,0:T(8,128)(2,1)S(1)}, bf16[512,768]{1,0...) custom-call(s32[9]{0:T(128)S(1)} %concatenate.55.info_ref, bf16[3,2,4,192,512]{4,3,2,1,0:T(8,128)(2,1)S(1)} %copy-done.1, ...), custom_call_target="tpu_custom_call" | custom-call | flops 3200000000 | bytes 15000000 | tf_op jit(solution)/shard_map/pallas_call | solution.py:227
  93.3 2.0 %fusion.20 = (bf16[2,4,191,256]{3,2,1,0:T(8,128)(2,1)S(1)}, bf16[2,4,191,256]{3,2,1,0:T(8,128)(2,1)S(1)}) fusion(bf16[2,4,192,256]{3,2,1,0:T(8,128)(2,1)} %collective-permute-done.15), kind=kLoop, calls=%fused_computation.80 | loop fusion | bytes 3129344 | tf_op jit(solution)/shard_map/slice | solution.py:102
  95.5 1.4 pad_maximum_fusion.2.x_pair_ref
  97.0 4.7 %shard_map.69 = (f32[4,4,3,2,32,256]{5,4,3,2,1,0:T(8,128)S(1)}, bf16[2,4,3,2,32,256]{5,4,3,2,1,0:T(8,128)(2,1)S(1)}) custom-call(s32[9]{0:T(128)S(1)} %pad_add_fusion.info_ref, bf16[512,768]{1,0:T(8,128)(2,1)S(1)} %get-tuple-element.44.turned_ref, bf16[512,768]{1,0:T(8,128)(2,1)S(1)} %collective-permute-done.21.turned_pair_ref, ...), custom_call_target="tpu_custom_call" | custom-call | flops 2400000000 | bytes 16000000 | tf_op jit(solution)/shard_map/pallas_call | solution.py:302
  101.6 2.6 %collective-permute-start.23 = (bf16[2,4,3,2,32,256]{5,4,3,2,1,0:T(8,128)(2,1)S(1)}, bf16[2,4,3,2,32,256]{5,4,3,2,1,0:T(8,128)(2,1)S(1)}, u32[]{:S(2)}, u32[]{:S(2)}) collective-permute-start(bf16[2,4,3,2,32,256]{5,4,3,2,1,0:T(8,128)(2,1)S(1)} %get-tuple-element.51), channel_id=1, source_target_pairs={{0,64},{64,0},{128,192},{192,128},{16,208},{80,144},{144,80},{208,... | collective-permute-start | bytes 2359304 | tf_op jit(solution)/shard_map/ppermute | solution.py:35
  104.3 4.7 %shard_map.70 = (f32[4,4,3,2,32,256]{5,4,3,2,1,0:T(8,128)S(1)}, bf16[2,4,3,2,32,256]{5,4,3,2,1,0:T(8,128)(2,1)S(1)}) custom-call(s32[9]{0:T(128)S(1)} %pad_add_fusion.info_ref, bf16[512,768]{1,0:T(8,128)(2,1)S(1)} %get-tuple-element.44.turned_ref, bf16[512,768]{1,0:T(8,128)(2,1)S(1)} %collective-permute-done.21.turned_pair_ref, ...), custom_call_target="tpu_custom_call" | custom-call | flops 2400000000 | bytes 16000000 | tf_op jit(solution)/shard_map/pallas_call | solution.py:302
  109.2 4.5 %collective-permute-done.23 = bf16[2,4,3,2,32,256]{5,4,3,2,1,0:T(8,128)(2,1)S(1)} collective-permute-done((bf16[2,4,3,2,32,256]{5,4,3,2,1,0:T(8,128)(2,1)S(1)}, bf16[2,4,3,2,32,256]{5,4,3,2,1,0:T(8,128)(2,1)S(1)}, u32[]{:S(2)}, u32[]{:S(2)}) %collective-permute-start.23) | collective-permute-done | bytes 786464 | tf_op jit(solution)/shard_map/ppermute | solution.py:35
  114.0 7.6 %collective-permute-done.27 = bf16[2,4,3,2,32,256]{5,4,3,2,1,0:T(8,128)(2,1)S(1)} collective-permute-done((bf16[2,4,3,2,32,256]{5,4,3,2,1,0:T(8,128)(2,1)S(1)}, bf16[2,4,3,2,32,256]{5,4,3,2,1,0:T(8,128)(2,1)S(1)}, u32[]{:S(2)}, u32[]{:S(2)}) %collective-permute-start.27) | collective-permute-done | bytes 786464 | tf_op jit(solution)/shard_map/ppermute | solution.py:35
  122.1 8.9 %collective-permute-done.28 = bf16[4,3,2,32,256]{4,3,2,1,0:T(8,128)(2,1)S(1)} collective-permute-done((bf16[4,3,2,32,256]{4,3,2,1,0:T(8,128)(2,1)S(1)}, bf16[4,3,2,32,256]{4,3,2,1,0:T(8,128)(2,1)S(1)}, u32[]{:S(2)}, u32[]{:S(2)}) %collective-permute-start.28) | collective-permute-done | bytes 393248 | tf_op jit(solution)/shard_map/ppermute | solution.py:35
  131.7 5.4 %collective-permute-start.32 = (bf16[2,1,192,512]{3,2,1,0:T(8,128)(2,1)S(1)}, bf16[2,1,192,512]{3,2,1,0:T(8,128)(2,1)S(1)}, u32[]{:S(2)}, u32[]{:S(2)}) collective-permute-start(bf16[2,1,192,512]{3,2,1,0:T(8,128)(2,1)S(1)} %get-tuple-element.77), channel_id=1, source_target_pairs={{1,0},{2,1},{3,2},{4,3},{5,4},{6,5},{7,6},{8,7},{9,8},{10,9},{11,1... | collective-permute-start | bytes 1179656 | tf_op jit(solution)/shard_map/ppermute | solution.py:86
  137.3 1.9 collective-permute-done.29
  139.3 5.0 %collective-permute-done.26 = f32[3,2,32,256]{3,2,1,0:T(8,128)S(1)} collective-permute-done((f32[3,2,32,256]{3,2,1,0:T(8,128)S(1)}, f32[3,2,32,256]{3,2,1,0:T(8,128)S(1)}, u32[]{:S(2)}, u32[]{:S(2)}) %collective-permute-start.26) | collective-permute-done | bytes 196640 | tf_op jit(solution)/shard_map/ppermute | solution.py:35
  144.4 0.7 copy.14
  145.1 3.4 %all-to-all-start = ((bf16[8,3,16,256]{3,2,1,0:T(8,128)(2,1)}), bf16[8,3,16,256]{3,2,1,0:T(8,128)(2,1)S(1)}, u32[]{:S(2)}, u32[]{:S(2)}) async-start(bf16[8,3,16,256]{3,2,1,0:T(8,128)(2,1)} %bitcast.49), calls=%async_computation | async-start | bytes 393216 | tf_op jit(solution)/shard_map/all_to_all | solution.py:440
  149.9 0.6 pad_maximum_fusion.1.x_ref
  150.5 1.3 copy-done.6
  151.8 1.0 copy-done.9
  152.7 3.8 %shard_map.71.refs_0_ = f32[2,384,512]{2,1,0:T(8,128)} custom-call(s32[1]{0:T(128)} %bitcast.info_ref, bf16[3,2,4,192,512]{4,3,2,1,0:T(8,128)(2,1)S(1)} %pad_maximum_fusion.1.x_ref, bf16[2,384,512]{2,1,0:T(8,128)(2,1)S(1)} %bitcast.103, bf16[4,4,3,4,32,256]{5,4,3,2,1,0:T(8,128)(2,1)S(1)} %copy-done.6, bf16[4,4,3,4,32,256]{5,4,3,2,1,0:T(8,128)(2,1)S(1)} %copy-done.9), custom_call_target="tpu_custom_call" | custom-call | flops 1800000000 | bytes 8000000 | tf_op jit(solution)/shard_map/pallas_call | solution.py:338
  156.5 2.2 %copy-done.2 = bf16[3,2,4,192,512]{4,3,2,1,0:T(8,128)(2,1)} copy-done((bf16[3,2,4,192,512]{4,3,2,1,0:T(8,128)(2,1)}, bf16[3,2,4,192,512]{4,3,2,1,0:T(8,128)(2,1)S(1)}, u32[]{:S(2)}) %copy-start.2) | copy-done | bytes 4718616
  158.7 0.8 broadcast_in_dim.30
  159.5 9.5 %all-to-all-start.1 = ((f32[8,3,16,256]{3,2,1,0:T(8,128)}), f32[8,3,16,256]{3,2,1,0:T(8,128)S(1)}, u32[]{:S(2)}, u32[]{:S(2)}) async-start(f32[8,3,16,256]{3,2,1,0:T(8,128)} %broadcast_in_dim.30), calls=%async_computation.1 | async-start | bytes 786432 | tf_op jit(solution)/shard_map/all_to_all | solution.py:73
  169.0 2.3 %copy-done.3 = bf16[3,2,4,192,512]{4,3,2,1,0:T(8,128)(2,1)S(1)} copy-done((bf16[3,2,4,192,512]{4,3,2,1,0:T(8,128)(2,1)S(1)}, bf16[3,2,4,192,512]{4,3,2,1,0:T(8,128)(2,1)}, u32[]{:S(2)}) %copy-start.3) | copy-done | bytes 4718616
  171.3 1.9 %copy-done.7 = bf16[4,4,3,4,32,256]{5,4,3,2,1,0:T(8,128)(2,1)S(1)} copy-done((bf16[4,4,3,4,32,256]{5,4,3,2,1,0:T(8,128)(2,1)S(1)}, bf16[4,4,3,4,32,256]{5,4,3,2,1,0:T(8,128)(2,1)}, u32[]{:S(2)}) %copy-start.7) | copy-done | bytes 3145752
  173.2 1.9 %copy-done.10 = bf16[4,4,3,4,32,256]{5,4,3,2,1,0:T(8,128)(2,1)S(1)} copy-done((bf16[4,4,3,4,32,256]{5,4,3,2,1,0:T(8,128)(2,1)S(1)}, bf16[4,4,3,4,32,256]{5,4,3,2,1,0:T(8,128)(2,1)}, u32[]{:S(2)}) %copy-start.10) | copy-done | bytes 3145752
  175.1 3.8 %shard_map.72 = f32[2,384,512]{2,1,0:T(8,128)} custom-call(s32[1]{0:T(128)} %bitcast.info_ref, bf16[3,2,4,192,512]{4,3,2,1,0:T(8,128)(2,1)S(1)} %copy-done.3, bf16[2,384,512]{2,1,0:T(8,128)(2,1)S(1)} %bitcast.104, bf16[4,4,3,4,32,256]{5,4,3,2,1,0:T(8,128)(2,1)S(1)} %copy-done.7, ...), custom_call_target="tpu_custom_call", output_to_operand_aliasing={{}: (5, {})} | custom-call | flops 1800000000 | bytes 8000000 | tf_op jit(solution)/shard_map/pallas_call | solution.py:338
  178.9 5.4 %collective-permute-start.33 = (f32[8,3,16,256]{3,2,1,0:T(8,128)S(1)}, f32[8,3,16,256]{3,2,1,0:T(8,128)S(1)}, u32[]{:S(2)}, u32[]{:S(2)}) collective-permute-start(f32[8,3,16,256]{3,2,1,0:T(8,128)S(1)} %all-to-all-done.1), channel_id=1, source_target_pairs={{0,16},{16,0},{1,17},{17,1},{2,18},{18,2},{3,19},{19,3},{4,20},{20... | collective-permute-start | bytes 1179656 | tf_op jit(solution)/shard_map/ppermute | solution.py:22
  184.2 1.3 collective-permute-done.33
  185.9 0.9 copy.15
  186.7 0.7 copy.16
  (111 shorter events, 8.5 us)
Async XLA Ops:
  1.5 29.3 %copy-start.4 = (bf16[2,2,192,512]{3,2,1,0:T(8,128)(2,1)S(1)}, bf16[2,2,192,512]{3,2,1,0:T(8,128)(2,1)}, u32[]{:S(2)}) copy-start(bf16[2,2,192,512]{3,2,1,0:T(8,128)(2,1)} %param.5) | copy-start | bytes 2359300
  1.5 16.3 %collective-permute-start = (bf16[3,32,256]{2,1,0:T(8,128)(2,1)S(1)}, bf16[3,32,256]{2,1,0:T(8,128)(2,1)S(1)}, u32[]{:S(2)}, u32[]{:S(2)}) collective-permute-start(bf16[3,32,256]{2,1,0:T(8,128)(2,1)S(1)} %fusion.10), channel_id=1, source_target_pairs={{0,12},{4,8},{8,4},{12,0},{1,13},{5,9},{9,5},{13,1},{2,14},{6,10},... | collective-permute-start | bytes 147464 | tf_op jit(solution)/shard_map/ppermute | solution.py:359
  8.4 9.4 %collective-permute-start.1 = (bf16[3,32,256]{2,1,0:T(8,128)(2,1)S(1)}, bf16[3,32,256]{2,1,0:T(8,128)(2,1)S(1)}, u32[]{:S(2)}, u32[]{:S(2)}) collective-permute-start(bf16[3,32,256]{2,1,0:T(8,128)(2,1)S(1)} %fusion.10), channel_id=1, source_target_pairs={{0,8},{4,12},{8,0},{12,4},{1,9},{5,13},{9,1},{13,5},{2,10},{6,14},... | collective-permute-start | bytes 147464 | tf_op jit(solution)/shard_map/ppermute | solution.py:359
  9.4 8.4 %collective-permute-start.2 = (bf16[3,32,256]{2,1,0:T(8,128)(2,1)S(1)}, bf16[3,32,256]{2,1,0:T(8,128)(2,1)S(1)}, u32[]{:S(2)}, u32[]{:S(2)}) collective-permute-start(bf16[3,32,256]{2,1,0:T(8,128)(2,1)S(1)} %fusion.10), channel_id=1, source_target_pairs={{0,4},{4,0},{8,12},{12,8},{1,5},{5,1},{9,13},{13,9},{2,6},{6,2},{1... | collective-permute-start | bytes 147464 | tf_op jit(solution)/shard_map/ppermute | solution.py:359
  11.8 26.3 %collective-permute-start.12 = (bf16[2,1,192,512]{3,2,1,0:T(8,128)(2,1)S(1)}, bf16[2,1,192,512]{3,2,1,0:T(8,128)(2,1)S(1)}, u32[]{:S(2)}, u32[]{:S(2)}) collective-permute-start(bf16[2,1,192,512]{3,2,1,0:T(8,128)(2,1)S(1)} %get-tuple-element.84), channel_id=1, source_target_pairs={{1,0},{2,1},{3,2},{4,3},{5,4},{6,5},{7,6},{8,7},{9,8},{10,9},{11,1... | collective-permute-start | bytes 1179656 | tf_op jit(solution)/shard_map/ppermute | solution.py:86
  17.8 24.0 %collective-permute-start.11 = (bf16[2,1,192,512]{3,2,1,0:T(8,128)(2,1)S(1)}, bf16[2,1,192,512]{3,2,1,0:T(8,128)(2,1)S(1)}, u32[]{:S(2)}, u32[]{:S(2)}) collective-permute-start(bf16[2,1,192,512]{3,2,1,0:T(8,128)(2,1)S(1)} %get-tuple-element.83), channel_id=1, source_target_pairs={{0,1},{1,2},{2,3},{3,4},{4,5},{5,6},{6,7},{7,8},{8,9},{9,10},{10,1... | collective-permute-start | bytes 1179656 | tf_op jit(solution)/shard_map/ppermute | solution.py:85
  17.9 4.8 %collective-permute-start.7 = (bf16[2,3,32,256]{3,2,1,0:T(8,128)(2,1)S(1)}, bf16[2,3,32,256]{3,2,1,0:T(8,128)(2,1)S(1)}, u32[]{:S(2)}, u32[]{:S(2)}) collective-permute-start(bf16[2,3,32,256]{3,2,1,0:T(8,128)(2,1)S(1)} %get-tuple-element.94), channel_id=1, source_target_pairs={{0,64},{64,0},{128,192},{192,128},{16,208},{80,144},{144,80},{208,... | collective-permute-start | bytes 294920 | tf_op jit(solution)/shard_map/ppermute | solution.py:35
  20.4 9.7 %collective-permute-start.3 = (bf16[2,3,32,256]{3,2,1,0:T(8,128)(2,1)S(1)}, bf16[2,3,32,256]{3,2,1,0:T(8,128)(2,1)S(1)}, u32[]{:S(2)}, u32[]{:S(2)}) collective-permute-start(bf16[2,3,32,256]{3,2,1,0:T(8,128)(2,1)S(1)} %get-tuple-element.96), channel_id=1, source_target_pairs={{0,1},{1,0},{2,3},{3,2},{16,19},{17,18},{18,17},{19,16},{4,5},{5,4... | collective-permute-start | bytes 294920 | tf_op jit(solution)/shard_map/ppermute | solution.py:35
  22.6 9.0 %collective-permute-start.8 = (bf16[2,2,3,32,256]{4,3,2,1,0:T(8,128)(2,1)S(1)}, bf16[2,2,3,32,256]{4,3,2,1,0:T(8,128)(2,1)S(1)}, u32[]{:S(2)}, u32[]{:S(2)}) collective-permute-start(bf16[2,2,3,32,256]{4,3,2,1,0:T(8,128)(2,1)S(1)} %pad_maximum_fusion.12), channel_id=1, source_target_pairs={{0,192},{64,128},{128,64},{192,0},{16,80},{80,16},{144,208},{208,1... | collective-permute-start | bytes 589832 | tf_op jit(solution)/shard_map/ppermute | solution.py:35
  30.8 5.1 %collective-permute-start.4 = (bf16[2,2,3,32,256]{4,3,2,1,0:T(8,128)(2,1)}, bf16[2,2,3,32,256]{4,3,2,1,0:T(8,128)(2,1)}, u32[]{:S(2)}, u32[]{:S(2)}) collective-permute-start(bf16[2,2,3,32,256]{4,3,2,1,0:T(8,128)(2,1)} %pad_maximum_fusion.11), channel_id=1, source_target_pairs={{0,3},{1,2},{2,1},{3,0},{16,17},{17,16},{18,19},{19,18},{4,7},{5,6... | collective-permute-start | bytes 589832 | tf_op jit(solution)/shard_map/ppermute | solution.py:35
  31.6 13.2 %collective-permute-start.14 = (bf16[1,2,192,512]{3,2,1,0:T(8,128)(2,1)}, bf16[1,2,192,512]{3,2,1,0:T(8,128)(2,1)}, u32[]{:S(2)}, u32[]{:S(2)}) collective-permute-start(bf16[1,2,192,512]{3,2,1,0:T(8,128)(2,1)} %get-tuple-element.82), channel_id=1, source_target_pairs={{16,0},{32,16},{48,32},{64,48},{80,64},{96,80},{112,96},{128,112},... | collective-permute-start | bytes 1179656 | tf_op jit(solution)/shard_map/ppermute | solution.py:86
  31.6 0.7 copy-start.18
  32.3 13.5 %collective-permute-start.13 = (bf16[1,2,192,512]{3,2,1,0:T(8,128)(2,1)S(1)}, bf16[1,2,192,512]{3,2,1,0:T(8,128)(2,1)S(1)}, u32[]{:S(2)}, u32[]{:S(2)}) collective-permute-start(bf16[1,2,192,512]{3,2,1,0:T(8,128)(2,1)S(1)} %get-tuple-element.81), channel_id=1, source_target_pairs={{0,16},{16,32},{32,48},{48,64},{64,80},{80,96},{96,112},{112,128},... | collective-permute-start | bytes 1179656 | tf_op jit(solution)/shard_map/ppermute | solution.py:85
  35.8 6.0 %copy-start.16 = (bf16[2,2,192,512]{3,2,1,0:T(8,128)(2,1)S(1)}, bf16[2,2,192,512]{3,2,1,0:T(8,128)(2,1)}, u32[]{:S(2)}) copy-start(bf16[2,2,192,512]{3,2,1,0:T(8,128)(2,1)} %param.4) | copy-start | bytes 2359300
  35.9 13.0 %collective-permute-start.9 = (bf16[4,2,3,32,256]{4,3,2,1,0:T(8,128)(2,1)}, bf16[4,2,3,32,256]{4,3,2,1,0:T(8,128)(2,1)}, u32[]{:S(2)}, u32[]{:S(2)}) collective-permute-start(bf16[4,2,3,32,256]{4,3,2,1,0:T(8,128)(2,1)} %get-tuple-element.86), channel_id=1, source_target_pairs={{0,1},{1,0},{2,3},{3,2},{16,19},{17,18},{18,17},{19,16},{4,5},{5,4... | collective-permute-start | bytes 1179656 | tf_op jit(solution)/shard_map/ppermute | solution.py:35
  38.1 12.7 %collective-permute-start.5 = (bf16[4,2,3,32,256]{4,3,2,1,0:T(8,128)(2,1)}, bf16[4,2,3,32,256]{4,3,2,1,0:T(8,128)(2,1)}, u32[]{:S(2)}, u32[]{:S(2)}) collective-permute-start(bf16[4,2,3,32,256]{4,3,2,1,0:T(8,128)(2,1)} %get-tuple-element.88), channel_id=1, source_target_pairs={{0,64},{64,0},{128,192},{192,128},{16,208},{80,144},{144,80},{208,... | collective-permute-start | bytes 1179656 | tf_op jit(solution)/shard_map/ppermute | solution.py:35
  43.2 2.7 %copy-start.13 = (bf16[2,4,192,512]{3,2,1,0:T(8,128)(2,1)}, bf16[2,4,192,512]{3,2,1,0:T(8,128)(2,1)S(1)}, u32[]{:S(2)}) copy-start(bf16[2,4,192,512]{3,2,1,0:T(8,128)(2,1)S(1)} %get-tuple-element.74) | copy-start | bytes 4718596
  44.2 13.5 %collective-permute-start.15 = (bf16[2,4,192,256]{3,2,1,0:T(8,128)(2,1)}, bf16[2,4,192,256]{3,2,1,0:T(8,128)(2,1)}, u32[]{:S(2)}, u32[]{:S(2)}) collective-permute-start(bf16[2,4,192,256]{3,2,1,0:T(8,128)(2,1)} %constant_dynamic-slice_fusion), channel_id=1, source_target_pairs={{0,16},{16,0},{1,17},{17,1},{2,18},{18,2},{3,19},{19,3},{4,20},{20... | collective-permute-start | bytes 2359304 | tf_op jit(solution)/shard_map/ppermute | solution.py:22
  49.0 1.8 copy-start.17
  49.0 4.4 %copy-start.14 = (bf16[2,4,192,512]{3,2,1,0:T(8,128)(2,1)S(1)}, bf16[2,4,192,512]{3,2,1,0:T(8,128)(2,1)}, u32[]{:S(2)}) copy-start(bf16[2,4,192,512]{3,2,1,0:T(8,128)(2,1)} %copy-done.13) | copy-start | bytes 4718596
  50.2 11.3 %collective-permute-start.10 = (bf16[2,4,2,3,32,256]{5,4,3,2,1,0:T(8,128)(2,1)S(1)}, bf16[2,4,2,3,32,256]{5,4,3,2,1,0:T(8,128)(2,1)}, u32[]{:S(2)}, u32[]{:S(2)}) collective-permute-start(bf16[2,4,2,3,32,256]{5,4,3,2,1,0:T(8,128)(2,1)S(1)} %pad_maximum_fusion.7.refs_2_), channel_id=1, source_target_pairs={{0,3},{1,2},{2,1},{3,0},{16,17},{17,16},{18,19},{19,18},{4,7},{5,6... | collective-permute-start | bytes 2359304 | tf_op jit(solution)/shard_map/ppermute | solution.py:35
  52.7 11.5 %collective-permute-start.6 = (bf16[2,4,2,3,32,256]{5,4,3,2,1,0:T(8,128)(2,1)}, bf16[2,4,2,3,32,256]{5,4,3,2,1,0:T(8,128)(2,1)}, u32[]{:S(2)}, u32[]{:S(2)}) collective-permute-start(bf16[2,4,2,3,32,256]{5,4,3,2,1,0:T(8,128)(2,1)} %pad_maximum_fusion.6.refs_0_), channel_id=1, source_target_pairs={{0,192},{64,128},{128,64},{192,0},{16,80},{80,16},{144,208},{208,1... | collective-permute-start | bytes 2359304 | tf_op jit(solution)/shard_map/ppermute | solution.py:35
  53.9 1.4 copy-start.15
  64.2 19.7 %collective-permute-start.16 = (bf16[512,1536]{1,0:T(8,128)(2,1)S(1)}, bf16[512,1536]{1,0:T(8,128)(2,1)}, u32[]{:S(2)}, u32[]{:S(2)}) collective-permute-start(bf16[512,1536]{1,0:T(8,128)(2,1)S(1)} %bitcast.100), channel_id=1, source_target_pairs={{0,16},{16,0},{1,17},{17,1},{2,18},{18,2},{3,19},{19,3},{4,20},{20... | collective-permute-start | bytes 4718600 | tf_op jit(solution)/shard_map/ppermute | solution.py:22
  70.3 13.5 %collective-permute-start.19 = (bf16[2,4,2,3,32,256]{5,4,3,2,1,0:T(8,128)(2,1)S(1)}, bf16[2,4,2,3,32,256]{5,4,3,2,1,0:T(8,128)(2,1)}, u32[]{:S(2)}, u32[]{:S(2)}) collective-permute-start(bf16[2,4,2,3,32,256]{5,4,3,2,1,0:T(8,128)(2,1)S(1)} %pad_maximum_fusion.7.refs_2_), channel_id=1, source_target_pairs={{0,16},{16,0},{1,17},{17,1},{2,18},{18,2},{3,19},{19,3},{4,20},{20... | collective-permute-start | bytes 2359304 | tf_op jit(solution)/shard_map/ppermute | solution.py:22
  70.3 13.5 %collective-permute-start.17 = (bf16[2,4,2,3,32,256]{5,4,3,2,1,0:T(8,128)(2,1)}, bf16[2,4,2,3,32,256]{5,4,3,2,1,0:T(8,128)(2,1)}, u32[]{:S(2)}, u32[]{:S(2)}) collective-permute-start(bf16[2,4,2,3,32,256]{5,4,3,2,1,0:T(8,128)(2,1)} %pad_maximum_fusion.6.refs_0_), channel_id=1, source_target_pairs={{0,16},{16,0},{1,17},{17,1},{2,18},{18,2},{3,19},{19,3},{4,20},{20... | collective-permute-start | bytes 2359304 | tf_op jit(solution)/shard_map/ppermute | solution.py:22
  70.8 13.0 %collective-permute-start.18 = (bf16[2,4,2,3,32,256]{5,4,3,2,1,0:T(8,128)(2,1)}, bf16[2,4,2,3,32,256]{5,4,3,2,1,0:T(8,128)(2,1)}, u32[]{:S(2)}, u32[]{:S(2)}) collective-permute-start(bf16[2,4,2,3,32,256]{5,4,3,2,1,0:T(8,128)(2,1)} %collective-permute-done.6.refs_1_), channel_id=1, source_target_pairs={{0,16},{16,0},{1,17},{17,1},{2,18},{18,2},{3,19},{19,3},{4,20},{20... | collective-permute-start | bytes 2359304 | tf_op jit(solution)/shard_map/ppermute | solution.py:22
  70.8 13.0 %collective-permute-start.20 = (bf16[2,4,2,3,32,256]{5,4,3,2,1,0:T(8,128)(2,1)}, bf16[2,4,2,3,32,256]{5,4,3,2,1,0:T(8,128)(2,1)}, u32[]{:S(2)}, u32[]{:S(2)}) collective-permute-start(bf16[2,4,2,3,32,256]{5,4,3,2,1,0:T(8,128)(2,1)} %collective-permute-done.10.refs_3_), channel_id=1, source_target_pairs={{0,16},{16,0},{1,17},{17,1},{2,18},{18,2},{3,19},{19,3},{4,20},{20... | collective-permute-start | bytes 2359304 | tf_op jit(solution)/shard_map/ppermute | solution.py:22
  71.5 2.3 %copy-start = (bf16[3,2,4,192,512]{4,3,2,1,0:T(8,128)(2,1)S(1)}, bf16[3,2,4,192,512]{4,3,2,1,0:T(8,128)(2,1)}, u32[]{:S(2)}) copy-start(bf16[3,2,4,192,512]{4,3,2,1,0:T(8,128)(2,1)} %pad_maximum_fusion.x_ref) | copy-start | bytes 14155780
  73.9 1.4 copy-start.11
  75.3 8.6 %copy-start.1 = (bf16[3,2,4,192,512]{4,3,2,1,0:T(8,128)(2,1)S(1)}, bf16[3,2,4,192,512]{4,3,2,1,0:T(8,128)(2,1)}, u32[]{:S(2)}) copy-start(bf16[3,2,4,192,512]{4,3,2,1,0:T(8,128)(2,1)} %pad_maximum_fusion.x_ref) | copy-start | bytes 14155780
  75.3 8.6 %copy-start.12 = (bf16[4,2,192,512]{3,2,1,0:T(8,128)(2,1)S(1)}, bf16[4,2,192,512]{3,2,1,0:T(8,128)(2,1)}, u32[]{:S(2)}) copy-start(bf16[4,2,192,512]{3,2,1,0:T(8,128)(2,1)} %pad_maximum_fusion.4.cot_ref) | copy-start | bytes 4718596
  82.1 1.7 copy-start.5
  92.6 2.7 %copy-start.8 = (bf16[4,4,3,4,32,256]{5,4,3,2,1,0:T(8,128)(2,1)}, bf16[4,4,3,4,32,256]{5,4,3,2,1,0:T(8,128)(2,1)S(1)}, u32[]{:S(2)}) copy-start(bf16[4,4,3,4,32,256]{5,4,3,2,1,0:T(8,128)(2,1)S(1)} %get-tuple-element.58.other_ref) | copy-start | bytes 9437188
  92.6 4.3 %collective-permute-start.21 = (bf16[512,768]{1,0:T(8,128)(2,1)S(1)}, bf16[512,768]{1,0:T(8,128)(2,1)S(1)}, u32[]{:S(2)}, u32[]{:S(2)}) collective-permute-start(bf16[512,768]{1,0:T(8,128)(2,1)S(1)} %get-tuple-element.44.turned_ref), channel_id=1, source_target_pairs={{0,16},{16,0},{1,17},{17,1},{2,18},{18,2},{3,19},{19,3},{4,20},{20... | collective-permute-start | bytes 2359304 | tf_op jit(solution)/shard_map/ppermute | solution.py:22
  92.8 4.2 %collective-permute-start.22 = (bf16[2,384,256]{2,1,0:T(8,128)(2,1)S(1)}, bf16[2,384,256]{2,1,0:T(8,128)(2,1)S(1)}, u32[]{:S(2)}, u32[]{:S(2)}) collective-permute-start(bf16[2,384,256]{2,1,0:T(8,128)(2,1)S(1)} %get-tuple-element.49), channel_id=1, source_target_pairs={{0,16},{16,0},{1,17},{17,1},{2,18},{18,2},{3,19},{19,3},{4,20},{20... | collective-permute-start | bytes 1179656 | tf_op jit(solution)/shard_map/ppermute | solution.py:22
  101.6 12.1 %collective-permute-start.23 = (bf16[2,4,3,2,32,256]{5,4,3,2,1,0:T(8,128)(2,1)S(1)}, bf16[2,4,3,2,32,256]{5,4,3,2,1,0:T(8,128)(2,1)S(1)}, u32[]{:S(2)}, u32[]{:S(2)}) collective-permute-start(bf16[2,4,3,2,32,256]{5,4,3,2,1,0:T(8,128)(2,1)S(1)} %get-tuple-element.51), channel_id=1, source_target_pairs={{0,64},{64,0},{128,192},{192,128},{16,208},{80,144},{144,80},{208,... | collective-permute-start | bytes 2359304 | tf_op jit(solution)/shard_map/ppermute | solution.py:35
  108.9 12.7 %collective-permute-start.27 = (bf16[2,4,3,2,32,256]{5,4,3,2,1,0:T(8,128)(2,1)S(1)}, bf16[2,4,3,2,32,256]{5,4,3,2,1,0:T(8,128)(2,1)S(1)}, u32[]{:S(2)}, u32[]{:S(2)}) collective-permute-start(bf16[2,4,3,2,32,256]{5,4,3,2,1,0:T(8,128)(2,1)S(1)} %get-tuple-element.53), channel_id=1, source_target_pairs={{0,1},{1,0},{2,3},{3,2},{16,19},{17,18},{18,17},{19,16},{4,5},{5,4... | collective-permute-start | bytes 2359304 | tf_op jit(solution)/shard_map/ppermute | solution.py:35
  113.9 7.9 %collective-permute-start.24 = (bf16[4,3,2,32,256]{4,3,2,1,0:T(8,128)(2,1)S(1)}, bf16[4,3,2,32,256]{4,3,2,1,0:T(8,128)(2,1)S(1)}, u32[]{:S(2)}, u32[]{:S(2)}) collective-permute-start(bf16[4,3,2,32,256]{4,3,2,1,0:T(8,128)(2,1)S(1)} %fusion), channel_id=1, source_target_pairs={{0,192},{64,128},{128,64},{192,0},{16,80},{80,16},{144,208},{208,1... | collective-permute-start | bytes 1179656 | tf_op jit(solution)/shard_map/ppermute | solution.py:35
  121.7 9.3 %collective-permute-start.28 = (bf16[4,3,2,32,256]{4,3,2,1,0:T(8,128)(2,1)S(1)}, bf16[4,3,2,32,256]{4,3,2,1,0:T(8,128)(2,1)S(1)}, u32[]{:S(2)}, u32[]{:S(2)}) collective-permute-start(bf16[4,3,2,32,256]{4,3,2,1,0:T(8,128)(2,1)S(1)} %fusion.1), channel_id=1, source_target_pairs={{0,3},{1,2},{2,1},{3,0},{16,17},{17,16},{18,19},{19,18},{4,7},{5,6... | collective-permute-start | bytes 1179656 | tf_op jit(solution)/shard_map/ppermute | solution.py:35
  122.0 15.1 %collective-permute-start.25 = (f32[2,3,2,32,256]{4,3,2,1,0:T(8,128)S(1)}, f32[2,3,2,32,256]{4,3,2,1,0:T(8,128)S(1)}, u32[]{:S(2)}, u32[]{:S(2)}) collective-permute-start(f32[2,3,2,32,256]{4,3,2,1,0:T(8,128)S(1)} %get-tuple-element.64), channel_id=1, source_target_pairs={{0,1},{1,0},{2,3},{3,2},{16,19},{17,18},{18,17},{19,16},{4,5},{5,4... | collective-permute-start | bytes 1179656 | tf_op jit(solution)/shard_map/ppermute | solution.py:35
  131.2 7.9 %collective-permute-start.29 = (f32[2,3,2,32,256]{4,3,2,1,0:T(8,128)S(1)}, f32[2,3,2,32,256]{4,3,2,1,0:T(8,128)S(1)}, u32[]{:S(2)}, u32[]{:S(2)}) collective-permute-start(f32[2,3,2,32,256]{4,3,2,1,0:T(8,128)S(1)} %get-tuple-element.66), channel_id=1, source_target_pairs={{0,64},{64,0},{128,192},{192,128},{16,208},{80,144},{144,80},{208,... | collective-permute-start | bytes 1179656 | tf_op jit(solution)/shard_map/ppermute | solution.py:35
  131.4 17.1 %collective-permute-start.31 = (bf16[2,1,192,512]{3,2,1,0:T(8,128)(2,1)S(1)}, bf16[2,1,192,512]{3,2,1,0:T(8,128)(2,1)S(1)}, u32[]{:S(2)}, u32[]{:S(2)}) collective-permute-start(bf16[2,1,192,512]{3,2,1,0:T(8,128)(2,1)S(1)} %get-tuple-element.78), channel_id=1, source_target_pairs={{0,1},{1,2},{2,3},{3,4},{4,5},{5,6},{6,7},{7,8},{8,9},{9,10},{10,1... | collective-permute-start | bytes 1179656 | tf_op jit(solution)/shard_map/ppermute | solution.py:85
  131.7 16.7 %collective-permute-start.32 = (bf16[2,1,192,512]{3,2,1,0:T(8,128)(2,1)S(1)}, bf16[2,1,192,512]{3,2,1,0:T(8,128)(2,1)S(1)}, u32[]{:S(2)}, u32[]{:S(2)}) collective-permute-start(bf16[2,1,192,512]{3,2,1,0:T(8,128)(2,1)S(1)} %get-tuple-element.77), channel_id=1, source_target_pairs={{1,0},{2,1},{3,2},{4,3},{5,4},{6,5},{7,6},{8,7},{9,8},{10,9},{11,1... | collective-permute-start | bytes 1179656 | tf_op jit(solution)/shard_map/ppermute | solution.py:86
  137.2 7.1 %collective-permute-start.26 = (f32[3,2,32,256]{3,2,1,0:T(8,128)S(1)}, f32[3,2,32,256]{3,2,1,0:T(8,128)S(1)}, u32[]{:S(2)}, u32[]{:S(2)}) collective-permute-start(f32[3,2,32,256]{3,2,1,0:T(8,128)S(1)} %fusion.6), channel_id=1, source_target_pairs={{0,3},{1,2},{2,1},{3,0},{16,17},{17,16},{18,19},{19,18},{4,7},{5,6... | collective-permute-start | bytes 589832 | tf_op jit(solution)/shard_map/ppermute | solution.py:35
  139.2 5.1 %collective-permute-start.30 = (f32[3,2,32,256]{3,2,1,0:T(8,128)S(1)}, f32[3,2,32,256]{3,2,1,0:T(8,128)S(1)}, u32[]{:S(2)}, u32[]{:S(2)}) collective-permute-start(f32[3,2,32,256]{3,2,1,0:T(8,128)S(1)} %fusion.2), channel_id=1, source_target_pairs={{0,192},{64,128},{128,64},{192,0},{16,80},{80,16},{144,208},{208,1... | collective-permute-start | bytes 589832 | tf_op jit(solution)/shard_map/ppermute | solution.py:35
  145.1 13.6 %all-to-all-start = ((bf16[8,3,16,256]{3,2,1,0:T(8,128)(2,1)}), bf16[8,3,16,256]{3,2,1,0:T(8,128)(2,1)S(1)}, u32[]{:S(2)}, u32[]{:S(2)}) async-start(bf16[8,3,16,256]{3,2,1,0:T(8,128)(2,1)} %bitcast.49), calls=%async_computation | async-start | bytes 393216 | tf_op jit(solution)/shard_map/all_to_all | solution.py:440
  149.9 1.9 %copy-start.6 = (bf16[4,4,3,4,32,256]{5,4,3,2,1,0:T(8,128)(2,1)S(1)}, bf16[4,4,3,4,32,256]{5,4,3,2,1,0:T(8,128)(2,1)}, u32[]{:S(2)}) copy-start(bf16[4,4,3,4,32,256]{5,4,3,2,1,0:T(8,128)(2,1)} %copy-done.5) | copy-start | bytes 9437188
  149.9 2.8 %copy-start.9 = (bf16[4,4,3,4,32,256]{5,4,3,2,1,0:T(8,128)(2,1)S(1)}, bf16[4,4,3,4,32,256]{5,4,3,2,1,0:T(8,128)(2,1)}, u32[]{:S(2)}) copy-start(bf16[4,4,3,4,32,256]{5,4,3,2,1,0:T(8,128)(2,1)} %copy-done.8) | copy-start | bytes 9437188
  156.5 2.2 %copy-start.2 = (bf16[3,2,4,192,512]{4,3,2,1,0:T(8,128)(2,1)}, bf16[3,2,4,192,512]{4,3,2,1,0:T(8,128)(2,1)S(1)}, u32[]{:S(2)}) copy-start(bf16[3,2,4,192,512]{4,3,2,1,0:T(8,128)(2,1)S(1)} %pad_maximum_fusion.1.x_ref) | copy-start | bytes 14155780
  159.5 19.3 %all-to-all-start.1 = ((f32[8,3,16,256]{3,2,1,0:T(8,128)}), f32[8,3,16,256]{3,2,1,0:T(8,128)S(1)}, u32[]{:S(2)}, u32[]{:S(2)}) async-start(f32[8,3,16,256]{3,2,1,0:T(8,128)} %broadcast_in_dim.30), calls=%async_computation.1 | async-start | bytes 786432 | tf_op jit(solution)/shard_map/all_to_all | solution.py:73
  169.0 2.3 %copy-start.3 = (bf16[3,2,4,192,512]{4,3,2,1,0:T(8,128)(2,1)S(1)}, bf16[3,2,4,192,512]{4,3,2,1,0:T(8,128)(2,1)}, u32[]{:S(2)}) copy-start(bf16[3,2,4,192,512]{4,3,2,1,0:T(8,128)(2,1)} %copy-done.2) | copy-start | bytes 14155780
  171.3 1.9 %copy-start.7 = (bf16[4,4,3,4,32,256]{5,4,3,2,1,0:T(8,128)(2,1)S(1)}, bf16[4,4,3,4,32,256]{5,4,3,2,1,0:T(8,128)(2,1)}, u32[]{:S(2)}) copy-start(bf16[4,4,3,4,32,256]{5,4,3,2,1,0:T(8,128)(2,1)} %copy-done.5) | copy-start | bytes 9437188
  173.2 1.9 %copy-start.10 = (bf16[4,4,3,4,32,256]{5,4,3,2,1,0:T(8,128)(2,1)S(1)}, bf16[4,4,3,4,32,256]{5,4,3,2,1,0:T(8,128)(2,1)}, u32[]{:S(2)}) copy-start(bf16[4,4,3,4,32,256]{5,4,3,2,1,0:T(8,128)(2,1)} %copy-done.8) | copy-start | bytes 9437188
  178.9 6.7 %collective-permute-start.33 = (f32[8,3,16,256]{3,2,1,0:T(8,128)S(1)}, f32[8,3,16,256]{3,2,1,0:T(8,128)S(1)}, u32[]{:S(2)}, u32[]{:S(2)}) collective-permute-start(f32[8,3,16,256]{3,2,1,0:T(8,128)S(1)} %all-to-all-done.1), channel_id=1, source_target_pairs={{0,16},{16,0},{1,17},{17,1},{2,18},{18,2},{3,19},{19,3},{4,20},{20... | collective-permute-start | bytes 1179656 | tf_op jit(solution)/shard_map/ppermute | solution.py:22

commit v8 on v4

--- a/solution.py
+++ b/solution.py
@@ -15,7 +15,7 @@
 VMEM = pl.BlockSpec(memory_space=pltpu.VMEM)
 ANY = pl.BlockSpec(memory_space=pl.ANY)
 SMEM = pl.BlockSpec(memory_space=pltpu.SMEM)
-PARAMS = pltpu.CompilerParams(vmem_limit_bytes=12 * 1024 * 1024)
+PARAMS = pltpu.CompilerParams(vmem_limit_bytes=24 * 1024 * 1024)
 
 
 def swap(block):
@@ -110,7 +110,7 @@
     return pl.ds(pl.multiple_of(index * half, half), half)
 
 
-def assemble(info_ref, parts, kernel_ref, sems):
+def assemble(info_ref, parts, kernel_ref, others, sems):
     copies = []
     for pair in range(2):
         for j in range(2):
@@ -125,6 +125,10 @@
     copies = [
         pltpu.make_async_copy(source, target, sems.at[i])
         for i, (source, target) in enumerate(copies)
+    ]
+    copies += [
+        pltpu.make_async_copy(source, target, sems.at[32 + i])
+        for i, (source, target) in enumerate(others)
     ]
     for copy in copies:
         copy.start()
@@ -168,17 +172,17 @@
     lax.fori_loop(0, frames, blend, 0)
 
 
-def first_kernel(info_ref, x_ref, cot_ref, *refs):
-    parts, (pre_ref, slope_ref, kernel_ref, sems) = refs[:4], refs[4:]
-    assemble(info_ref, parts, kernel_ref, sems)
+def first_kernel(info_ref, x_hbm, cot_hbm, *refs):
+    parts, (pre_ref, slope_ref, kernel_ref, x_ref, cot_ref, sems) = refs[:4], refs[4:]
+    assemble(info_ref, parts, kernel_ref, ((x_hbm, x_ref), (cot_hbm, cot_ref)), sems)
     add_terms(info_ref[0], x_ref, cot_ref, kernel_ref, pre_ref, slope_ref, None)
 
 
-def second_kernel(info_ref, x_ref, cot_ref, *refs):
+def second_kernel(info_ref, x_hbm, cot_hbm, *refs):
     parts, (start_ref, mine_ref), refs = refs[:4], refs[4:6], refs[6:]
     hid_mine_ref, hid_other_ref, slope_ref, turned_ref, kernel_ref = refs[:5]
-    pre_ref, other_ref, work_ref, sems = refs[5:]
-    assemble(info_ref, parts, kernel_ref, sems)
+    pre_ref, other_ref, work_ref, x_ref, cot_ref, sems = refs[5:]
+    assemble(info_ref, parts, kernel_ref, ((x_hbm, x_ref), (cot_hbm, cot_ref)), sems)
     other = info_ref[0]
     add_terms(other, x_ref, cot_ref, kernel_ref, pre_ref, other_ref, start_ref)
     frames, block, chans = pre_ref.shape
@@ -214,13 +218,17 @@
     part = jax.ShapeDtypeStruct((frames, block, half), jnp.float32)
     hid = jax.ShapeDtypeStruct((frames, block, half), jnp.bfloat16)
     kernel = jax.ShapeDtypeStruct((4, 4, 3, 4) + parts[0].shape[-2:], parts[0].dtype)
-    sems = pltpu.SemaphoreType.DMA((32,))
+    held = [
+        pltpu.VMEM(shifts.shape, shifts.dtype),
+        pltpu.VMEM(cot_pad.shape, cot_pad.dtype),
+        pltpu.SemaphoreType.DMA((34,)),
+    ]
     pre, mine, k_mine = pl.pallas_call(
         first_kernel,
         out_shape=(full, part, kernel),
-        in_specs=[SMEM, VMEM, VMEM] + [ANY] * 4,
+        in_specs=[SMEM] + [ANY] * 6,
         out_specs=(VMEM,) * 3,
-        scratch_shapes=[sems],
+        scratch_shapes=held,
         compiler_params=PARAMS,
         cost_estimate=pl.CostEstimate(flops=3200000000, bytes_accessed=12000000, transcendentals=0),
     )(infos[0], shifts, cot_pad, *parts)
@@ -233,14 +241,14 @@
             jax.ShapeDtypeStruct((chans, frames * block), jnp.bfloat16),
             kernel,
         ),
-        in_specs=[SMEM, VMEM, VMEM] + [ANY] * 4 + [VMEM] * 2,
+        in_specs=[SMEM] + [ANY] * 6 + [VMEM] * 2,
         out_specs=(VMEM,) * 5,
         scratch_shapes=[
             pltpu.VMEM(full.shape, jnp.float32),
             pltpu.VMEM(part.shape, jnp.float32),
             pltpu.VMEM(full.shape, jnp.float32),
-            sems,
-        ],
+        ]
+        + held,
         compiler_params=PARAMS,
         cost_estimate=pl.CostEstimate(flops=3200000000, bytes_accessed=15000000, transcendentals=0),
     )(infos[1], shifts, cot_pad, *parts_other, pre, mine)
@@ -389,8 +397,9 @@
     x_pair = swap(lax.dynamic_slice_in_dim(x_wide, (1 - core[0]) * half, half, axis=3))
     shifts = column_shifts(x_wide)
     cot_turned = cot_pad.reshape((frames + 2) * rows * width, chans).T
-    waited = (shifts, cot_pad, cot_turned)
-    parts, parts_other, (shifts, cot_pad, cot_turned) = kernel_parts(unit, waited)
+    waited = (shifts, cot_pad, cot_turned, x_pair)
+    parts, parts_other, waited = kernel_parts(unit, waited)
+    shifts, cot_pad, cot_turned, x_pair = waited
     cot_turned_pair = swap(cot_turned)
     cot_turned_pair, parts_other = lax.optimization_barrier((cot_turned_pair, parts_other))
 
@@ -417,18 +426,19 @@
     slope_edges, _ = lax.optimization_barrier((slope_edges, (sent_lower, sent_upper)))
     slope_wide = widened(slope_maps, slope_edges, SPACE, 1)
     shifts_slope = column_shifts(slope_wide)
-    grad = input_gradient(0, core, shifts_slope, cotangent, k_mine, k_other)
 
     came_lower = exchange(sent_lower, "x", 0)
     came_upper = exchange(sent_upper, "y", 0)
-    came_lower, grad = lax.optimization_barrier((came_lower, grad))
     passed = (lower[1] + widen(came_lower[1])).astype(jnp.bfloat16)
+    last_lower = exchange(passed, "x", 1)
     info, _ = lax.optimization_barrier((core, passed))
-    grad = input_gradient(1, info, shifts_slope, cotangent, k_mine, k_other, (grad,))
-    last_lower = exchange(passed, "x", 1)
+    grad = input_gradient(0, info, shifts_slope, cotangent, k_mine, k_other)
     came_upper, grad = lax.optimization_barrier((came_upper, grad))
     passed = (upper[1] + widen(came_upper[1])).astype(jnp.bfloat16)
     last_upper = exchange(passed, "y", 1)
+    info, _ = lax.optimization_barrier((core, passed))
+    grad = input_gradient(1, info, shifts_slope, cotangent, k_mine, k_other, (grad,))
+    last_lower, grad = lax.optimization_barrier((last_lower, grad))
 
     def total(terms, came, last, slots):
         return terms[0, slots] + widen(came[0, slots]) + widen(last[slots])
@@ -441,9 +451,11 @@
     terms = jnp.concatenate([lower, upper], axis=1)
     terms = terms.reshape(3, 4, 2, own // 2, half).transpose(1, 2, 0, 3, 4)
     terms = terms.reshape(8, 3, own // 2, half).astype(jnp.bfloat16)
-    terms = scattered(terms, ("zh", "zl"))
+
+    terms = lax.all_to_all(terms, ("zh", "zl"), 0, 0, tiled=True)
     pixels = count * lax.axis_size(TM) * lax.axis_size(SPACE)
-    terms = gathered(terms * (1.0 / math.sqrt(pixels)), ("x", "zl"))
+    terms = jnp.sum(widen(terms), axis=0) * (1.0 / math.sqrt(pixels))
+    terms = gathered(terms, ("x", "zl"))
     came = swap(terms)
     terms = jnp.concatenate(
         [jnp.where(core[0] == 0, terms, came), jnp.where(core[0] == 0, came, terms)], axis=3

time: 191 us -> 183 us (0.958)
  waiting for transfers between devices: 42.5 us -> 36.2 us
  starting transfers between devices: 61.4 us -> 55.7 us
  local copies, waits for them, and re-layouts: 11.2 us -> 15.9 us
    ppermute x3, waiting for transfers between devices: 6.27 us -> 0.01 us  [edges_of(): high = lax.ppermute(lax.slice_in_dim(block, 0, 1, axis=dim), axis, backward)]
    ppermute x16, starting transfers between devices: 17.8 us -> 14 us  [exchange(): return lax.ppermute(block, names, pairs)]
    ppermute x9, waiting for transfers between devices: 4.27 us -> 1.37 us  [swap(): return lax.ppermute(block, 'core', PAIR)]
    unnamed x16 -> x22, local copies, waits for them, and re-layouts: 2.41 us -> 5.3 us
    ppermute x3, waiting for transfers between devices: 0.01 us -> 2.05 us  [edges_of(): lax.ppermute(lax.slice_in_dim(block, size - 1, size, axis=dim), axis, for...]
  transfers between devices with their start and end apart: 34 -> 34, of which waited for: 14 -> 14; matrix products, arithmetic and copies ran while one was open for 13% -> 14% of each run, Pallas kernels for 17% -> 13%
where the time goes in v8:
time: 183 us
  starting transfers between devices  55.7 us (30%)
  waiting for transfers between devices  36.2 us (20%)
  Pallas kernels  32.4 us (18%)
  blocking collectives  23.2 us (13%)
  other arithmetic  18 us (10%)
  local copies, waits for them, and re-layouts  15.9 us (9%)
    ppermute x16, waiting for transfers between devices, exchange(): return lax.ppermute(block, names, pairs)  32.7 us
    ppermute x9, starting transfers between devices, swap(): return lax.ppermute(block, 'core', PAIR)  19.1 us
    ppermute x16, starting transfers between devices, exchange(): return lax.ppermute(block, names, pairs)  14 us
    all_to_all x1, blocking collectives, per_device(): terms = lax.all_to_all(terms, ('zh', 'zl'), 0, 0, tiled=True)  12.3 us
    ppermute x3, starting transfers between devices, edges_of(): high = lax.ppermute(lax.slice_in_dim(block, 0, 1, axis=dim), axis, backward)  11.7 us
    all_to_all x1, blocking collectives, gathered(): return lax.all_to_all(spread, axis, 0, 0, tiled=True)  10.9 us
    pallas_call x2, Pallas kernels, weight_terms(): pl.pallas_call(functools.partial(weight_kernel, upper), out_shape=(jax.Sh...  9.29 us
    ppermute x3, starting transfers between devices, kernel_unit(): slots.append(lax.ppermute(unit, 'zh', [(i, i ^ k) for i in range(4)]))  9.12 us
  transfers between devices with their start and end apart: 34, of which 14 were waited for; matrix products, arithmetic and copies ran while one was open for 14% of the time, Pallas kernels for 13%

profile of v8, /device:TPU:1, one launch (start us, length us, event | category | flops | bytes accessed | tf_op | source)
XLA Modules:
  0.0 182.7 jit_solution(7642133914220706385)
XLA Ops:
  0.6 0.8 fusion.10
  1.5 6.9 %collective-permute-start = (bf16[3,32,256]{2,1,0:T(8,128)(2,1)S(1)}, bf16[3,32,256]{2,1,0:T(8,128)(2,1)S(1)}, u32[]{:S(2)}, u32[]{:S(2)}) collective-permute-start(bf16[3,32,256]{2,1,0:T(8,128)(2,1)S(1)} %fusion.10), channel_id=1, source_target_pairs={{0,12},{4,8},{8,4},{12,0},{1,13},{5,9},{9,5},{13,1},{2,14},{6,10},... | collective-permute-start | bytes 147464 | tf_op jit(solution)/shard_map/ppermute | solution.py:367
  8.4 1.0 collective-permute-start.1
  9.4 1.2 collective-permute-start.2
  10.6 1.2 fusion.22
  11.8 6.0 %collective-permute-start.12 = (bf16[2,1,192,512]{3,2,1,0:T(8,128)(2,1)S(1)}, bf16[2,1,192,512]{3,2,1,0:T(8,128)(2,1)S(1)}, u32[]{:S(2)}, u32[]{:S(2)}) collective-permute-start(bf16[2,1,192,512]{3,2,1,0:T(8,128)(2,1)S(1)} %get-tuple-element.88), channel_id=1, source_target_pairs={{1,0},{2,1},{3,2},{4,3},{5,4},{6,5},{7,6},{8,7},{9,8},{10,9},{11,1... | collective-permute-start | bytes 1179656 | tf_op jit(solution)/shard_map/ppermute | solution.py:86
  17.9 2.6 %collective-permute-start.7 = (bf16[2,3,32,256]{3,2,1,0:T(8,128)(2,1)S(1)}, bf16[2,3,32,256]{3,2,1,0:T(8,128)(2,1)S(1)}, u32[]{:S(2)}, u32[]{:S(2)}) collective-permute-start(bf16[2,3,32,256]{3,2,1,0:T(8,128)(2,1)S(1)} %get-tuple-element.98), channel_id=1, source_target_pairs={{0,64},{64,0},{128,192},{192,128},{16,208},{80,144},{144,80},{208,... | collective-permute-start | bytes 294920 | tf_op jit(solution)/shard_map/ppermute | solution.py:35
  20.4 1.4 collective-permute-start.3
  21.8 0.8 collective-permute-done.7
  23.0 7.1 %collective-permute-done.3 = bf16[2,3,32,256]{3,2,1,0:T(8,128)(2,1)S(1)} collective-permute-done((bf16[2,3,32,256]{3,2,1,0:T(8,128)(2,1)S(1)}, bf16[2,3,32,256]{3,2,1,0:T(8,128)(2,1)S(1)}, u32[]{:S(2)}, u32[]{:S(2)}) %collective-permute-start.3) | collective-permute-done | bytes 98336 | tf_op jit(solution)/shard_map/ppermute | solution.py:35
  30.1 0.7 pad_maximum_fusion.11
  30.8 0.8 fusion.21
  31.6 0.7 copy-done.10
  32.3 1.7 collective-permute-start.13
  34.1 1.7 fusion.13
  36.2 1.9 %fusion.14 = (bf16[1,4,2,3,32,256]{5,4,3,2,1,0:T(8,128)(2,1)}, bf16[4,2,3,32,256]{4,3,2,1,0:T(8,128)(2,1)}) fusion(bf16[2,2,3,32,256]{4,3,2,1,0:T(8,128)(2,1)} %collective-permute-done.4, bf16[1,2,3,32,256]{4,3,2,1,0:T(8,128)(2,1)S(1)} %bitcast.119, bf16[1,2,3,32,256]{4,3,2,1,0:T(8,128)(2,1)S(1)} %get-tuple-element.99), kind=kLoop, calls=%fused_computation.74 | loop fusion | flops 393216 | bytes 1179648 | tf_op jit(solution)/shard_map/stack | solution.py:67
  38.1 3.6 %collective-permute-start.5 = (bf16[4,2,3,32,256]{4,3,2,1,0:T(8,128)(2,1)}, bf16[4,2,3,32,256]{4,3,2,1,0:T(8,128)(2,1)}, u32[]{:S(2)}, u32[]{:S(2)}) collective-permute-start(bf16[4,2,3,32,256]{4,3,2,1,0:T(8,128)(2,1)} %get-tuple-element.92), channel_id=1, source_target_pairs={{0,64},{64,0},{128,192},{192,128},{16,208},{80,144},{144,80},{208,... | collective-permute-start | bytes 1179656 | tf_op jit(solution)/shard_map/ppermute | solution.py:35
  41.9 1.4 fusion.16
  43.2 1.0 constant_dynamic-slice_fusion
  44.2 0.7 collective-permute-start.15
  44.9 1.0 broadcast_select_fusion
  46.0 1.4 pad_maximum_fusion.4.cot_hbm
  47.3 1.7 copy.13
  49.1 1.2 pad_maximum_fusion.7.refs_2_
  50.3 0.6 collective-permute-start.10
  50.9 2.0 %pad_maximum_fusion.6.refs_0_ = bf16[2,4,2,3,32,256]{5,4,3,2,1,0:T(8,128)(2,1)} fusion(bf16[1,4,2,3,32,256]{5,4,3,2,1,0:T(8,128)(2,1)} %bitcast.16, bf16[1,4,2,3,32,256]{5,4,3,2,1,0:T(8,128)(2,1)S(1)} %copy-done.9), kind=kLoop, calls=%fused_computation.10 | loop fusion | flops 393216 | bytes 1572864 | tf_op jit(solution)/shard_map/stack | solution.py:67
  52.8 0.6 collective-permute-start.6
  53.4 0.5 fusion.18
  53.9 0.5 pad_bitcast_fusion.2
  54.5 0.8 copy-done.7
  55.3 2.4 %pad_maximum_fusion.x_hbm.x_ref = bf16[3,2,4,192,512]{4,3,2,1,0:T(8,128)(2,1)} fusion(bf16[1,2,4,192,512]{4,3,2,1,0:T(8,128)(2,1)S(1)} %get-tuple-element.101, bf16[1,2,4,192,512]{4,3,2,1,0:T(8,128)(2,1)S(1)} %copy-done.7, bf16[1,2,4,192,512]{4,3,2,1,0:T(8,128)(2,1)S(1)} %get-tuple-element.102), kind=kLoop, calls=%fused_computation | loop fusion | flops 4718592 | bytes 9437184 | tf_op jit(solution)/shard_map/stack | solution.py:100
  57.8 3.9 %collective-permute-done.10.refs_3_ = bf16[2,4,2,3,32,256]{5,4,3,2,1,0:T(8,128)(2,1)} collective-permute-done((bf16[2,4,2,3,32,256]{5,4,3,2,1,0:T(8,128)(2,1)S(1)}, bf16[2,4,2,3,32,256]{5,4,3,2,1,0:T(8,128)(2,1)}, u32[]{:S(2)}, u32[]{:S(2)}) %collective-permute-start.10) | collective-permute-done | bytes 786464 | tf_op jit(solution)/shard_map/ppermute | solution.py:35
  61.6 2.6 %collective-permute-done.6.refs_1_ = bf16[2,4,2,3,32,256]{5,4,3,2,1,0:T(8,128)(2,1)} collective-permute-done((bf16[2,4,2,3,32,256]{5,4,3,2,1,0:T(8,128)(2,1)}, bf16[2,4,2,3,32,256]{5,4,3,2,1,0:T(8,128)(2,1)}, u32[]{:S(2)}, u32[]{:S(2)}) %collective-permute-start.6) | collective-permute-done | bytes 786464 | tf_op jit(solution)/shard_map/ppermute | solution.py:35
  64.3 6.1 %collective-permute-start.16 = (bf16[512,1536]{1,0:T(8,128)(2,1)S(1)}, bf16[512,1536]{1,0:T(8,128)(2,1)}, u32[]{:S(2)}, u32[]{:S(2)}) collective-permute-start(bf16[512,1536]{1,0:T(8,128)(2,1)S(1)} %bitcast.100), channel_id=1, source_target_pairs={{0,16},{16,0},{1,17},{17,1},{2,18},{18,2},{3,19},{19,3},{4,20},{20... | collective-permute-start | bytes 4718600 | tf_op jit(solution)/shard_map/ppermute | solution.py:22
  70.4 0.5 collective-permute-start.17
  71.7 2.3 %copy-done = bf16[3,2,4,192,512]{4,3,2,1,0:T(8,128)(2,1)S(1)} copy-done((bf16[3,2,4,192,512]{4,3,2,1,0:T(8,128)(2,1)S(1)}, bf16[3,2,4,192,512]{4,3,2,1,0:T(8,128)(2,1)}, u32[]{:S(2)}) %copy-start) | copy-done | bytes 4718616
  74.0 1.4 copy-done.3
  75.4 6.8 %shard_map.67 = (f32[2,384,512]{2,1,0:T(8,128)S(1)}, f32[2,384,256]{2,1,0:T(8,128)S(1)}, bf16[4,4,3,4,32,256]{5,4,3,2,1,0:T(8,128)(2,1)S(1)}) custom-call(s32[9]{0:T(128)S(1)} %concatenate.63.info_ref, bf16[3,2,4,192,512]{4,3,2,1,0:T(8,128)(2,1)S(1)} %copy-done, bf16[4,2,192,512]{3,2,1,0:T(8,128)(2,1)S(1)} %copy-done.3, ...), custom_call_target="tpu_custom_call" | custom-call | flops 3200000000 | bytes 12000000 | tf_op jit(solution)/shard_map/pallas_call | solution.py:226
  82.3 8.8 %shard_map.68 = (bf16[2,384,256]{2,1,0:T(8,128)(2,1)S(1)}, bf16[2,384,256]{2,1,0:T(8,128)(2,1)S(1)}, bf16[2,384,512]{2,1,0:T(8,128)(2,1)S(1)}, bf16[512,768]{1,0...) custom-call(s32[9]{0:T(128)S(1)} %concatenate.55.info_ref, bf16[3,2,4,192,512]{4,3,2,1,0:T(8,128)(2,1)S(1)} %copy-done.1, ...), custom_call_target="tpu_custom_call" | custom-call | flops 3200000000 | bytes 15000000 | tf_op jit(solution)/shard_map/pallas_call | solution.py:235
  91.8 5.7 %collective-permute-start.27 = (bf16[2,1,192,512]{3,2,1,0:T(8,128)(2,1)S(1)}, bf16[2,1,192,512]{3,2,1,0:T(8,128)(2,1)S(1)}, u32[]{:S(2)}, u32[]{:S(2)}) collective-permute-start(bf16[2,1,192,512]{3,2,1,0:T(8,128)(2,1)S(1)} %get-tuple-element.81), channel_id=1, source_target_pairs={{1,0},{2,1},{3,2},{4,3},{5,4},{6,5},{7,6},{8,7},{9,8},{10,9},{11,1... | collective-permute-start | bytes 1179656 | tf_op jit(solution)/shard_map/ppermute | solution.py:86
  97.5 1.7 fusion.20
  99.5 1.4 pad_maximum_fusion.2.x_pair_ref
  100.9 4.6 %shard_map.69 = (f32[4,4,3,2,32,256]{5,4,3,2,1,0:T(8,128)S(1)}, bf16[2,4,3,2,32,256]{5,4,3,2,1,0:T(8,128)(2,1)S(1)}) custom-call(s32[9]{0:T(128)S(1)} %pad_add_fusion.info_ref, bf16[512,768]{1,0:T(8,128)(2,1)S(1)} %get-tuple-element.46.turned_ref, bf16[512,768]{1,0:T(8,128)(2,1)S(1)} %collective-permute-done.21.turned_pair_ref, ...), custom_call_target="tpu_custom_call" | custom-call | flops 2400000000 | bytes 16000000 | tf_op jit(solution)/shard_map/pallas_call | solution.py:310
  105.5 2.8 %collective-permute-start.23 = (bf16[2,4,3,2,32,256]{5,4,3,2,1,0:T(8,128)(2,1)S(1)}, bf16[2,4,3,2,32,256]{5,4,3,2,1,0:T(8,128)(2,1)S(1)}, u32[]{:S(2)}, u32[]{:S(2)}) collective-permute-start(bf16[2,4,3,2,32,256]{5,4,3,2,1,0:T(8,128)(2,1)S(1)} %get-tuple-element.53), channel_id=1, source_target_pairs={{0,64},{64,0},{128,192},{192,128},{16,208},{80,144},{144,80},{208,... | collective-permute-start | bytes 2359304 | tf_op jit(solution)/shard_map/ppermute | solution.py:35
  108.4 4.6 %shard_map.70 = (f32[4,4,3,2,32,256]{5,4,3,2,1,0:T(8,128)S(1)}, bf16[2,4,3,2,32,256]{5,4,3,2,1,0:T(8,128)(2,1)S(1)}) custom-call(s32[9]{0:T(128)S(1)} %pad_add_fusion.info_ref, bf16[512,768]{1,0:T(8,128)(2,1)S(1)} %get-tuple-element.46.turned_ref, bf16[512,768]{1,0:T(8,128)(2,1)S(1)} %collective-permute-done.21.turned_pair_ref, ...), custom_call_target="tpu_custom_call" | custom-call | flops 2400000000 | bytes 16000000 | tf_op jit(solution)/shard_map/pallas_call | solution.py:310
  113.1 2.0 %collective-permute-done.26 = bf16[2,1,192,512]{3,2,1,0:T(8,128)(2,1)S(1)} collective-permute-done((bf16[2,1,192,512]{3,2,1,0:T(8,128)(2,1)S(1)}, bf16[2,1,192,512]{3,2,1,0:T(8,128)(2,1)S(1)}, u32[]{:S(2)}, u32[]{:S(2)}) %collective-permute-start.26) | collective-permute-done | bytes 393248 | tf_op jit(solution)/shard_map/ppermute | solution.py:85
  115.5 0.5 fusion.17
  116.5 0.6 pad_maximum_fusion.1.x_ref
  117.1 0.8 collective-permute-done.23
  118.1 3.8 %shard_map.71.refs_0_ = f32[2,384,512]{2,1,0:T(8,128)} custom-call(s32[1]{0:T(128)} %bitcast.info_ref, bf16[3,2,4,192,512]{4,3,2,1,0:T(8,128)(2,1)S(1)} %pad_maximum_fusion.1.x_ref, bf16[2,384,512]{2,1,0:T(8,128)(2,1)S(1)} %bitcast.103, bf16[4,4,3,4,32,256]{5,4,3,2,1,0:T(8,128)(2,1)S(1)} %get-tuple-element.60.mine_ref, ...), custom_call_target="tpu_custom_call" | custom-call | flops 1800000000 | bytes 8000000 | tf_op jit(solution)/shard_map/pallas_call | solution.py:346
  121.9 3.6 %collective-permute-done.25 = bf16[2,4,3,2,32,256]{5,4,3,2,1,0:T(8,128)(2,1)S(1)} collective-permute-done((bf16[2,4,3,2,32,256]{5,4,3,2,1,0:T(8,128)(2,1)S(1)}, bf16[2,4,3,2,32,256]{5,4,3,2,1,0:T(8,128)(2,1)S(1)}, u32[]{:S(2)}, u32[]{:S(2)}) %collective-permute-start.25) | collective-permute-done | bytes 786464 | tf_op jit(solution)/shard_map/ppermute | solution.py:35
  125.7 3.8 %shard_map.72 = f32[2,384,512]{2,1,0:T(8,128)} custom-call(s32[1]{0:T(128)} %bitcast.info_ref, bf16[3,2,4,192,512]{4,3,2,1,0:T(8,128)(2,1)S(1)} %pad_maximum_fusion.1.x_ref, bf16[2,384,512]{2,1,0:T(8,128)(2,1)S(1)} %bitcast.104, bf16[4,4,3,4,32,256]{5,4,3,2,1,0:T(8,128)(2,1)S(1)} %get-tuple-element.60.mine_ref, ...), custom_call_target="tpu_custom_call", output_to_operand_aliasing={{}: (5, {})} | custom-call | flops 1800000000 | bytes 8000000 | tf_op jit(solution)/shard_map/pallas_call | solution.py:346
  129.8 2.8 %collective-permute-done.30 = bf16[4,3,2,32,256]{4,3,2,1,0:T(8,128)(2,1)S(1)} collective-permute-done((bf16[4,3,2,32,256]{4,3,2,1,0:T(8,128)(2,1)S(1)}, bf16[4,3,2,32,256]{4,3,2,1,0:T(8,128)(2,1)S(1)}, u32[]{:S(2)}, u32[]{:S(2)}) %collective-permute-start.30) | collective-permute-done | bytes 393248 | tf_op jit(solution)/shard_map/ppermute | solution.py:35
  132.8 1.2 collective-permute-start.31
  134.0 4.1 %collective-permute-done.28 = f32[2,3,2,32,256]{4,3,2,1,0:T(8,128)S(1)} collective-permute-done((f32[2,3,2,32,256]{4,3,2,1,0:T(8,128)S(1)}, f32[2,3,2,32,256]{4,3,2,1,0:T(8,128)S(1)}, u32[]{:S(2)}, u32[]{:S(2)}) %collective-permute-start.28) | collective-permute-done | bytes 393248 | tf_op jit(solution)/shard_map/ppermute | solution.py:35
  138.2 2.5 %collective-permute-done.31 = f32[2,3,2,32,256]{4,3,2,1,0:T(8,128)S(1)} collective-permute-done((f32[2,3,2,32,256]{4,3,2,1,0:T(8,128)S(1)}, f32[2,3,2,32,256]{4,3,2,1,0:T(8,128)S(1)}, u32[]{:S(2)}, u32[]{:S(2)}) %collective-permute-start.31) | collective-permute-done | bytes 393248 | tf_op jit(solution)/shard_map/ppermute | solution.py:35
  140.8 2.1 %collective-permute-done.29 = f32[3,2,32,256]{3,2,1,0:T(8,128)S(1)} collective-permute-done((f32[3,2,32,256]{3,2,1,0:T(8,128)S(1)}, f32[3,2,32,256]{3,2,1,0:T(8,128)S(1)}, u32[]{:S(2)}, u32[]{:S(2)}) %collective-permute-start.29) | collective-permute-done | bytes 196640 | tf_op jit(solution)/shard_map/ppermute | solution.py:35
  143.0 2.3 %collective-permute-done.32 = f32[3,2,32,256]{3,2,1,0:T(8,128)S(1)} collective-permute-done((f32[3,2,32,256]{3,2,1,0:T(8,128)S(1)}, f32[3,2,32,256]{3,2,1,0:T(8,128)S(1)}, u32[]{:S(2)}, u32[]{:S(2)}) %collective-permute-start.32) | collective-permute-done | bytes 196640 | tf_op jit(solution)/shard_map/ppermute | solution.py:35
  145.4 12.3 %all_to_all.10 = bf16[8,3,16,256]{3,2,1,0:T(8,128)(2,1)S(1)} all-to-all(bf16[8,3,16,256]{3,2,1,0:T(8,128)(2,1)S(1)} %bitcast.116), channel_id=1, replica_groups=mesh['x'=4,'zl'=2,'core'=2,'zh'=4,'y'=4] {'zh','zl'}, dimensions={0} | all-to-all | bytes 393216 | tf_op jit(solution)/shard_map/all_to_all | solution.py:455
  157.8 10.9 %all_to_all.11 = f32[8,3,16,256]{3,2,1,0:T(8,128)S(1)} all-to-all(f32[8,3,16,256]{3,2,1,0:T(8,128)S(1)} %broadcast_in_dim.30), channel_id=1, replica_groups=mesh['x'=4,'zl'=2,'core'=2,'zh'=4,'y'=4] {'x','zl'}, dimensions={0} | all-to-all | bytes 786432 | tf_op jit(solution)/shard_map/all_to_all | solution.py:73
  168.7 10.8 %collective-permute-start.33 = (f32[8,3,16,256]{3,2,1,0:T(8,128)S(1)}, f32[8,3,16,256]{3,2,1,0:T(8,128)S(1)}, u32[]{:S(2)}, u32[]{:S(2)}) collective-permute-start(f32[8,3,16,256]{3,2,1,0:T(8,128)S(1)} %all_to_all.11), channel_id=1, source_target_pairs={{0,16},{16,0},{1,17},{17,1},{2,18},{18,2},{3,19},{19,3},{4,20},{20... | collective-permute-start | bytes 1179656 | tf_op jit(solution)/shard_map/ppermute | solution.py:22
  179.5 1.3 collective-permute-done.33
  181.1 0.9 copy.15
  182.0 0.7 copy.16
  (93 shorter events, 5.4 us)
Async XLA Ops:
  1.5 29.3 %copy-start.2 = (bf16[2,2,192,512]{3,2,1,0:T(8,128)(2,1)S(1)}, bf16[2,2,192,512]{3,2,1,0:T(8,128)(2,1)}, u32[]{:S(2)}) copy-start(bf16[2,2,192,512]{3,2,1,0:T(8,128)(2,1)} %param.5) | copy-start | bytes 2359300
  1.5 16.3 %collective-permute-start = (bf16[3,32,256]{2,1,0:T(8,128)(2,1)S(1)}, bf16[3,32,256]{2,1,0:T(8,128)(2,1)S(1)}, u32[]{:S(2)}, u32[]{:S(2)}) collective-permute-start(bf16[3,32,256]{2,1,0:T(8,128)(2,1)S(1)} %fusion.10), channel_id=1, source_target_pairs={{0,12},{4,8},{8,4},{12,0},{1,13},{5,9},{9,5},{13,1},{2,14},{6,10},... | collective-permute-start | bytes 147464 | tf_op jit(solution)/shard_map/ppermute | solution.py:367
  8.4 9.4 %collective-permute-start.1 = (bf16[3,32,256]{2,1,0:T(8,128)(2,1)S(1)}, bf16[3,32,256]{2,1,0:T(8,128)(2,1)S(1)}, u32[]{:S(2)}, u32[]{:S(2)}) collective-permute-start(bf16[3,32,256]{2,1,0:T(8,128)(2,1)S(1)} %fusion.10), channel_id=1, source_target_pairs={{0,8},{4,12},{8,0},{12,4},{1,9},{5,13},{9,1},{13,5},{2,10},{6,14},... | collective-permute-start | bytes 147464 | tf_op jit(solution)/shard_map/ppermute | solution.py:367
  9.4 8.4 %collective-permute-start.2 = (bf16[3,32,256]{2,1,0:T(8,128)(2,1)S(1)}, bf16[3,32,256]{2,1,0:T(8,128)(2,1)S(1)}, u32[]{:S(2)}, u32[]{:S(2)}) collective-permute-start(bf16[3,32,256]{2,1,0:T(8,128)(2,1)S(1)} %fusion.10), channel_id=1, source_target_pairs={{0,4},{4,0},{8,12},{12,8},{1,5},{5,1},{9,13},{13,9},{2,6},{6,2},{1... | collective-permute-start | bytes 147464 | tf_op jit(solution)/shard_map/ppermute | solution.py:367
  11.8 26.4 %collective-permute-start.12 = (bf16[2,1,192,512]{3,2,1,0:T(8,128)(2,1)S(1)}, bf16[2,1,192,512]{3,2,1,0:T(8,128)(2,1)S(1)}, u32[]{:S(2)}, u32[]{:S(2)}) collective-permute-start(bf16[2,1,192,512]{3,2,1,0:T(8,128)(2,1)S(1)} %get-tuple-element.88), channel_id=1, source_target_pairs={{1,0},{2,1},{3,2},{4,3},{5,4},{6,5},{7,6},{8,7},{9,8},{10,9},{11,1... | collective-permute-start | bytes 1179656 | tf_op jit(solution)/shard_map/ppermute | solution.py:86
  17.8 24.0 %collective-permute-start.11 = (bf16[2,1,192,512]{3,2,1,0:T(8,128)(2,1)S(1)}, bf16[2,1,192,512]{3,2,1,0:T(8,128)(2,1)S(1)}, u32[]{:S(2)}, u32[]{:S(2)}) collective-permute-start(bf16[2,1,192,512]{3,2,1,0:T(8,128)(2,1)S(1)} %get-tuple-element.87), channel_id=1, source_target_pairs={{0,1},{1,2},{2,3},{3,4},{4,5},{5,6},{6,7},{7,8},{8,9},{9,10},{10,1... | collective-permute-start | bytes 1179656 | tf_op jit(solution)/shard_map/ppermute | solution.py:85
  17.9 4.8 %collective-permute-start.7 = (bf16[2,3,32,256]{3,2,1,0:T(8,128)(2,1)S(1)}, bf16[2,3,32,256]{3,2,1,0:T(8,128)(2,1)S(1)}, u32[]{:S(2)}, u32[]{:S(2)}) collective-permute-start(bf16[2,3,32,256]{3,2,1,0:T(8,128)(2,1)S(1)} %get-tuple-element.98), channel_id=1, source_target_pairs={{0,64},{64,0},{128,192},{192,128},{16,208},{80,144},{144,80},{208,... | collective-permute-start | bytes 294920 | tf_op jit(solution)/shard_map/ppermute | solution.py:35
  20.4 9.7 %collective-permute-start.3 = (bf16[2,3,32,256]{3,2,1,0:T(8,128)(2,1)S(1)}, bf16[2,3,32,256]{3,2,1,0:T(8,128)(2,1)S(1)}, u32[]{:S(2)}, u32[]{:S(2)}) collective-permute-start(bf16[2,3,32,256]{3,2,1,0:T(8,128)(2,1)S(1)} %get-tuple-element.100), channel_id=1, source_target_pairs={{0,1},{1,0},{2,3},{3,2},{16,19},{17,18},{18,17},{19,16},{4,5},{5,4... | collective-permute-start | bytes 294920 | tf_op jit(solution)/shard_map/ppermute | solution.py:35
  22.6 9.0 %collective-permute-start.8 = (bf16[2,2,3,32,256]{4,3,2,1,0:T(8,128)(2,1)S(1)}, bf16[2,2,3,32,256]{4,3,2,1,0:T(8,128)(2,1)S(1)}, u32[]{:S(2)}, u32[]{:S(2)}) collective-permute-start(bf16[2,2,3,32,256]{4,3,2,1,0:T(8,128)(2,1)S(1)} %pad_maximum_fusion.12), channel_id=1, source_target_pairs={{0,192},{64,128},{128,64},{192,0},{16,80},{80,16},{144,208},{208,1... | collective-permute-start | bytes 589832 | tf_op jit(solution)/shard_map/ppermute | solution.py:35
  30.8 5.1 %collective-permute-start.4 = (bf16[2,2,3,32,256]{4,3,2,1,0:T(8,128)(2,1)}, bf16[2,2,3,32,256]{4,3,2,1,0:T(8,128)(2,1)}, u32[]{:S(2)}, u32[]{:S(2)}) collective-permute-start(bf16[2,2,3,32,256]{4,3,2,1,0:T(8,128)(2,1)} %pad_maximum_fusion.11), channel_id=1, source_target_pairs={{0,3},{1,2},{2,1},{3,0},{16,17},{17,16},{18,19},{19,18},{4,7},{5,6... | collective-permute-start | bytes 589832 | tf_op jit(solution)/shard_map/ppermute | solution.py:35
  31.6 13.2 %collective-permute-start.14 = (bf16[1,2,192,512]{3,2,1,0:T(8,128)(2,1)}, bf16[1,2,192,512]{3,2,1,0:T(8,128)(2,1)}, u32[]{:S(2)}, u32[]{:S(2)}) collective-permute-start(bf16[1,2,192,512]{3,2,1,0:T(8,128)(2,1)} %get-tuple-element.86), channel_id=1, source_target_pairs={{16,0},{32,16},{48,32},{64,48},{80,64},{96,80},{112,96},{128,112},... | collective-permute-start | bytes 1179656 | tf_op jit(solution)/shard_map/ppermute | solution.py:86
  31.6 0.7 copy-start.10
  32.3 13.6 %collective-permute-start.13 = (bf16[1,2,192,512]{3,2,1,0:T(8,128)(2,1)S(1)}, bf16[1,2,192,512]{3,2,1,0:T(8,128)(2,1)S(1)}, u32[]{:S(2)}, u32[]{:S(2)}) collective-permute-start(bf16[1,2,192,512]{3,2,1,0:T(8,128)(2,1)S(1)} %get-tuple-element.85), channel_id=1, source_target_pairs={{0,16},{16,32},{32,48},{48,64},{64,80},{80,96},{96,112},{112,128},... | collective-permute-start | bytes 1179656 | tf_op jit(solution)/shard_map/ppermute | solution.py:85
  35.8 6.1 %copy-start.8 = (bf16[2,2,192,512]{3,2,1,0:T(8,128)(2,1)S(1)}, bf16[2,2,192,512]{3,2,1,0:T(8,128)(2,1)}, u32[]{:S(2)}) copy-start(bf16[2,2,192,512]{3,2,1,0:T(8,128)(2,1)} %param.4) | copy-start | bytes 2359300
  35.9 13.1 %collective-permute-start.9 = (bf16[4,2,3,32,256]{4,3,2,1,0:T(8,128)(2,1)}, bf16[4,2,3,32,256]{4,3,2,1,0:T(8,128)(2,1)}, u32[]{:S(2)}, u32[]{:S(2)}) collective-permute-start(bf16[4,2,3,32,256]{4,3,2,1,0:T(8,128)(2,1)} %get-tuple-element.90), channel_id=1, source_target_pairs={{0,1},{1,0},{2,3},{3,2},{16,19},{17,18},{18,17},{19,16},{4,5},{5,4... | collective-permute-start | bytes 1179656 | tf_op jit(solution)/shard_map/ppermute | solution.py:35
  38.1 12.7 %collective-permute-start.5 = (bf16[4,2,3,32,256]{4,3,2,1,0:T(8,128)(2,1)}, bf16[4,2,3,32,256]{4,3,2,1,0:T(8,128)(2,1)}, u32[]{:S(2)}, u32[]{:S(2)}) collective-permute-start(bf16[4,2,3,32,256]{4,3,2,1,0:T(8,128)(2,1)} %get-tuple-element.92), channel_id=1, source_target_pairs={{0,64},{64,0},{128,192},{192,128},{16,208},{80,144},{144,80},{208,... | collective-permute-start | bytes 1179656 | tf_op jit(solution)/shard_map/ppermute | solution.py:35
  43.2 2.7 %copy-start.5 = (bf16[2,4,192,512]{3,2,1,0:T(8,128)(2,1)}, bf16[2,4,192,512]{3,2,1,0:T(8,128)(2,1)S(1)}, u32[]{:S(2)}) copy-start(bf16[2,4,192,512]{3,2,1,0:T(8,128)(2,1)S(1)} %get-tuple-element.78) | copy-start | bytes 4718596
  44.2 13.5 %collective-permute-start.15 = (bf16[2,4,192,256]{3,2,1,0:T(8,128)(2,1)}, bf16[2,4,192,256]{3,2,1,0:T(8,128)(2,1)}, u32[]{:S(2)}, u32[]{:S(2)}) collective-permute-start(bf16[2,4,192,256]{3,2,1,0:T(8,128)(2,1)} %constant_dynamic-slice_fusion), channel_id=1, source_target_pairs={{0,16},{16,0},{1,17},{17,1},{2,18},{18,2},{3,19},{19,3},{4,20},{20... | collective-permute-start | bytes 2359304 | tf_op jit(solution)/shard_map/ppermute | solution.py:22
  49.1 1.8 copy-start.9
  49.1 4.3 %copy-start.6 = (bf16[2,4,192,512]{3,2,1,0:T(8,128)(2,1)S(1)}, bf16[2,4,192,512]{3,2,1,0:T(8,128)(2,1)}, u32[]{:S(2)}) copy-start(bf16[2,4,192,512]{3,2,1,0:T(8,128)(2,1)} %copy-done.5) | copy-start | bytes 4718596
  50.3 11.3 %collective-permute-start.10 = (bf16[2,4,2,3,32,256]{5,4,3,2,1,0:T(8,128)(2,1)S(1)}, bf16[2,4,2,3,32,256]{5,4,3,2,1,0:T(8,128)(2,1)}, u32[]{:S(2)}, u32[]{:S(2)}) collective-permute-start(bf16[2,4,2,3,32,256]{5,4,3,2,1,0:T(8,128)(2,1)S(1)} %pad_maximum_fusion.7.refs_2_), channel_id=1, source_target_pairs={{0,3},{1,2},{2,1},{3,0},{16,17},{17,16},{18,19},{19,18},{4,7},{5,6... | collective-permute-start | bytes 2359304 | tf_op jit(solution)/shard_map/ppermute | solution.py:35
  52.8 11.5 %collective-permute-start.6 = (bf16[2,4,2,3,32,256]{5,4,3,2,1,0:T(8,128)(2,1)}, bf16[2,4,2,3,32,256]{5,4,3,2,1,0:T(8,128)(2,1)}, u32[]{:S(2)}, u32[]{:S(2)}) collective-permute-start(bf16[2,4,2,3,32,256]{5,4,3,2,1,0:T(8,128)(2,1)} %pad_maximum_fusion.6.refs_0_), channel_id=1, source_target_pairs={{0,192},{64,128},{128,64},{192,0},{16,80},{80,16},{144,208},{208,1... | collective-permute-start | bytes 2359304 | tf_op jit(solution)/shard_map/ppermute | solution.py:35
  53.9 1.4 copy-start.7
  64.3 18.0 %collective-permute-start.16 = (bf16[512,1536]{1,0:T(8,128)(2,1)S(1)}, bf16[512,1536]{1,0:T(8,128)(2,1)}, u32[]{:S(2)}, u32[]{:S(2)}) collective-permute-start(bf16[512,1536]{1,0:T(8,128)(2,1)S(1)} %bitcast.100), channel_id=1, source_target_pairs={{0,16},{16,0},{1,17},{17,1},{2,18},{18,2},{3,19},{19,3},{4,20},{20... | collective-permute-start | bytes 4718600 | tf_op jit(solution)/shard_map/ppermute | solution.py:22
  70.4 11.9 %collective-permute-start.19 = (bf16[2,4,2,3,32,256]{5,4,3,2,1,0:T(8,128)(2,1)S(1)}, bf16[2,4,2,3,32,256]{5,4,3,2,1,0:T(8,128)(2,1)}, u32[]{:S(2)}, u32[]{:S(2)}) collective-permute-start(bf16[2,4,2,3,32,256]{5,4,3,2,1,0:T(8,128)(2,1)S(1)} %pad_maximum_fusion.7.refs_2_), channel_id=1, source_target_pairs={{0,16},{16,0},{1,17},{17,1},{2,18},{18,2},{3,19},{19,3},{4,20},{20... | collective-permute-start | bytes 2359304 | tf_op jit(solution)/shard_map/ppermute | solution.py:22
  70.4 11.9 %collective-permute-start.17 = (bf16[2,4,2,3,32,256]{5,4,3,2,1,0:T(8,128)(2,1)}, bf16[2,4,2,3,32,256]{5,4,3,2,1,0:T(8,128)(2,1)}, u32[]{:S(2)}, u32[]{:S(2)}) collective-permute-start(bf16[2,4,2,3,32,256]{5,4,3,2,1,0:T(8,128)(2,1)} %pad_maximum_fusion.6.refs_0_), channel_id=1, source_target_pairs={{0,16},{16,0},{1,17},{17,1},{2,18},{18,2},{3,19},{19,3},{4,20},{20... | collective-permute-start | bytes 2359304 | tf_op jit(solution)/shard_map/ppermute | solution.py:22
  70.9 11.4 %collective-permute-start.18 = (bf16[2,4,2,3,32,256]{5,4,3,2,1,0:T(8,128)(2,1)}, bf16[2,4,2,3,32,256]{5,4,3,2,1,0:T(8,128)(2,1)}, u32[]{:S(2)}, u32[]{:S(2)}) collective-permute-start(bf16[2,4,2,3,32,256]{5,4,3,2,1,0:T(8,128)(2,1)} %collective-permute-done.6.refs_1_), channel_id=1, source_target_pairs={{0,16},{16,0},{1,17},{17,1},{2,18},{18,2},{3,19},{19,3},{4,20},{20... | collective-permute-start | bytes 2359304 | tf_op jit(solution)/shard_map/ppermute | solution.py:22
  70.9 11.4 %collective-permute-start.20 = (bf16[2,4,2,3,32,256]{5,4,3,2,1,0:T(8,128)(2,1)}, bf16[2,4,2,3,32,256]{5,4,3,2,1,0:T(8,128)(2,1)}, u32[]{:S(2)}, u32[]{:S(2)}) collective-permute-start(bf16[2,4,2,3,32,256]{5,4,3,2,1,0:T(8,128)(2,1)} %collective-permute-done.10.refs_3_), channel_id=1, source_target_pairs={{0,16},{16,0},{1,17},{17,1},{2,18},{18,2},{3,19},{19,3},{4,20},{20... | collective-permute-start | bytes 2359304 | tf_op jit(solution)/shard_map/ppermute | solution.py:22
  71.6 2.3 %copy-start = (bf16[3,2,4,192,512]{4,3,2,1,0:T(8,128)(2,1)S(1)}, bf16[3,2,4,192,512]{4,3,2,1,0:T(8,128)(2,1)}, u32[]{:S(2)}) copy-start(bf16[3,2,4,192,512]{4,3,2,1,0:T(8,128)(2,1)} %pad_maximum_fusion.x_hbm.x_ref) | copy-start | bytes 14155780
  74.0 1.4 copy-start.3
  75.4 6.9 %copy-start.1 = (bf16[3,2,4,192,512]{4,3,2,1,0:T(8,128)(2,1)S(1)}, bf16[3,2,4,192,512]{4,3,2,1,0:T(8,128)(2,1)}, u32[]{:S(2)}) copy-start(bf16[3,2,4,192,512]{4,3,2,1,0:T(8,128)(2,1)} %pad_maximum_fusion.x_hbm.x_ref) | copy-start | bytes 14155780
  75.4 6.9 %copy-start.4 = (bf16[4,2,192,512]{3,2,1,0:T(8,128)(2,1)S(1)}, bf16[4,2,192,512]{3,2,1,0:T(8,128)(2,1)}, u32[]{:S(2)}) copy-start(bf16[4,2,192,512]{3,2,1,0:T(8,128)(2,1)} %pad_maximum_fusion.4.cot_hbm) | copy-start | bytes 4718596
  91.1 9.8 %collective-permute-start.21 = (bf16[512,768]{1,0:T(8,128)(2,1)S(1)}, bf16[512,768]{1,0:T(8,128)(2,1)S(1)}, u32[]{:S(2)}, u32[]{:S(2)}) collective-permute-start(bf16[512,768]{1,0:T(8,128)(2,1)S(1)} %get-tuple-element.46.turned_ref), channel_id=1, source_target_pairs={{0,16},{16,0},{1,17},{17,1},{2,18},{18,2},{3,19},{19,3},{4,20},{20... | collective-permute-start | bytes 2359304 | tf_op jit(solution)/shard_map/ppermute | solution.py:22
  91.2 9.7 %collective-permute-start.22 = (bf16[2,384,256]{2,1,0:T(8,128)(2,1)S(1)}, bf16[2,384,256]{2,1,0:T(8,128)(2,1)S(1)}, u32[]{:S(2)}, u32[]{:S(2)}) collective-permute-start(bf16[2,384,256]{2,1,0:T(8,128)(2,1)S(1)} %get-tuple-element.51), channel_id=1, source_target_pairs={{0,16},{16,0},{1,17},{17,1},{2,18},{18,2},{3,19},{19,3},{4,20},{20... | collective-permute-start | bytes 1179656 | tf_op jit(solution)/shard_map/ppermute | solution.py:22
  91.7 23.4 %collective-permute-start.26 = (bf16[2,1,192,512]{3,2,1,0:T(8,128)(2,1)S(1)}, bf16[2,1,192,512]{3,2,1,0:T(8,128)(2,1)S(1)}, u32[]{:S(2)}, u32[]{:S(2)}) collective-permute-start(bf16[2,1,192,512]{3,2,1,0:T(8,128)(2,1)S(1)} %get-tuple-element.82), channel_id=1, source_target_pairs={{0,1},{1,2},{2,3},{3,4},{4,5},{5,6},{6,7},{7,8},{8,9},{9,10},{10,1... | collective-permute-start | bytes 1179656 | tf_op jit(solution)/shard_map/ppermute | solution.py:85
  91.8 23.4 %collective-permute-start.27 = (bf16[2,1,192,512]{3,2,1,0:T(8,128)(2,1)S(1)}, bf16[2,1,192,512]{3,2,1,0:T(8,128)(2,1)S(1)}, u32[]{:S(2)}, u32[]{:S(2)}) collective-permute-start(bf16[2,1,192,512]{3,2,1,0:T(8,128)(2,1)S(1)} %get-tuple-element.81), channel_id=1, source_target_pairs={{1,0},{2,1},{3,2},{4,3},{5,4},{6,5},{7,6},{8,7},{9,8},{10,9},{11,1... | collective-permute-start | bytes 1179656 | tf_op jit(solution)/shard_map/ppermute | solution.py:86
  105.5 12.4 %collective-permute-start.23 = (bf16[2,4,3,2,32,256]{5,4,3,2,1,0:T(8,128)(2,1)S(1)}, bf16[2,4,3,2,32,256]{5,4,3,2,1,0:T(8,128)(2,1)S(1)}, u32[]{:S(2)}, u32[]{:S(2)}) collective-permute-start(bf16[2,4,3,2,32,256]{5,4,3,2,1,0:T(8,128)(2,1)S(1)} %get-tuple-element.53), channel_id=1, source_target_pairs={{0,64},{64,0},{128,192},{192,128},{16,208},{80,144},{144,80},{208,... | collective-permute-start | bytes 2359304 | tf_op jit(solution)/shard_map/ppermute | solution.py:35
  113.0 12.4 %collective-permute-start.25 = (bf16[2,4,3,2,32,256]{5,4,3,2,1,0:T(8,128)(2,1)S(1)}, bf16[2,4,3,2,32,256]{5,4,3,2,1,0:T(8,128)(2,1)S(1)}, u32[]{:S(2)}, u32[]{:S(2)}) collective-permute-start(bf16[2,4,3,2,32,256]{5,4,3,2,1,0:T(8,128)(2,1)S(1)} %get-tuple-element.55), channel_id=1, source_target_pairs={{0,1},{1,0},{2,3},{3,2},{16,19},{17,18},{18,17},{19,16},{4,5},{5,4... | collective-permute-start | bytes 2359304 | tf_op jit(solution)/shard_map/ppermute | solution.py:35
  118.0 11.5 %collective-permute-start.24 = (bf16[4,3,2,32,256]{4,3,2,1,0:T(8,128)(2,1)S(1)}, bf16[4,3,2,32,256]{4,3,2,1,0:T(8,128)(2,1)S(1)}, u32[]{:S(2)}, u32[]{:S(2)}) collective-permute-start(bf16[4,3,2,32,256]{4,3,2,1,0:T(8,128)(2,1)S(1)} %fusion), channel_id=1, source_target_pairs={{0,192},{64,128},{128,64},{192,0},{16,80},{80,16},{144,208},{208,1... | collective-permute-start | bytes 1179656 | tf_op jit(solution)/shard_map/ppermute | solution.py:35
  125.6 7.0 %collective-permute-start.30 = (bf16[4,3,2,32,256]{4,3,2,1,0:T(8,128)(2,1)S(1)}, bf16[4,3,2,32,256]{4,3,2,1,0:T(8,128)(2,1)S(1)}, u32[]{:S(2)}, u32[]{:S(2)}) collective-permute-start(bf16[4,3,2,32,256]{4,3,2,1,0:T(8,128)(2,1)S(1)} %fusion.1), channel_id=1, source_target_pairs={{0,3},{1,2},{2,1},{3,0},{16,17},{17,16},{18,19},{19,18},{4,7},{5,6... | collective-permute-start | bytes 1179656 | tf_op jit(solution)/shard_map/ppermute | solution.py:35
  129.7 8.4 %collective-permute-start.28 = (f32[2,3,2,32,256]{4,3,2,1,0:T(8,128)S(1)}, f32[2,3,2,32,256]{4,3,2,1,0:T(8,128)S(1)}, u32[]{:S(2)}, u32[]{:S(2)}) collective-permute-start(f32[2,3,2,32,256]{4,3,2,1,0:T(8,128)S(1)} %get-tuple-element.68), channel_id=1, source_target_pairs={{0,1},{1,0},{2,3},{3,2},{16,19},{17,18},{18,17},{19,16},{4,5},{5,4... | collective-permute-start | bytes 1179656 | tf_op jit(solution)/shard_map/ppermute | solution.py:35
  132.8 7.9 %collective-permute-start.31 = (f32[2,3,2,32,256]{4,3,2,1,0:T(8,128)S(1)}, f32[2,3,2,32,256]{4,3,2,1,0:T(8,128)S(1)}, u32[]{:S(2)}, u32[]{:S(2)}) collective-permute-start(f32[2,3,2,32,256]{4,3,2,1,0:T(8,128)S(1)} %get-tuple-element.70), channel_id=1, source_target_pairs={{0,64},{64,0},{128,192},{192,128},{16,208},{80,144},{144,80},{208,... | collective-permute-start | bytes 1179656 | tf_op jit(solution)/shard_map/ppermute | solution.py:35
  138.0 4.9 %collective-permute-start.29 = (f32[3,2,32,256]{3,2,1,0:T(8,128)S(1)}, f32[3,2,32,256]{3,2,1,0:T(8,128)S(1)}, u32[]{:S(2)}, u32[]{:S(2)}) collective-permute-start(f32[3,2,32,256]{3,2,1,0:T(8,128)S(1)} %fusion.6), channel_id=1, source_target_pairs={{0,3},{1,2},{2,1},{3,0},{16,17},{17,16},{18,19},{19,18},{4,7},{5,6... | collective-permute-start | bytes 589832 | tf_op jit(solution)/shard_map/ppermute | solution.py:35
  140.7 4.6 %collective-permute-start.32 = (f32[3,2,32,256]{3,2,1,0:T(8,128)S(1)}, f32[3,2,32,256]{3,2,1,0:T(8,128)S(1)}, u32[]{:S(2)}, u32[]{:S(2)}) collective-permute-start(f32[3,2,32,256]{3,2,1,0:T(8,128)S(1)} %fusion.2), channel_id=1, source_target_pairs={{0,192},{64,128},{128,64},{192,0},{16,80},{80,16},{144,208},{208,1... | collective-permute-start | bytes 589832 | tf_op jit(solution)/shard_map/ppermute | solution.py:35
  168.7 12.1 %collective-permute-start.33 = (f32[8,3,16,256]{3,2,1,0:T(8,128)S(1)}, f32[8,3,16,256]{3,2,1,0:T(8,128)S(1)}, u32[]{:S(2)}, u32[]{:S(2)}) collective-permute-start(f32[8,3,16,256]{3,2,1,0:T(8,128)S(1)} %all_to_all.11), channel_id=1, source_target_pairs={{0,16},{16,0},{1,17},{17,1},{2,18},{18,2},{3,19},{19,3},{4,20},{20... | collective-permute-start | bytes 1179656 | tf_op jit(solution)/shard_map/ppermute | solution.py:22

commit v9 on v8

--- a/solution.py
+++ b/solution.py
@@ -64,7 +64,7 @@
 
 
 def ring_gather(block, axis):
-    pair = jnp.stack([block, exchange(block, axis, 0)])
+    pair = jnp.stack(lax.optimization_barrier((block, exchange(block, axis, 0))))
     return pair, exchange(pair, axis, 1)
 
 
@@ -187,7 +187,7 @@
     add_terms(other, x_ref, cot_ref, kernel_ref, pre_ref, other_ref, start_ref)
     frames, block, chans = pre_ref.shape
     half = chans // 2
-    part = 32
+    part = 96
     for hid_ref, source_ref, index in (
         (hid_mine_ref, mine_ref, 1 - other),
         (hid_other_ref, other_ref, other),

time: 183 us -> 182 us (level)
    another operation x10 -> x6, other arithmetic: 7.66 us -> 4.09 us  [the longest x4 4 us: ring_gather(): jnp.stack(lax.optimization_barrier((block, exchange(block, axis, 0))))]
    concatenate x0 -> x2, other arithmetic: none -> 2.71 us  [the longest x1 1.74 us: kernel_parts(): lower = jnp.concatenate(ring_gather(unit[0], 'y'))]
    unnamed x22 -> x20, local copies, waits for them, and re-layouts: 5.3 us -> 5.29 us
where the time goes in v9:
time: 182 us; the launch traced here: 181 us
  starting transfers between devices  55.6 us (31%)
  waiting for transfers between devices  36.7 us (20%)
  Pallas kernels  31.6 us (17%)
  blocking collectives  23 us (13%)
  other arithmetic  17.2 us (9%)
  local copies, waits for them, and re-layouts  16 us (9%)
    ppermute x16, waiting for transfers between devices, exchange(): return lax.ppermute(block, names, pairs)  33.3 us
    ppermute x9, starting transfers between devices, swap(): return lax.ppermute(block, 'core', PAIR)  19.4 us
    ppermute x16, starting transfers between devices, exchange(): return lax.ppermute(block, names, pairs)  13.6 us
    all_to_all x1, blocking collectives, per_device(): terms = lax.all_to_all(terms, ('zh', 'zl'), 0, 0, tiled=True)  12.4 us
    ppermute x3, starting transfers between devices, edges_of(): high = lax.ppermute(lax.slice_in_dim(block, 0, 1, axis=dim), axis, backward)  11.7 us
    all_to_all x1, blocking collectives, gathered(): return lax.all_to_all(spread, axis, 0, 0, tiled=True)  10.6 us
    pallas_call x2, Pallas kernels, weight_terms(): pl.pallas_call(functools.partial(weight_kernel, upper), out_shape=(jax.Sh...  9.29 us
    ppermute x3, starting transfers between devices, kernel_unit(): slots.append(lax.ppermute(unit, 'zh', [(i, i ^ k) for i in range(4)]))  9.12 us
  transfers between devices with their start and end apart: 34, of which 14 were waited for; matrix products, arithmetic and copies ran while one was open for 14% of the time, Pallas kernels for 13%

profile of v9, /device:TPU:1, one launch (start us, length us, event | category | flops | bytes accessed | tf_op | source)
XLA Modules:
  0.0 181.2 jit_solution(16973593340257890953)
XLA Ops:
  0.6 0.8 fusion.10
  1.5 6.9 %collective-permute-start = (bf16[3,32,256]{2,1,0:T(8,128)(2,1)S(1)}, bf16[3,32,256]{2,1,0:T(8,128)(2,1)S(1)}, u32[]{:S(2)}, u32[]{:S(2)}) collective-permute-start(bf16[3,32,256]{2,1,0:T(8,128)(2,1)S(1)} %fusion.10), channel_id=1, source_target_pairs={{0,12},{4,8},{8,4},{12,0},{1,13},{5,9},{9,5},{13,1},{2,14},{6,10},... | collective-permute-start | bytes 147464 | tf_op jit(solution)/shard_map/ppermute | solution.py:367
  8.4 1.0 collective-permute-start.1
  9.4 1.2 collective-permute-start.2
  10.6 1.2 fusion.18
  11.8 6.0 %collective-permute-start.12 = (bf16[2,1,192,512]{3,2,1,0:T(8,128)(2,1)S(1)}, bf16[2,1,192,512]{3,2,1,0:T(8,128)(2,1)S(1)}, u32[]{:S(2)}, u32[]{:S(2)}) collective-permute-start(bf16[2,1,192,512]{3,2,1,0:T(8,128)(2,1)S(1)} %get-tuple-element.104), channel_id=1, source_target_pairs={{1,0},{2,1},{3,2},{4,3},{5,4},{6,5},{7,6},{8,7},{9,8},{10,9},{11,1... | collective-permute-start | bytes 1179656 | tf_op jit(solution)/shard_map/ppermute | solution.py:86
  17.9 2.6 %collective-permute-start.7 = (bf16[2,3,32,256]{3,2,1,0:T(8,128)(2,1)S(1)}, bf16[2,3,32,256]{3,2,1,0:T(8,128)(2,1)S(1)}, u32[]{:S(2)}, u32[]{:S(2)}) collective-permute-start(bf16[2,3,32,256]{3,2,1,0:T(8,128)(2,1)S(1)} %pad_maximum_fusion.15), channel_id=1, source_target_pairs={{0,64},{64,0},{128,192},{192,128},{16,208},{80,144},{144,80},{208,... | collective-permute-start | bytes 294920 | tf_op jit(solution)/shard_map/ppermute | solution.py:35
  20.4 1.4 collective-permute-start.3
  21.8 0.8 collective-permute-done.7
  23.0 7.1 %collective-permute-done.3 = bf16[2,3,32,256]{3,2,1,0:T(8,128)(2,1)S(1)} collective-permute-done((bf16[2,3,32,256]{3,2,1,0:T(8,128)(2,1)S(1)}, bf16[2,3,32,256]{3,2,1,0:T(8,128)(2,1)S(1)}, u32[]{:S(2)}, u32[]{:S(2)}) %collective-permute-start.3) | collective-permute-done | bytes 98336 | tf_op jit(solution)/shard_map/ppermute | solution.py:35
  30.1 0.7 pad_maximum_fusion.11
  30.8 0.8 fusion.17
  31.6 0.7 copy-done.9
  32.3 1.7 collective-permute-start.13
  34.1 1.0 pad_maximum_fusion.10
  35.0 0.9 collective-permute-done.4
  35.9 1.7 pad_maximum_fusion.9
  37.7 3.2 %collective-permute-start.5 = (bf16[4,2,3,32,256]{4,3,2,1,0:T(8,128)(2,1)}, bf16[4,2,3,32,256]{4,3,2,1,0:T(8,128)(2,1)}, u32[]{:S(2)}, u32[]{:S(2)}) collective-permute-start(bf16[4,2,3,32,256]{4,3,2,1,0:T(8,128)(2,1)} %pad_maximum_fusion.9), channel_id=1, source_target_pairs={{0,64},{64,0},{128,192},{192,128},{16,208},{80,144},{144,80},{208,... | collective-permute-start | bytes 1179656 | tf_op jit(solution)/shard_map/ppermute | solution.py:35
  41.0 1.4 fusion.12
  42.4 1.0 constant_dynamic-slice_fusion
  43.4 1.3 collective-permute-start.15
  44.7 1.0 broadcast_select_fusion
  45.8 1.3 pad_maximum_fusion.4.cot_hbm
  47.2 1.7 copy.13
  48.9 1.2 pad_maximum_fusion.7.refs_2_
  50.1 0.6 collective-permute-start.10
  50.7 2.1 %pad_maximum_fusion.6.refs_0_ = bf16[2,4,2,3,32,256]{5,4,3,2,1,0:T(8,128)(2,1)} fusion(bf16[1,4,2,3,32,256]{5,4,3,2,1,0:T(8,128)(2,1)} %bitcast.16, bf16[1,4,2,3,32,256]{5,4,3,2,1,0:T(8,128)(2,1)} %bitcast.15), kind=kLoop, calls=%fused_computation.10 | loop fusion | flops 393216 | bytes 1572864 | tf_op jit(solution)/shard_map/stack | solution.py:67
  52.8 0.7 collective-permute-start.6
  54.0 0.5 pad_bitcast_fusion.2
  54.5 0.8 copy-done.7
  55.4 2.5 %pad_maximum_fusion.x_hbm.x_ref = bf16[3,2,4,192,512]{4,3,2,1,0:T(8,128)(2,1)} fusion(bf16[1,2,4,192,512]{4,3,2,1,0:T(8,128)(2,1)S(1)} %get-tuple-element.109, bf16[1,2,4,192,512]{4,3,2,1,0:T(8,128)(2,1)S(1)} %copy-done.7, bf16[1,2,4,192,512]{4,3,2,1,0:T(8,128)(2,1)S(1)} %get-tuple-element.110), kind=kLoop, calls=%fused_computation | loop fusion | flops 4718592 | bytes 9437184 | tf_op jit(solution)/shard_map/stack | solution.py:100
  57.8 3.6 %collective-permute-done.10.refs_3_ = bf16[2,4,2,3,32,256]{5,4,3,2,1,0:T(8,128)(2,1)} collective-permute-done((bf16[2,4,2,3,32,256]{5,4,3,2,1,0:T(8,128)(2,1)S(1)}, bf16[2,4,2,3,32,256]{5,4,3,2,1,0:T(8,128)(2,1)}, u32[]{:S(2)}, u32[]{:S(2)}) %collective-permute-start.10) | collective-permute-done | bytes 786464 | tf_op jit(solution)/shard_map/ppermute | solution.py:35
  61.4 2.8 %collective-permute-done.6.refs_1_ = bf16[2,4,2,3,32,256]{5,4,3,2,1,0:T(8,128)(2,1)} collective-permute-done((bf16[2,4,2,3,32,256]{5,4,3,2,1,0:T(8,128)(2,1)}, bf16[2,4,2,3,32,256]{5,4,3,2,1,0:T(8,128)(2,1)}, u32[]{:S(2)}, u32[]{:S(2)}) %collective-permute-start.6) | collective-permute-done | bytes 786464 | tf_op jit(solution)/shard_map/ppermute | solution.py:35
  64.2 6.2 %collective-permute-start.16 = (bf16[512,1536]{1,0:T(8,128)(2,1)S(1)}, bf16[512,1536]{1,0:T(8,128)(2,1)}, u32[]{:S(2)}, u32[]{:S(2)}) collective-permute-start(bf16[512,1536]{1,0:T(8,128)(2,1)S(1)} %bitcast.96), channel_id=1, source_target_pairs={{0,16},{16,0},{1,17},{17,1},{2,18},{18,2},{3,19},{19,3},{4,20},{20... | collective-permute-start | bytes 4718600 | tf_op jit(solution)/shard_map/ppermute | solution.py:22
  70.4 0.5 collective-permute-start.17
  71.0 0.5 collective-permute-start.20
  71.7 2.3 %copy-done = bf16[3,2,4,192,512]{4,3,2,1,0:T(8,128)(2,1)S(1)} copy-done((bf16[3,2,4,192,512]{4,3,2,1,0:T(8,128)(2,1)S(1)}, bf16[3,2,4,192,512]{4,3,2,1,0:T(8,128)(2,1)}, u32[]{:S(2)}) %copy-start) | copy-done | bytes 4718616
  74.1 1.4 copy-done.3
  75.5 6.8 %shard_map.67 = (f32[2,384,512]{2,1,0:T(8,128)S(1)}, f32[2,384,256]{2,1,0:T(8,128)S(1)}, bf16[4,4,3,4,32,256]{5,4,3,2,1,0:T(8,128)(2,1)S(1)}) custom-call(s32[9]{0:T(128)S(1)} %concatenate.63.info_ref, bf16[3,2,4,192,512]{4,3,2,1,0:T(8,128)(2,1)S(1)} %copy-done, bf16[4,2,192,512]{3,2,1,0:T(8,128)(2,1)S(1)} %copy-done.3, ...), custom_call_target="tpu_custom_call" | custom-call | flops 3200000000 | bytes 12000000 | tf_op jit(solution)/shard_map/pallas_call | solution.py:226
  82.4 7.9 %shard_map.68 = (bf16[2,384,256]{2,1,0:T(8,128)(2,1)S(1)}, bf16[2,384,256]{2,1,0:T(8,128)(2,1)S(1)}, bf16[2,384,512]{2,1,0:T(8,128)(2,1)S(1)}, bf16[512,768]{1,0...) custom-call(s32[9]{0:T(128)S(1)} %concatenate.55.info_ref, bf16[3,2,4,192,512]{4,3,2,1,0:T(8,128)(2,1)S(1)} %copy-done.1, ...), custom_call_target="tpu_custom_call" | custom-call | flops 3200000000 | bytes 15000000 | tf_op jit(solution)/shard_map/pallas_call | solution.py:235
  91.0 5.7 %collective-permute-start.27 = (bf16[2,1,192,512]{3,2,1,0:T(8,128)(2,1)S(1)}, bf16[2,1,192,512]{3,2,1,0:T(8,128)(2,1)S(1)}, u32[]{:S(2)}, u32[]{:S(2)}) collective-permute-start(bf16[2,1,192,512]{3,2,1,0:T(8,128)(2,1)S(1)} %get-tuple-element.97), channel_id=1, source_target_pairs={{1,0},{2,1},{3,2},{4,3},{5,4},{6,5},{7,6},{8,7},{9,8},{10,9},{11,1... | collective-permute-start | bytes 1179656 | tf_op jit(solution)/shard_map/ppermute | solution.py:86
  96.7 1.7 fusion.16
  98.7 1.4 pad_maximum_fusion.2.x_pair_ref
  100.1 4.6 %shard_map.69 = (f32[4,4,3,2,32,256]{5,4,3,2,1,0:T(8,128)S(1)}, bf16[2,4,3,2,32,256]{5,4,3,2,1,0:T(8,128)(2,1)S(1)}) custom-call(s32[9]{0:T(128)S(1)} %pad_add_fusion.info_ref, bf16[512,768]{1,0:T(8,128)(2,1)S(1)} %get-tuple-element.62.turned_ref, bf16[512,768]{1,0:T(8,128)(2,1)S(1)} %collective-permute-done.21.turned_pair_ref, ...), custom_call_target="tpu_custom_call" | custom-call | flops 2400000000 | bytes 16000000 | tf_op jit(solution)/shard_map/pallas_call | solution.py:310
  104.8 2.9 %collective-permute-start.23 = (bf16[2,4,3,2,32,256]{5,4,3,2,1,0:T(8,128)(2,1)S(1)}, bf16[2,4,3,2,32,256]{5,4,3,2,1,0:T(8,128)(2,1)S(1)}, u32[]{:S(2)}, u32[]{:S(2)}) collective-permute-start(bf16[2,4,3,2,32,256]{5,4,3,2,1,0:T(8,128)(2,1)S(1)} %get-tuple-element.69), channel_id=1, source_target_pairs={{0,64},{64,0},{128,192},{192,128},{16,208},{80,144},{144,80},{208,... | collective-permute-start | bytes 2359304 | tf_op jit(solution)/shard_map/ppermute | solution.py:35
  107.6 4.6 %shard_map.70 = (f32[4,4,3,2,32,256]{5,4,3,2,1,0:T(8,128)S(1)}, bf16[2,4,3,2,32,256]{5,4,3,2,1,0:T(8,128)(2,1)S(1)}) custom-call(s32[9]{0:T(128)S(1)} %pad_add_fusion.info_ref, bf16[512,768]{1,0:T(8,128)(2,1)S(1)} %get-tuple-element.62.turned_ref, bf16[512,768]{1,0:T(8,128)(2,1)S(1)} %collective-permute-done.21.turned_pair_ref, ...), custom_call_target="tpu_custom_call" | custom-call | flops 2400000000 | bytes 16000000 | tf_op jit(solution)/shard_map/pallas_call | solution.py:310
  112.4 2.0 %collective-permute-done.26 = bf16[2,1,192,512]{3,2,1,0:T(8,128)(2,1)S(1)} collective-permute-done((bf16[2,1,192,512]{3,2,1,0:T(8,128)(2,1)S(1)}, bf16[2,1,192,512]{3,2,1,0:T(8,128)(2,1)S(1)}, u32[]{:S(2)}, u32[]{:S(2)}) %collective-permute-start.26) | collective-permute-done | bytes 393248 | tf_op jit(solution)/shard_map/ppermute | solution.py:85
  115.8 0.6 pad_maximum_fusion.1.x_ref
  116.3 0.8 collective-permute-done.23
  117.4 3.8 %shard_map.71.refs_0_ = f32[2,384,512]{2,1,0:T(8,128)} custom-call(s32[1]{0:T(128)} %bitcast.info_ref, bf16[3,2,4,192,512]{4,3,2,1,0:T(8,128)(2,1)S(1)} %pad_maximum_fusion.1.x_ref, bf16[2,384,512]{2,1,0:T(8,128)(2,1)S(1)} %bitcast.99, bf16[4,4,3,4,32,256]{5,4,3,2,1,0:T(8,128)(2,1)S(1)} %get-tuple-element.76.mine_ref, ...), custom_call_target="tpu_custom_call" | custom-call | flops 1800000000 | bytes 8000000 | tf_op jit(solution)/shard_map/pallas_call | solution.py:346
  121.1 3.6 %collective-permute-done.25 = bf16[2,4,3,2,32,256]{5,4,3,2,1,0:T(8,128)(2,1)S(1)} collective-permute-done((bf16[2,4,3,2,32,256]{5,4,3,2,1,0:T(8,128)(2,1)S(1)}, bf16[2,4,3,2,32,256]{5,4,3,2,1,0:T(8,128)(2,1)S(1)}, u32[]{:S(2)}, u32[]{:S(2)}) %collective-permute-start.25) | collective-permute-done | bytes 786464 | tf_op jit(solution)/shard_map/ppermute | solution.py:35
  124.9 3.8 %shard_map.72 = f32[2,384,512]{2,1,0:T(8,128)} custom-call(s32[1]{0:T(128)} %bitcast.info_ref, bf16[3,2,4,192,512]{4,3,2,1,0:T(8,128)(2,1)S(1)} %pad_maximum_fusion.1.x_ref, bf16[2,384,512]{2,1,0:T(8,128)(2,1)S(1)} %bitcast.100, bf16[4,4,3,4,32,256]{5,4,3,2,1,0:T(8,128)(2,1)S(1)} %get-tuple-element.76.mine_ref, ...), custom_call_target="tpu_custom_call", output_to_operand_aliasing={{}: (5, {})} | custom-call | flops 1800000000 | bytes 8000000 | tf_op jit(solution)/shard_map/pallas_call | solution.py:346
  129.0 2.8 %collective-permute-done.30 = bf16[4,3,2,32,256]{4,3,2,1,0:T(8,128)(2,1)S(1)} collective-permute-done((bf16[4,3,2,32,256]{4,3,2,1,0:T(8,128)(2,1)S(1)}, bf16[4,3,2,32,256]{4,3,2,1,0:T(8,128)(2,1)S(1)}, u32[]{:S(2)}, u32[]{:S(2)}) %collective-permute-start.30) | collective-permute-done | bytes 393248 | tf_op jit(solution)/shard_map/ppermute | solution.py:35
  132.0 1.3 collective-permute-start.31
  133.3 4.0 %collective-permute-done.28 = f32[2,3,2,32,256]{4,3,2,1,0:T(8,128)S(1)} collective-permute-done((f32[2,3,2,32,256]{4,3,2,1,0:T(8,128)S(1)}, f32[2,3,2,32,256]{4,3,2,1,0:T(8,128)S(1)}, u32[]{:S(2)}, u32[]{:S(2)}) %collective-permute-start.28) | collective-permute-done | bytes 393248 | tf_op jit(solution)/shard_map/ppermute | solution.py:35
  137.5 2.5 %collective-permute-done.31 = f32[2,3,2,32,256]{4,3,2,1,0:T(8,128)S(1)} collective-permute-done((f32[2,3,2,32,256]{4,3,2,1,0:T(8,128)S(1)}, f32[2,3,2,32,256]{4,3,2,1,0:T(8,128)S(1)}, u32[]{:S(2)}, u32[]{:S(2)}) %collective-permute-start.31) | collective-permute-done | bytes 393248 | tf_op jit(solution)/shard_map/ppermute | solution.py:35
  140.1 2.1 %collective-permute-done.29 = f32[3,2,32,256]{3,2,1,0:T(8,128)S(1)} collective-permute-done((f32[3,2,32,256]{3,2,1,0:T(8,128)S(1)}, f32[3,2,32,256]{3,2,1,0:T(8,128)S(1)}, u32[]{:S(2)}, u32[]{:S(2)}) %collective-permute-start.29) | collective-permute-done | bytes 196640 | tf_op jit(solution)/shard_map/ppermute | solution.py:35
  142.2 2.3 %collective-permute-done.32 = f32[3,2,32,256]{3,2,1,0:T(8,128)S(1)} collective-permute-done((f32[3,2,32,256]{3,2,1,0:T(8,128)S(1)}, f32[3,2,32,256]{3,2,1,0:T(8,128)S(1)}, u32[]{:S(2)}, u32[]{:S(2)}) %collective-permute-start.32) | collective-permute-done | bytes 196640 | tf_op jit(solution)/shard_map/ppermute | solution.py:35
  144.7 12.4 %all_to_all.10 = bf16[8,3,16,256]{3,2,1,0:T(8,128)(2,1)S(1)} all-to-all(bf16[8,3,16,256]{3,2,1,0:T(8,128)(2,1)S(1)} %bitcast.117), channel_id=1, replica_groups=mesh['x'=4,'zl'=2,'core'=2,'zh'=4,'y'=4] {'zh','zl'}, dimensions={0} | all-to-all | bytes 393216 | tf_op jit(solution)/shard_map/all_to_all | solution.py:455
  157.2 10.6 %all_to_all.11 = f32[8,3,16,256]{3,2,1,0:T(8,128)S(1)} all-to-all(f32[8,3,16,256]{3,2,1,0:T(8,128)S(1)} %broadcast_in_dim.30), channel_id=1, replica_groups=mesh['x'=4,'zl'=2,'core'=2,'zh'=4,'y'=4] {'x','zl'}, dimensions={0} | all-to-all | bytes 786432 | tf_op jit(solution)/shard_map/all_to_all | solution.py:73
  167.8 10.2 %collective-permute-start.33 = (f32[8,3,16,256]{3,2,1,0:T(8,128)S(1)}, f32[8,3,16,256]{3,2,1,0:T(8,128)S(1)}, u32[]{:S(2)}, u32[]{:S(2)}) collective-permute-start(f32[8,3,16,256]{3,2,1,0:T(8,128)S(1)} %all_to_all.11), channel_id=1, source_target_pairs={{0,16},{16,0},{1,17},{17,1},{2,18},{18,2},{3,19},{19,3},{4,20},{20... | collective-permute-start | bytes 1179656 | tf_op jit(solution)/shard_map/ppermute | solution.py:22
  178.0 1.3 collective-permute-done.33
  179.7 0.9 copy.15
  180.5 0.7 copy.16
  (91 shorter events, 5.5 us)
Async XLA Ops:
  1.5 29.3 %copy-start.2 = (bf16[2,2,192,512]{3,2,1,0:T(8,128)(2,1)S(1)}, bf16[2,2,192,512]{3,2,1,0:T(8,128)(2,1)}, u32[]{:S(2)}) copy-start(bf16[2,2,192,512]{3,2,1,0:T(8,128)(2,1)} %param.5) | copy-start | bytes 2359300
  1.5 16.3 %collective-permute-start = (bf16[3,32,256]{2,1,0:T(8,128)(2,1)S(1)}, bf16[3,32,256]{2,1,0:T(8,128)(2,1)S(1)}, u32[]{:S(2)}, u32[]{:S(2)}) collective-permute-start(bf16[3,32,256]{2,1,0:T(8,128)(2,1)S(1)} %fusion.10), channel_id=1, source_target_pairs={{0,12},{4,8},{8,4},{12,0},{1,13},{5,9},{9,5},{13,1},{2,14},{6,10},... | collective-permute-start | bytes 147464 | tf_op jit(solution)/shard_map/ppermute | solution.py:367
  8.4 9.4 %collective-permute-start.1 = (bf16[3,32,256]{2,1,0:T(8,128)(2,1)S(1)}, bf16[3,32,256]{2,1,0:T(8,128)(2,1)S(1)}, u32[]{:S(2)}, u32[]{:S(2)}) collective-permute-start(bf16[3,32,256]{2,1,0:T(8,128)(2,1)S(1)} %fusion.10), channel_id=1, source_target_pairs={{0,8},{4,12},{8,0},{12,4},{1,9},{5,13},{9,1},{13,5},{2,10},{6,14},... | collective-permute-start | bytes 147464 | tf_op jit(solution)/shard_map/ppermute | solution.py:367
  9.4 8.4 %collective-permute-start.2 = (bf16[3,32,256]{2,1,0:T(8,128)(2,1)S(1)}, bf16[3,32,256]{2,1,0:T(8,128)(2,1)S(1)}, u32[]{:S(2)}, u32[]{:S(2)}) collective-permute-start(bf16[3,32,256]{2,1,0:T(8,128)(2,1)S(1)} %fusion.10), channel_id=1, source_target_pairs={{0,4},{4,0},{8,12},{12,8},{1,5},{5,1},{9,13},{13,9},{2,6},{6,2},{1... | collective-permute-start | bytes 147464 | tf_op jit(solution)/shard_map/ppermute | solution.py:367
  11.8 25.9 %collective-permute-start.12 = (bf16[2,1,192,512]{3,2,1,0:T(8,128)(2,1)S(1)}, bf16[2,1,192,512]{3,2,1,0:T(8,128)(2,1)S(1)}, u32[]{:S(2)}, u32[]{:S(2)}) collective-permute-start(bf16[2,1,192,512]{3,2,1,0:T(8,128)(2,1)S(1)} %get-tuple-element.104), channel_id=1, source_target_pairs={{1,0},{2,1},{3,2},{4,3},{5,4},{6,5},{7,6},{8,7},{9,8},{10,9},{11,1... | collective-permute-start | bytes 1179656 | tf_op jit(solution)/shard_map/ppermute | solution.py:86
  17.8 23.2 %collective-permute-start.11 = (bf16[2,1,192,512]{3,2,1,0:T(8,128)(2,1)S(1)}, bf16[2,1,192,512]{3,2,1,0:T(8,128)(2,1)S(1)}, u32[]{:S(2)}, u32[]{:S(2)}) collective-permute-start(bf16[2,1,192,512]{3,2,1,0:T(8,128)(2,1)S(1)} %get-tuple-element.103), channel_id=1, source_target_pairs={{0,1},{1,2},{2,3},{3,4},{4,5},{5,6},{6,7},{7,8},{8,9},{9,10},{10,1... | collective-permute-start | bytes 1179656 | tf_op jit(solution)/shard_map/ppermute | solution.py:85
  17.9 4.8 %collective-permute-start.7 = (bf16[2,3,32,256]{3,2,1,0:T(8,128)(2,1)S(1)}, bf16[2,3,32,256]{3,2,1,0:T(8,128)(2,1)S(1)}, u32[]{:S(2)}, u32[]{:S(2)}) collective-permute-start(bf16[2,3,32,256]{3,2,1,0:T(8,128)(2,1)S(1)} %pad_maximum_fusion.15), channel_id=1, source_target_pairs={{0,64},{64,0},{128,192},{192,128},{16,208},{80,144},{144,80},{208,... | collective-permute-start | bytes 294920 | tf_op jit(solution)/shard_map/ppermute | solution.py:35
  20.4 9.7 %collective-permute-start.3 = (bf16[2,3,32,256]{3,2,1,0:T(8,128)(2,1)S(1)}, bf16[2,3,32,256]{3,2,1,0:T(8,128)(2,1)S(1)}, u32[]{:S(2)}, u32[]{:S(2)}) collective-permute-start(bf16[2,3,32,256]{3,2,1,0:T(8,128)(2,1)S(1)} %pad_maximum_fusion.14), channel_id=1, source_target_pairs={{0,1},{1,0},{2,3},{3,2},{16,19},{17,18},{18,17},{19,16},{4,5},{5,4... | collective-permute-start | bytes 294920 | tf_op jit(solution)/shard_map/ppermute | solution.py:35
  22.6 9.0 %collective-permute-start.8 = (bf16[2,2,3,32,256]{4,3,2,1,0:T(8,128)(2,1)S(1)}, bf16[2,2,3,32,256]{4,3,2,1,0:T(8,128)(2,1)S(1)}, u32[]{:S(2)}, u32[]{:S(2)}) collective-permute-start(bf16[2,2,3,32,256]{4,3,2,1,0:T(8,128)(2,1)S(1)} %pad_maximum_fusion.12), channel_id=1, source_target_pairs={{0,192},{64,128},{128,64},{192,0},{16,80},{80,16},{144,208},{208,1... | collective-permute-start | bytes 589832 | tf_op jit(solution)/shard_map/ppermute | solution.py:35
  30.8 5.1 %collective-permute-start.4 = (bf16[2,2,3,32,256]{4,3,2,1,0:T(8,128)(2,1)}, bf16[2,2,3,32,256]{4,3,2,1,0:T(8,128)(2,1)}, u32[]{:S(2)}, u32[]{:S(2)}) collective-permute-start(bf16[2,2,3,32,256]{4,3,2,1,0:T(8,128)(2,1)} %pad_maximum_fusion.11), channel_id=1, source_target_pairs={{0,3},{1,2},{2,1},{3,0},{16,17},{17,16},{18,19},{19,18},{4,7},{5,6... | collective-permute-start | bytes 589832 | tf_op jit(solution)/shard_map/ppermute | solution.py:35
  31.6 13.1 %collective-permute-start.14 = (bf16[1,2,192,512]{3,2,1,0:T(8,128)(2,1)}, bf16[1,2,192,512]{3,2,1,0:T(8,128)(2,1)}, u32[]{:S(2)}, u32[]{:S(2)}) collective-permute-start(bf16[1,2,192,512]{3,2,1,0:T(8,128)(2,1)} %get-tuple-element.102), channel_id=1, source_target_pairs={{16,0},{32,16},{48,32},{64,48},{80,64},{96,80},{112,96},{128,112},... | collective-permute-start | bytes 1179656 | tf_op jit(solution)/shard_map/ppermute | solution.py:86
  31.6 0.7 copy-start.9
  32.3 8.7 %copy-start.8 = (bf16[2,2,192,512]{3,2,1,0:T(8,128)(2,1)S(1)}, bf16[2,2,192,512]{3,2,1,0:T(8,128)(2,1)}, u32[]{:S(2)}) copy-start(bf16[2,2,192,512]{3,2,1,0:T(8,128)(2,1)} %param.4) | copy-start | bytes 2359300
  32.3 13.5 %collective-permute-start.13 = (bf16[1,2,192,512]{3,2,1,0:T(8,128)(2,1)S(1)}, bf16[1,2,192,512]{3,2,1,0:T(8,128)(2,1)S(1)}, u32[]{:S(2)}, u32[]{:S(2)}) collective-permute-start(bf16[1,2,192,512]{3,2,1,0:T(8,128)(2,1)S(1)} %get-tuple-element.101), channel_id=1, source_target_pairs={{0,16},{16,32},{32,48},{48,64},{64,80},{80,96},{96,112},{112,128},... | collective-permute-start | bytes 1179656 | tf_op jit(solution)/shard_map/ppermute | solution.py:85
  35.9 13.0 %collective-permute-start.9 = (bf16[4,2,3,32,256]{4,3,2,1,0:T(8,128)(2,1)S(1)}, bf16[4,2,3,32,256]{4,3,2,1,0:T(8,128)(2,1)}, u32[]{:S(2)}, u32[]{:S(2)}) collective-permute-start(bf16[4,2,3,32,256]{4,3,2,1,0:T(8,128)(2,1)S(1)} %pad_maximum_fusion.10), channel_id=1, source_target_pairs={{0,1},{1,0},{2,3},{3,2},{16,19},{17,18},{18,17},{19,16},{4,5},{5,4... | collective-permute-start | bytes 1179656 | tf_op jit(solution)/shard_map/ppermute | solution.py:35
  37.7 13.0 %collective-permute-start.5 = (bf16[4,2,3,32,256]{4,3,2,1,0:T(8,128)(2,1)}, bf16[4,2,3,32,256]{4,3,2,1,0:T(8,128)(2,1)}, u32[]{:S(2)}, u32[]{:S(2)}) collective-permute-start(bf16[4,2,3,32,256]{4,3,2,1,0:T(8,128)(2,1)} %pad_maximum_fusion.9), channel_id=1, source_target_pairs={{0,64},{64,0},{128,192},{192,128},{16,208},{80,144},{144,80},{208,... | collective-permute-start | bytes 1179656 | tf_op jit(solution)/shard_map/ppermute | solution.py:35
  42.4 3.4 %copy-start.5 = (bf16[2,4,192,512]{3,2,1,0:T(8,128)(2,1)}, bf16[2,4,192,512]{3,2,1,0:T(8,128)(2,1)S(1)}, u32[]{:S(2)}) copy-start(bf16[2,4,192,512]{3,2,1,0:T(8,128)(2,1)S(1)} %get-tuple-element.94) | copy-start | bytes 4718596
  43.4 14.4 %collective-permute-start.15 = (bf16[2,4,192,256]{3,2,1,0:T(8,128)(2,1)}, bf16[2,4,192,256]{3,2,1,0:T(8,128)(2,1)}, u32[]{:S(2)}, u32[]{:S(2)}) collective-permute-start(bf16[2,4,192,256]{3,2,1,0:T(8,128)(2,1)} %constant_dynamic-slice_fusion), channel_id=1, source_target_pairs={{0,16},{16,0},{1,17},{17,1},{2,18},{18,2},{3,19},{19,3},{4,20},{20... | collective-permute-start | bytes 2359304 | tf_op jit(solution)/shard_map/ppermute | solution.py:22
  48.9 4.6 %copy-start.6 = (bf16[2,4,192,512]{3,2,1,0:T(8,128)(2,1)S(1)}, bf16[2,4,192,512]{3,2,1,0:T(8,128)(2,1)}, u32[]{:S(2)}) copy-start(bf16[2,4,192,512]{3,2,1,0:T(8,128)(2,1)} %copy-done.5) | copy-start | bytes 4718596
  50.1 11.3 %collective-permute-start.10 = (bf16[2,4,2,3,32,256]{5,4,3,2,1,0:T(8,128)(2,1)S(1)}, bf16[2,4,2,3,32,256]{5,4,3,2,1,0:T(8,128)(2,1)}, u32[]{:S(2)}, u32[]{:S(2)}) collective-permute-start(bf16[2,4,2,3,32,256]{5,4,3,2,1,0:T(8,128)(2,1)S(1)} %pad_maximum_fusion.7.refs_2_), channel_id=1, source_target_pairs={{0,3},{1,2},{2,1},{3,0},{16,17},{17,16},{18,19},{19,18},{4,7},{5,6... | collective-permute-start | bytes 2359304 | tf_op jit(solution)/shard_map/ppermute | solution.py:35
  52.8 11.5 %collective-permute-start.6 = (bf16[2,4,2,3,32,256]{5,4,3,2,1,0:T(8,128)(2,1)}, bf16[2,4,2,3,32,256]{5,4,3,2,1,0:T(8,128)(2,1)}, u32[]{:S(2)}, u32[]{:S(2)}) collective-permute-start(bf16[2,4,2,3,32,256]{5,4,3,2,1,0:T(8,128)(2,1)} %pad_maximum_fusion.6.refs_0_), channel_id=1, source_target_pairs={{0,192},{64,128},{128,64},{192,0},{16,80},{80,16},{144,208},{208,1... | collective-permute-start | bytes 2359304 | tf_op jit(solution)/shard_map/ppermute | solution.py:35
  54.0 1.4 copy-start.7
  64.2 18.1 %collective-permute-start.16 = (bf16[512,1536]{1,0:T(8,128)(2,1)S(1)}, bf16[512,1536]{1,0:T(8,128)(2,1)}, u32[]{:S(2)}, u32[]{:S(2)}) collective-permute-start(bf16[512,1536]{1,0:T(8,128)(2,1)S(1)} %bitcast.96), channel_id=1, source_target_pairs={{0,16},{16,0},{1,17},{17,1},{2,18},{18,2},{3,19},{19,3},{4,20},{20... | collective-permute-start | bytes 4718600 | tf_op jit(solution)/shard_map/ppermute | solution.py:22
  70.4 11.9 %collective-permute-start.19 = (bf16[2,4,2,3,32,256]{5,4,3,2,1,0:T(8,128)(2,1)S(1)}, bf16[2,4,2,3,32,256]{5,4,3,2,1,0:T(8,128)(2,1)}, u32[]{:S(2)}, u32[]{:S(2)}) collective-permute-start(bf16[2,4,2,3,32,256]{5,4,3,2,1,0:T(8,128)(2,1)S(1)} %pad_maximum_fusion.7.refs_2_), channel_id=1, source_target_pairs={{0,16},{16,0},{1,17},{17,1},{2,18},{18,2},{3,19},{19,3},{4,20},{20... | collective-permute-start | bytes 2359304 | tf_op jit(solution)/shard_map/ppermute | solution.py:22
  70.4 11.9 %collective-permute-start.17 = (bf16[2,4,2,3,32,256]{5,4,3,2,1,0:T(8,128)(2,1)}, bf16[2,4,2,3,32,256]{5,4,3,2,1,0:T(8,128)(2,1)}, u32[]{:S(2)}, u32[]{:S(2)}) collective-permute-start(bf16[2,4,2,3,32,256]{5,4,3,2,1,0:T(8,128)(2,1)} %pad_maximum_fusion.6.refs_0_), channel_id=1, source_target_pairs={{0,16},{16,0},{1,17},{17,1},{2,18},{18,2},{3,19},{19,3},{4,20},{20... | collective-permute-start | bytes 2359304 | tf_op jit(solution)/shard_map/ppermute | solution.py:22
  70.9 11.4 %collective-permute-start.18 = (bf16[2,4,2,3,32,256]{5,4,3,2,1,0:T(8,128)(2,1)}, bf16[2,4,2,3,32,256]{5,4,3,2,1,0:T(8,128)(2,1)}, u32[]{:S(2)}, u32[]{:S(2)}) collective-permute-start(bf16[2,4,2,3,32,256]{5,4,3,2,1,0:T(8,128)(2,1)} %collective-permute-done.6.refs_1_), channel_id=1, source_target_pairs={{0,16},{16,0},{1,17},{17,1},{2,18},{18,2},{3,19},{19,3},{4,20},{20... | collective-permute-start | bytes 2359304 | tf_op jit(solution)/shard_map/ppermute | solution.py:22
  71.0 11.4 %collective-permute-start.20 = (bf16[2,4,2,3,32,256]{5,4,3,2,1,0:T(8,128)(2,1)}, bf16[2,4,2,3,32,256]{5,4,3,2,1,0:T(8,128)(2,1)}, u32[]{:S(2)}, u32[]{:S(2)}) collective-permute-start(bf16[2,4,2,3,32,256]{5,4,3,2,1,0:T(8,128)(2,1)} %collective-permute-done.10.refs_3_), channel_id=1, source_target_pairs={{0,16},{16,0},{1,17},{17,1},{2,18},{18,2},{3,19},{19,3},{4,20},{20... | collective-permute-start | bytes 2359304 | tf_op jit(solution)/shard_map/ppermute | solution.py:22
  71.7 2.3 %copy-start = (bf16[3,2,4,192,512]{4,3,2,1,0:T(8,128)(2,1)S(1)}, bf16[3,2,4,192,512]{4,3,2,1,0:T(8,128)(2,1)}, u32[]{:S(2)}) copy-start(bf16[3,2,4,192,512]{4,3,2,1,0:T(8,128)(2,1)} %pad_maximum_fusion.x_hbm.x_ref) | copy-start | bytes 14155780
  74.1 1.4 copy-start.3
  75.5 6.9 %copy-start.1 = (bf16[3,2,4,192,512]{4,3,2,1,0:T(8,128)(2,1)S(1)}, bf16[3,2,4,192,512]{4,3,2,1,0:T(8,128)(2,1)}, u32[]{:S(2)}) copy-start(bf16[3,2,4,192,512]{4,3,2,1,0:T(8,128)(2,1)} %pad_maximum_fusion.x_hbm.x_ref) | copy-start | bytes 14155780
  75.5 6.9 %copy-start.4 = (bf16[4,2,192,512]{3,2,1,0:T(8,128)(2,1)S(1)}, bf16[4,2,192,512]{3,2,1,0:T(8,128)(2,1)}, u32[]{:S(2)}) copy-start(bf16[4,2,192,512]{3,2,1,0:T(8,128)(2,1)} %pad_maximum_fusion.4.cot_hbm) | copy-start | bytes 4718596
  90.3 9.8 %collective-permute-start.21 = (bf16[512,768]{1,0:T(8,128)(2,1)S(1)}, bf16[512,768]{1,0:T(8,128)(2,1)S(1)}, u32[]{:S(2)}, u32[]{:S(2)}) collective-permute-start(bf16[512,768]{1,0:T(8,128)(2,1)S(1)} %get-tuple-element.62.turned_ref), channel_id=1, source_target_pairs={{0,16},{16,0},{1,17},{17,1},{2,18},{18,2},{3,19},{19,3},{4,20},{20... | collective-permute-start | bytes 2359304 | tf_op jit(solution)/shard_map/ppermute | solution.py:22
  90.4 9.7 %collective-permute-start.22 = (bf16[2,384,256]{2,1,0:T(8,128)(2,1)S(1)}, bf16[2,384,256]{2,1,0:T(8,128)(2,1)S(1)}, u32[]{:S(2)}, u32[]{:S(2)}) collective-permute-start(bf16[2,384,256]{2,1,0:T(8,128)(2,1)S(1)} %get-tuple-element.67), channel_id=1, source_target_pairs={{0,16},{16,0},{1,17},{17,1},{2,18},{18,2},{3,19},{19,3},{4,20},{20... | collective-permute-start | bytes 1179656 | tf_op jit(solution)/shard_map/ppermute | solution.py:22
  90.9 23.4 %collective-permute-start.26 = (bf16[2,1,192,512]{3,2,1,0:T(8,128)(2,1)S(1)}, bf16[2,1,192,512]{3,2,1,0:T(8,128)(2,1)S(1)}, u32[]{:S(2)}, u32[]{:S(2)}) collective-permute-start(bf16[2,1,192,512]{3,2,1,0:T(8,128)(2,1)S(1)} %get-tuple-element.98), channel_id=1, source_target_pairs={{0,1},{1,2},{2,3},{3,4},{4,5},{5,6},{6,7},{7,8},{8,9},{9,10},{10,1... | collective-permute-start | bytes 1179656 | tf_op jit(solution)/shard_map/ppermute | solution.py:85
  91.0 23.4 %collective-permute-start.27 = (bf16[2,1,192,512]{3,2,1,0:T(8,128)(2,1)S(1)}, bf16[2,1,192,512]{3,2,1,0:T(8,128)(2,1)S(1)}, u32[]{:S(2)}, u32[]{:S(2)}) collective-permute-start(bf16[2,1,192,512]{3,2,1,0:T(8,128)(2,1)S(1)} %get-tuple-element.97), channel_id=1, source_target_pairs={{1,0},{2,1},{3,2},{4,3},{5,4},{6,5},{7,6},{8,7},{9,8},{10,9},{11,1... | collective-permute-start | bytes 1179656 | tf_op jit(solution)/shard_map/ppermute | solution.py:86
  104.8 12.4 %collective-permute-start.23 = (bf16[2,4,3,2,32,256]{5,4,3,2,1,0:T(8,128)(2,1)S(1)}, bf16[2,4,3,2,32,256]{5,4,3,2,1,0:T(8,128)(2,1)S(1)}, u32[]{:S(2)}, u32[]{:S(2)}) collective-permute-start(bf16[2,4,3,2,32,256]{5,4,3,2,1,0:T(8,128)(2,1)S(1)} %get-tuple-element.69), channel_id=1, source_target_pairs={{0,64},{64,0},{128,192},{192,128},{16,208},{80,144},{144,80},{208,... | collective-permute-start | bytes 2359304 | tf_op jit(solution)/shard_map/ppermute | solution.py:35
  112.3 12.4 %collective-permute-start.25 = (bf16[2,4,3,2,32,256]{5,4,3,2,1,0:T(8,128)(2,1)S(1)}, bf16[2,4,3,2,32,256]{5,4,3,2,1,0:T(8,128)(2,1)S(1)}, u32[]{:S(2)}, u32[]{:S(2)}) collective-permute-start(bf16[2,4,3,2,32,256]{5,4,3,2,1,0:T(8,128)(2,1)S(1)} %get-tuple-element.71), channel_id=1, source_target_pairs={{0,1},{1,0},{2,3},{3,2},{16,19},{17,18},{18,17},{19,16},{4,5},{5,4... | collective-permute-start | bytes 2359304 | tf_op jit(solution)/shard_map/ppermute | solution.py:35
  117.3 11.5 %collective-permute-start.24 = (bf16[4,3,2,32,256]{4,3,2,1,0:T(8,128)(2,1)S(1)}, bf16[4,3,2,32,256]{4,3,2,1,0:T(8,128)(2,1)S(1)}, u32[]{:S(2)}, u32[]{:S(2)}) collective-permute-start(bf16[4,3,2,32,256]{4,3,2,1,0:T(8,128)(2,1)S(1)} %fusion), channel_id=1, source_target_pairs={{0,192},{64,128},{128,64},{192,0},{16,80},{80,16},{144,208},{208,1... | collective-permute-start | bytes 1179656 | tf_op jit(solution)/shard_map/ppermute | solution.py:35
  124.8 7.0 %collective-permute-start.30 = (bf16[4,3,2,32,256]{4,3,2,1,0:T(8,128)(2,1)S(1)}, bf16[4,3,2,32,256]{4,3,2,1,0:T(8,128)(2,1)S(1)}, u32[]{:S(2)}, u32[]{:S(2)}) collective-permute-start(bf16[4,3,2,32,256]{4,3,2,1,0:T(8,128)(2,1)S(1)} %fusion.1), channel_id=1, source_target_pairs={{0,3},{1,2},{2,1},{3,0},{16,17},{17,16},{18,19},{19,18},{4,7},{5,6... | collective-permute-start | bytes 1179656 | tf_op jit(solution)/shard_map/ppermute | solution.py:35
  128.9 8.4 %collective-permute-start.28 = (f32[2,3,2,32,256]{4,3,2,1,0:T(8,128)S(1)}, f32[2,3,2,32,256]{4,3,2,1,0:T(8,128)S(1)}, u32[]{:S(2)}, u32[]{:S(2)}) collective-permute-start(f32[2,3,2,32,256]{4,3,2,1,0:T(8,128)S(1)} %get-tuple-element.84), channel_id=1, source_target_pairs={{0,1},{1,0},{2,3},{3,2},{16,19},{17,18},{18,17},{19,16},{4,5},{5,4... | collective-permute-start | bytes 1179656 | tf_op jit(solution)/shard_map/ppermute | solution.py:35
  132.0 7.9 %collective-permute-start.31 = (f32[2,3,2,32,256]{4,3,2,1,0:T(8,128)S(1)}, f32[2,3,2,32,256]{4,3,2,1,0:T(8,128)S(1)}, u32[]{:S(2)}, u32[]{:S(2)}) collective-permute-start(f32[2,3,2,32,256]{4,3,2,1,0:T(8,128)S(1)} %get-tuple-element.86), channel_id=1, source_target_pairs={{0,64},{64,0},{128,192},{192,128},{16,208},{80,144},{144,80},{208,... | collective-permute-start | bytes 1179656 | tf_op jit(solution)/shard_map/ppermute | solution.py:35
  137.3 4.9 %collective-permute-start.29 = (f32[3,2,32,256]{3,2,1,0:T(8,128)S(1)}, f32[3,2,32,256]{3,2,1,0:T(8,128)S(1)}, u32[]{:S(2)}, u32[]{:S(2)}) collective-permute-start(f32[3,2,32,256]{3,2,1,0:T(8,128)S(1)} %fusion.6), channel_id=1, source_target_pairs={{0,3},{1,2},{2,1},{3,0},{16,17},{17,16},{18,19},{19,18},{4,7},{5,6... | collective-permute-start | bytes 589832 | tf_op jit(solution)/shard_map/ppermute | solution.py:35
  140.0 4.6 %collective-permute-start.32 = (f32[3,2,32,256]{3,2,1,0:T(8,128)S(1)}, f32[3,2,32,256]{3,2,1,0:T(8,128)S(1)}, u32[]{:S(2)}, u32[]{:S(2)}) collective-permute-start(f32[3,2,32,256]{3,2,1,0:T(8,128)S(1)} %fusion.2), channel_id=1, source_target_pairs={{0,192},{64,128},{128,64},{192,0},{16,80},{80,16},{144,208},{208,1... | collective-permute-start | bytes 589832 | tf_op jit(solution)/shard_map/ppermute | solution.py:35
  167.8 11.6 %collective-permute-start.33 = (f32[8,3,16,256]{3,2,1,0:T(8,128)S(1)}, f32[8,3,16,256]{3,2,1,0:T(8,128)S(1)}, u32[]{:S(2)}, u32[]{:S(2)}) collective-permute-start(f32[8,3,16,256]{3,2,1,0:T(8,128)S(1)} %all_to_all.11), channel_id=1, source_target_pairs={{0,16},{16,0},{1,17},{17,1},{2,18},{18,2},{3,19},{19,3},{4,20},{20... | collective-permute-start | bytes 1179656 | tf_op jit(solution)/shard_map/ppermute | solution.py:22

commit v10 on v9

--- a/solution.py
+++ b/solution.py
@@ -409,7 +409,6 @@
     x_pair, _ = lax.optimization_barrier((x_pair, turned))
     shifts_pair = column_shifts(x_pair)
     slope_maps = slope_pre.reshape(frames, rows, width, chans)
-    slope_edges = edges_of(slope_maps, SPACE, 1)
     operands = (
         turned,
         turned_pair,
@@ -423,20 +422,19 @@
     info = jnp.concatenate([core, slots_of("x"), slots_of("y")])
     lower, sent_lower = weight_terms(0, own, info, *operands)
     upper, sent_upper = weight_terms(1, own, info, *operands)
-    slope_edges, _ = lax.optimization_barrier((slope_edges, (sent_lower, sent_upper)))
-    slope_wide = widened(slope_maps, slope_edges, SPACE, 1)
-    shifts_slope = column_shifts(slope_wide)
 
     came_lower = exchange(sent_lower, "x", 0)
     came_upper = exchange(sent_upper, "y", 0)
     passed = (lower[1] + widen(came_lower[1])).astype(jnp.bfloat16)
     last_lower = exchange(passed, "x", 1)
-    info, _ = lax.optimization_barrier((core, passed))
-    grad = input_gradient(0, info, shifts_slope, cotangent, k_mine, k_other)
-    came_upper, grad = lax.optimization_barrier((came_upper, grad))
+    slope_maps, _ = lax.optimization_barrier((slope_maps, passed))
+    slope_edges = edges_of(slope_maps, SPACE, 1)
+    slope_wide = widened(slope_maps, slope_edges, SPACE, 1)
+    shifts_slope = column_shifts(slope_wide)
     passed = (upper[1] + widen(came_upper[1])).astype(jnp.bfloat16)
     last_upper = exchange(passed, "y", 1)
     info, _ = lax.optimization_barrier((core, passed))
+    grad = input_gradient(0, info, shifts_slope, cotangent, k_mine, k_other)
     grad = input_gradient(1, info, shifts_slope, cotangent, k_mine, k_other, (grad,))
     last_lower, grad = lax.optimization_barrier((last_lower, grad))
 

time: 182 us -> 201 us (1.10)
  waiting for transfers between devices: 36.7 us -> 58.1 us
  local copies, waits for them, and re-layouts: 16 us -> 11 us
    ppermute x3, waiting for transfers between devices: 2.01 us -> 14.7 us  [edges_of(): lax.ppermute(lax.slice_in_dim(block, size - 1, size, axis=dim), axis, for...]
    ppermute x9, starting transfers between devices: 19.4 us -> 8.24 us  [swap(): return lax.ppermute(block, 'core', PAIR)]
    ppermute x3, waiting for transfers between devices: 0.01 us -> 7.71 us  [edges_of(): high = lax.ppermute(lax.slice_in_dim(block, 0, 1, axis=dim), axis, backward)]
    ppermute x16, starting transfers between devices: 13.6 us -> 21.1 us  [exchange(): return lax.ppermute(block, names, pairs)]
    ppermute x16, waiting for transfers between devices: 33.3 us -> 27.7 us  [exchange(): return lax.ppermute(block, names, pairs)]
    ppermute x3, waiting for transfers between devices: 0.01 us -> 5.12 us  [kernel_unit(): slots.append(lax.ppermute(unit, 'zh', [(i, i ^ k) for i in range(4)]))]
    ppermute x3, starting transfers between devices: 11.7 us -> 14.1 us  [edges_of(): high = lax.ppermute(lax.slice_in_dim(block, 0, 1, axis=dim), axis, backward)]
    unnamed x20 -> x16, local copies, waits for them, and re-layouts: 5.29 us -> 3.76 us
  transfers between devices with their start and end apart: 34 -> 34, of which waited for: 14 -> 13; matrix products, arithmetic and copies ran while one was open for 14% -> 11% of each run, Pallas kernels for 13% -> 10%
where the time goes in v10:
time: 201 us; the launch traced here: 200 us
  waiting for transfers between devices  58.1 us (29%)
  starting transfers between devices  56.1 us (28%)
  Pallas kernels  31.6 us (16%)
  blocking collectives  24.3 us (12%)
  other arithmetic  18.2 us (9%)
  local copies, waits for them, and re-layouts  11 us (5%)
    ppermute x16, waiting for transfers between devices, exchange(): return lax.ppermute(block, names, pairs)  27.7 us
    ppermute x16, starting transfers between devices, exchange(): return lax.ppermute(block, names, pairs)  21.1 us
    ppermute x3, waiting for transfers between devices, edges_of(): lax.ppermute(lax.slice_in_dim(block, size - 1, size, axis=dim), axis, for...  14.7 us
    ppermute x3, starting transfers between devices, edges_of(): high = lax.ppermute(lax.slice_in_dim(block, 0, 1, axis=dim), axis, backward)  14.1 us
    all_to_all x1, blocking collectives, per_device(): terms = lax.all_to_all(terms, ('zh', 'zl'), 0, 0, tiled=True)  14 us
    all_to_all x1, blocking collectives, gathered(): return lax.all_to_all(spread, axis, 0, 0, tiled=True)  10.3 us
    pallas_call x2, Pallas kernels, weight_terms(): pl.pallas_call(functools.partial(weight_kernel, upper), out_shape=(jax.Sh...  9.31 us
    ppermute x3, starting transfers between devices, kernel_unit(): slots.append(lax.ppermute(unit, 'zh', [(i, i ^ k) for i in range(4)]))  9.02 us
  transfers between devices with their start and end apart: 34, of which 13 were waited for; matrix products, arithmetic and copies ran while one was open for 11% of the time, Pallas kernels for 10%

profile of v10, /device:TPU:1, one launch (start us, length us, event | category | flops | bytes accessed | tf_op | source)
XLA Modules:
  0.0 200.4 jit_solution(17807338804048295892)
XLA Ops:
  0.6 0.9 fusion.10
  1.6 3.9 %collective-permute-start.2 = (bf16[3,32,256]{2,1,0:T(8,128)(2,1)S(1)}, bf16[3,32,256]{2,1,0:T(8,128)(2,1)S(1)}, u32[]{:S(2)}, u32[]{:S(2)}) collective-permute-start(bf16[3,32,256]{2,1,0:T(8,128)(2,1)S(1)} %fusion.10), channel_id=1, source_target_pairs={{0,4},{4,0},{8,12},{12,8},{1,5},{5,1},{9,13},{13,9},{2,6},{6,2},{1... | collective-permute-start | bytes 147464 | tf_op jit(solution)/shard_map/ppermute | solution.py:367
  5.5 5.1 %collective-permute-start.1 = (bf16[3,32,256]{2,1,0:T(8,128)(2,1)S(1)}, bf16[3,32,256]{2,1,0:T(8,128)(2,1)S(1)}, u32[]{:S(2)}, u32[]{:S(2)}) collective-permute-start(bf16[3,32,256]{2,1,0:T(8,128)(2,1)S(1)} %fusion.10), channel_id=1, source_target_pairs={{0,8},{4,12},{8,0},{12,4},{1,9},{5,13},{9,1},{13,5},{2,10},{6,14},... | collective-permute-start | bytes 147464 | tf_op jit(solution)/shard_map/ppermute | solution.py:367
  10.6 2.1 %collective-permute-done.1 = bf16[3,32,256]{2,1,0:T(8,128)(2,1)S(1)} collective-permute-done((bf16[3,32,256]{2,1,0:T(8,128)(2,1)S(1)}, bf16[3,32,256]{2,1,0:T(8,128)(2,1)S(1)}, u32[]{:S(2)}, u32[]{:S(2)}) %collective-permute-start.1) | collective-permute-done | bytes 49184 | tf_op jit(solution)/shard_map/ppermute | solution.py:367
  12.7 3.0 %collective-permute-done = bf16[3,32,256]{2,1,0:T(8,128)(2,1)S(1)} collective-permute-done((bf16[3,32,256]{2,1,0:T(8,128)(2,1)S(1)}, bf16[3,32,256]{2,1,0:T(8,128)(2,1)S(1)}, u32[]{:S(2)}, u32[]{:S(2)}) %collective-permute-start) | collective-permute-done | bytes 49184 | tf_op jit(solution)/shard_map/ppermute | solution.py:367
  15.8 2.8 %collective-permute-start.3 = (bf16[2,3,32,256]{3,2,1,0:T(8,128)(2,1)S(1)}, bf16[2,3,32,256]{3,2,1,0:T(8,128)(2,1)S(1)}, u32[]{:S(2)}, u32[]{:S(2)}) collective-permute-start(bf16[2,3,32,256]{3,2,1,0:T(8,128)(2,1)S(1)} %pad_maximum_fusion.14), channel_id=1, source_target_pairs={{0,1},{1,0},{2,3},{3,2},{16,19},{17,18},{18,17},{19,16},{4,5},{5,4... | collective-permute-start | bytes 294920 | tf_op jit(solution)/shard_map/ppermute | solution.py:35
  18.6 2.6 %collective-permute-start.7 = (bf16[2,3,32,256]{3,2,1,0:T(8,128)(2,1)S(1)}, bf16[2,3,32,256]{3,2,1,0:T(8,128)(2,1)S(1)}, u32[]{:S(2)}, u32[]{:S(2)}) collective-permute-start(bf16[2,3,32,256]{3,2,1,0:T(8,128)(2,1)S(1)} %pad_maximum_fusion.15), channel_id=1, source_target_pairs={{0,64},{64,0},{128,192},{192,128},{16,208},{80,144},{144,80},{208,... | collective-permute-start | bytes 294920 | tf_op jit(solution)/shard_map/ppermute | solution.py:35
  21.3 5.7 %collective-permute-start.12 = (bf16[2,1,192,512]{3,2,1,0:T(8,128)(2,1)S(1)}, bf16[2,1,192,512]{3,2,1,0:T(8,128)(2,1)S(1)}, u32[]{:S(2)}, u32[]{:S(2)}) collective-permute-start(bf16[2,1,192,512]{3,2,1,0:T(8,128)(2,1)S(1)} %get-tuple-element.96), channel_id=1, source_target_pairs={{1,0},{2,1},{3,2},{4,3},{5,4},{6,5},{7,6},{8,7},{9,8},{10,9},{11,1... | collective-permute-start | bytes 1179656 | tf_op jit(solution)/shard_map/ppermute | solution.py:86
  27.0 0.7 pad_maximum_fusion.11
  27.7 0.7 pad_maximum_fusion.12
  28.4 0.9 fusion.17
  29.3 3.4 %collective-permute-start.13 = (bf16[1,2,192,512]{3,2,1,0:T(8,128)(2,1)}, bf16[1,2,192,512]{3,2,1,0:T(8,128)(2,1)}, u32[]{:S(2)}, u32[]{:S(2)}) collective-permute-start(bf16[1,2,192,512]{3,2,1,0:T(8,128)(2,1)} %get-tuple-element.93), channel_id=1, source_target_pairs={{0,16},{16,32},{32,48},{48,64},{64,80},{80,96},{96,112},{112,128},... | collective-permute-start | bytes 1179656 | tf_op jit(solution)/shard_map/ppermute | solution.py:85
  32.8 0.7 collective-permute-done.8
  33.5 2.9 %collective-permute-start.14 = (bf16[1,2,192,512]{3,2,1,0:T(8,128)(2,1)}, bf16[1,2,192,512]{3,2,1,0:T(8,128)(2,1)S(1)}, u32[]{:S(2)}, u32[]{:S(2)}) collective-permute-start(bf16[1,2,192,512]{3,2,1,0:T(8,128)(2,1)} %get-tuple-element.94), channel_id=1, source_target_pairs={{16,0},{32,16},{48,32},{64,48},{80,64},{96,80},{112,96},{128,112},... | collective-permute-start | bytes 1179656 | tf_op jit(solution)/shard_map/ppermute | solution.py:86
  36.4 1.7 pad_maximum_fusion.10
  38.1 3.0 %collective-permute-start.9 = (bf16[4,2,3,32,256]{4,3,2,1,0:T(8,128)(2,1)}, bf16[4,2,3,32,256]{4,3,2,1,0:T(8,128)(2,1)}, u32[]{:S(2)}, u32[]{:S(2)}) collective-permute-start(bf16[4,2,3,32,256]{4,3,2,1,0:T(8,128)(2,1)} %pad_maximum_fusion.10), channel_id=1, source_target_pairs={{0,1},{1,0},{2,3},{3,2},{16,19},{17,18},{18,17},{19,16},{4,5},{5,4... | collective-permute-start | bytes 1179656 | tf_op jit(solution)/shard_map/ppermute | solution.py:35
  41.1 1.7 pad_maximum_fusion.9
  42.8 1.8 collective-permute-start.5
  44.6 0.8 broadcast_select_fusion.3
  45.4 1.0 broadcast_select_fusion.1
  46.5 7.7 %collective-permute-done.14 = bf16[1,2,192,512]{3,2,1,0:T(8,128)(2,1)S(1)} collective-permute-done((bf16[1,2,192,512]{3,2,1,0:T(8,128)(2,1)}, bf16[1,2,192,512]{3,2,1,0:T(8,128)(2,1)S(1)}, u32[]{:S(2)}, u32[]{:S(2)}) %collective-permute-start.14) | collective-permute-done | bytes 393248 | tf_op jit(solution)/shard_map/ppermute | solution.py:86
  54.2 1.3 pad_maximum_fusion.4.cot_hbm
  55.5 1.7 copy.13
  57.2 1.2 fusion.12
  58.7 1.2 pad_maximum_fusion.6.refs_0_
  59.8 2.5 %collective-permute-start.6 = (bf16[2,4,2,3,32,256]{5,4,3,2,1,0:T(8,128)(2,1)S(1)}, bf16[2,4,2,3,32,256]{5,4,3,2,1,0:T(8,128)(2,1)}, u32[]{:S(2)}, u32[]{:S(2)}) collective-permute-start(bf16[2,4,2,3,32,256]{5,4,3,2,1,0:T(8,128)(2,1)S(1)} %pad_maximum_fusion.6.refs_0_), channel_id=1, source_target_pairs={{0,192},{64,128},{128,64},{192,0},{16,80},{80,16},{144,208},{208,1... | collective-permute-start | bytes 2359304 | tf_op jit(solution)/shard_map/ppermute | solution.py:35
  62.4 2.2 %pad_maximum_fusion.7.refs_2_ = bf16[2,4,2,3,32,256]{5,4,3,2,1,0:T(8,128)(2,1)} fusion(bf16[1,4,2,3,32,256]{5,4,3,2,1,0:T(8,128)(2,1)} %bitcast.22, bf16[1,4,2,3,32,256]{5,4,3,2,1,0:T(8,128)(2,1)} %bitcast.21), kind=kLoop, calls=%fused_computation.11 | loop fusion | flops 393216 | bytes 1572864 | tf_op jit(solution)/shard_map/stack | solution.py:67
  64.5 0.5 fusion.14
  65.0 0.5 pad_bitcast_fusion.2
  65.6 2.5 %pad_maximum_fusion.x_hbm.x_ref = bf16[3,2,4,192,512]{4,3,2,1,0:T(8,128)(2,1)} fusion(bf16[1,2,4,192,512]{4,3,2,1,0:T(8,128)(2,1)S(1)} %get-tuple-element.101, bf16[1,2,4,192,512]{4,3,2,1,0:T(8,128)(2,1)S(1)} %get-tuple-element.85, bf16[1,2,4,192,512]{4,3,2,1,0:T(8,128)(2,1)S(1)} %get-tuple-element.102), kind=kLoop, calls=%fused_computation | loop fusion | flops 4718592 | bytes 9437184 | tf_op jit(solution)/shard_map/stack | solution.py:100
  68.1 4.1 %collective-permute-done.6.refs_1_ = bf16[2,4,2,3,32,256]{5,4,3,2,1,0:T(8,128)(2,1)} collective-permute-done((bf16[2,4,2,3,32,256]{5,4,3,2,1,0:T(8,128)(2,1)S(1)}, bf16[2,4,2,3,32,256]{5,4,3,2,1,0:T(8,128)(2,1)}, u32[]{:S(2)}, u32[]{:S(2)}) %collective-permute-start.6) | collective-permute-done | bytes 786464 | tf_op jit(solution)/shard_map/ppermute | solution.py:35
  72.1 3.8 %collective-permute-done.10.refs_3_ = bf16[2,4,2,3,32,256]{5,4,3,2,1,0:T(8,128)(2,1)} collective-permute-done((bf16[2,4,2,3,32,256]{5,4,3,2,1,0:T(8,128)(2,1)}, bf16[2,4,2,3,32,256]{5,4,3,2,1,0:T(8,128)(2,1)}, u32[]{:S(2)}, u32[]{:S(2)}) %collective-permute-start.10) | collective-permute-done | bytes 786464 | tf_op jit(solution)/shard_map/ppermute | solution.py:35
  76.0 1.0 collective-permute-start.16
  76.9 0.5 collective-permute-start.19
  77.5 0.5 collective-permute-start.20
  78.2 2.3 %copy-done = bf16[3,2,4,192,512]{4,3,2,1,0:T(8,128)(2,1)S(1)} copy-done((bf16[3,2,4,192,512]{4,3,2,1,0:T(8,128)(2,1)S(1)}, bf16[3,2,4,192,512]{4,3,2,1,0:T(8,128)(2,1)}, u32[]{:S(2)}) %copy-start) | copy-done | bytes 4718616
  80.5 1.4 copy-done.3
  81.9 6.8 %shard_map.67 = (f32[2,384,512]{2,1,0:T(8,128)S(1)}, f32[2,384,256]{2,1,0:T(8,128)S(1)}, bf16[4,4,3,4,32,256]{5,4,3,2,1,0:T(8,128)(2,1)S(1)}) custom-call(s32[9]{0:T(128)S(1)} %concatenate.63.info_ref, bf16[3,2,4,192,512]{4,3,2,1,0:T(8,128)(2,1)S(1)} %copy-done, bf16[4,2,192,512]{3,2,1,0:T(8,128)(2,1)S(1)} %copy-done.3, ...), custom_call_target="tpu_custom_call" | custom-call | flops 3200000000 | bytes 12000000 | tf_op jit(solution)/shard_map/pallas_call | solution.py:226
  88.8 7.9 %shard_map.68 = (bf16[2,384,256]{2,1,0:T(8,128)(2,1)S(1)}, bf16[2,384,256]{2,1,0:T(8,128)(2,1)S(1)}, bf16[2,384,512]{2,1,0:T(8,128)(2,1)S(1)}, bf16[512,768]{1,0...) custom-call(s32[9]{0:T(128)S(1)} %concatenate.55.info_ref, bf16[3,2,4,192,512]{4,3,2,1,0:T(8,128)(2,1)S(1)} %copy-done.1, ...), custom_call_target="tpu_custom_call" | custom-call | flops 3200000000 | bytes 15000000 | tf_op jit(solution)/shard_map/pallas_call | solution.py:235
  96.9 0.5 collective-permute-start.22
  98.2 1.4 collective-permute-done.22
  99.7 4.7 %shard_map.70 = (f32[4,4,3,2,32,256]{5,4,3,2,1,0:T(8,128)S(1)}, bf16[2,4,3,2,32,256]{5,4,3,2,1,0:T(8,128)(2,1)S(1)}) custom-call(s32[9]{0:T(128)S(1)} %pad_add_fusion.info_ref, bf16[512,768]{1,0:T(8,128)(2,1)S(1)} %get-tuple-element.58.turned_ref, bf16[512,768]{1,0:T(8,128)(2,1)S(1)} %collective-permute-done.21.turned_pair_ref, ...), custom_call_target="tpu_custom_call" | custom-call | flops 2400000000 | bytes 16000000 | tf_op jit(solution)/shard_map/pallas_call | solution.py:310
  104.7 4.7 %shard_map.69 = (f32[4,4,3,2,32,256]{5,4,3,2,1,0:T(8,128)S(1)}, bf16[2,4,3,2,32,256]{5,4,3,2,1,0:T(8,128)(2,1)S(1)}) custom-call(s32[9]{0:T(128)S(1)} %pad_add_fusion.info_ref, bf16[512,768]{1,0:T(8,128)(2,1)S(1)} %get-tuple-element.58.turned_ref, bf16[512,768]{1,0:T(8,128)(2,1)S(1)} %collective-permute-done.21.turned_pair_ref, ...), custom_call_target="tpu_custom_call" | custom-call | flops 2400000000 | bytes 16000000 | tf_op jit(solution)/shard_map/pallas_call | solution.py:310
  109.3 2.2 %collective-permute-start.23 = (bf16[2,4,3,2,32,256]{5,4,3,2,1,0:T(8,128)(2,1)S(1)}, bf16[2,4,3,2,32,256]{5,4,3,2,1,0:T(8,128)(2,1)S(1)}, u32[]{:S(2)}, u32[]{:S(2)}) collective-permute-start(bf16[2,4,3,2,32,256]{5,4,3,2,1,0:T(8,128)(2,1)S(1)} %get-tuple-element.65), channel_id=1, source_target_pairs={{0,64},{64,0},{128,192},{192,128},{16,208},{80,144},{144,80},{208,... | collective-permute-start | bytes 2359304 | tf_op jit(solution)/shard_map/ppermute | solution.py:35
  111.5 5.2 %collective-permute-done.25 = bf16[2,4,3,2,32,256]{5,4,3,2,1,0:T(8,128)(2,1)S(1)} collective-permute-done((bf16[2,4,3,2,32,256]{5,4,3,2,1,0:T(8,128)(2,1)S(1)}, bf16[2,4,3,2,32,256]{5,4,3,2,1,0:T(8,128)(2,1)S(1)}, u32[]{:S(2)}, u32[]{:S(2)}) %collective-permute-start.25) | collective-permute-done | bytes 786464 | tf_op jit(solution)/shard_map/ppermute | solution.py:35
  116.9 4.8 %collective-permute-done.23 = bf16[2,4,3,2,32,256]{5,4,3,2,1,0:T(8,128)(2,1)S(1)} collective-permute-done((bf16[2,4,3,2,32,256]{5,4,3,2,1,0:T(8,128)(2,1)S(1)}, bf16[2,4,3,2,32,256]{5,4,3,2,1,0:T(8,128)(2,1)S(1)}, u32[]{:S(2)}, u32[]{:S(2)}) %collective-permute-start.23) | collective-permute-done | bytes 786464 | tf_op jit(solution)/shard_map/ppermute | solution.py:35
  122.3 5.6 %collective-permute-start.27 = (bf16[2,1,192,512]{3,2,1,0:T(8,128)(2,1)S(1)}, bf16[2,1,192,512]{3,2,1,0:T(8,128)(2,1)S(1)}, u32[]{:S(2)}, u32[]{:S(2)}) collective-permute-start(bf16[2,1,192,512]{3,2,1,0:T(8,128)(2,1)S(1)} %get-tuple-element.90), channel_id=1, source_target_pairs={{1,0},{2,1},{3,2},{4,3},{5,4},{6,5},{7,6},{8,7},{9,8},{10,9},{11,1... | collective-permute-start | bytes 1179656 | tf_op jit(solution)/shard_map/ppermute | solution.py:86
  128.1 2.2 %collective-permute-start.31 = (f32[2,3,2,32,256]{4,3,2,1,0:T(8,128)S(1)}, f32[2,3,2,32,256]{4,3,2,1,0:T(8,128)S(1)}, u32[]{:S(2)}, u32[]{:S(2)}) collective-permute-start(f32[2,3,2,32,256]{4,3,2,1,0:T(8,128)S(1)} %get-tuple-element.78), channel_id=1, source_target_pairs={{0,64},{64,0},{128,192},{192,128},{16,208},{80,144},{144,80},{208,... | collective-permute-start | bytes 1179656 | tf_op jit(solution)/shard_map/ppermute | solution.py:35
  130.2 14.7 %collective-permute-done.26 = bf16[2,1,192,512]{3,2,1,0:T(8,128)(2,1)S(1)} collective-permute-done((bf16[2,1,192,512]{3,2,1,0:T(8,128)(2,1)S(1)}, bf16[2,1,192,512]{3,2,1,0:T(8,128)(2,1)S(1)}, u32[]{:S(2)}, u32[]{:S(2)}) %collective-permute-start.26) | collective-permute-done | bytes 393248 | tf_op jit(solution)/shard_map/ppermute | solution.py:85
  145.3 0.5 fusion.13
  145.8 0.4 pad_bitcast_fusion.1
  146.3 0.6 pad_maximum_fusion.1.x_ref
  146.9 3.8 %shard_map.71.refs_0_ = f32[2,384,512]{2,1,0:T(8,128)} custom-call(s32[1]{0:T(128)} %bitcast.info_ref, bf16[3,2,4,192,512]{4,3,2,1,0:T(8,128)(2,1)S(1)} %pad_maximum_fusion.1.x_ref, bf16[2,384,512]{2,1,0:T(8,128)(2,1)S(1)} %bitcast.99, bf16[4,4,3,4,32,256]{5,4,3,2,1,0:T(8,128)(2,1)S(1)} %get-tuple-element.71.mine_ref, ...), custom_call_target="tpu_custom_call" | custom-call | flops 1800000000 | bytes 8000000 | tf_op jit(solution)/shard_map/pallas_call | solution.py:346
  150.7 3.8 %shard_map.72 = f32[2,384,512]{2,1,0:T(8,128)} custom-call(s32[1]{0:T(128)} %bitcast.info_ref, bf16[3,2,4,192,512]{4,3,2,1,0:T(8,128)(2,1)S(1)} %pad_maximum_fusion.1.x_ref, bf16[2,384,512]{2,1,0:T(8,128)(2,1)S(1)} %bitcast.100, bf16[4,4,3,4,32,256]{5,4,3,2,1,0:T(8,128)(2,1)S(1)} %get-tuple-element.71.mine_ref, ...), custom_call_target="tpu_custom_call", output_to_operand_aliasing={{}: (5, {})} | custom-call | flops 1800000000 | bytes 8000000 | tf_op jit(solution)/shard_map/pallas_call | solution.py:346
  154.6 1.8 collective-permute-start.28
  156.4 1.5 collective-permute-start.32
  157.9 4.6 %collective-permute-done.28 = f32[2,3,2,32,256]{4,3,2,1,0:T(8,128)S(1)} collective-permute-done((f32[2,3,2,32,256]{4,3,2,1,0:T(8,128)S(1)}, f32[2,3,2,32,256]{4,3,2,1,0:T(8,128)S(1)}, u32[]{:S(2)}, u32[]{:S(2)}) %collective-permute-start.28) | collective-permute-done | bytes 393248 | tf_op jit(solution)/shard_map/ppermute | solution.py:35
  162.7 4.4 %collective-permute-done.29 = f32[3,2,32,256]{3,2,1,0:T(8,128)S(1)} collective-permute-done((f32[3,2,32,256]{3,2,1,0:T(8,128)S(1)}, f32[3,2,32,256]{3,2,1,0:T(8,128)S(1)}, u32[]{:S(2)}, u32[]{:S(2)}) %collective-permute-start.29) | collective-permute-done | bytes 196640 | tf_op jit(solution)/shard_map/ppermute | solution.py:35
  167.3 14.0 %all_to_all.10 = bf16[8,3,16,256]{3,2,1,0:T(8,128)(2,1)S(1)} all-to-all(bf16[8,3,16,256]{3,2,1,0:T(8,128)(2,1)S(1)} %bitcast.117), channel_id=1, replica_groups=mesh['x'=4,'zl'=2,'core'=2,'zh'=4,'y'=4] {'zh','zl'}, dimensions={0} | all-to-all | bytes 393216 | tf_op jit(solution)/shard_map/all_to_all | solution.py:453
  181.4 10.3 %all_to_all.11 = f32[8,3,16,256]{3,2,1,0:T(8,128)S(1)} all-to-all(f32[8,3,16,256]{3,2,1,0:T(8,128)S(1)} %broadcast_in_dim.30), channel_id=1, replica_groups=mesh['x'=4,'zl'=2,'core'=2,'zh'=4,'y'=4] {'x','zl'}, dimensions={0} | all-to-all | bytes 786432 | tf_op jit(solution)/shard_map/all_to_all | solution.py:73
  191.7 5.6 %collective-permute-start.33 = (f32[8,3,16,256]{3,2,1,0:T(8,128)S(1)}, f32[8,3,16,256]{3,2,1,0:T(8,128)S(1)}, u32[]{:S(2)}, u32[]{:S(2)}) collective-permute-start(f32[8,3,16,256]{3,2,1,0:T(8,128)S(1)} %all_to_all.11), channel_id=1, source_target_pairs={{0,16},{16,0},{1,17},{17,1},{2,18},{18,2},{3,19},{19,3},{4,20},{20... | collective-permute-start | bytes 1179656 | tf_op jit(solution)/shard_map/ppermute | solution.py:22
  197.2 1.3 collective-permute-done.33
  198.9 0.9 copy.15
  199.7 0.7 copy.16
  (87 shorter events, 4.0 us)
Async XLA Ops:
  0.6 20.5 %copy-start.7 = (bf16[2,2,192,512]{3,2,1,0:T(8,128)(2,1)S(1)}, bf16[2,2,192,512]{3,2,1,0:T(8,128)(2,1)}, u32[]{:S(2)}) copy-start(bf16[2,2,192,512]{3,2,1,0:T(8,128)(2,1)} %param.4) | copy-start | bytes 2359300
  1.6 9.0 %collective-permute-start.2 = (bf16[3,32,256]{2,1,0:T(8,128)(2,1)S(1)}, bf16[3,32,256]{2,1,0:T(8,128)(2,1)S(1)}, u32[]{:S(2)}, u32[]{:S(2)}) collective-permute-start(bf16[3,32,256]{2,1,0:T(8,128)(2,1)S(1)} %fusion.10), channel_id=1, source_target_pairs={{0,4},{4,0},{8,12},{12,8},{1,5},{5,1},{9,13},{13,9},{2,6},{6,2},{1... | collective-permute-start | bytes 147464 | tf_op jit(solution)/shard_map/ppermute | solution.py:367
  5.5 7.3 %collective-permute-start.1 = (bf16[3,32,256]{2,1,0:T(8,128)(2,1)S(1)}, bf16[3,32,256]{2,1,0:T(8,128)(2,1)S(1)}, u32[]{:S(2)}, u32[]{:S(2)}) collective-permute-start(bf16[3,32,256]{2,1,0:T(8,128)(2,1)S(1)} %fusion.10), channel_id=1, source_target_pairs={{0,8},{4,12},{8,0},{12,4},{1,9},{5,13},{9,1},{13,5},{2,10},{6,14},... | collective-permute-start | bytes 147464 | tf_op jit(solution)/shard_map/ppermute | solution.py:367
  10.6 5.1 %collective-permute-start = (bf16[3,32,256]{2,1,0:T(8,128)(2,1)S(1)}, bf16[3,32,256]{2,1,0:T(8,128)(2,1)S(1)}, u32[]{:S(2)}, u32[]{:S(2)}) collective-permute-start(bf16[3,32,256]{2,1,0:T(8,128)(2,1)S(1)} %fusion.10), channel_id=1, source_target_pairs={{0,12},{4,8},{8,4},{12,0},{1,13},{5,9},{9,5},{13,1},{2,14},{6,10},... | collective-permute-start | bytes 147464 | tf_op jit(solution)/shard_map/ppermute | solution.py:367
  10.6 17.8 %copy-start.2 = (bf16[2,2,192,512]{3,2,1,0:T(8,128)(2,1)S(1)}, bf16[2,2,192,512]{3,2,1,0:T(8,128)(2,1)}, u32[]{:S(2)}) copy-start(bf16[2,2,192,512]{3,2,1,0:T(8,128)(2,1)} %param.5) | copy-start | bytes 2359300
  15.8 11.2 %collective-permute-start.3 = (bf16[2,3,32,256]{3,2,1,0:T(8,128)(2,1)S(1)}, bf16[2,3,32,256]{3,2,1,0:T(8,128)(2,1)S(1)}, u32[]{:S(2)}, u32[]{:S(2)}) collective-permute-start(bf16[2,3,32,256]{3,2,1,0:T(8,128)(2,1)S(1)} %pad_maximum_fusion.14), channel_id=1, source_target_pairs={{0,1},{1,0},{2,3},{3,2},{16,19},{17,18},{18,17},{19,16},{4,5},{5,4... | collective-permute-start | bytes 294920 | tf_op jit(solution)/shard_map/ppermute | solution.py:35
  18.6 8.4 %collective-permute-start.7 = (bf16[2,3,32,256]{3,2,1,0:T(8,128)(2,1)S(1)}, bf16[2,3,32,256]{3,2,1,0:T(8,128)(2,1)S(1)}, u32[]{:S(2)}, u32[]{:S(2)}) collective-permute-start(bf16[2,3,32,256]{3,2,1,0:T(8,128)(2,1)S(1)} %pad_maximum_fusion.15), channel_id=1, source_target_pairs={{0,64},{64,0},{128,192},{192,128},{16,208},{80,144},{144,80},{208,... | collective-permute-start | bytes 294920 | tf_op jit(solution)/shard_map/ppermute | solution.py:35
  21.2 21.6 %collective-permute-start.11 = (bf16[2,1,192,512]{3,2,1,0:T(8,128)(2,1)S(1)}, bf16[2,1,192,512]{3,2,1,0:T(8,128)(2,1)S(1)}, u32[]{:S(2)}, u32[]{:S(2)}) collective-permute-start(bf16[2,1,192,512]{3,2,1,0:T(8,128)(2,1)S(1)} %get-tuple-element.95), channel_id=1, source_target_pairs={{0,1},{1,2},{2,3},{3,4},{4,5},{5,6},{6,7},{7,8},{8,9},{9,10},{10,1... | collective-permute-start | bytes 1179656 | tf_op jit(solution)/shard_map/ppermute | solution.py:85
  21.3 23.3 %collective-permute-start.12 = (bf16[2,1,192,512]{3,2,1,0:T(8,128)(2,1)S(1)}, bf16[2,1,192,512]{3,2,1,0:T(8,128)(2,1)S(1)}, u32[]{:S(2)}, u32[]{:S(2)}) collective-permute-start(bf16[2,1,192,512]{3,2,1,0:T(8,128)(2,1)S(1)} %get-tuple-element.96), channel_id=1, source_target_pairs={{1,0},{2,1},{3,2},{4,3},{5,4},{6,5},{7,6},{8,7},{9,8},{10,9},{11,1... | collective-permute-start | bytes 1179656 | tf_op jit(solution)/shard_map/ppermute | solution.py:86
  27.7 10.4 %collective-permute-start.4 = (bf16[2,2,3,32,256]{4,3,2,1,0:T(8,128)(2,1)}, bf16[2,2,3,32,256]{4,3,2,1,0:T(8,128)(2,1)}, u32[]{:S(2)}, u32[]{:S(2)}) collective-permute-start(bf16[2,2,3,32,256]{4,3,2,1,0:T(8,128)(2,1)} %pad_maximum_fusion.11), channel_id=1, source_target_pairs={{0,3},{1,2},{2,1},{3,0},{16,17},{17,16},{18,19},{19,18},{4,7},{5,6... | collective-permute-start | bytes 589832 | tf_op jit(solution)/shard_map/ppermute | solution.py:35
  28.4 5.1 %collective-permute-start.8 = (bf16[2,2,3,32,256]{4,3,2,1,0:T(8,128)(2,1)}, bf16[2,2,3,32,256]{4,3,2,1,0:T(8,128)(2,1)}, u32[]{:S(2)}, u32[]{:S(2)}) collective-permute-start(bf16[2,2,3,32,256]{4,3,2,1,0:T(8,128)(2,1)} %pad_maximum_fusion.12), channel_id=1, source_target_pairs={{0,192},{64,128},{128,64},{192,0},{16,80},{80,16},{144,208},{208,1... | collective-permute-start | bytes 589832 | tf_op jit(solution)/shard_map/ppermute | solution.py:35
  29.3 16.1 %collective-permute-start.13 = (bf16[1,2,192,512]{3,2,1,0:T(8,128)(2,1)}, bf16[1,2,192,512]{3,2,1,0:T(8,128)(2,1)}, u32[]{:S(2)}, u32[]{:S(2)}) collective-permute-start(bf16[1,2,192,512]{3,2,1,0:T(8,128)(2,1)} %get-tuple-element.93), channel_id=1, source_target_pairs={{0,16},{16,32},{32,48},{48,64},{64,80},{80,96},{96,112},{112,128},... | collective-permute-start | bytes 1179656 | tf_op jit(solution)/shard_map/ppermute | solution.py:85
  33.5 20.7 %collective-permute-start.14 = (bf16[1,2,192,512]{3,2,1,0:T(8,128)(2,1)}, bf16[1,2,192,512]{3,2,1,0:T(8,128)(2,1)S(1)}, u32[]{:S(2)}, u32[]{:S(2)}) collective-permute-start(bf16[1,2,192,512]{3,2,1,0:T(8,128)(2,1)} %get-tuple-element.94), channel_id=1, source_target_pairs={{16,0},{32,16},{48,32},{64,48},{80,64},{96,80},{112,96},{128,112},... | collective-permute-start | bytes 1179656 | tf_op jit(solution)/shard_map/ppermute | solution.py:86
  38.1 20.5 %collective-permute-start.9 = (bf16[4,2,3,32,256]{4,3,2,1,0:T(8,128)(2,1)}, bf16[4,2,3,32,256]{4,3,2,1,0:T(8,128)(2,1)}, u32[]{:S(2)}, u32[]{:S(2)}) collective-permute-start(bf16[4,2,3,32,256]{4,3,2,1,0:T(8,128)(2,1)} %pad_maximum_fusion.10), channel_id=1, source_target_pairs={{0,1},{1,0},{2,3},{3,2},{16,19},{17,18},{18,17},{19,16},{4,5},{5,4... | collective-permute-start | bytes 1179656 | tf_op jit(solution)/shard_map/ppermute | solution.py:35
  42.8 15.9 %collective-permute-start.5 = (bf16[4,2,3,32,256]{4,3,2,1,0:T(8,128)(2,1)}, bf16[4,2,3,32,256]{4,3,2,1,0:T(8,128)(2,1)}, u32[]{:S(2)}, u32[]{:S(2)}) collective-permute-start(bf16[4,2,3,32,256]{4,3,2,1,0:T(8,128)(2,1)} %pad_maximum_fusion.9), channel_id=1, source_target_pairs={{0,64},{64,0},{128,192},{192,128},{16,208},{80,144},{144,80},{208,... | collective-permute-start | bytes 1179656 | tf_op jit(solution)/shard_map/ppermute | solution.py:35
  58.5 9.5 %collective-permute-start.15 = (bf16[2,4,192,256]{3,2,1,0:T(8,128)(2,1)S(1)}, bf16[2,4,192,256]{3,2,1,0:T(8,128)(2,1)S(1)}, u32[]{:S(2)}, u32[]{:S(2)}) collective-permute-start(bf16[2,4,192,256]{3,2,1,0:T(8,128)(2,1)S(1)} %constant_dynamic-slice_fusion), channel_id=1, source_target_pairs={{0,16},{16,0},{1,17},{17,1},{2,18},{18,2},{3,19},{19,3},{4,20},{20... | collective-permute-start | bytes 2359304 | tf_op jit(solution)/shard_map/ppermute | solution.py:22
  59.8 12.3 %collective-permute-start.6 = (bf16[2,4,2,3,32,256]{5,4,3,2,1,0:T(8,128)(2,1)S(1)}, bf16[2,4,2,3,32,256]{5,4,3,2,1,0:T(8,128)(2,1)}, u32[]{:S(2)}, u32[]{:S(2)}) collective-permute-start(bf16[2,4,2,3,32,256]{5,4,3,2,1,0:T(8,128)(2,1)S(1)} %pad_maximum_fusion.6.refs_0_), channel_id=1, source_target_pairs={{0,192},{64,128},{128,64},{192,0},{16,80},{80,16},{144,208},{208,1... | collective-permute-start | bytes 2359304 | tf_op jit(solution)/shard_map/ppermute | solution.py:35
  64.5 11.5 %collective-permute-start.10 = (bf16[2,4,2,3,32,256]{5,4,3,2,1,0:T(8,128)(2,1)}, bf16[2,4,2,3,32,256]{5,4,3,2,1,0:T(8,128)(2,1)}, u32[]{:S(2)}, u32[]{:S(2)}) collective-permute-start(bf16[2,4,2,3,32,256]{5,4,3,2,1,0:T(8,128)(2,1)} %pad_maximum_fusion.7.refs_2_), channel_id=1, source_target_pairs={{0,3},{1,2},{2,1},{3,0},{16,17},{17,16},{18,19},{19,18},{4,7},{5,6... | collective-permute-start | bytes 2359304 | tf_op jit(solution)/shard_map/ppermute | solution.py:35
  68.1 7.9 %copy-start.5 = (bf16[2,4,192,256]{3,2,1,0:T(8,128)(2,1)}, bf16[2,4,192,256]{3,2,1,0:T(8,128)(2,1)S(1)}, u32[]{:S(2)}) copy-start(bf16[2,4,192,256]{3,2,1,0:T(8,128)(2,1)S(1)} %collective-permute-done.15) | copy-start | bytes 2359300
  76.0 12.8 %collective-permute-start.16 = (bf16[512,1536]{1,0:T(8,128)(2,1)S(1)}, bf16[512,1536]{1,0:T(8,128)(2,1)}, u32[]{:S(2)}, u32[]{:S(2)}) collective-permute-start(bf16[512,1536]{1,0:T(8,128)(2,1)S(1)} %bitcast.96), channel_id=1, source_target_pairs={{0,16},{16,0},{1,17},{17,1},{2,18},{18,2},{3,19},{19,3},{4,20},{20... | collective-permute-start | bytes 4718600 | tf_op jit(solution)/shard_map/ppermute | solution.py:22
  76.9 11.8 %collective-permute-start.17 = (bf16[2,4,2,3,32,256]{5,4,3,2,1,0:T(8,128)(2,1)S(1)}, bf16[2,4,2,3,32,256]{5,4,3,2,1,0:T(8,128)(2,1)}, u32[]{:S(2)}, u32[]{:S(2)}) collective-permute-start(bf16[2,4,2,3,32,256]{5,4,3,2,1,0:T(8,128)(2,1)S(1)} %pad_maximum_fusion.6.refs_0_), channel_id=1, source_target_pairs={{0,16},{16,0},{1,17},{17,1},{2,18},{18,2},{3,19},{19,3},{4,20},{20... | collective-permute-start | bytes 2359304 | tf_op jit(solution)/shard_map/ppermute | solution.py:22
  76.9 11.8 %collective-permute-start.19 = (bf16[2,4,2,3,32,256]{5,4,3,2,1,0:T(8,128)(2,1)}, bf16[2,4,2,3,32,256]{5,4,3,2,1,0:T(8,128)(2,1)}, u32[]{:S(2)}, u32[]{:S(2)}) collective-permute-start(bf16[2,4,2,3,32,256]{5,4,3,2,1,0:T(8,128)(2,1)} %pad_maximum_fusion.7.refs_2_), channel_id=1, source_target_pairs={{0,16},{16,0},{1,17},{17,1},{2,18},{18,2},{3,19},{19,3},{4,20},{20... | collective-permute-start | bytes 2359304 | tf_op jit(solution)/shard_map/ppermute | solution.py:22
  77.5 11.3 %collective-permute-start.18 = (bf16[2,4,2,3,32,256]{5,4,3,2,1,0:T(8,128)(2,1)}, bf16[2,4,2,3,32,256]{5,4,3,2,1,0:T(8,128)(2,1)}, u32[]{:S(2)}, u32[]{:S(2)}) collective-permute-start(bf16[2,4,2,3,32,256]{5,4,3,2,1,0:T(8,128)(2,1)} %collective-permute-done.6.refs_1_), channel_id=1, source_target_pairs={{0,16},{16,0},{1,17},{17,1},{2,18},{18,2},{3,19},{19,3},{4,20},{20... | collective-permute-start | bytes 2359304 | tf_op jit(solution)/shard_map/ppermute | solution.py:22
  77.5 11.3 %collective-permute-start.20 = (bf16[2,4,2,3,32,256]{5,4,3,2,1,0:T(8,128)(2,1)}, bf16[2,4,2,3,32,256]{5,4,3,2,1,0:T(8,128)(2,1)}, u32[]{:S(2)}, u32[]{:S(2)}) collective-permute-start(bf16[2,4,2,3,32,256]{5,4,3,2,1,0:T(8,128)(2,1)} %collective-permute-done.10.refs_3_), channel_id=1, source_target_pairs={{0,16},{16,0},{1,17},{17,1},{2,18},{18,2},{3,19},{19,3},{4,20},{20... | collective-permute-start | bytes 2359304 | tf_op jit(solution)/shard_map/ppermute | solution.py:22
  78.2 2.3 %copy-start = (bf16[3,2,4,192,512]{4,3,2,1,0:T(8,128)(2,1)S(1)}, bf16[3,2,4,192,512]{4,3,2,1,0:T(8,128)(2,1)}, u32[]{:S(2)}) copy-start(bf16[3,2,4,192,512]{4,3,2,1,0:T(8,128)(2,1)} %pad_maximum_fusion.x_hbm.x_ref) | copy-start | bytes 14155780
  80.5 1.4 copy-start.3
  81.9 6.9 %copy-start.1 = (bf16[3,2,4,192,512]{4,3,2,1,0:T(8,128)(2,1)S(1)}, bf16[3,2,4,192,512]{4,3,2,1,0:T(8,128)(2,1)}, u32[]{:S(2)}) copy-start(bf16[3,2,4,192,512]{4,3,2,1,0:T(8,128)(2,1)} %pad_maximum_fusion.x_hbm.x_ref) | copy-start | bytes 14155780
  81.9 6.9 %copy-start.4 = (bf16[4,2,192,512]{3,2,1,0:T(8,128)(2,1)S(1)}, bf16[4,2,192,512]{3,2,1,0:T(8,128)(2,1)}, u32[]{:S(2)}) copy-start(bf16[4,2,192,512]{3,2,1,0:T(8,128)(2,1)} %pad_maximum_fusion.4.cot_hbm) | copy-start | bytes 4718596
  88.8 8.6 %copy-start.6 = (bf16[2,4,192,256]{3,2,1,0:T(8,128)(2,1)S(1)}, bf16[2,4,192,256]{3,2,1,0:T(8,128)(2,1)}, u32[]{:S(2)}) copy-start(bf16[2,4,192,256]{3,2,1,0:T(8,128)(2,1)} %copy-done.5) | copy-start | bytes 2359300
  96.7 2.9 %collective-permute-start.21 = (bf16[512,768]{1,0:T(8,128)(2,1)S(1)}, bf16[512,768]{1,0:T(8,128)(2,1)S(1)}, u32[]{:S(2)}, u32[]{:S(2)}) collective-permute-start(bf16[512,768]{1,0:T(8,128)(2,1)S(1)} %get-tuple-element.58.turned_ref), channel_id=1, source_target_pairs={{0,16},{16,0},{1,17},{17,1},{2,18},{18,2},{3,19},{19,3},{4,20},{20... | collective-permute-start | bytes 2359304 | tf_op jit(solution)/shard_map/ppermute | solution.py:22
  96.9 2.8 %collective-permute-start.22 = (bf16[2,384,256]{2,1,0:T(8,128)(2,1)S(1)}, bf16[2,384,256]{2,1,0:T(8,128)(2,1)S(1)}, u32[]{:S(2)}, u32[]{:S(2)}) collective-permute-start(bf16[2,384,256]{2,1,0:T(8,128)(2,1)S(1)} %get-tuple-element.63), channel_id=1, source_target_pairs={{0,16},{16,0},{1,17},{17,1},{2,18},{18,2},{3,19},{19,3},{4,20},{20... | collective-permute-start | bytes 1179656 | tf_op jit(solution)/shard_map/ppermute | solution.py:22
  104.3 12.4 %collective-permute-start.25 = (bf16[2,4,3,2,32,256]{5,4,3,2,1,0:T(8,128)(2,1)S(1)}, bf16[2,4,3,2,32,256]{5,4,3,2,1,0:T(8,128)(2,1)S(1)}, u32[]{:S(2)}, u32[]{:S(2)}) collective-permute-start(bf16[2,4,3,2,32,256]{5,4,3,2,1,0:T(8,128)(2,1)S(1)} %get-tuple-element.67), channel_id=1, source_target_pairs={{0,1},{1,0},{2,3},{3,2},{16,19},{17,18},{18,17},{19,16},{4,5},{5,4... | collective-permute-start | bytes 2359304 | tf_op jit(solution)/shard_map/ppermute | solution.py:35
  109.3 12.4 %collective-permute-start.23 = (bf16[2,4,3,2,32,256]{5,4,3,2,1,0:T(8,128)(2,1)S(1)}, bf16[2,4,3,2,32,256]{5,4,3,2,1,0:T(8,128)(2,1)S(1)}, u32[]{:S(2)}, u32[]{:S(2)}) collective-permute-start(bf16[2,4,3,2,32,256]{5,4,3,2,1,0:T(8,128)(2,1)S(1)} %get-tuple-element.65), channel_id=1, source_target_pairs={{0,64},{64,0},{128,192},{192,128},{16,208},{80,144},{144,80},{208,... | collective-permute-start | bytes 2359304 | tf_op jit(solution)/shard_map/ppermute | solution.py:35
  116.8 11.1 %collective-permute-start.30 = (bf16[4,3,2,32,256]{4,3,2,1,0:T(8,128)(2,1)S(1)}, bf16[4,3,2,32,256]{4,3,2,1,0:T(8,128)(2,1)S(1)}, u32[]{:S(2)}, u32[]{:S(2)}) collective-permute-start(bf16[4,3,2,32,256]{4,3,2,1,0:T(8,128)(2,1)S(1)} %fusion.1), channel_id=1, source_target_pairs={{0,3},{1,2},{2,1},{3,0},{16,17},{17,16},{18,19},{19,18},{4,7},{5,6... | collective-permute-start | bytes 1179656 | tf_op jit(solution)/shard_map/ppermute | solution.py:35
  122.0 23.0 %collective-permute-start.26 = (bf16[2,1,192,512]{3,2,1,0:T(8,128)(2,1)S(1)}, bf16[2,1,192,512]{3,2,1,0:T(8,128)(2,1)S(1)}, u32[]{:S(2)}, u32[]{:S(2)}) collective-permute-start(bf16[2,1,192,512]{3,2,1,0:T(8,128)(2,1)S(1)} %get-tuple-element.89), channel_id=1, source_target_pairs={{0,1},{1,2},{2,3},{3,4},{4,5},{5,6},{6,7},{7,8},{8,9},{9,10},{10,1... | collective-permute-start | bytes 1179656 | tf_op jit(solution)/shard_map/ppermute | solution.py:85
  122.0 32.4 %collective-permute-start.24 = (bf16[4,3,2,32,256]{4,3,2,1,0:T(8,128)(2,1)S(1)}, bf16[4,3,2,32,256]{4,3,2,1,0:T(8,128)(2,1)S(1)}, u32[]{:S(2)}, u32[]{:S(2)}) collective-permute-start(bf16[4,3,2,32,256]{4,3,2,1,0:T(8,128)(2,1)S(1)} %fusion), channel_id=1, source_target_pairs={{0,192},{64,128},{128,64},{192,0},{16,80},{80,16},{144,208},{208,1... | collective-permute-start | bytes 1179656 | tf_op jit(solution)/shard_map/ppermute | solution.py:35
  122.3 22.7 %collective-permute-start.27 = (bf16[2,1,192,512]{3,2,1,0:T(8,128)(2,1)S(1)}, bf16[2,1,192,512]{3,2,1,0:T(8,128)(2,1)S(1)}, u32[]{:S(2)}, u32[]{:S(2)}) collective-permute-start(bf16[2,1,192,512]{3,2,1,0:T(8,128)(2,1)S(1)} %get-tuple-element.90), channel_id=1, source_target_pairs={{1,0},{2,1},{3,2},{4,3},{5,4},{6,5},{7,6},{8,7},{9,8},{10,9},{11,1... | collective-permute-start | bytes 1179656 | tf_op jit(solution)/shard_map/ppermute | solution.py:86
  128.1 28.3 %collective-permute-start.31 = (f32[2,3,2,32,256]{4,3,2,1,0:T(8,128)S(1)}, f32[2,3,2,32,256]{4,3,2,1,0:T(8,128)S(1)}, u32[]{:S(2)}, u32[]{:S(2)}) collective-permute-start(f32[2,3,2,32,256]{4,3,2,1,0:T(8,128)S(1)} %get-tuple-element.78), channel_id=1, source_target_pairs={{0,64},{64,0},{128,192},{192,128},{16,208},{80,144},{144,80},{208,... | collective-permute-start | bytes 1179656 | tf_op jit(solution)/shard_map/ppermute | solution.py:35
  154.6 7.9 %collective-permute-start.28 = (f32[2,3,2,32,256]{4,3,2,1,0:T(8,128)S(1)}, f32[2,3,2,32,256]{4,3,2,1,0:T(8,128)S(1)}, u32[]{:S(2)}, u32[]{:S(2)}) collective-permute-start(f32[2,3,2,32,256]{4,3,2,1,0:T(8,128)S(1)} %get-tuple-element.76), channel_id=1, source_target_pairs={{0,1},{1,0},{2,3},{3,2},{16,19},{17,18},{18,17},{19,16},{4,5},{5,4... | collective-permute-start | bytes 1179656 | tf_op jit(solution)/shard_map/ppermute | solution.py:35
  156.4 6.3 %collective-permute-start.32 = (f32[3,2,32,256]{3,2,1,0:T(8,128)S(1)}, f32[3,2,32,256]{3,2,1,0:T(8,128)S(1)}, u32[]{:S(2)}, u32[]{:S(2)}) collective-permute-start(f32[3,2,32,256]{3,2,1,0:T(8,128)S(1)} %fusion.2), channel_id=1, source_target_pairs={{0,192},{64,128},{128,64},{192,0},{16,80},{80,16},{144,208},{208,1... | collective-permute-start | bytes 589832 | tf_op jit(solution)/shard_map/ppermute | solution.py:35
  162.6 4.6 %collective-permute-start.29 = (f32[3,2,32,256]{3,2,1,0:T(8,128)S(1)}, f32[3,2,32,256]{3,2,1,0:T(8,128)S(1)}, u32[]{:S(2)}, u32[]{:S(2)}) collective-permute-start(f32[3,2,32,256]{3,2,1,0:T(8,128)S(1)} %fusion.6), channel_id=1, source_target_pairs={{0,3},{1,2},{2,1},{3,0},{16,17},{17,16},{18,19},{19,18},{4,7},{5,6... | collective-permute-start | bytes 589832 | tf_op jit(solution)/shard_map/ppermute | solution.py:35
  191.7 6.9 %collective-permute-start.33 = (f32[8,3,16,256]{3,2,1,0:T(8,128)S(1)}, f32[8,3,16,256]{3,2,1,0:T(8,128)S(1)}, u32[]{:S(2)}, u32[]{:S(2)}) collective-permute-start(f32[8,3,16,256]{3,2,1,0:T(8,128)S(1)} %all_to_all.11), channel_id=1, source_target_pairs={{0,16},{16,0},{1,17},{17,1},{2,18},{18,2},{3,19},{19,3},{4,20},{20... | collective-permute-start | bytes 1179656 | tf_op jit(solution)/shard_map/ppermute | solution.py:22
